TPU v7x, 32 devices: a whole 2x2x4 slice. The times are simulated.
32 devices in a mesh: dp: 4 (over y, x), seq: 8 (over z, core).
Axes of the slice: x: 2, y: 2, z: 4, core: 2. Of those that a mesh axis runs over, the one named last changes fastest.
Arguments:
- layer_input: bfloat16 [4, 1024, 2048], P('dp', 'seq'), may hold values from -6 to 6
- doc_lengths: int32 [4, 8], P('dp'), may hold values from 1 to 960, 1024 in all within a row
- language: int32 [4], P('dp'), may hold values from 0 to 6
- lang_table: bfloat16 [7, 2048], P(None, ('dp', 'seq')), may hold values from -3 to 3
- attn_norm_gain: bfloat16 [2048], P(('dp', 'seq')), may hold values from 0.5 to 1.5
- attn_norm_bias: bfloat16 [2048], P(('dp', 'seq')), may hold values from -3 to 3
- qkv_weight: bfloat16 [2048, 6144], P(('dp', 'seq')), may hold values from -0.125 to 0.125
- qkv_bias: bfloat16 [3, 2048], P(None, ('dp', 'seq')), may hold values from -0.119628906 to 0.119628906
- out_weight: bfloat16 [2048, 2048], P(('dp', 'seq')), may hold values from -2 to 2
- mlp_norm_gain: bfloat16 [2048], P(('dp', 'seq')), may hold values from 0.5 to 1.5
- mlp_norm_bias: bfloat16 [2048], P(('dp', 'seq')), may hold values from -3 to 3
- gate_weight: bfloat16 [2048, 5632], P(None, ('dp', 'seq')), may hold values from -0.125 to 0.125
- up_weight: bfloat16 [2048, 5632], P(None, ('dp', 'seq')), may hold values from -0.125 to 0.125
- down_weight: bfloat16 [5632, 2048], P(('dp', 'seq')), may hold values from -0.078125 to 0.078125
- cotangent: bfloat16 [4, 1024, 2048], P('dp', 'seq'), may hold values from -6 to 6
Outputs:
- layer_output: bfloat16 [4, 1024, 2048], P('dp', 'seq')
- grad_input: float32 [4, 1024, 2048], P('dp', 'seq')
- grad_lang_table: float32 [7, 2048], P(None, ('dp', 'seq'))
- grad_attn_norm_gain: float32 [2048], P(('dp', 'seq'))
- grad_attn_norm_bias: float32 [2048], P(('dp', 'seq'))
- grad_qkv_weight: float32 [2048, 6144], P(('dp', 'seq'))
- grad_qkv_bias: float32 [3, 2048], P(None, ('dp', 'seq'))
- grad_out_weight: float32 [2048, 2048], P(('dp', 'seq'))
- grad_mlp_norm_gain: float32 [2048], P(('dp', 'seq'))
- grad_mlp_norm_bias: float32 [2048], P(('dp', 'seq'))
- grad_gate_weight: float32 [2048, 5632], P(None, ('dp', 'seq'))
- grad_up_weight: float32 [2048, 5632], P(None, ('dp', 'seq'))
- grad_down_weight: float32 [5632, 2048], P(('dp', 'seq'))
Inputs may be any that keep to these rules, and one draw needn't show every extreme that they name: `doc_lengths`: in each row the 8 lengths sum to 1024, and the longest is exactly 960.
All inputs are finite; a program needn't handle non-finite values.
Results may differ from a plain program's by a relative error of at most 0.015.
Values may be sent and summed in bfloat16 or wider, within the bound.
No kernel may reach another device: no remote copies, remote signals or barrier semaphores. Data moves between devices by JAX's collectives and lax.ppermute only.
A program may use at most 256 MiB of HBM per device.

v0:
```python
import jax
import jax.numpy as jnp
from jax import lax
from jax.sharding import PartitionSpec as P

D = 2048
HEADS = 32
HEAD = 64
ROT = 16
LANGS = 7


EPS = 1e-05
BASE = 10000.0
NEG = -1e30


def contract(left, right, left_dim, right_dim):
    return lax.dot_general(
        left, right, (((left_dim,), (right_dim,)), ((), ())), preferred_element_type=jnp.float32
    )


def norm_forward(values, gain, bias):
    average = jnp.mean(values, axis=-1, keepdims=True)
    centered = values - average
    variance = jnp.mean(centered * centered, axis=-1, keepdims=True)
    inverse = lax.rsqrt(variance + EPS)
    scaled = centered * inverse
    return (scaled * gain + bias, scaled, inverse)


def norm_backward(grad_normed, scaled, inverse, gain):
    grad_scaled = grad_normed * gain
    grad_values = inverse * (
        grad_scaled
        - jnp.mean(grad_scaled, axis=-1, keepdims=True)
        - scaled * jnp.mean(grad_scaled * scaled, axis=-1, keepdims=True)
    )
    return (grad_values, jnp.sum(grad_normed * scaled, axis=0), jnp.sum(grad_normed, axis=0))


def row_tables(doc_lengths, length):
    ends = jnp.cumsum(doc_lengths)
    starts = ends - doc_lengths
    places = jnp.arange(length, dtype=jnp.int32)
    segment = jnp.sum((places[:, None] >= ends[None, :]).astype(jnp.int32), axis=1)
    member = segment[:, None] == jnp.arange(ends.shape[0], dtype=jnp.int32)[None, :]
    offsets = jnp.sum(jnp.where(member, starts[None, :], 0), axis=1)
    position = (places - offsets).astype(jnp.float32)
    half_rot = ROT // 2
    freq = BASE ** (-(2.0 * jnp.arange(half_rot, dtype=jnp.float32)) / ROT)
    angles = position[:, None] * freq[None, :]
    return (segment, jnp.cos(angles), jnp.sin(angles))


def rotate(values, cosines, sines, direction):
    half_rot = ROT // 2
    former = values[..., :half_rot]
    latter = values[..., half_rot:ROT]
    cos_part = cosines[:, None, :]
    sin_part = direction * sines[:, None, :]
    return jnp.concatenate(
        [
            former * cos_part - latter * sin_part,
            latter * cos_part + former * sin_part,
            values[..., ROT:],
        ],
        axis=-1,
    )


def block_scores(query_block, key_heads, segment, index_query, index_key, block_rows):
    key_block = lax.dynamic_slice_in_dim(key_heads, index_key * block_rows, block_rows, 0)
    raw = jnp.einsum(
        "qhd,khd->hqk", query_block, key_block, preferred_element_type=jnp.float32
    ) * HEAD ** (-0.5)
    query_seg = lax.dynamic_slice_in_dim(segment, index_query * block_rows, block_rows, 0)
    key_seg = lax.dynamic_slice_in_dim(segment, index_key * block_rows, block_rows, 0)
    offsets = jnp.arange(block_rows, dtype=jnp.int32)
    allowed = (query_seg[:, None] == key_seg[None, :]) & (
        index_key * block_rows + offsets[None, :] <= index_query * block_rows + offsets[:, None]
    )
    allowed = allowed[None]
    return (jnp.where(allowed, raw, NEG), allowed, key_block)


def attention_forward(queries, key_heads, value_heads, segment):
    length, heads_here = (queries.shape[0], queries.shape[1])
    block_rows = min(512, length)

    def per_block(index_query):
        query_block = lax.dynamic_slice_in_dim(queries, index_query * block_rows, block_rows, 0)

        def gather_stats(index_key, carry):
            running, denominator = carry
            masked, allowed, unused = block_scores(
                query_block, key_heads, segment, index_query, index_key, block_rows
            )
            newest = jnp.maximum(running, jnp.max(masked, axis=-1))
            denominator = denominator * jnp.exp(running - newest) + jnp.sum(
                jnp.where(allowed, jnp.exp(masked - newest[..., None]), 0.0), axis=-1
            )
            return (newest, denominator)

        initial = (
            jnp.full((heads_here, block_rows), NEG, jnp.float32),
            jnp.zeros((heads_here, block_rows), jnp.float32),
        )
        running, denominator = lax.fori_loop(0, index_query + 1, gather_stats, initial)
        logsum = running + jnp.log(denominator)

        def weigh(index_key, accumulated):
            masked, allowed, unused = block_scores(
                query_block, key_heads, segment, index_query, index_key, block_rows
            )
            probabilities = jnp.where(allowed, jnp.exp(masked - logsum[..., None]), 0.0).astype(
                jnp.bfloat16
            )
            value_block = lax.dynamic_slice_in_dim(
                value_heads, index_key * block_rows, block_rows, 0
            )
            return accumulated + jnp.einsum(
                "hqk,khd->qhd", probabilities, value_block, preferred_element_type=jnp.float32
            )

        accumulated = lax.fori_loop(
            0, index_query + 1, weigh, jnp.zeros((block_rows, heads_here, HEAD), jnp.float32)
        )
        return (accumulated, logsum)

    context, logsum = lax.map(per_block, jnp.arange(length // block_rows, dtype=jnp.int32))
    return (context.reshape(length, heads_here, HEAD), logsum)


def attention_backward(queries, key_heads, value_heads, segment, context, logsum, grad_context):
    length, heads_here = (queries.shape[0], queries.shape[1])
    block_rows = min(512, length)
    deltas = jnp.sum(grad_context.astype(jnp.float32) * context, axis=-1)
    zeros_all = jnp.zeros((length, heads_here, HEAD), jnp.float32)

    def per_query(index_query, carry):
        grad_queries, grad_keys, grad_values = carry
        query_block = lax.dynamic_slice_in_dim(queries, index_query * block_rows, block_rows, 0)
        grad_block = lax.dynamic_slice_in_dim(grad_context, index_query * block_rows, block_rows, 0)
        delta_block = lax.dynamic_slice_in_dim(deltas, index_query * block_rows, block_rows, 0).T
        logsum_block = logsum[index_query]

        def per_key(index_key, inner):
            grad_query, grad_keys, grad_values = inner
            masked, allowed, key_block = block_scores(
                query_block, key_heads, segment, index_query, index_key, block_rows
            )
            soft = jnp.where(allowed, jnp.exp(masked - logsum_block[..., None]), 0.0)
            value_block = lax.dynamic_slice_in_dim(
                value_heads, index_key * block_rows, block_rows, 0
            )
            grad_soft = jnp.einsum(
                "qhd,khd->hqk", grad_block, value_block, preferred_element_type=jnp.float32
            )
            grad_scores = (soft * (grad_soft - delta_block[..., None])).astype(jnp.bfloat16)
            grad_query = grad_query + jnp.einsum(
                "hqk,khd->qhd", grad_scores, key_block, preferred_element_type=jnp.float32
            ) * HEAD ** (-0.5)
            key_part = jnp.einsum(
                "hqk,qhd->khd", grad_scores, query_block, preferred_element_type=jnp.float32
            ) * HEAD ** (-0.5)
            value_part = jnp.einsum(
                "hqk,qhd->khd",
                soft.astype(jnp.bfloat16),
                grad_block,
                preferred_element_type=jnp.float32,
            )
            offset = index_key * block_rows
            grad_keys = lax.dynamic_update_slice_in_dim(
                grad_keys,
                lax.dynamic_slice_in_dim(grad_keys, offset, block_rows, 0) + key_part,
                offset,
                0,
            )
            grad_values = lax.dynamic_update_slice_in_dim(
                grad_values,
                lax.dynamic_slice_in_dim(grad_values, offset, block_rows, 0) + value_part,
                offset,
                0,
            )
            return (grad_query, grad_keys, grad_values)

        initial = (jnp.zeros((block_rows, heads_here, HEAD), jnp.float32), grad_keys, grad_values)
        grad_query, grad_keys, grad_values = lax.fori_loop(0, index_query + 1, per_key, initial)
        grad_queries = lax.dynamic_update_slice_in_dim(
            grad_queries, grad_query, index_query * block_rows, 0
        )
        return (grad_queries, grad_keys, grad_values)

    return lax.fori_loop(0, length // block_rows, per_query, (zeros_all, zeros_all, zeros_all))


def gate_backward(gate_values, up_values, grad_hidden):
    sigmoid_gate = jax.nn.sigmoid(gate_values)
    silu_gate = gate_values * sigmoid_gate
    grad_gate = (
        grad_hidden * up_values * sigmoid_gate * (1.0 + gate_values * (1.0 - sigmoid_gate))
    ).astype(jnp.bfloat16)
    grad_up = (grad_hidden * silu_gate).astype(jnp.bfloat16)
    return (grad_gate, grad_up)


def per_device(
    layer_input,
    doc_lengths,
    language,
    lang_table,
    attn_norm_gain,
    attn_norm_bias,
    qkv_weight,
    qkv_bias,
    out_weight,
    mlp_norm_gain,
    mlp_norm_bias,
    gate_weight,
    up_weight,
    down_weight,
    cotangent,
):
    tokens = layer_input.shape[1]
    groups = lax.axis_size("seq")
    length = tokens * groups
    heads_here = HEADS // groups
    local_width = heads_here * HEAD
    segment, cosines, sines = row_tables(doc_lengths[0], length)
    chooser = (jnp.arange(LANGS, dtype=jnp.int32) == language[0]).astype(jnp.float32)
    params = (
        lax.all_gather(qkv_weight, ("dp", "seq"), axis=0, tiled=True),
        lax.all_gather(out_weight, ("dp", "seq"), axis=0, tiled=True),
        lax.all_gather(attn_norm_gain, ("dp", "seq"), axis=0, tiled=True),
        lax.all_gather(attn_norm_bias, ("dp", "seq"), axis=0, tiled=True),
        lax.all_gather(qkv_bias, ("dp", "seq"), axis=1, tiled=True),
        lax.all_gather(mlp_norm_gain, ("dp", "seq"), axis=0, tiled=True),
        lax.all_gather(mlp_norm_bias, ("dp", "seq"), axis=0, tiled=True),
        lax.all_gather(lang_table, ("dp", "seq"), axis=1, tiled=True),
    )
    full_qkv = params[0]
    full_out = params[1]
    gain_attn = params[2].astype(jnp.float32)
    bias_attn = params[3].astype(jnp.float32)
    bias_qkv = params[4].astype(jnp.float32).reshape(3 * D)
    gain_mlp = params[5].astype(jnp.float32)
    bias_mlp = params[6].astype(jnp.float32)
    lang_rows = params[7].astype(jnp.float32)
    resid_in = (
        layer_input[0].astype(jnp.float32) + jnp.sum(chooser[:, None] * lang_rows, axis=0)[None, :]
    )
    normed_attn, scaled_attn, inverse_attn = norm_forward(resid_in, gain_attn, bias_attn)
    normed_attn = normed_attn.astype(jnp.bfloat16)
    projected = (
        jnp.dot(normed_attn, full_qkv, preferred_element_type=jnp.float32) + bias_qkv
    ).astype(jnp.bfloat16)
    head_rows = lax.all_to_all(
        projected.reshape(tokens, 3, D), "seq", split_axis=2, concat_axis=0, tiled=True
    )
    rot_query = rotate(
        head_rows[:, 0].reshape(length, heads_here, HEAD).astype(jnp.float32), cosines, sines, 1.0
    ).astype(jnp.bfloat16)
    rot_key = rotate(
        head_rows[:, 1].reshape(length, heads_here, HEAD).astype(jnp.float32), cosines, sines, 1.0
    ).astype(jnp.bfloat16)
    value_heads = head_rows[:, 2].reshape(length, heads_here, HEAD)
    context, logsum = attention_forward(rot_query, rot_key, value_heads, segment)
    context_tokens = lax.all_to_all(
        context.astype(jnp.bfloat16).reshape(length, local_width),
        "seq",
        split_axis=0,
        concat_axis=1,
        tiled=True,
    )
    resid_mid = resid_in + jnp.dot(context_tokens, full_out, preferred_element_type=jnp.float32)
    normed_mlp, scaled_mlp, inverse_mlp = norm_forward(resid_mid, gain_mlp, bias_mlp)
    normed_mlp = normed_mlp.astype(jnp.bfloat16)
    grad_out = cotangent[0]
    cols_gate, cols_up, cols_down = (
        lax.all_gather(gate_weight, "dp", axis=1, tiled=True),
        lax.all_gather(up_weight, "dp", axis=1, tiled=True),
        lax.all_gather(down_weight, "dp", axis=0, tiled=True),
    )
    rows_all = lax.all_gather(normed_mlp, "seq", axis=0, tiled=True)
    gate_values = jnp.dot(rows_all, cols_gate, preferred_element_type=jnp.float32)
    up_values = jnp.dot(rows_all, cols_up, preferred_element_type=jnp.float32)
    hidden = (jax.nn.silu(gate_values) * up_values).astype(jnp.bfloat16)
    mlp_out = lax.psum_scatter(
        jnp.dot(hidden, cols_down, preferred_element_type=jnp.float32).astype(jnp.bfloat16),
        "seq",
        scatter_dimension=0,
        tiled=True,
    ).astype(jnp.float32)
    grad_all = lax.all_gather(grad_out, "seq", axis=0, tiled=True)
    grad_hidden = contract(grad_all, cols_down, 1, 1)
    grad_gate, grad_up = gate_backward(gate_values, up_values, grad_hidden)
    grad_rows = contract(grad_gate, cols_gate, 1, 1) + contract(grad_up, cols_up, 1, 1)
    grad_normed_mlp = lax.psum_scatter(
        grad_rows.astype(jnp.bfloat16), "seq", scatter_dimension=0, tiled=True
    ).astype(jnp.float32)
    out_gate, out_up, out_down = (
        lax.psum_scatter(
            contract(rows_all, grad_gate, 0, 0).astype(jnp.bfloat16),
            "dp",
            scatter_dimension=1,
            tiled=True,
        ).astype(jnp.float32),
        lax.psum_scatter(
            contract(rows_all, grad_up, 0, 0).astype(jnp.bfloat16),
            "dp",
            scatter_dimension=1,
            tiled=True,
        ).astype(jnp.float32),
        lax.psum_scatter(
            contract(hidden, grad_all, 0, 0).astype(jnp.bfloat16),
            "dp",
            scatter_dimension=0,
            tiled=True,
        ).astype(jnp.float32),
    )
    layer_output = (resid_mid + mlp_out).astype(jnp.bfloat16)
    grad_mid_norm, grad_gain_mlp, grad_bias_mlp = norm_backward(
        grad_normed_mlp, scaled_mlp, inverse_mlp, gain_mlp
    )
    grad_mid = grad_out.astype(jnp.float32) + grad_mid_norm
    grad_branch = grad_mid.astype(jnp.bfloat16)
    grad_out_w = contract(context_tokens, grad_branch, 0, 0)
    grad_context = contract(grad_branch, full_out, 1, 1).astype(jnp.bfloat16)
    grad_heads = lax.all_to_all(
        grad_context, "seq", split_axis=1, concat_axis=0, tiled=True
    ).reshape(length, heads_here, HEAD)
    grad_queries, grad_keys, grad_values = attention_backward(
        rot_query, rot_key, value_heads, segment, context, logsum, grad_heads
    )
    grad_query_raw = rotate(grad_queries, cosines, sines, -1.0).reshape(length, local_width)
    grad_key_raw = rotate(grad_keys, cosines, sines, -1.0).reshape(length, local_width)
    grad_stack = jnp.stack(
        [grad_query_raw, grad_key_raw, grad_values.reshape(length, local_width)], axis=1
    ).astype(jnp.bfloat16)
    grad_projected = lax.all_to_all(
        grad_stack, "seq", split_axis=0, concat_axis=2, tiled=True
    ).reshape(tokens, 3 * D)
    grad_bias_qkv = jnp.sum(grad_projected.astype(jnp.float32), axis=0).reshape(3, D)
    grad_normed_attn = contract(grad_projected, full_qkv, 1, 1)
    grad_in_norm, grad_gain_attn, grad_bias_attn = norm_backward(
        grad_normed_attn, scaled_attn, inverse_attn, gain_attn
    )
    grad_input = grad_mid + grad_in_norm
    grad_lang = chooser[:, None] * jnp.sum(grad_input, axis=0)[None, :]
    normed_all = lax.all_gather(normed_attn, "seq", axis=0, tiled=True)
    slice_terms = jnp.einsum(
        "td,tcw->dcw", normed_all, grad_stack, preferred_element_type=jnp.float32
    )
    slice_summed = lax.psum_scatter(
        slice_terms.astype(jnp.bfloat16), "dp", scatter_dimension=0, tiled=True
    ).astype(jnp.float32)
    grad_qkv_out = (
        lax.all_to_all(
            slice_summed.astype(jnp.bfloat16), "seq", split_axis=0, concat_axis=2, tiled=True
        )
        .astype(slice_summed.dtype)
        .reshape(-1, 3 * D)
    )
    small = (
        lax.psum_scatter(grad_out_w, ("dp", "seq"), scatter_dimension=0, tiled=True),
        lax.psum_scatter(grad_gain_attn, ("dp", "seq"), scatter_dimension=0, tiled=True),
        lax.psum_scatter(grad_bias_attn, ("dp", "seq"), scatter_dimension=0, tiled=True),
        lax.psum_scatter(grad_bias_qkv, ("dp", "seq"), scatter_dimension=1, tiled=True),
        lax.psum_scatter(grad_gain_mlp, ("dp", "seq"), scatter_dimension=0, tiled=True),
        lax.psum_scatter(grad_bias_mlp, ("dp", "seq"), scatter_dimension=0, tiled=True),
        lax.psum_scatter(grad_lang, ("dp", "seq"), scatter_dimension=1, tiled=True),
    )
    out_proj, gain_a, bias_a, bias_q, gain_m, bias_m, lang_g = small
    return (
        layer_output[None],
        grad_input[None],
        lang_g,
        gain_a,
        bias_a,
        grad_qkv_out,
        bias_q,
        out_proj,
        gain_m,
        bias_m,
        out_gate,
        out_up,
        out_down,
    )


def solution(mesh):
    placed = (
        P("dp", "seq", None),
        P("dp", None),
        P("dp"),
        P(None, ("dp", "seq")),
        P(("dp", "seq")),
        P(("dp", "seq")),
        P(("dp", "seq"), None),
        P(None, ("dp", "seq")),
        P(("dp", "seq"), None),
        P(("dp", "seq")),
        P(("dp", "seq")),
        P(None, ("dp", "seq")),
        P(None, ("dp", "seq")),
        P(("dp", "seq"), None),
        P("dp", "seq", None),
    )
    return jax.shard_map(
        per_device,
        mesh=mesh,
        in_specs=placed,
        out_specs=(
            P("dp", "seq", None),
            P("dp", "seq", None),
            P(None, ("dp", "seq")),
            P(("dp", "seq")),
            P(("dp", "seq")),
            P(("dp", "seq"), None),
            P(None, ("dp", "seq")),
            P(("dp", "seq"), None),
            P(("dp", "seq")),
            P(("dp", "seq")),
            P(None, ("dp", "seq")),
            P(None, ("dp", "seq")),
            P(("dp", "seq"), None),
        ),
        check_vma=False,
    )
```

profile of v0, /device:TPU:0, one launch (start us, length us, event | category | flops | bytes accessed | tf_op | source)
XLA Modules:
  0.0 1354.6 jit_solution(15594054687534446965)
XLA Ops:
  9.3 44.2 %all-gather.1 = bf16[32,64,7]{1,2,0:T(8,128)(2,1)S(1)} all-gather(bf16[1,64,7]{1,2,0:T(8,128)(2,1)} %bitcast.279), channel_id=1, replica_groups=mesh['dp'=4,'seq'=8] {'dp','seq'}, dimensions={0}, use_global_device_ids=true | all-gather | bytes 29568 | tf_op jit(solution)/shard_map/all_gather | solution.py:241
  57.0 38.8 %all-reduce.9 = (bf16[2048]{0:T(1024)(128)(2,1)S(1)}, bf16[2048]{0:T(1024)(128)(2,1)S(1)}, bf16[2048]{0:T(1024)(128)(2,1)}, bf16[2048]{0:T(1024)(128)(2,1)}) all-reduce(bf16[2048]{0:T(1024)(128)(2,1)S(1)} %dynamic-update-slice.1, bf16[2048]{0:T(1024)(128)(2,1)S(1)} %dynamic-update-slice, ...), channel_id=1, replica_groups=mesh['dp'=4,'seq'=8] {'dp','seq'}, use_global_device_ids=true, to_apply=%add.1 | all-reduce | flops 8192 | bytes 32768
  95.8 41.4 %all-gather.2 = bf16[32,64,3]{1,2,0:T(4,128)(2,1)S(1)} all-gather(bf16[1,64,3]{1,2,0:T(4,128)(2,1)} %bitcast.280), channel_id=1, replica_groups=mesh['dp'=4,'seq'=8] {'dp','seq'}, dimensions={0}, use_global_device_ids=true | all-gather | bytes 12672 | tf_op jit(solution)/shard_map/all_gather | solution.py:238
  140.6 29.6 %all-gather.12.cloned.1.call-done = bf16[2048,6144]{1,0:T(8,128)(2,1)} async-done(((bf16[64,6144]{1,0:T(8,128)(2,1)}), bf16[2048,6144]{1,0:T(8,128)(2,1)}) %all-gather.12.cloned.1.call-update) | async-done | bytes 25165840 | tf_op jit(solution)/shard_map/all_gather | solution.py:234
  170.2 11.6 fusion.51
  193.2 80.2 %all-to-all-done = bf16[128,3,2048]{0,1,2:T(4,128)(2,1)S(1)} async-done(((bf16[128,3,2048]{0,1,2:T(4,128)(2,1)}), bf16[128,3,2048]{0,1,2:T(4,128)(2,1)S(1)}, u32[]{:S(2)}, u32[]{:S(2)}) %all-to-all-start) | async-done | bytes 1572896 | tf_op jit(solution)/shard_map/all_to_all | solution.py:259
  284.2 22.1 %while.89 = (s32[]{:T(128)}, f32[2,512,4,64]{1,3,2,0:T(8,128)S(1)}, f32[2,4,512]{2,1,0:T(4,128)}, s32[2]{0:T(128)S(1)}, bf16[1024,4,64]{0,2,1:T(8,128)(2,1)S(1)}...) while((s32[]{:T(128)}, f32[2,512,4,64]{1,3,2,0:T(8,128)S(1)}, ...), condition=%wide.region_13.14_spmd, body=%wide.region_6.13_spmd.sunk | while | flops 417996800 | bytes 14489545 | solution.py:132
  314.1 15.2 %all-to-all-done.1 = bf16[8,128,256]{1,2,0:T(8,128)(2,1)S(1)} async-done(((bf16[8,128,256]{1,2,0:T(8,128)(2,1)}), bf16[8,128,256]{1,2,0:T(8,128)(2,1)S(1)}, u32[]{:S(2)}, u32[]{:S(2)}) %all-to-all-start.1) | async-done | bytes 524320 | tf_op jit(solution)/shard_map/all_to_all | solution.py:270
  338.1 42.8 %all-gather.16.cloned.1.call-done = bf16[1024,2048]{1,0:T(8,128)(2,1)} async-done(((bf16[128,2048]{1,0:T(8,128)(2,1)}), bf16[1024,2048]{1,0:T(8,128)(2,1)}) %all-gather.16.cloned.1.call-update) | async-done | bytes 4194320 | tf_op jit(solution)/shard_map/all_gather | solution.py:286
  380.9 7.8 fusion.100
  388.7 34.4 %all-gather.18.cloned.1.call-done = bf16[2048,704]{0,1:T(8,128)(2,1)} async-done(((bf16[2048,176]{0,1:T(8,128)(2,1)}), bf16[2048,704]{0,1:T(8,128)(2,1)}) %all-gather.18.cloned.1.call-update) | async-done | bytes 2883600 | tf_op jit(solution)/shard_map/all_gather | solution.py:282
  423.1 7.9 fusion.99
  431.0 35.7 %all-gather.22.cloned.1.call-done = bf16[704,2048]{1,0:T(8,128)(2,1)} async-done(((bf16[176,2048]{1,0:T(8,128)(2,1)}), bf16[704,2048]{1,0:T(8,128)(2,1)}) %all-gather.22.cloned.1.call-update) | async-done | bytes 2883600 | tf_op jit(solution)/shard_map/all_gather | solution.py:284
  466.6 48.8 %all-gather.26.cloned.1.call-done = bf16[1,1024,2048]{2,1,0:T(8,128)(2,1)} async-done(((bf16[1,128,2048]{2,1,0:T(8,128)(2,1)}), bf16[1,1024,2048]{2,1,0:T(8,128)(2,1)}) %all-gather.26.cloned.1.call-update) | async-done | bytes 4194320 | tf_op jit(solution)/shard_map/all_gather | solution.py:296
  515.4 10.1 multiply_convert_fusion
  534.6 7.7 convolution_convert_fusion
  542.3 41.1 %reduce-scatter.16.cloned.1.call-done = bf16[128,2048]{1,0:T(8,128)(2,1)} async-done(((bf16[1024,2048]{1,0:T(8,128)(2,1)}), bf16[128,2048]{1,0:T(8,128)(2,1)}) %reduce-scatter.16.cloned.1.call-update) | async-done | bytes 524304 | tf_op jit(solution)/shard_map/reduce_scatter | solution.py:300
  585.6 48.3 %reduce-scatter.14.cloned.1.call-done = bf16[128,2048]{1,0:T(8,128)(2,1)} async-done(((bf16[1024,2048]{1,0:T(8,128)(2,1)}), bf16[128,2048]{1,0:T(8,128)(2,1)}) %reduce-scatter.14.cloned.1.call-update) | async-done | bytes 524304 | tf_op jit(solution)/shard_map/reduce_scatter | solution.py:290
  649.0 14.8 %all-to-all-done.2 = bf16[128,8,256]{0,2,1:T(8,128)(2,1)S(1)} async-done(((bf16[128,8,256]{0,2,1:T(8,128)(2,1)}), bf16[128,8,256]{0,2,1:T(8,128)(2,1)S(1)}, u32[]{:S(2)}, u32[]{:S(2)}) %all-to-all-start.2) | async-done | bytes 524320 | tf_op jit(solution)/shard_map/all_to_all | solution.py:331
  674.4 26.5 %while.91 = (s32[]{:T(128)}, f32[1024,4,64]{0,2,1:T(8,128)}, f32[1024,4,64]{0,2,1:T(8,128)S(1)}, f32[1024,4,64]{0,2,1:T(8,128)}, bf16[1024,4,64]{0,2,1:T(8,128)(...) while((s32[]{:T(128)}, f32[1024,4,64]{0,2,1:T(8,128)}, ...), condition=%wide.region_24.25_spmd, body=%wide.region_21.24_spmd.sunk | while | flops 685114368 | bytes 29438628 | solution.py:196
  675.8 7.5 while.94
  685.2 14.9 %while.94 = (s32[]{:T(128)}, f32[512,4,64]{0,2,1:T(8,128)S(1)}, f32[1024,4,64]{0,2,1:T(8,128)S(1)}, f32[1024,4,64]{0,2,1:T(8,128)}, s32[]{:T(128)}, /*index=5*/b...) while((s32[]{:T(128)}, f32[512,4,64]{0,2,1:T(8,128)S(1)}, ...), condition=%wide.region_23.23_spmd, body=%wide.region_22.22_spmd.sunk | while | flops 685114368 | bytes 26779920 | solution.py:190
  705.3 7.4 fusion.58
  739.3 52.9 %all_to_all.74 = bf16[1024,3,256]{2,1,0:T(4,128)(2,1)S(1)} all-to-all(bf16[1024,3,256]{2,1,0:T(4,128)(2,1)S(1)} %copy.210), channel_id=1, replica_groups=mesh['dp'=4,'seq'=8] {'seq'}, dimensions={0} | all-to-all | bytes 3145728 | tf_op jit(solution)/shard_map/all_to_all | solution.py:342
  797.2 14.5 %fusion.87 = (f32[2048]{0:T(1024)S(1)}, f32[128]{0:T(128)S(1)}, f32[128]{0:T(128)S(1)}, f32[2048]{0:T(1024)S(1)}, f32[128,2048]{1,0:T(8,128)}) fusion(bf16[1,128,2048]{2,1,0:T(8,128)(2,1)S(1)} %copy-done.2, f32[128]{0:T(128)S(1)} %copy-done.28, f32[128]{0:T(128)S(1)} %copy-done.26, f32[2048]{0:T(1024)S(1)} %copy-done.15, f32[2048]{0:T(1024)S(1)} %copy-done.18, ...), kind=kOutput, calls=%fused_computation.118 | convolution fusion | flops 3224104960 | bytes 28346368 | tf_op jit(solution)/shard_map/dot_general | solution.py:19
  816.0 8.4 fusion.91
  833.3 13.2 reduce-scatter.24.cloned.1.call-done
  848.9 42.3 %reduce-scatter.26.cloned.1.call-done = bf16[176,2048]{1,0:T(8,128)(2,1)} async-done(((bf16[704,2048]{1,0:T(8,128)(2,1)}), bf16[176,2048]{1,0:T(8,128)(2,1)}) %reduce-scatter.26.cloned.1.call-update) | async-done | bytes 720912 | tf_op jit(solution)/shard_map/reduce_scatter | solution.py:316
  893.6 40.0 %all-reduce.8 = (f32[2048]{0:T(1024)S(1)}, f32[2048]{0:T(1024)S(1)}, f32[2048]{0:T(1024)S(1)}, f32[2048]{0:T(1024)S(1)}) all-reduce(f32[2048]{0:T(1024)S(1)} %get-tuple-element.691, f32[2048]{0:T(1024)S(1)} %get-tuple-element.696, f32[2048]{0:T(1024)S(1)} %copy-done.23, ...), channel_id=6, replica_groups=mesh['dp'=4,'seq'=8] {'dp','seq'}, use_global_device_ids=true, to_apply=%region_30.31.clone | all-reduce | flops 8192 | bytes 65536
  935.9 92.4 %reduce-scatter.30.cloned.1.call-done = f32[64,3]{1,0:T(8,128)} async-done(((f32[2048,3]{1,0:T(8,128)}), f32[64,3]{1,0:T(8,128)}) %reduce-scatter.30.cloned.1.call-update) | async-done | bytes 784
  1029.7 132.5 %reduce-scatter.28.cloned.1.call-done = f32[64,7]{1,0:T(8,128)} async-done(((f32[2048,7]{1,0:T(8,128)}), f32[64,7]{1,0:T(8,128)}) %reduce-scatter.28.cloned.1.call-update) | async-done | bytes 1808
  1166.4 181.4 %reduce-scatter.20.cloned.1.call-done = f32[64,2048]{1,0:T(8,128)} async-done(((f32[2048,2048]{1,0:T(8,128)}), f32[64,2048]{1,0:T(8,128)}) %reduce-scatter.20.cloned.1.call-update) | async-done | bytes 524304 | tf_op jit(solution)/shard_map/reduce_scatter | solution.py:367
  (336 shorter events, 206.8 us)
Async XLA Ops:
  7.2 132.9 %copy-start = (bf16[1,128,2048]{2,1,0:T(8,128)(2,1)S(1)}, bf16[1,128,2048]{2,1,0:T(8,128)(2,1)}, u32[]{:S(2)}) copy-start(bf16[1,128,2048]{2,1,0:T(8,128)(2,1)} %param.25) | copy-start | bytes 1572868
  7.2 163.0 %all-gather.12.cloned.1.call-start = ((), (), s32[]{:S(2)}) async-start(), calls=%async_computation.14 | async-start | bytes 25952256 | tf_op jit(solution)/shard_map/all_gather | solution.py:234
  7.9 306.1 %all-gather.14.cloned.1.call-start = ((), (), s32[]{:S(2)}) async-start(), calls=%async_computation.15 | async-start | bytes 8650752 | tf_op jit(solution)/shard_map/all_gather | solution.py:235
  95.8 44.6 %copy-start.17 = (f32[2048]{0:T(1024)}, f32[2048]{0:T(1024)S(1)}, u32[]{:S(2)}) copy-start(f32[2048]{0:T(1024)S(1)} %convert_element_type.170) | copy-start | bytes 24580
  138.7 43.1 %copy-start.25 = (f32[128]{0:T(128)}, f32[128]{0:T(128)S(1)}, u32[]{:S(2)}) copy-start(f32[128]{0:T(128)S(1)} %broadcast_multiply_fusion.7) | copy-start | bytes 1540
  140.3 41.5 %copy-start.7 = (bf16[128,2048]{1,0:T(8,128)(2,1)}, bf16[128,2048]{1,0:T(8,128)(2,1)S(1)}, u32[]{:S(2)}) copy-start(bf16[128,2048]{1,0:T(8,128)(2,1)S(1)} %fusion.82) | copy-start | bytes 1572868
  187.5 85.9 %all-to-all-start = ((bf16[128,3,2048]{0,1,2:T(4,128)(2,1)}), bf16[128,3,2048]{0,1,2:T(4,128)(2,1)S(1)}, u32[]{:S(2)}, u32[]{:S(2)}) async-start(bf16[128,3,2048]{0,1,2:T(4,128)(2,1)} %copy.195), calls=%async_computation | async-start | bytes 4194304 | tf_op jit(solution)/shard_map/all_to_all | solution.py:259
  191.3 146.8 %all-gather.20.cloned.1.call-start = ((), (), s32[]{:S(2)}) async-start(), calls=%async_computation.18 | async-start | bytes 3604480 | tf_op jit(solution)/shard_map/all_gather | solution.py:283
  307.3 21.9 %copy-start.1 = (bf16[1,128,2048]{2,1,0:T(8,128)(2,1)S(1)}, bf16[1,128,2048]{2,1,0:T(8,128)(2,1)}, u32[]{:S(2)}) copy-start(bf16[1,128,2048]{2,1,0:T(8,128)(2,1)} %param.25) | copy-start | bytes 1572868
  307.3 21.9 %copy-start.14 = (f32[2048]{0:T(1024)S(1)}, f32[2048]{0:T(1024)}, u32[]{:S(2)}) copy-start(f32[2048]{0:T(1024)} %copy-done.13) | copy-start | bytes 24580
  310.4 18.8 %all-to-all-start.1 = ((bf16[8,128,256]{1,2,0:T(8,128)(2,1)}), bf16[8,128,256]{1,2,0:T(8,128)(2,1)S(1)}, u32[]{:S(2)}, u32[]{:S(2)}) async-start(bf16[8,128,256]{1,2,0:T(8,128)(2,1)} %copy.202), calls=%async_computation.1 | async-start | bytes 1048576 | tf_op jit(solution)/shard_map/all_to_all | solution.py:270
  313.9 66.9 %all-gather.16.cloned.1.call-start = ((), (), s32[]{:S(2)}) async-start(), calls=%async_computation.16 | async-start | bytes 4718592 | tf_op jit(solution)/shard_map/all_gather | solution.py:286
  335.5 87.6 %all-gather.18.cloned.1.call-start = ((), (), s32[]{:S(2)}) async-start(), calls=%async_computation.17 | async-start | bytes 3604480 | tf_op jit(solution)/shard_map/all_gather | solution.py:282
  336.1 130.5 %all-gather.22.cloned.1.call-start = ((), (), s32[]{:S(2)}) async-start(), calls=%async_computation.19 | async-start | bytes 3604480 | tf_op jit(solution)/shard_map/all_gather | solution.py:284
  336.7 178.7 %all-gather.26.cloned.1.call-start = ((), (), s32[]{:S(2)}) async-start(), calls=%async_computation.28 | async-start | bytes 4718592 | tf_op jit(solution)/shard_map/all_gather | solution.py:296
  337.5 246.0 %reduce-scatter.16.cloned.1.call-start = ((), (), s32[]{:S(2)}) async-start(), calls=%async_computation.21 | async-start | bytes 4718592 | tf_op jit(solution)/shard_map/reduce_scatter | solution.py:300
  534.6 99.3 %reduce-scatter.14.cloned.1.call-start = ((), (), s32[]{:S(2)}) async-start(), calls=%async_computation.20 | async-start | bytes 4718592 | tf_op jit(solution)/shard_map/reduce_scatter | solution.py:290
  542.3 91.6 %copy-start.11 = (bf16[1,128,2048]{2,1,0:T(8,128)(2,1)S(1)}, bf16[1,128,2048]{2,1,0:T(8,128)(2,1)}, u32[]{:S(2)}) copy-start(bf16[1,128,2048]{2,1,0:T(8,128)(2,1)} %param.39) | copy-start | bytes 1572868
  644.8 19.0 %all-to-all-start.2 = ((bf16[128,8,256]{0,2,1:T(8,128)(2,1)}), bf16[128,8,256]{0,2,1:T(8,128)(2,1)S(1)}, u32[]{:S(2)}, u32[]{:S(2)}) async-start(bf16[128,8,256]{0,2,1:T(8,128)(2,1)} %bitcast.37), calls=%async_computation.4 | async-start | bytes 1048576 | tf_op jit(solution)/shard_map/all_to_all | solution.py:331
  648.3 56.9 %all-gather.24.cloned.1.call-start = ((), (), s32[]{:S(2)}) async-start(), calls=%async_computation.22 | async-start | bytes 4718592 | tf_op jit(solution)/shard_map/all_gather | solution.py:352
  648.9 175.6 %reduce-scatter.18.cloned.1.call-start = ((), (), s32[]{:S(2)}) async-start(), calls=%async_computation.23 | async-start | bytes 3932160 | tf_op jit(solution)/shard_map/reduce_scatter | solution.py:356
  674.4 27.8 %copy-start.16 = (f32[1024,8]{0,1:T(8,128)S(1)}, f32[1024,8]{0,1:T(8,128)}, u32[]{:S(2)}) copy-start(f32[1024,8]{0,1:T(8,128)} %get-tuple-element.849) | copy-start | bytes 98308
  674.4 27.8 %copy-start.19 = (f32[1024,8]{0,1:T(8,128)S(1)}, f32[1024,8]{0,1:T(8,128)}, u32[]{:S(2)}) copy-start(f32[1024,8]{0,1:T(8,128)} %get-tuple-element.847) | copy-start | bytes 98308
  712.7 118.2 %reduce-scatter.22.cloned.1.call-start = ((), (), s32[]{:S(2)}) async-start(), calls=%async_computation.25 | async-start | bytes 3604480 | tf_op jit(solution)/shard_map/reduce_scatter | solution.py:304
  720.8 125.8 %reduce-scatter.24.cloned.1.call-start = ((), (), s32[]{:S(2)}) async-start(), calls=%async_computation.26 | async-start | bytes 3604480 | tf_op jit(solution)/shard_map/reduce_scatter | solution.py:310
  728.9 162.4 %reduce-scatter.26.cloned.1.call-start = ((), (), s32[]{:S(2)}) async-start(), calls=%async_computation.27 | async-start | bytes 3604480 | tf_op jit(solution)/shard_map/reduce_scatter | solution.py:316
  737.7 290.6 %reduce-scatter.30.cloned.1.call-start = ((), (), s32[]{:S(2)}) async-start(), calls=%async_computation.30 | async-start | bytes 1081344
  811.7 350.5 %reduce-scatter.28.cloned.1.call-start = ((), (), s32[]{:S(2)}) async-start(), calls=%async_computation.29 | async-start | bytes 1081344
  816.0 531.9 %reduce-scatter.20.cloned.1.call-start = ((), (), s32[]{:S(2)}) async-start(), calls=%async_computation.24 | async-start | bytes 17301504 | tf_op jit(solution)/shard_map/reduce_scatter | solution.py:367
  827.3 336.3 %all-to-all-start.4 = ((bf16[512,3,256]{2,1,0:T(4,128)(2,1)}), bf16[512,3,256]{2,1,0:T(4,128)(2,1)S(1)}, u32[]{:S(2)}, u32[]{:S(2)}) async-start(bf16[512,3,256]{2,1,0:T(4,128)(2,1)} %copy.214), calls=%async_computation.7 | async-start | bytes 2097152 | tf_op jit(solution)/shard_map/all_to_all | solution.py:360
  830.9 62.7 %copy-start.23 = (f32[2048]{0:T(1024)S(1)}, f32[2048]{0:T(1024)}, u32[]{:S(2)}) copy-start(f32[2048]{0:T(1024)} %get-tuple-element.693) | copy-start | bytes 24580
  830.9 62.7 %copy-start.24 = (f32[2048]{0:T(1024)S(1)}, f32[2048]{0:T(1024)}, u32[]{:S(2)}) copy-start(f32[2048]{0:T(1024)} %get-tuple-element.698) | copy-start | bytes 24580
  (34 other events, 134.4 us)
Sparse Core Ops, SparseCore 0:
  11.0 159.1 all-gather.11
  173.2 102.9 all-gather.13
  278.0 39.9 all-gather.19
  335.7 45.1 all-gather.15
  382.5 40.5 all-gather.17
  424.8 41.7 all-gather.21
  468.2 47.1 all-gather.25
  534.7 48.7 reduce-scatter.15
  585.8 48.1 reduce-scatter.13
  650.5 48.6 all-gather.23
  712.9 44.1 reduce-scatter.17
  760.0 41.7 reduce-scatter.21
  804.8 41.7 reduce-scatter.23
  849.5 41.7 reduce-scatter.25
  893.3 134.9 reduce-scatter.29
  1031.0 131.1 reduce-scatter.27
  1164.9 182.8 reduce-scatter.19
where the time goes:
time: 1360 us; the launch traced here: 1350 us
  waiting for transfers between devices  857 us (63%)
  blocking collectives  217 us (16%)
  matrix products  148 us (11%)
  local copies, waits for them, and re-layouts  59.3 us (4%)
  other arithmetic  37.8 us (3%)
  starting transfers between devices  15.8 us (1%)
  between operations  15.6 us (1%)
    unnamed x19, waiting for transfers between devices  229 us
    reduce_scatter x1, waiting for transfers between devices, per_device(): lax.psum_scatter(grad_out_w, ('dp', 'seq'), scatter_dimension=0, tiled=True)  181 us
    all_to_all x1, waiting for transfers between devices, per_device(): lax.all_to_all(projected.reshape(tokens, 3, D), 'seq', split_axis=2, conc...  80.2 us
    unnamed x2, blocking collectives  78.7 us
    dot_general x9, matrix products, contract(): lax.dot_general(left, right, (((left_dim,), (right_dim,)), ((), ())), pre...  69 us
    all_to_all x1, blocking collectives, per_device(): lax.all_to_all(grad_stack, 'seq', split_axis=0, concat_axis=2, tiled=True)  52.9 us
    all_gather x1, waiting for transfers between devices, per_device(): grad_all = lax.all_gather(grad_out, 'seq', axis=0, tiled=True)  48.8 us
    reduce_scatter x1, waiting for transfers between devices, per_device(): lax.psum_scatter(jnp.dot(hidden, cols_down, preferred_element_type=jnp.fl...  48.3 us
  transfers between devices with their start and end apart: 21, of which 15 were waited for; matrix products, arithmetic and copies ran while one was open for 15% of the time, Pallas kernels for 0%

commit v1 on v0

--- a/solution.py
+++ b/solution.py
@@ -204,6 +204,62 @@
     ).astype(jnp.bfloat16)
     grad_up = (grad_hidden * silu_gate).astype(jnp.bfloat16)
     return (grad_gate, grad_up)
+
+
+def permute(value, axis, offset):
+    size = lax.axis_size(axis)
+    return lax.ppermute(value, axis, [(i, i ^ offset) for i in range(size)])
+
+
+def gather_dp(piece):
+    return [piece] + [permute(piece, "dp", k) for k in range(1, lax.axis_size("dp"))]
+
+
+def scatter_dp(pieces):
+    total = pieces[0].astype(jnp.float32)
+    for k in range(1, len(pieces)):
+        total = total + permute(pieces[k].astype(jnp.bfloat16), "dp", k).astype(jnp.float32)
+    return total
+
+
+def gather_seq(piece):
+    chips = lax.axis_size("seq") // 2
+    same = [piece] + [permute(piece, "seq", 2 * k) for k in range(1, chips)]
+    pieces = []
+    for part in same:
+        pieces += [part, permute(part, "seq", 1)]
+    return pieces
+
+
+def scatter_seq(terms):
+    size = lax.axis_size("seq")
+    block = terms.shape[0] // size
+    stack = terms.reshape(size // 2, 2, block, terms.shape[1])
+    pairs = stack[:, 0].astype(jnp.float32) + permute(
+        stack[:, 1].astype(jnp.bfloat16), "seq", 1
+    ).astype(jnp.float32)
+    total = pairs[0]
+    for k in range(1, size // 2):
+        total = total + permute(pairs[k].astype(jnp.bfloat16), "seq", 2 * k).astype(jnp.float32)
+    return total
+
+
+def reorder(values, index, count):
+    block = values.shape[0] // count
+    result = jnp.zeros_like(values)
+    for m in range(count):
+        result = lax.dynamic_update_slice_in_dim(
+            result, values[m * block : (m + 1) * block], (index ^ m) * block, 0
+        )
+    return result
+
+
+def place(pieces, index):
+    block = pieces[0].shape[0]
+    result = jnp.zeros((block * len(pieces),) + pieces[0].shape[1:], pieces[0].dtype)
+    for k, piece in enumerate(pieces):
+        result = lax.dynamic_update_slice_in_dim(result, piece, (index ^ k) * block, 0)
+    return result
 
 
 def per_device(
@@ -225,165 +281,191 @@
 ):
     tokens = layer_input.shape[1]
     groups = lax.axis_size("seq")
+    rows = lax.axis_size("dp")
+    devices = rows * groups
+    at_dp = lax.axis_index("dp")
+    at_seq = lax.axis_index("seq")
     length = tokens * groups
     heads_here = HEADS // groups
     local_width = heads_here * HEAD
-    segment, cosines, sines = row_tables(doc_lengths[0], length)
+    own = D // devices
+    owner = [(i, (i % groups) * rows + i // groups) for i in range(devices)]
+    back = [(b, a) for a, b in owner]
+    small = jnp.concatenate(
+        [
+            lang_table,
+            attn_norm_gain[None],
+            attn_norm_bias[None],
+            mlp_norm_gain[None],
+            mlp_norm_bias[None],
+            qkv_bias,
+            jnp.broadcast_to(language.astype(jnp.bfloat16)[:, None], (1, own)),
+            jnp.zeros((1, own), jnp.bfloat16),
+        ],
+        axis=0,
+    )
+    spread = lax.all_to_all(
+        jnp.broadcast_to(small[None], (devices,) + small.shape),
+        ("dp", "seq"),
+        split_axis=0,
+        concat_axis=0,
+        tiled=True,
+    )
+    table = jnp.swapaxes(spread, 0, 1).reshape(small.shape[0], D).astype(jnp.float32)
+    languages = spread[:, LANGS + 7, 0].astype(jnp.int32)
+    gain_attn = table[LANGS]
+    bias_attn = table[LANGS + 1]
+    gain_mlp = table[LANGS + 2]
+    bias_mlp = table[LANGS + 3]
+    bias_qkv = lax.dynamic_slice_in_dim(
+        table[LANGS + 4 : LANGS + 7], at_seq * local_width, local_width, 1
+    ).reshape(3 * local_width)
     chooser = (jnp.arange(LANGS, dtype=jnp.int32) == language[0]).astype(jnp.float32)
-    params = (
-        lax.all_gather(qkv_weight, ("dp", "seq"), axis=0, tiled=True),
-        lax.all_gather(out_weight, ("dp", "seq"), axis=0, tiled=True),
-        lax.all_gather(attn_norm_gain, ("dp", "seq"), axis=0, tiled=True),
-        lax.all_gather(attn_norm_bias, ("dp", "seq"), axis=0, tiled=True),
-        lax.all_gather(qkv_bias, ("dp", "seq"), axis=1, tiled=True),
-        lax.all_gather(mlp_norm_gain, ("dp", "seq"), axis=0, tiled=True),
-        lax.all_gather(mlp_norm_bias, ("dp", "seq"), axis=0, tiled=True),
-        lax.all_gather(lang_table, ("dp", "seq"), axis=1, tiled=True),
-    )
-    full_qkv = params[0]
-    full_out = params[1]
-    gain_attn = params[2].astype(jnp.float32)
-    bias_attn = params[3].astype(jnp.float32)
-    bias_qkv = params[4].astype(jnp.float32).reshape(3 * D)
-    gain_mlp = params[5].astype(jnp.float32)
-    bias_mlp = params[6].astype(jnp.float32)
-    lang_rows = params[7].astype(jnp.float32)
-    resid_in = (
-        layer_input[0].astype(jnp.float32) + jnp.sum(chooser[:, None] * lang_rows, axis=0)[None, :]
-    )
-    normed_attn, scaled_attn, inverse_attn = norm_forward(resid_in, gain_attn, bias_attn)
-    normed_attn = normed_attn.astype(jnp.bfloat16)
-    projected = (
-        jnp.dot(normed_attn, full_qkv, preferred_element_type=jnp.float32) + bias_qkv
-    ).astype(jnp.bfloat16)
-    head_rows = lax.all_to_all(
-        projected.reshape(tokens, 3, D), "seq", split_axis=2, concat_axis=0, tiled=True
-    )
-    rot_query = rotate(
-        head_rows[:, 0].reshape(length, heads_here, HEAD).astype(jnp.float32), cosines, sines, 1.0
-    ).astype(jnp.bfloat16)
-    rot_key = rotate(
-        head_rows[:, 1].reshape(length, heads_here, HEAD).astype(jnp.float32), cosines, sines, 1.0
-    ).astype(jnp.bfloat16)
-    value_heads = head_rows[:, 2].reshape(length, heads_here, HEAD)
-    context, logsum = attention_forward(rot_query, rot_key, value_heads, segment)
-    context_tokens = lax.all_to_all(
-        context.astype(jnp.bfloat16).reshape(length, local_width),
+    lang_row = jnp.sum(chooser[:, None] * table[:LANGS], axis=0)[None, :]
+    qkv_part = lax.all_to_all(
+        qkv_weight.reshape(own, 3, groups, local_width).transpose(2, 0, 1, 3).reshape(
+            groups, own, 3 * local_width
+        ),
         "seq",
         split_axis=0,
-        concat_axis=1,
+        concat_axis=0,
         tiled=True,
-    )
-    resid_mid = resid_in + jnp.dot(context_tokens, full_out, preferred_element_type=jnp.float32)
+    ).reshape(groups * own, 3 * local_width)
+    head_qkv = place(gather_dp(qkv_part), at_dp)
+    head_out = place(gather_dp(lax.ppermute(out_weight, ("dp", "seq"), back)), at_dp)
+    cols_gate = jnp.concatenate(gather_dp(gate_weight.T), axis=0)
+    cols_up = jnp.concatenate(gather_dp(up_weight.T), axis=0)
+    cols_down = jnp.concatenate(gather_dp(down_weight), axis=0)
+    segment, cosines, sines = row_tables(doc_lengths[0], length)
+    grad_out = cotangent[0]
+    input_all = jnp.concatenate(gather_seq(layer_input[0]), axis=0)
+    grad_all = jnp.concatenate(gather_seq(grad_out), axis=0)
+    normed_all = norm_forward(input_all.astype(jnp.float32) + lang_row, gain_attn, bias_attn)[
+        0
+    ].astype(jnp.bfloat16)
+    resid_in = layer_input[0].astype(jnp.float32) + lang_row
+    unused, scaled_attn, inverse_attn = norm_forward(resid_in, gain_attn, bias_attn)
+    projected = (
+        jnp.dot(normed_all, head_qkv, preferred_element_type=jnp.float32) + bias_qkv
+    ).astype(jnp.bfloat16)
+    head_rows = reorder(projected, at_seq, groups).reshape(length, 3, heads_here, HEAD)
+    rot_query = rotate(head_rows[:, 0].astype(jnp.float32), cosines, sines, 1.0).astype(
+        jnp.bfloat16
+    )
+    rot_key = rotate(head_rows[:, 1].astype(jnp.float32), cosines, sines, 1.0).astype(jnp.bfloat16)
+    value_heads = head_rows[:, 2]
+    context, logsum = attention_forward(rot_query, rot_key, value_heads, segment)
+    context_all = reorder(
+        context.astype(jnp.bfloat16).reshape(length, local_width), at_seq, groups
+    )
+    resid_mid = resid_in + scatter_seq(
+        jnp.dot(context_all, head_out, preferred_element_type=jnp.float32)
+    )
     normed_mlp, scaled_mlp, inverse_mlp = norm_forward(resid_mid, gain_mlp, bias_mlp)
-    normed_mlp = normed_mlp.astype(jnp.bfloat16)
-    grad_out = cotangent[0]
-    cols_gate, cols_up, cols_down = (
-        lax.all_gather(gate_weight, "dp", axis=1, tiled=True),
-        lax.all_gather(up_weight, "dp", axis=1, tiled=True),
-        lax.all_gather(down_weight, "dp", axis=0, tiled=True),
-    )
-    rows_all = lax.all_gather(normed_mlp, "seq", axis=0, tiled=True)
-    gate_values = jnp.dot(rows_all, cols_gate, preferred_element_type=jnp.float32)
-    up_values = jnp.dot(rows_all, cols_up, preferred_element_type=jnp.float32)
+    rows_all = jnp.concatenate(gather_seq(normed_mlp.astype(jnp.bfloat16)), axis=0)
+    gate_values = contract(rows_all, cols_gate, 1, 1)
+    up_values = contract(rows_all, cols_up, 1, 1)
     hidden = (jax.nn.silu(gate_values) * up_values).astype(jnp.bfloat16)
-    mlp_out = lax.psum_scatter(
-        jnp.dot(hidden, cols_down, preferred_element_type=jnp.float32).astype(jnp.bfloat16),
-        "seq",
-        scatter_dimension=0,
-        tiled=True,
-    ).astype(jnp.float32)
-    grad_all = lax.all_gather(grad_out, "seq", axis=0, tiled=True)
     grad_hidden = contract(grad_all, cols_down, 1, 1)
     grad_gate, grad_up = gate_backward(gate_values, up_values, grad_hidden)
-    grad_rows = contract(grad_gate, cols_gate, 1, 1) + contract(grad_up, cols_up, 1, 1)
-    grad_normed_mlp = lax.psum_scatter(
-        grad_rows.astype(jnp.bfloat16), "seq", scatter_dimension=0, tiled=True
-    ).astype(jnp.float32)
-    out_gate, out_up, out_down = (
-        lax.psum_scatter(
-            contract(rows_all, grad_gate, 0, 0).astype(jnp.bfloat16),
-            "dp",
-            scatter_dimension=1,
-            tiled=True,
-        ).astype(jnp.float32),
-        lax.psum_scatter(
-            contract(rows_all, grad_up, 0, 0).astype(jnp.bfloat16),
-            "dp",
-            scatter_dimension=1,
-            tiled=True,
-        ).astype(jnp.float32),
-        lax.psum_scatter(
-            contract(hidden, grad_all, 0, 0).astype(jnp.bfloat16),
-            "dp",
-            scatter_dimension=0,
-            tiled=True,
-        ).astype(jnp.float32),
-    )
+    grad_rows = contract(grad_gate, cols_gate, 1, 0) + contract(grad_up, cols_up, 1, 0)
+    grad_normed_mlp = scatter_seq(grad_rows)
+    mlp_out = scatter_seq(jnp.dot(hidden, cols_down, preferred_element_type=jnp.float32))
     layer_output = (resid_mid + mlp_out).astype(jnp.bfloat16)
+
+    def to_owner(terms):
+        return scatter_dp(jnp.split(terms.astype(jnp.bfloat16), rows, axis=0))
+
+    out_gate = to_owner(contract(grad_gate, rows_all, 0, 0)).T
+    out_up = to_owner(contract(grad_up, rows_all, 0, 0)).T
+    out_down = to_owner(contract(hidden, grad_all, 0, 0))
     grad_mid_norm, grad_gain_mlp, grad_bias_mlp = norm_backward(
         grad_normed_mlp, scaled_mlp, inverse_mlp, gain_mlp
     )
     grad_mid = grad_out.astype(jnp.float32) + grad_mid_norm
-    grad_branch = grad_mid.astype(jnp.bfloat16)
-    grad_out_w = contract(context_tokens, grad_branch, 0, 0)
-    grad_context = contract(grad_branch, full_out, 1, 1).astype(jnp.bfloat16)
-    grad_heads = lax.all_to_all(
-        grad_context, "seq", split_axis=1, concat_axis=0, tiled=True
+    branch_all = jnp.concatenate(gather_seq(grad_mid.astype(jnp.bfloat16)), axis=0)
+    grad_heads = reorder(
+        contract(branch_all, head_out, 1, 1).astype(jnp.bfloat16), at_seq, groups
     ).reshape(length, heads_here, HEAD)
     grad_queries, grad_keys, grad_values = attention_backward(
         rot_query, rot_key, value_heads, segment, context, logsum, grad_heads
     )
     grad_query_raw = rotate(grad_queries, cosines, sines, -1.0).reshape(length, local_width)
     grad_key_raw = rotate(grad_keys, cosines, sines, -1.0).reshape(length, local_width)
-    grad_stack = jnp.stack(
-        [grad_query_raw, grad_key_raw, grad_values.reshape(length, local_width)], axis=1
-    ).astype(jnp.bfloat16)
-    grad_projected = lax.all_to_all(
-        grad_stack, "seq", split_axis=0, concat_axis=2, tiled=True
-    ).reshape(tokens, 3 * D)
-    grad_bias_qkv = jnp.sum(grad_projected.astype(jnp.float32), axis=0).reshape(3, D)
-    grad_normed_attn = contract(grad_projected, full_qkv, 1, 1)
+    grad_stack = reorder(
+        jnp.concatenate(
+            [grad_query_raw, grad_key_raw, grad_values.reshape(length, local_width)], axis=1
+        ).astype(jnp.bfloat16),
+        at_seq,
+        groups,
+    )
+    grad_normed_attn = scatter_seq(contract(grad_stack, head_qkv, 1, 1))
     grad_in_norm, grad_gain_attn, grad_bias_attn = norm_backward(
         grad_normed_attn, scaled_attn, inverse_attn, gain_attn
     )
     grad_input = grad_mid + grad_in_norm
-    grad_lang = chooser[:, None] * jnp.sum(grad_input, axis=0)[None, :]
-    normed_all = lax.all_gather(normed_attn, "seq", axis=0, tiled=True)
-    slice_terms = jnp.einsum(
-        "td,tcw->dcw", normed_all, grad_stack, preferred_element_type=jnp.float32
-    )
-    slice_summed = lax.psum_scatter(
-        slice_terms.astype(jnp.bfloat16), "dp", scatter_dimension=0, tiled=True
-    ).astype(jnp.float32)
+
+    def dp_terms(terms):
+        block = terms.shape[0] // rows
+        return [
+            lax.dynamic_slice_in_dim(terms, (at_dp ^ k) * block, block, 0) for k in range(rows)
+        ]
+
+    slice_summed = scatter_dp(dp_terms(contract(normed_all, grad_stack, 0, 0).astype(jnp.bfloat16)))
     grad_qkv_out = (
         lax.all_to_all(
-            slice_summed.astype(jnp.bfloat16), "seq", split_axis=0, concat_axis=2, tiled=True
+            slice_summed.astype(jnp.bfloat16).reshape(groups, own, 3 * local_width),
+            "seq",
+            split_axis=0,
+            concat_axis=0,
+            tiled=True,
         )
-        .astype(slice_summed.dtype)
-        .reshape(-1, 3 * D)
-    )
-    small = (
-        lax.psum_scatter(grad_out_w, ("dp", "seq"), scatter_dimension=0, tiled=True),
-        lax.psum_scatter(grad_gain_attn, ("dp", "seq"), scatter_dimension=0, tiled=True),
-        lax.psum_scatter(grad_bias_attn, ("dp", "seq"), scatter_dimension=0, tiled=True),
-        lax.psum_scatter(grad_bias_qkv, ("dp", "seq"), scatter_dimension=1, tiled=True),
-        lax.psum_scatter(grad_gain_mlp, ("dp", "seq"), scatter_dimension=0, tiled=True),
-        lax.psum_scatter(grad_bias_mlp, ("dp", "seq"), scatter_dimension=0, tiled=True),
-        lax.psum_scatter(grad_lang, ("dp", "seq"), scatter_dimension=1, tiled=True),
-    )
-    out_proj, gain_a, bias_a, bias_q, gain_m, bias_m, lang_g = small
+        .reshape(groups, own, 3, local_width)
+        .transpose(1, 2, 0, 3)
+        .reshape(own, 3 * D)
+        .astype(jnp.float32)
+    )
+    head_out_terms = scatter_dp(
+        dp_terms(contract(context_all, branch_all, 0, 0).astype(jnp.bfloat16))
+    )
+    out_proj = lax.ppermute(head_out_terms, ("dp", "seq"), owner)
+    grad_bias_qkv = jnp.sum(grad_stack.astype(jnp.float32), axis=0).reshape(3, local_width)
+    terms = jnp.concatenate(
+        [
+            grad_gain_attn[None],
+            grad_bias_attn[None],
+            grad_gain_mlp[None],
+            grad_bias_mlp[None],
+            jnp.sum(grad_input, axis=0)[None],
+            lax.dynamic_update_slice(
+                jnp.zeros((3, D), jnp.float32), grad_bias_qkv, (0, at_seq * local_width)
+            ),
+        ],
+        axis=0,
+    )
+    arrived = lax.all_to_all(
+        terms.reshape(terms.shape[0], devices, own).swapaxes(0, 1),
+        ("dp", "seq"),
+        split_axis=0,
+        concat_axis=0,
+        tiled=True,
+    )
+    summed = jnp.sum(arrived, axis=0)
+    members = (languages[:, None] == jnp.arange(LANGS, dtype=jnp.int32)[None, :]).astype(
+        jnp.float32
+    )
+    lang_g = jnp.sum(members[:, :, None] * arrived[:, 4][:, None, :], axis=0)
     return (
         layer_output[None],
         grad_input[None],
         lang_g,
-        gain_a,
-        bias_a,
+        summed[0],
+        summed[1],
         grad_qkv_out,
-        bias_q,
+        summed[5:8],
         out_proj,
-        gain_m,
-        bias_m,
+        summed[2],
+        summed[3],
         out_gate,
         out_up,
         out_down,

time: 1360 us -> 747 us (0.55)
  waiting for transfers between devices: 857 us -> 345 us
  blocking collectives: 217 us -> 0 us
  starting transfers between devices: 15.8 us -> 142 us
  matrix products: 148 us -> 90.8 us
  local copies, waits for them, and re-layouts: 59.3 us -> 94.1 us
  other arithmetic: 37.8 us -> 63.7 us
    reduce_scatter x7 -> x0, waiting for transfers between devices: 326 us -> none  [the longest x1 181 us: per_device(): lax.psum_scatter(grad_out_w, ('dp', 'seq'), scatter_dimension=0, tiled=True)]
    ppermute x0 -> x76, waiting for transfers between devices: none -> 286 us  [the longest x74 286 us: permute(): return lax.ppermute(value, axis, [(i, i ^ offset) for i in range(size)])]
    unnamed x19 -> x0, waiting for transfers between devices: 229 us -> none
    all_gather x8 -> x0, waiting for transfers between devices: 191 us -> none  [the longest x1 48.8 us: per_device(): grad_all = lax.all_gather(grad_out, 'seq', axis=0, tiled=True)]
    ppermute x0 -> x76, starting transfers between devices: none -> 114 us  [the longest x74 112 us: permute(): return lax.ppermute(value, axis, [(i, i ^ offset) for i in range(size)])]
    all_gather x2 -> x0, blocking collectives: 85.6 us -> none  [the longest x1 44.2 us: per_device(): lax.all_gather(lang_table, ('dp', 'seq'), axis=1, tiled=True)]
    unnamed x2 -> x0, blocking collectives: 78.7 us -> none
    all_to_all x1 -> x0, blocking collectives: 52.9 us -> none  [per_device(): lax.all_to_all(grad_stack, 'seq', split_axis=0, concat_axis=2, tiled=True)]
  transfers between devices with their start and end apart: 21 -> 80, of which waited for: 15 -> 27; matrix products, arithmetic and copies ran while one was open for 15% -> 23% of each run, Pallas kernels for 0% -> 0%
where the time goes in v1:
time: 747 us; the launch traced here: 742 us
  waiting for transfers between devices  345 us (46%)
  starting transfers between devices  142 us (19%)
  local copies, waits for them, and re-layouts  94.1 us (13%)
  matrix products  90.8 us (12%)
  other arithmetic  63.7 us (9%)
    ppermute x74, waiting for transfers between devices, permute(): return lax.ppermute(value, axis, [(i, i ^ offset) for i in range(size)])  286 us
    ppermute x74, starting transfers between devices, permute(): return lax.ppermute(value, axis, [(i, i ^ offset) for i in range(size)])  112 us
    unnamed x152, local copies, waits for them, and re-layouts  51 us
    dot_general x12, matrix products, contract(): lax.dot_general(left, right, (((left_dim,), (right_dim,)), ((), ())), pre...  48.6 us
    all_to_all x1, waiting for transfers between devices, per_device(): lax.all_to_all(jnp.broadcast_to(small[None], (devices,) + small.shape), (...  34.2 us
    all_to_all x1, waiting for transfers between devices, per_device(): lax.all_to_all(slice_summed.astype(jnp.bfloat16).reshape(groups, own, 3 *...  23.9 us
    another operation x8, other arithmetic  18.4 us
  transfers between devices with their start and end apart: 80, of which 27 were waited for; matrix products, arithmetic and copies ran while one was open for 23% of the time, Pallas kernels for 0%

profile of v1, /device:TPU:0, one launch (start us, length us, event | category | flops | bytes accessed | tf_op | source)
XLA Modules:
  0.0 742.1 jit_solution(12586095634011654644)
XLA Ops:
  9.3 6.1 all-to-all-start
  26.8 34.2 %all-to-all-done = bf16[32,2,512]{2,1,0:T(2,128)(2,1)S(1)} async-done(((bf16[32,2,512]{2,1,0:T(2,128)(2,1)}), bf16[32,2,512]{2,1,0:T(2,128)(2,1)S(1)}, u32[]{:S(2)}, u32[]{:S(2)}) %all-to-all-start) | async-done | bytes 65568 | tf_op jit(solution)/shard_map/all_to_all | solution.py:307
  104.3 12.9 %collective-permute-done.7 = bf16[512,768]{1,0:T(8,128)(2,1)S(1)} collective-permute-done((bf16[512,768]{1,0:T(8,128)(2,1)S(1)}, bf16[512,768]{1,0:T(8,128)(2,1)S(1)}, u32[]{:S(2)}, u32[]{:S(2)}) %collective-permute-start.7) | collective-permute-done | bytes 786464 | tf_op jit(solution)/shard_map/ppermute | solution.py:211
  117.9 16.0 %collective-permute-done.8 = bf16[512,768]{1,0:T(8,128)(2,1)S(1)} collective-permute-done((bf16[512,768]{1,0:T(8,128)(2,1)S(1)}, bf16[512,768]{1,0:T(8,128)(2,1)S(1)}, u32[]{:S(2)}, u32[]{:S(2)}) %collective-permute-start.8) | collective-permute-done | bytes 786464 | tf_op jit(solution)/shard_map/ppermute | solution.py:211
  140.9 21.4 %while.89 = (s32[]{:T(128)}, f32[2,512,4,64]{1,3,2,0:T(8,128)S(1)}, f32[2,4,512]{2,1,0:T(4,128)S(1)}, s32[2]{0:T(128)S(1)}, bf16[1024,4,64]{0,2,1:T(8,128)(2,1)S...) while((s32[]{:T(128)}, f32[2,512,4,64]{1,3,2,0:T(8,128)S(1)}, ...), condition=%wide.region_13.14_spmd, body=%wide.region_6.13_spmd.sunk | while | flops 417996800 | bytes 14358417 | solution.py:132
  155.9 6.3 while.93
  193.8 7.9 %collective-permute-done.33 = bf16[176,2048]{1,0:T(8,128)(2,1)S(1)} collective-permute-done((bf16[176,2048]{1,0:T(8,128)(2,1)}, bf16[176,2048]{1,0:T(8,128)(2,1)S(1)}, u32[]{:S(2)}, u32[]{:S(2)}) %collective-permute-start.33) | collective-permute-done | bytes 720928 | tf_op jit(solution)/shard_map/ppermute | solution.py:211
  204.9 9.4 %collective-permute-done.41 = bf16[128,2048]{1,0:T(8,128)(2,1)S(1)} collective-permute-done((bf16[128,2048]{1,0:T(8,128)(2,1)}, bf16[128,2048]{1,0:T(8,128)(2,1)S(1)}, u32[]{:S(2)}, u32[]{:S(2)}) %collective-permute-start.41) | collective-permute-done | bytes 524320 | tf_op jit(solution)/shard_map/ppermute | solution.py:211
  216.3 8.5 %collective-permute-done.15 = bf16[128,2048]{1,0:T(8,128)(2,1)S(1)} collective-permute-done((bf16[128,2048]{1,0:T(8,128)(2,1)S(1)}, bf16[128,2048]{1,0:T(8,128)(2,1)S(1)}, u32[]{:S(2)}, u32[]{:S(2)}) %collective-permute-start.15) | collective-permute-done | bytes 524320 | tf_op jit(solution)/shard_map/ppermute | solution.py:211
  224.8 34.0 %collective-permute-done.16 = bf16[128,2048]{1,0:T(8,128)(2,1)S(1)} collective-permute-done((bf16[128,2048]{1,0:T(8,128)(2,1)S(1)}, bf16[128,2048]{1,0:T(8,128)(2,1)S(1)}, u32[]{:S(2)}, u32[]{:S(2)}) %collective-permute-start.16) | collective-permute-done | bytes 524320 | tf_op jit(solution)/shard_map/ppermute | solution.py:211
  259.9 11.6 %collective-permute-start.19 = (bf16[128,2048]{1,0:T(8,128)(2,1)S(1)}, bf16[128,2048]{1,0:T(8,128)(2,1)S(1)}, u32[]{:S(2)}, u32[]{:S(2)}) collective-permute-start(bf16[128,2048]{1,0:T(8,128)(2,1)S(1)} %get-tuple-element.804), channel_id=1, source_target_pairs={{0,2},{1,3},{2,0},{3,1},{4,6},{5,7},{6,4},{7,5},{8,10},{9,11},{10,... | collective-permute-start | bytes 1572872 | tf_op jit(solution)/shard_map/ppermute | solution.py:211
  274.2 19.0 %collective-permute-done.19 = bf16[128,2048]{1,0:T(8,128)(2,1)S(1)} collective-permute-done((bf16[128,2048]{1,0:T(8,128)(2,1)S(1)}, bf16[128,2048]{1,0:T(8,128)(2,1)S(1)}, u32[]{:S(2)}, u32[]{:S(2)}) %collective-permute-start.19) | collective-permute-done | bytes 524320 | tf_op jit(solution)/shard_map/ppermute | solution.py:211
  295.5 14.4 %collective-permute-done.21 = bf16[128,2048]{1,0:T(8,128)(2,1)S(1)} collective-permute-done((bf16[128,2048]{1,0:T(8,128)(2,1)S(1)}, bf16[128,2048]{1,0:T(8,128)(2,1)S(1)}, u32[]{:S(2)}, u32[]{:S(2)}) %collective-permute-start.21) | collective-permute-done | bytes 524320 | tf_op jit(solution)/shard_map/ppermute | solution.py:211
  316.9 12.9 %collective-permute-done.30 = bf16[176,2048]{1,0:T(8,128)(2,1)S(1)} collective-permute-done((bf16[176,2048]{1,0:T(8,128)(2,1)S(1)}, bf16[176,2048]{1,0:T(8,128)(2,1)S(1)}, u32[]{:S(2)}, u32[]{:S(2)}) %collective-permute-start.30) | collective-permute-done | bytes 720928 | tf_op jit(solution)/shard_map/ppermute | solution.py:211
  333.2 12.5 %collective-permute-done.25 = bf16[176,2048]{1,0:T(8,128)(2,1)S(1)} collective-permute-done((bf16[176,2048]{1,0:T(8,128)(2,1)S(1)}, bf16[176,2048]{1,0:T(8,128)(2,1)S(1)}, u32[]{:S(2)}, u32[]{:S(2)}) %collective-permute-start.25) | collective-permute-done | bytes 720928 | tf_op jit(solution)/shard_map/ppermute | solution.py:211
  345.6 14.9 %collective-permute-done.27 = bf16[176,2048]{1,0:T(8,128)(2,1)S(1)} collective-permute-done((bf16[176,2048]{1,0:T(8,128)(2,1)S(1)}, bf16[176,2048]{1,0:T(8,128)(2,1)S(1)}, u32[]{:S(2)}, u32[]{:S(2)}) %collective-permute-start.27) | collective-permute-done | bytes 720928 | tf_op jit(solution)/shard_map/ppermute | solution.py:211
  407.8 10.3 %collective-permute-start.35 = (bf16[128,2048]{1,0:T(8,128)(2,1)S(1)}, bf16[128,2048]{1,0:T(8,128)(2,1)S(1)}, u32[]{:S(2)}, u32[]{:S(2)}) collective-permute-start(bf16[128,2048]{1,0:T(8,128)(2,1)S(1)} %get-tuple-element.840), channel_id=1, source_target_pairs={{0,2},{1,3},{2,0},{3,1},{4,6},{5,7},{6,4},{7,5},{8,10},{9,11},{10,... | collective-permute-start | bytes 1572872 | tf_op jit(solution)/shard_map/ppermute | solution.py:211
  426.5 14.5 %collective-permute-done.35 = bf16[128,2048]{1,0:T(8,128)(2,1)S(1)} collective-permute-done((bf16[128,2048]{1,0:T(8,128)(2,1)S(1)}, bf16[128,2048]{1,0:T(8,128)(2,1)S(1)}, u32[]{:S(2)}, u32[]{:S(2)}) %collective-permute-start.35) | collective-permute-done | bytes 524320 | tf_op jit(solution)/shard_map/ppermute | solution.py:211
  445.0 11.6 %collective-permute-done.36 = bf16[128,2048]{1,0:T(8,128)(2,1)S(1)} collective-permute-done((bf16[128,2048]{1,0:T(8,128)(2,1)}, bf16[128,2048]{1,0:T(8,128)(2,1)S(1)}, u32[]{:S(2)}, u32[]{:S(2)}) %collective-permute-start.36) | collective-permute-done | bytes 524320 | tf_op jit(solution)/shard_map/ppermute | solution.py:211
  466.9 34.6 %collective-permute-done.47 = bf16[128,2048]{1,0:T(8,128)(2,1)S(1)} collective-permute-done((bf16[128,2048]{1,0:T(8,128)(2,1)S(1)}, bf16[128,2048]{1,0:T(8,128)(2,1)S(1)}, u32[]{:S(2)}, u32[]{:S(2)}) %collective-permute-start.47) | collective-permute-done | bytes 524320 | tf_op jit(solution)/shard_map/ppermute | solution.py:211
  511.0 9.5 %collective-permute-start.50 = (bf16[128,2048]{1,0:T(8,128)(2,1)}, bf16[128,2048]{1,0:T(8,128)(2,1)S(1)}, u32[]{:S(2)}, u32[]{:S(2)}) collective-permute-start(bf16[128,2048]{1,0:T(8,128)(2,1)} %get-tuple-element.796), channel_id=1, source_target_pairs={{0,2},{1,3},{2,0},{3,1},{4,6},{5,7},{6,4},{7,5},{8,10},{9,11},{10,... | collective-permute-start | bytes 1572872 | tf_op jit(solution)/shard_map/ppermute | solution.py:211
  524.1 8.5 %collective-permute-done.71 = bf16[176,2048]{1,0:T(8,128)(2,1)S(1)} collective-permute-done((bf16[176,2048]{1,0:T(8,128)(2,1)S(1)}, bf16[176,2048]{1,0:T(8,128)(2,1)S(1)}, u32[]{:S(2)}, u32[]{:S(2)}) %collective-permute-start.71) | collective-permute-done | bytes 720928 | tf_op jit(solution)/shard_map/ppermute | solution.py:211
  537.8 23.8 %collective-permute-done.52 = bf16[128,2048]{1,0:T(8,128)(2,1)} collective-permute-done((bf16[128,2048]{1,0:T(8,128)(2,1)}, bf16[128,2048]{1,0:T(8,128)(2,1)}, u32[]{:S(2)}, u32[]{:S(2)}) %collective-permute-start.52) | collective-permute-done | bytes 524320 | tf_op jit(solution)/shard_map/ppermute | solution.py:211
  582.0 25.9 %while.91 = (s32[]{:T(128)}, f32[1024,4,64]{0,2,1:T(8,128)}, f32[1024,4,64]{0,2,1:T(8,128)S(1)}, f32[1024,4,64]{0,2,1:T(8,128)}, bf16[1024,4,64]{0,2,1:T(8,128)(...) while((s32[]{:T(128)}, f32[1024,4,64]{0,2,1:T(8,128)}, ...), condition=%wide.region_24.25_spmd, body=%wide.region_21.24_spmd.sunk | while | flops 685114368 | bytes 30487232 | solution.py:196
  583.0 7.5 %while.94 = (s32[]{:T(128)}, f32[512,4,64]{0,2,1:T(8,128)S(1)}, f32[1024,4,64]{0,2,1:T(8,128)S(1)}, f32[1024,4,64]{0,2,1:T(8,128)}, s32[]{:T(128)}, /*index=5*/b...) while((s32[]{:T(128)}, f32[512,4,64]{0,2,1:T(8,128)S(1)}, ...), condition=%wide.region_23.23_spmd, body=%wide.region_22.22_spmd.sunk | while | flops 685114368 | bytes 27828524 | solution.py:190
  592.2 14.9 %while.94 = (s32[]{:T(128)}, f32[512,4,64]{0,2,1:T(8,128)S(1)}, f32[1024,4,64]{0,2,1:T(8,128)S(1)}, f32[1024,4,64]{0,2,1:T(8,128)}, s32[]{:T(128)}, /*index=5*/b...) while((s32[]{:T(128)}, f32[512,4,64]{0,2,1:T(8,128)S(1)}, ...), condition=%wide.region_23.23_spmd, body=%wide.region_22.22_spmd.sunk | while | flops 685114368 | bytes 27828524 | solution.py:190
  637.3 6.0 fusion.96
  646.1 8.6 %collective-permute-start.57 = (bf16[128,2048]{1,0:T(8,128)(2,1)}, bf16[128,2048]{1,0:T(8,128)(2,1)}, u32[]{:S(2)}, u32[]{:S(2)}) collective-permute-start(bf16[128,2048]{1,0:T(8,128)(2,1)} %get-tuple-element.834), channel_id=1, source_target_pairs={{0,2},{1,3},{2,0},{3,1},{4,6},{5,7},{6,4},{7,5},{8,10},{9,11},{10,... | collective-permute-start | bytes 1572872 | tf_op jit(solution)/shard_map/ppermute | solution.py:211
  659.3 10.5 %collective-permute-done.61 = bf16[512,768]{1,0:T(8,128)(2,1)S(1)} collective-permute-done((bf16[512,768]{1,0:T(8,128)(2,1)}, bf16[512,768]{1,0:T(8,128)(2,1)S(1)}, u32[]{:S(2)}, u32[]{:S(2)}) %collective-permute-start.61) | collective-permute-done | bytes 786464 | tf_op jit(solution)/shard_map/ppermute | solution.py:211
  677.3 10.4 %all-to-all-start.3 = ((bf16[8,64,768]{2,1,0:T(8,128)(2,1)}), bf16[8,64,768]{2,1,0:T(8,128)(2,1)S(1)}, u32[]{:S(2)}, u32[]{:S(2)}) async-start(bf16[8,64,768]{2,1,0:T(8,128)(2,1)} %bitcast.371), calls=%async_computation.3 | async-start | bytes 1572864 | tf_op jit(solution)/shard_map/all_to_all | solution.py:416
  700.0 23.9 %all-to-all-done.3 = bf16[8,64,768]{2,1,0:T(8,128)(2,1)S(1)} async-done(((bf16[8,64,768]{2,1,0:T(8,128)(2,1)}), bf16[8,64,768]{2,1,0:T(8,128)(2,1)S(1)}, u32[]{:S(2)}, u32[]{:S(2)}) %all-to-all-start.3) | async-done | bytes 786464 | tf_op jit(solution)/shard_map/all_to_all | solution.py:416
  724.0 6.5 all-to-all-start.2
  (572 shorter events, 352.7 us)
Async XLA Ops:
  0.6 77.8 %collective-permute-start.1 = (bf16[128,2048]{1,0:T(8,128)(2,1)}, bf16[128,2048]{1,0:T(8,128)(2,1)}, u32[]{:S(2)}, u32[]{:S(2)}) collective-permute-start(bf16[128,2048]{1,0:T(8,128)(2,1)} %bitcast.351), channel_id=1, source_target_pairs={{0,2},{1,3},{2,0},{3,1},{4,6},{5,7},{6,4},{7,5},{8,10},{9,11},{10,... | collective-permute-start | bytes 1572872 | tf_op jit(solution)/shard_map/ppermute | solution.py:211
  3.7 66.0 %collective-permute-start = (bf16[128,2048]{1,0:T(8,128)(2,1)}, bf16[128,2048]{1,0:T(8,128)(2,1)}, u32[]{:S(2)}, u32[]{:S(2)}) collective-permute-start(bf16[128,2048]{1,0:T(8,128)(2,1)} %bitcast.352), channel_id=1, source_target_pairs={{0,1},{1,0},{2,3},{3,2},{4,5},{5,4},{6,7},{7,6},{8,9},{9,8},{10,11... | collective-permute-start | bytes 1572872 | tf_op jit(solution)/shard_map/ppermute | solution.py:211
  3.7 77.9 %collective-permute-start.3 = (bf16[128,2048]{1,0:T(8,128)(2,1)}, bf16[128,2048]{1,0:T(8,128)(2,1)}, u32[]{:S(2)}, u32[]{:S(2)}) collective-permute-start(bf16[128,2048]{1,0:T(8,128)(2,1)} %bitcast.353), channel_id=1, source_target_pairs={{0,4},{1,5},{2,6},{3,7},{4,0},{5,1},{6,2},{7,3},{8,12},{9,13},{10,... | collective-permute-start | bytes 1572872 | tf_op jit(solution)/shard_map/ppermute | solution.py:211
  6.3 75.8 %collective-permute-start.5 = (bf16[128,2048]{1,0:T(8,128)(2,1)}, bf16[128,2048]{1,0:T(8,128)(2,1)}, u32[]{:S(2)}, u32[]{:S(2)}) collective-permute-start(bf16[128,2048]{1,0:T(8,128)(2,1)} %bitcast.354), channel_id=1, source_target_pairs={{0,6},{1,7},{2,4},{3,5},{4,2},{5,3},{6,0},{7,1},{8,14},{9,15},{10,... | collective-permute-start | bytes 1572872 | tf_op jit(solution)/shard_map/ppermute | solution.py:211
  9.3 51.7 %all-to-all-start = ((bf16[32,2,512]{2,1,0:T(2,128)(2,1)}), bf16[32,2,512]{2,1,0:T(2,128)(2,1)S(1)}, u32[]{:S(2)}, u32[]{:S(2)}) async-start(bf16[32,2,512]{2,1,0:T(2,128)(2,1)} %reshape.575), calls=%async_computation | async-start | bytes 131072 | tf_op jit(solution)/shard_map/all_to_all | solution.py:307
  15.3 51.9 %collective-permute-start.10 = (bf16[64,2048]{1,0:T(8,128)(2,1)}, bf16[64,2048]{1,0:T(8,128)(2,1)S(1)}, u32[]{:S(2)}, u32[]{:S(2)}) collective-permute-start(bf16[64,2048]{1,0:T(8,128)(2,1)} %param.33), channel_id=1, source_target_pairs={{0,0},{4,1},{8,2},{12,3},{16,4},{20,5},{24,6},{28,7},{1,8},{5,9},{... | collective-permute-start | bytes 786440 | tf_op jit(solution)/shard_map/ppermute | solution.py:335
  76.1 103.8 %collective-permute-start.39 = (bf16[128,2048]{1,0:T(8,128)(2,1)}, bf16[128,2048]{1,0:T(8,128)(2,1)}, u32[]{:S(2)}, u32[]{:S(2)}) collective-permute-start(bf16[128,2048]{1,0:T(8,128)(2,1)} %bitcast.57), channel_id=1, source_target_pairs={{0,2},{1,3},{2,0},{3,1},{4,6},{5,7},{6,4},{7,5},{8,10},{9,11},{10,... | collective-permute-start | bytes 1572872 | tf_op jit(solution)/shard_map/ppermute | solution.py:211
  81.6 94.0 %collective-permute-start.38 = (bf16[128,2048]{1,0:T(8,128)(2,1)}, bf16[128,2048]{1,0:T(8,128)(2,1)}, u32[]{:S(2)}, u32[]{:S(2)}) collective-permute-start(bf16[128,2048]{1,0:T(8,128)(2,1)} %bitcast.57), channel_id=1, source_target_pairs={{0,1},{1,0},{2,3},{3,2},{4,5},{5,4},{6,7},{7,6},{8,9},{9,8},{10,11... | collective-permute-start | bytes 1572872 | tf_op jit(solution)/shard_map/ppermute | solution.py:211
  117.2 65.3 %collective-permute-start.31 = (bf16[176,2048]{1,0:T(8,128)(2,1)}, bf16[176,2048]{1,0:T(8,128)(2,1)}, u32[]{:S(2)}, u32[]{:S(2)}) collective-permute-start(bf16[176,2048]{1,0:T(8,128)(2,1)} %param.38), channel_id=1, source_target_pairs={{0,8},{8,0},{16,24},{24,16},{1,9},{9,1},{17,25},{25,17},{2,10},{10... | collective-permute-start | bytes 2162696 | tf_op jit(solution)/shard_map/ppermute | solution.py:211
  133.9 53.5 %collective-permute-start.32 = (bf16[176,2048]{1,0:T(8,128)(2,1)}, bf16[176,2048]{1,0:T(8,128)(2,1)}, u32[]{:S(2)}, u32[]{:S(2)}) collective-permute-start(bf16[176,2048]{1,0:T(8,128)(2,1)} %param.38), channel_id=1, source_target_pairs={{0,16},{8,24},{16,0},{24,8},{1,17},{9,25},{17,1},{25,9},{2,18},{10... | collective-permute-start | bytes 2162696 | tf_op jit(solution)/shard_map/ppermute | solution.py:211
  175.6 38.7 %collective-permute-start.41 = (bf16[128,2048]{1,0:T(8,128)(2,1)}, bf16[128,2048]{1,0:T(8,128)(2,1)S(1)}, u32[]{:S(2)}, u32[]{:S(2)}) collective-permute-start(bf16[128,2048]{1,0:T(8,128)(2,1)} %bitcast.57), channel_id=1, source_target_pairs={{0,4},{1,5},{2,6},{3,7},{4,0},{5,1},{6,2},{7,3},{8,12},{9,13},{10,... | collective-permute-start | bytes 1572872 | tf_op jit(solution)/shard_map/ppermute | solution.py:211
  201.7 57.1 %collective-permute-start.16 = (bf16[128,2048]{1,0:T(8,128)(2,1)S(1)}, bf16[128,2048]{1,0:T(8,128)(2,1)S(1)}, u32[]{:S(2)}, u32[]{:S(2)}) collective-permute-start(bf16[128,2048]{1,0:T(8,128)(2,1)S(1)} %get-tuple-element.845), channel_id=1, source_target_pairs={{0,4},{1,5},{2,6},{3,7},{4,0},{5,1},{6,2},{7,3},{8,12},{9,13},{10,... | collective-permute-start | bytes 1572872 | tf_op jit(solution)/shard_map/ppermute | solution.py:211
  203.0 55.8 %collective-permute-start.17 = (bf16[128,2048]{1,0:T(8,128)(2,1)S(1)}, bf16[128,2048]{1,0:T(8,128)(2,1)S(1)}, u32[]{:S(2)}, u32[]{:S(2)}) collective-permute-start(bf16[128,2048]{1,0:T(8,128)(2,1)S(1)} %get-tuple-element.844), channel_id=1, source_target_pairs={{0,6},{1,7},{2,4},{3,5},{4,2},{5,3},{6,0},{7,1},{8,14},{9,15},{10,... | collective-permute-start | bytes 1572872 | tf_op jit(solution)/shard_map/ppermute | solution.py:211
  214.3 101.1 %collective-permute-start.28 = (bf16[176,2048]{1,0:T(8,128)(2,1)S(1)}, bf16[176,2048]{1,0:T(8,128)(2,1)S(1)}, u32[]{:S(2)}, u32[]{:S(2)}) collective-permute-start(bf16[176,2048]{1,0:T(8,128)(2,1)S(1)} %bitcast.403), channel_id=1, source_target_pairs={{0,8},{8,0},{16,24},{24,16},{1,9},{9,1},{17,25},{25,17},{2,10},{10... | collective-permute-start | bytes 2162696 | tf_op jit(solution)/shard_map/ppermute | solution.py:211
  216.2 55.3 %collective-permute-start.42 = (bf16[128,2048]{1,0:T(8,128)(2,1)S(1)}, bf16[128,2048]{1,0:T(8,128)(2,1)S(1)}, u32[]{:S(2)}, u32[]{:S(2)}) collective-permute-start(bf16[128,2048]{1,0:T(8,128)(2,1)S(1)} %collective-permute-done.41), channel_id=1, source_target_pairs={{0,1},{1,0},{2,3},{3,2},{4,5},{5,4},{6,7},{7,6},{8,9},{9,8},{10,11... | collective-permute-start | bytes 1572872 | tf_op jit(solution)/shard_map/ppermute | solution.py:211
  224.8 47.9 %collective-permute-start.44 = (bf16[128,2048]{1,0:T(8,128)(2,1)S(1)}, bf16[128,2048]{1,0:T(8,128)(2,1)S(1)}, u32[]{:S(2)}, u32[]{:S(2)}) collective-permute-start(bf16[128,2048]{1,0:T(8,128)(2,1)S(1)} %collective-permute-done.43), channel_id=1, source_target_pairs={{0,1},{1,0},{2,3},{3,2},{4,5},{5,4},{6,7},{7,6},{8,9},{9,8},{10,11... | collective-permute-start | bytes 1572872 | tf_op jit(solution)/shard_map/ppermute | solution.py:211
  315.3 45.1 %collective-permute-start.27 = (bf16[176,2048]{1,0:T(8,128)(2,1)S(1)}, bf16[176,2048]{1,0:T(8,128)(2,1)S(1)}, u32[]{:S(2)}, u32[]{:S(2)}) collective-permute-start(bf16[176,2048]{1,0:T(8,128)(2,1)S(1)} %bitcast.381), channel_id=1, source_target_pairs={{0,24},{8,16},{16,8},{24,0},{1,25},{9,17},{17,9},{25,1},{2,26},{10... | collective-permute-start | bytes 2162696 | tf_op jit(solution)/shard_map/ppermute | solution.py:211
  419.0 39.4 %collective-permute-start.37 = (bf16[128,2048]{1,0:T(8,128)(2,1)}, bf16[128,2048]{1,0:T(8,128)(2,1)S(1)}, u32[]{:S(2)}, u32[]{:S(2)}) collective-permute-start(bf16[128,2048]{1,0:T(8,128)(2,1)} %get-tuple-element.841), channel_id=1, source_target_pairs={{0,6},{1,7},{2,4},{3,5},{4,2},{5,3},{6,0},{7,1},{8,14},{9,15},{10,... | collective-permute-start | bytes 1572872 | tf_op jit(solution)/shard_map/ppermute | solution.py:211
  423.5 40.8 %collective-permute-start.46 = (bf16[128,2048]{1,0:T(8,128)(2,1)S(1)}, bf16[128,2048]{1,0:T(8,128)(2,1)S(1)}, u32[]{:S(2)}, u32[]{:S(2)}) collective-permute-start(bf16[128,2048]{1,0:T(8,128)(2,1)S(1)} %get-tuple-element.837), channel_id=1, source_target_pairs={{0,2},{1,3},{2,0},{3,1},{4,6},{5,7},{6,4},{7,5},{8,10},{9,11},{10,... | collective-permute-start | bytes 1572872 | tf_op jit(solution)/shard_map/ppermute | solution.py:211
  424.6 76.9 %collective-permute-start.47 = (bf16[128,2048]{1,0:T(8,128)(2,1)S(1)}, bf16[128,2048]{1,0:T(8,128)(2,1)S(1)}, u32[]{:S(2)}, u32[]{:S(2)}) collective-permute-start(bf16[128,2048]{1,0:T(8,128)(2,1)S(1)} %get-tuple-element.839), channel_id=1, source_target_pairs={{0,4},{1,5},{2,6},{3,7},{4,0},{5,1},{6,2},{7,3},{8,12},{9,13},{10,... | collective-permute-start | bytes 1572872 | tf_op jit(solution)/shard_map/ppermute | solution.py:211
  441.0 62.4 %collective-permute-start.48 = (bf16[128,2048]{1,0:T(8,128)(2,1)S(1)}, bf16[128,2048]{1,0:T(8,128)(2,1)S(1)}, u32[]{:S(2)}, u32[]{:S(2)}) collective-permute-start(bf16[128,2048]{1,0:T(8,128)(2,1)S(1)} %get-tuple-element.838), channel_id=1, source_target_pairs={{0,6},{1,7},{2,4},{3,5},{4,2},{5,3},{6,0},{7,1},{8,14},{9,15},{10,... | collective-permute-start | bytes 1572872 | tf_op jit(solution)/shard_map/ppermute | solution.py:211
  456.6 51.2 %collective-permute-start.73 = (bf16[176,2048]{1,0:T(8,128)(2,1)}, bf16[176,2048]{1,0:T(8,128)(2,1)S(1)}, u32[]{:S(2)}, u32[]{:S(2)}) collective-permute-start(bf16[176,2048]{1,0:T(8,128)(2,1)} %get-tuple-element.825), channel_id=1, source_target_pairs={{0,8},{8,0},{16,24},{24,16},{1,9},{9,1},{17,25},{25,17},{2,10},{10... | collective-permute-start | bytes 2162696 | tf_op jit(solution)/shard_map/ppermute | solution.py:211
  458.4 52.5 %collective-permute-start.74 = (bf16[176,2048]{1,0:T(8,128)(2,1)}, bf16[176,2048]{1,0:T(8,128)(2,1)S(1)}, u32[]{:S(2)}, u32[]{:S(2)}) collective-permute-start(bf16[176,2048]{1,0:T(8,128)(2,1)} %get-tuple-element.827), channel_id=1, source_target_pairs={{0,16},{8,24},{16,0},{24,8},{1,17},{9,25},{17,1},{25,9},{2,18},{10... | collective-permute-start | bytes 2162696 | tf_op jit(solution)/shard_map/ppermute | solution.py:211
  464.3 56.2 %collective-permute-start.75 = (bf16[176,2048]{1,0:T(8,128)(2,1)}, bf16[176,2048]{1,0:T(8,128)(2,1)S(1)}, u32[]{:S(2)}, u32[]{:S(2)}) collective-permute-start(bf16[176,2048]{1,0:T(8,128)(2,1)} %get-tuple-element.826), channel_id=1, source_target_pairs={{0,24},{8,16},{16,8},{24,0},{1,25},{9,17},{17,9},{25,1},{2,26},{10... | collective-permute-start | bytes 2162696 | tf_op jit(solution)/shard_map/ppermute | solution.py:211
  646.1 41.6 %collective-permute-start.57 = (bf16[128,2048]{1,0:T(8,128)(2,1)}, bf16[128,2048]{1,0:T(8,128)(2,1)}, u32[]{:S(2)}, u32[]{:S(2)}) collective-permute-start(bf16[128,2048]{1,0:T(8,128)(2,1)} %get-tuple-element.834), channel_id=1, source_target_pairs={{0,2},{1,3},{2,0},{3,1},{4,6},{5,7},{6,4},{7,5},{8,10},{9,11},{10,... | collective-permute-start | bytes 1572872 | tf_op jit(solution)/shard_map/ppermute | solution.py:211
  654.7 39.5 %collective-permute-start.58 = (bf16[128,2048]{1,0:T(8,128)(2,1)}, bf16[128,2048]{1,0:T(8,128)(2,1)}, u32[]{:S(2)}, u32[]{:S(2)}) collective-permute-start(bf16[128,2048]{1,0:T(8,128)(2,1)} %get-tuple-element.836), channel_id=1, source_target_pairs={{0,4},{1,5},{2,6},{3,7},{4,0},{5,1},{6,2},{7,3},{8,12},{9,13},{10,... | collective-permute-start | bytes 1572872 | tf_op jit(solution)/shard_map/ppermute | solution.py:211
  655.7 39.2 %collective-permute-start.59 = (bf16[128,2048]{1,0:T(8,128)(2,1)}, bf16[128,2048]{1,0:T(8,128)(2,1)}, u32[]{:S(2)}, u32[]{:S(2)}) collective-permute-start(bf16[128,2048]{1,0:T(8,128)(2,1)} %get-tuple-element.835), channel_id=1, source_target_pairs={{0,6},{1,7},{2,4},{3,5},{4,2},{5,3},{6,0},{7,1},{8,14},{9,15},{10,... | collective-permute-start | bytes 1572872 | tf_op jit(solution)/shard_map/ppermute | solution.py:211
  669.8 60.6 %collective-permute-start.67 = (bf16[176,2048]{1,0:T(8,128)(2,1)}, bf16[176,2048]{1,0:T(8,128)(2,1)}, u32[]{:S(2)}, u32[]{:S(2)}) collective-permute-start(bf16[176,2048]{1,0:T(8,128)(2,1)} %get-tuple-element.831), channel_id=1, source_target_pairs={{0,8},{8,0},{16,24},{24,16},{1,9},{9,1},{17,25},{25,17},{2,10},{10... | collective-permute-start | bytes 2162696 | tf_op jit(solution)/shard_map/ppermute | solution.py:211
  673.3 57.2 %collective-permute-start.68 = (bf16[176,2048]{1,0:T(8,128)(2,1)}, bf16[176,2048]{1,0:T(8,128)(2,1)}, u32[]{:S(2)}, u32[]{:S(2)}) collective-permute-start(bf16[176,2048]{1,0:T(8,128)(2,1)} %get-tuple-element.833), channel_id=1, source_target_pairs={{0,16},{8,24},{16,0},{24,8},{1,17},{9,25},{17,1},{25,9},{2,18},{10... | collective-permute-start | bytes 2162696 | tf_op jit(solution)/shard_map/ppermute | solution.py:211
  677.3 46.6 %all-to-all-start.3 = ((bf16[8,64,768]{2,1,0:T(8,128)(2,1)}), bf16[8,64,768]{2,1,0:T(8,128)(2,1)S(1)}, u32[]{:S(2)}, u32[]{:S(2)}) async-start(bf16[8,64,768]{2,1,0:T(8,128)(2,1)} %bitcast.371), calls=%async_computation.3 | async-start | bytes 1572864 | tf_op jit(solution)/shard_map/all_to_all | solution.py:416
  687.7 42.7 %collective-permute-start.69 = (bf16[176,2048]{1,0:T(8,128)(2,1)}, bf16[176,2048]{1,0:T(8,128)(2,1)}, u32[]{:S(2)}, u32[]{:S(2)}) collective-permute-start(bf16[176,2048]{1,0:T(8,128)(2,1)} %get-tuple-element.832), channel_id=1, source_target_pairs={{0,24},{8,16},{16,8},{24,0},{1,25},{9,17},{17,9},{25,1},{2,26},{10... | collective-permute-start | bytes 2162696 | tf_op jit(solution)/shard_map/ppermute | solution.py:211
  694.2 39.6 %collective-permute-start.66 = (f32[64,2048]{1,0:T(8,128)S(1)}, f32[64,2048]{1,0:T(8,128)S(1)}, u32[]{:S(2)}, u32[]{:S(2)}) collective-permute-start(f32[64,2048]{1,0:T(8,128)S(1)} %convert_add_fusion.3), channel_id=1, source_target_pairs={{0,0},{1,4},{2,8},{3,12},{4,16},{5,20},{6,24},{7,28},{8,1},{9,5},{... | collective-permute-start | bytes 1572872 | tf_op jit(solution)/shard_map/ppermute | solution.py:431
  (109 other events, 2509.0 us)

commit v2 on v1

v2 whole, which is shorter than its diff:
```python
import jax
import jax.numpy as jnp
from jax import lax
from jax.experimental import pallas as pl
from jax.experimental.pallas import tpu as pltpu
from jax.sharding import PartitionSpec as P

D = 2048
HEADS = 32
HEAD = 64
ROT = 16
LANGS = 7


EPS = 1e-05
BASE = 10000.0
NEG = -1e30


def contract(left, right, left_dim, right_dim):
    return lax.dot_general(
        left, right, (((left_dim,), (right_dim,)), ((), ())), preferred_element_type=jnp.float32
    )


def norm_forward(values, gain, bias):
    average = jnp.mean(values, axis=-1, keepdims=True)
    centered = values - average
    variance = jnp.mean(centered * centered, axis=-1, keepdims=True)
    inverse = lax.rsqrt(variance + EPS)
    scaled = centered * inverse
    return (scaled * gain + bias, scaled, inverse)


def norm_backward(grad_normed, scaled, inverse, gain):
    grad_scaled = grad_normed * gain
    grad_values = inverse * (
        grad_scaled
        - jnp.mean(grad_scaled, axis=-1, keepdims=True)
        - scaled * jnp.mean(grad_scaled * scaled, axis=-1, keepdims=True)
    )
    return (grad_values, jnp.sum(grad_normed * scaled, axis=0), jnp.sum(grad_normed, axis=0))


def row_tables(doc_lengths, length):
    ends = jnp.cumsum(doc_lengths)
    starts = ends - doc_lengths
    places = jnp.arange(length, dtype=jnp.int32)
    segment = jnp.sum((places[:, None] >= ends[None, :]).astype(jnp.int32), axis=1)
    member = segment[:, None] == jnp.arange(ends.shape[0], dtype=jnp.int32)[None, :]
    offsets = jnp.sum(jnp.where(member, starts[None, :], 0), axis=1)
    position = (places - offsets).astype(jnp.float32)
    half_rot = ROT // 2
    freq = BASE ** (-(2.0 * jnp.arange(half_rot, dtype=jnp.float32)) / ROT)
    angles = position[:, None] * freq[None, :]
    return (offsets, jnp.cos(angles), jnp.sin(angles))


def head_lanes(shape, dim, head):
    place = lax.broadcasted_iota(jnp.int32, shape, dim)
    return (place >= head * HEAD) & (place < (head + 1) * HEAD)


def turn(values, tables, direction):
    lanes = values.shape[1]
    cosines, sines_former, sines_latter = tables
    after = pltpu.roll(values, lanes - ROT // 2, 1)
    before = pltpu.roll(values, ROT // 2, 1)
    return values * cosines + direction * (before * sines_latter - after * sines_former)


def allowed_pairs(first_ref, start, block, keys):
    key_at = lax.broadcasted_iota(jnp.int32, (keys, block), 0)
    query_at = start + lax.broadcasted_iota(jnp.int32, (keys, block), 1)
    return (key_at >= first_ref[:, pl.ds(start, block)]) & (key_at <= query_at)


def over_blocks(length, block, step):
    count = length // block
    if count <= 4:
        for i in range(count):
            step(i * block, (i + 1) * block)
    else:

        def body(i, carry):
            step(pl.multiple_of(i * block, block), length)
            return carry

        lax.fori_loop(0, count, body, 0)


def forward_kernel(
    qkv_ref, cos_ref, former_ref, latter_ref, first_ref,
    query_ref, key_ref, context_ref, logsum_ref, value_t,
):
    length, width = query_ref.shape
    lanes = cos_ref.shape[1]
    block = min(256, length)
    tables = (cos_ref[...], former_ref[...], latter_ref[...])
    for group in range(width // lanes):
        part = slice(group * lanes, (group + 1) * lanes)

        def columns(c):
            begin = c * width + group * lanes
            return qkv_ref[:, begin : begin + lanes].astype(jnp.float32)

        query_ref[:, part] = turn(columns(0), tables, 1.0).astype(jnp.bfloat16)
        key_ref[:, part] = turn(columns(1), tables, 1.0).astype(jnp.bfloat16)
        value_t[...] = columns(2).T.astype(jnp.bfloat16)

        def step(start, keys):
            queries = query_ref[pl.ds(start, block), part].astype(jnp.float32) * HEAD ** (-0.5)
            allowed = allowed_pairs(first_ref, start, block, keys)
            found = []
            for head in range(lanes // HEAD):
                own = jnp.where(head_lanes(queries.shape, 1, head), queries, 0.0)
                scores = contract(key_ref[0:keys, part], own.astype(jnp.bfloat16), 1, 1)
                scores = jnp.where(allowed, scores, NEG)
                most = jnp.max(scores, axis=0, keepdims=True)
                weights = jnp.exp(scores - most)
                total = jnp.sum(weights, axis=0, keepdims=True)
                probs = (weights * (1.0 / total)).astype(jnp.bfloat16)
                logsum_ref[
                    pl.ds(group * (lanes // HEAD) + head, 1), pl.ds(start, block)
                ] = most + jnp.log(total)
                context = contract(value_t[:, 0:keys], probs, 1, 0)
                found.append(context[head * HEAD : (head + 1) * HEAD])
            context_ref[pl.ds(start, block), part] = (
                jnp.concatenate(found, axis=0).T.astype(jnp.bfloat16)
            )

        over_blocks(length, block, step)


def backward_kernel(
    query_ref, key_ref, qkv_ref, context_grad_ref, logsum_ref, cos_ref, former_ref, latter_ref,
    first_ref, grad_ref, key_t, grad_query, grad_key, grad_value,
):
    length, width = query_ref.shape
    lanes = cos_ref.shape[1]
    block = min(256, length)
    scale = HEAD ** (-0.5)
    tables = (cos_ref[...], former_ref[...], latter_ref[...])
    for group in range(width // lanes):
        part = slice(group * lanes, (group + 1) * lanes)
        value_part = slice(2 * width + group * lanes, 2 * width + (group + 1) * lanes)
        key_t[...] = key_ref[:, part].astype(jnp.float32).T.astype(jnp.bfloat16)
        grad_key[...] = jnp.zeros_like(grad_key)
        grad_value[...] = jnp.zeros_like(grad_value)

        def step(start, keys):
            queries = query_ref[pl.ds(start, block), part].astype(jnp.float32) * scale
            grads = context_grad_ref[pl.ds(start, block), part].astype(jnp.float32)
            allowed = allowed_pairs(first_ref, start, block, keys)
            found = []
            for head in range(lanes // HEAD):
                mine = head_lanes(queries.shape, 1, head)
                own_query = jnp.where(mine, queries, 0.0).astype(jnp.bfloat16)
                own_grad = jnp.where(mine, grads, 0.0).astype(jnp.bfloat16)
                scores = contract(key_ref[0:keys, part], own_query, 1, 1)
                logsum = logsum_ref[
                    pl.ds(group * (lanes // HEAD) + head, 1), pl.ds(start, block)
                ]
                soft = jnp.exp(jnp.where(allowed, scores, NEG) - logsum)
                grad_soft = contract(qkv_ref[0:keys, value_part], own_grad, 1, 1)
                weighed = soft * grad_soft
                delta = jnp.sum(weighed, axis=0, keepdims=True)
                grad_scores = (weighed - soft * delta).astype(jnp.bfloat16)
                grad_value[0:keys] += contract(soft.astype(jnp.bfloat16), own_grad, 1, 0)
                grad_key[0:keys] += contract(grad_scores, own_query, 1, 0)
                turned = contract(key_t[:, 0:keys], grad_scores, 1, 0)
                found.append(turned[head * HEAD : (head + 1) * HEAD])
            grad_query[pl.ds(start, block), :] = jnp.concatenate(found, axis=0).T * scale

        over_blocks(length, block, step)
        for c, grads in ((0, grad_query), (1, grad_key)):
            begin = c * width + group * lanes
            grad_ref[:, begin : begin + lanes] = turn(grads[...], tables, -1.0).astype(
                jnp.bfloat16
            )
        grad_ref[:, value_part] = grad_value[...].astype(jnp.bfloat16)


def rotation_tables(cosines, sines, lanes):
    length = cosines.shape[0]
    rest = jnp.ones((length, HEAD - ROT), jnp.float32)
    none = jnp.zeros_like(sines)
    heads = lanes // HEAD
    return (
        jnp.tile(jnp.concatenate([cosines, cosines, rest], axis=1), (1, heads)),
        jnp.tile(jnp.concatenate([sines, none, 0.0 * rest], axis=1), (1, heads)),
        jnp.tile(jnp.concatenate([none, sines, 0.0 * rest], axis=1), (1, heads)),
    )


VMEM_BYTES = 48 * 1024 * 1024


def attention_forward(projected, tables, first):
    length, width = projected.shape[0], projected.shape[1] // 3
    lanes = tables[0].shape[1]
    rows = jax.ShapeDtypeStruct((length, width), jnp.bfloat16)
    return pl.pallas_call(
        forward_kernel,
        out_shape=(
            rows,
            rows,
            rows,
            jax.ShapeDtypeStruct((width // HEAD, length), jnp.float32),
        ),
        scratch_shapes=[pltpu.VMEM((lanes, length), jnp.bfloat16)],
        compiler_params=pltpu.CompilerParams(vmem_limit_bytes=VMEM_BYTES),
        cost_estimate=pl.CostEstimate(
            flops=4 * length * length * width,
            bytes_accessed=12 * length * width,
            transcendentals=length * length * width // HEAD,
        ),
        name="attention_forward",
    )(projected, *tables, first)


def attention_backward(queries, key_heads, projected, grad_context, logsum, tables, first):
    length, width = queries.shape
    lanes = tables[0].shape[1]
    return pl.pallas_call(
        backward_kernel,
        out_shape=jax.ShapeDtypeStruct((length, 3 * width), jnp.bfloat16),
        scratch_shapes=[
            pltpu.VMEM((lanes, length), jnp.bfloat16),
            pltpu.VMEM((length, lanes), jnp.float32),
            pltpu.VMEM((length, lanes), jnp.float32),
            pltpu.VMEM((length, lanes), jnp.float32),
        ],
        compiler_params=pltpu.CompilerParams(vmem_limit_bytes=VMEM_BYTES),
        cost_estimate=pl.CostEstimate(
            flops=10 * length * length * width,
            bytes_accessed=18 * length * width,
            transcendentals=length * length * width // HEAD,
        ),
        name="attention_backward",
    )(queries, key_heads, projected, grad_context, logsum, *tables, first)


def gate_backward(gate_values, up_values, grad_hidden):
    sigmoid_gate = jax.nn.sigmoid(gate_values)
    silu_gate = gate_values * sigmoid_gate
    grad_gate = (
        grad_hidden * up_values * sigmoid_gate * (1.0 + gate_values * (1.0 - sigmoid_gate))
    ).astype(jnp.bfloat16)
    grad_up = (grad_hidden * silu_gate).astype(jnp.bfloat16)
    return (grad_gate, grad_up)


def permute(value, axis, offset):
    size = lax.axis_size(axis)
    return lax.ppermute(value, axis, [(i, i ^ offset) for i in range(size)])


def gather_dp(piece):
    return [piece] + [permute(piece, "dp", k) for k in range(1, lax.axis_size("dp"))]


def scatter_dp(pieces):
    total = pieces[0].astype(jnp.float32)
    for k in range(1, len(pieces)):
        total = total + permute(pieces[k].astype(jnp.bfloat16), "dp", k).astype(jnp.float32)
    return total


def gather_seq(piece):
    return lax.all_gather(piece, "seq", axis=0, tiled=True)


def scatter_seq(terms):
    return lax.psum_scatter(
        terms.astype(jnp.bfloat16), "seq", scatter_dimension=0, tiled=True
    ).astype(jnp.float32)


def after(value, *others):
    return lax.optimization_barrier((value,) + others)[0]


def place(pieces, index):
    block = pieces[0].shape[0]
    result = jnp.zeros((block * len(pieces),) + pieces[0].shape[1:], pieces[0].dtype)
    for k, piece in enumerate(pieces):
        result = lax.dynamic_update_slice_in_dim(result, piece, (index ^ k) * block, 0)
    return result


def per_device(
    layer_input,
    doc_lengths,
    language,
    lang_table,
    attn_norm_gain,
    attn_norm_bias,
    qkv_weight,
    qkv_bias,
    out_weight,
    mlp_norm_gain,
    mlp_norm_bias,
    gate_weight,
    up_weight,
    down_weight,
    cotangent,
):
    tokens = layer_input.shape[1]
    groups = lax.axis_size("seq")
    rows = lax.axis_size("dp")
    devices = rows * groups
    at_dp = lax.axis_index("dp")
    at_seq = lax.axis_index("seq")
    length = tokens * groups
    heads_here = HEADS // groups
    local_width = heads_here * HEAD
    own = D // devices
    owner = [(i, (i % groups) * rows + i // groups) for i in range(devices)]
    back = [(b, a) for a, b in owner]
    small = jnp.concatenate(
        [
            lang_table,
            attn_norm_gain[None],
            attn_norm_bias[None],
            mlp_norm_gain[None],
            mlp_norm_bias[None],
            qkv_bias,
            jnp.broadcast_to(language.astype(jnp.bfloat16)[:, None], (1, own)),
            jnp.zeros((1, own), jnp.bfloat16),
        ],
        axis=0,
    )
    spread = lax.all_to_all(
        jnp.broadcast_to(small[None], (devices,) + small.shape),
        ("dp", "seq"),
        split_axis=0,
        concat_axis=0,
        tiled=True,
    )
    table = jnp.swapaxes(spread, 0, 1).reshape(small.shape[0], D).astype(jnp.float32)
    languages = spread[:, LANGS + 7, 0].astype(jnp.int32)
    gain_attn = table[LANGS]
    bias_attn = table[LANGS + 1]
    gain_mlp = table[LANGS + 2]
    bias_mlp = table[LANGS + 3]
    bias_qkv = lax.dynamic_slice_in_dim(
        table[LANGS + 4 : LANGS + 7], at_seq * local_width, local_width, 1
    ).reshape(3 * local_width)
    chooser = (jnp.arange(LANGS, dtype=jnp.int32) == language[0]).astype(jnp.float32)
    lang_row = jnp.sum(chooser[:, None] * table[:LANGS], axis=0)[None, :]
    qkv_part = lax.all_to_all(
        qkv_weight.reshape(own, 3, groups, local_width).transpose(2, 0, 1, 3).reshape(
            groups, own, 3 * local_width
        ),
        "seq",
        split_axis=0,
        concat_axis=0,
        tiled=True,
    ).reshape(groups * own, 3 * local_width)
    head_qkv = place(gather_dp(qkv_part), at_dp)
    head_out = place(gather_dp(lax.ppermute(out_weight, ("dp", "seq"), back)), at_dp)
    cols_gate = jnp.concatenate(gather_dp(gate_weight.T), axis=0)
    cols_up = jnp.concatenate(gather_dp(up_weight.T), axis=0)
    cols_down = jnp.concatenate(gather_dp(down_weight), axis=0)
    offsets, cosines, sines = row_tables(doc_lengths[0], length)
    tables = rotation_tables(cosines, sines, min(128, local_width))
    first = offsets[None, :]
    grad_out = cotangent[0]
    input_all = gather_seq(layer_input[0])
    grad_all = gather_seq(after(grad_out, input_all))
    normed_all = norm_forward(input_all.astype(jnp.float32) + lang_row, gain_attn, bias_attn)[
        0
    ].astype(jnp.bfloat16)
    resid_in = layer_input[0].astype(jnp.float32) + lang_row
    unused, scaled_attn, inverse_attn = norm_forward(resid_in, gain_attn, bias_attn)
    projected = (
        jnp.dot(normed_all, head_qkv, preferred_element_type=jnp.float32) + bias_qkv
    ).astype(jnp.bfloat16)
    rot_query, rot_key, context_all, logsum = attention_forward(projected, tables, first)
    resid_mid = resid_in + scatter_seq(
        jnp.dot(context_all, head_out, preferred_element_type=jnp.float32)
    )
    normed_mlp, scaled_mlp, inverse_mlp = norm_forward(resid_mid, gain_mlp, bias_mlp)
    rows_all = gather_seq(normed_mlp.astype(jnp.bfloat16))
    gate_values = contract(rows_all, cols_gate, 1, 1)
    up_values = contract(rows_all, cols_up, 1, 1)
    hidden = (jax.nn.silu(gate_values) * up_values).astype(jnp.bfloat16)
    grad_hidden = contract(grad_all, cols_down, 1, 1)
    grad_gate, grad_up = gate_backward(gate_values, up_values, grad_hidden)
    grad_rows = contract(grad_gate, cols_gate, 1, 0) + contract(grad_up, cols_up, 1, 0)
    grad_normed_mlp = scatter_seq(grad_rows)
    def to_owner(terms):
        return scatter_dp(jnp.split(terms.astype(jnp.bfloat16), rows, axis=0))

    out_gate = to_owner(contract(grad_gate, rows_all, 0, 0)).T
    out_up = to_owner(contract(grad_up, rows_all, 0, 0)).T
    out_down = to_owner(contract(hidden, grad_all, 0, 0))
    grad_mid_norm, grad_gain_mlp, grad_bias_mlp = norm_backward(
        grad_normed_mlp, scaled_mlp, inverse_mlp, gain_mlp
    )
    grad_mid = grad_out.astype(jnp.float32) + grad_mid_norm
    branch_all = gather_seq(grad_mid.astype(jnp.bfloat16))
    mlp_terms = jnp.dot(hidden, cols_down, preferred_element_type=jnp.float32)
    mlp_out = scatter_seq(after(mlp_terms.astype(jnp.bfloat16), branch_all))
    layer_output = (resid_mid + mlp_out).astype(jnp.bfloat16)
    grad_heads = contract(branch_all, head_out, 1, 1).astype(jnp.bfloat16)
    grad_stack = attention_backward(
        rot_query, rot_key, projected, grad_heads, logsum, tables, first
    )
    grad_normed_attn = scatter_seq(contract(grad_stack, head_qkv, 1, 1))
    grad_in_norm, grad_gain_attn, grad_bias_attn = norm_backward(
        grad_normed_attn, scaled_attn, inverse_attn, gain_attn
    )
    grad_input = grad_mid + grad_in_norm

    def dp_terms(terms):
        block = terms.shape[0] // rows
        return [
            lax.dynamic_slice_in_dim(terms, (at_dp ^ k) * block, block, 0) for k in range(rows)
        ]

    slice_summed = scatter_dp(dp_terms(contract(normed_all, grad_stack, 0, 0).astype(jnp.bfloat16)))
    grad_qkv_out = (
        lax.all_to_all(
            slice_summed.astype(jnp.bfloat16).reshape(groups, own, 3 * local_width),
            "seq",
            split_axis=0,
            concat_axis=0,
            tiled=True,
        )
        .reshape(groups, own, 3, local_width)
        .transpose(1, 2, 0, 3)
        .reshape(own, 3 * D)
        .astype(jnp.float32)
    )
    head_out_terms = scatter_dp(
        dp_terms(contract(context_all, branch_all, 0, 0).astype(jnp.bfloat16))
    )
    out_proj = lax.ppermute(head_out_terms, ("dp", "seq"), owner)
    grad_bias_qkv = jnp.sum(grad_stack.astype(jnp.float32), axis=0).reshape(3, local_width)
    terms = jnp.concatenate(
        [
            grad_gain_attn[None],
            grad_bias_attn[None],
            grad_gain_mlp[None],
            grad_bias_mlp[None],
            jnp.sum(grad_input, axis=0)[None],
            lax.dynamic_update_slice(
                jnp.zeros((3, D), jnp.float32), grad_bias_qkv, (0, at_seq * local_width)
            ),
        ],
        axis=0,
    )
    arrived = lax.all_to_all(
        terms.reshape(terms.shape[0], devices, own).swapaxes(0, 1),
        ("dp", "seq"),
        split_axis=0,
        concat_axis=0,
        tiled=True,
    )
    summed = jnp.sum(arrived, axis=0)
    members = (languages[:, None] == jnp.arange(LANGS, dtype=jnp.int32)[None, :]).astype(
        jnp.float32
    )
    lang_g = jnp.sum(members[:, :, None] * arrived[:, 4][:, None, :], axis=0)
    return (
        layer_output[None],
        grad_input[None],
        lang_g,
        summed[0],
        summed[1],
        grad_qkv_out,
        summed[5:8],
        out_proj,
        summed[2],
        summed[3],
        out_gate,
        out_up,
        out_down,
    )


def solution(mesh):
    placed = (
        P("dp", "seq", None),
        P("dp", None),
        P("dp"),
        P(None, ("dp", "seq")),
        P(("dp", "seq")),
        P(("dp", "seq")),
        P(("dp", "seq"), None),
        P(None, ("dp", "seq")),
        P(("dp", "seq"), None),
        P(("dp", "seq")),
        P(("dp", "seq")),
        P(None, ("dp", "seq")),
        P(None, ("dp", "seq")),
        P(("dp", "seq"), None),
        P("dp", "seq", None),
    )
    return jax.shard_map(
        per_device,
        mesh=mesh,
        in_specs=placed,
        out_specs=(
            P("dp", "seq", None),
            P("dp", "seq", None),
            P(None, ("dp", "seq")),
            P(("dp", "seq")),
            P(("dp", "seq")),
            P(("dp", "seq"), None),
            P(None, ("dp", "seq")),
            P(("dp", "seq"), None),
            P(("dp", "seq")),
            P(("dp", "seq")),
            P(None, ("dp", "seq")),
            P(None, ("dp", "seq")),
            P(("dp", "seq"), None),
        ),
        check_vma=False,
    )
```

time: 747 us -> 665 us (0.89)
  local copies, waits for them, and re-layouts: 94.1 us -> 37.8 us
  starting transfers between devices: 142 us -> 91.3 us
  other arithmetic: 63.7 us -> 35.2 us
  waiting for transfers between devices: 345 us -> 372 us
  Pallas kernels: 0 us -> 20.9 us
  between operations: 3.15 us -> 15.8 us
  matrix products: 90.8 us -> 80.7 us
    reduce_scatter x0 -> x4, waiting for transfers between devices: none -> 98.5 us  [scatter_seq(): lax.psum_scatter(terms.astype(jnp.bfloat16), 'seq', scatter_dimension=0,...]
    ppermute x74 -> x30, waiting for transfers between devices: 286 us -> 188 us  [permute(): return lax.ppermute(value, axis, [(i, i ^ offset) for i in range(size)])]
    ppermute x74 -> x30, starting transfers between devices: 112 us -> 62.3 us  [permute(): return lax.ppermute(value, axis, [(i, i ^ offset) for i in range(size)])]
    all_gather x0 -> x4, waiting for transfers between devices: none -> 45.2 us  [gather_seq(): return lax.all_gather(piece, 'seq', axis=0, tiled=True)]
    unnamed x152 -> x73, local copies, waits for them, and re-layouts: 51 us -> 15.2 us
    all_to_all x1, waiting for transfers between devices: 34.2 us -> 0.01 us  [per_device(): lax.all_to_all(jnp.broadcast_to(small[None], (devices,) + small.shape), (...]
    dot_general x22 -> x1, matrix products: 35.5 us -> 7.68 us  [per_device(): mlp_terms = jnp.dot(hidden, cols_down, preferred_element_type=jnp.float32)]
    pallas_call x0 -> x2, Pallas kernels: none -> 20.9 us  [the longest x1 10.8 us: attention_backward(): pl.pallas_call(backward_kernel, out_shape=jax.ShapeDtypeStruct((length, 3...]
  transfers between devices with their start and end apart: 80 -> 44, of which waited for: 27 -> 19; matrix products, arithmetic and copies ran while one was open for 23% -> 14% of each run, Pallas kernels for 0% -> 0%
where the time goes in v2:
time: 665 us; the launch traced here: 654 us
  waiting for transfers between devices  372 us (56%)
  starting transfers between devices  91.3 us (14%)
  matrix products  80.7 us (12%)
  local copies, waits for them, and re-layouts  37.8 us (6%)
  other arithmetic  35.2 us (5%)
  Pallas kernels  20.9 us (3%)
  between operations  15.8 us (2%)
    ppermute x30, waiting for transfers between devices, permute(): return lax.ppermute(value, axis, [(i, i ^ offset) for i in range(size)])  188 us
    reduce_scatter x4, waiting for transfers between devices, scatter_seq(): lax.psum_scatter(terms.astype(jnp.bfloat16), 'seq', scatter_dimension=0,...  98.5 us
    dot_general x12, matrix products, contract(): lax.dot_general(left, right, (((left_dim,), (right_dim,)), ((), ())), pre...  63.7 us
    ppermute x30, starting transfers between devices, permute(): return lax.ppermute(value, axis, [(i, i ^ offset) for i in range(size)])  62.3 us
    all_gather x4, waiting for transfers between devices, gather_seq(): return lax.all_gather(piece, 'seq', axis=0, tiled=True)  45.2 us
    all_to_all x1, waiting for transfers between devices, per_device(): lax.all_to_all(qkv_weight.reshape(own, 3, groups, local_width).transpose(...  20.8 us
    all_to_all x1, waiting for transfers between devices, per_device(): lax.all_to_all(slice_summed.astype(jnp.bfloat16).reshape(groups, own, 3 *...  18.1 us
    unnamed x73, local copies, waits for them, and re-layouts  15.2 us
  transfers between devices with their start and end apart: 44, of which 19 were waited for; matrix products, arithmetic and copies ran while one was open for 14% of the time, Pallas kernels for 0%

profile of v2, /device:TPU:0, one launch (start us, length us, event | category | flops | bytes accessed | tf_op | source)
XLA Modules:
  0.0 653.9 jit_solution(12206635348578598756)
XLA Ops:
  10.8 7.3 %all-to-all-start = ((bf16[32,2,512]{2,1,0:T(2,128)(2,1)}), bf16[32,2,512]{2,1,0:T(2,128)(2,1)S(1)}, u32[]{:S(2)}, u32[]{:S(2)}) async-start(bf16[32,2,512]{2,1,0:T(2,128)(2,1)} %reshape.234), calls=%async_computation | async-start | bytes 131072 | tf_op jit(solution)/shard_map/all_to_all | solution.py:334
  27.0 5.0 all-to-all-start.1
  36.0 24.8 %collective-permute-start.6 = (bf16[64,2048]{1,0:T(8,128)(2,1)}, bf16[64,2048]{1,0:T(8,128)(2,1)S(1)}, u32[]{:S(2)}, u32[]{:S(2)}) collective-permute-start(bf16[64,2048]{1,0:T(8,128)(2,1)} %collective-permute-done.3), channel_id=1, source_target_pairs={{0,24},{8,16},{16,8},{24,0},{1,25},{9,17},{17,9},{25,1},{2,26},{10... | collective-permute-start | bytes 786440 | tf_op jit(solution)/shard_map/ppermute | solution.py:256
  62.5 20.8 %all-to-all-done.1 = bf16[8,64,768]{2,1,0:T(8,128)(2,1)} async-done(((bf16[8,64,768]{2,1,0:T(8,128)(2,1)}), bf16[8,64,768]{2,1,0:T(8,128)(2,1)}, u32[]{:S(2)}, u32[]{:S(2)}) %all-to-all-start.1) | async-done | bytes 786464 | tf_op jit(solution)/shard_map/all_to_all | solution.py:352
  92.0 11.9 %collective-permute-done = bf16[512,768]{1,0:T(8,128)(2,1)S(1)} collective-permute-done((bf16[512,768]{1,0:T(8,128)(2,1)}, bf16[512,768]{1,0:T(8,128)(2,1)S(1)}, u32[]{:S(2)}, u32[]{:S(2)}) %collective-permute-start) | collective-permute-done | bytes 786464 | tf_op jit(solution)/shard_map/ppermute | solution.py:256
  105.8 15.4 %collective-permute-done.2 = bf16[512,768]{1,0:T(8,128)(2,1)S(1)} collective-permute-done((bf16[512,768]{1,0:T(8,128)(2,1)}, bf16[512,768]{1,0:T(8,128)(2,1)S(1)}, u32[]{:S(2)}, u32[]{:S(2)}) %collective-permute-start.2) | collective-permute-done | bytes 786464 | tf_op jit(solution)/shard_map/ppermute | solution.py:256
  127.1 6.1 add_convert_fusion.2.qkv_ref
  133.2 10.1 %attention_forward.1 = (bf16[1024,256]{1,0:T(8,128)(2,1)S(1)}, bf16[1024,256]{1,0:T(8,128)(2,1)S(1)}, bf16[1024,256]{1,0:T(8,128)(2,1)S(1)}, f32[4,1024]{1,0:T(4,128)S(1)}) custom-call(bf16[1024,768]{1,0:T(8,128)(2,1)S(1)} %add_convert_fusion.2.qkv_ref, f32[1024,128]{1,0:T(8,128)S(1)} %copy.80.cos_ref, f32[1024,128]{1,0:T(8,128)S(1)} %copy.81.former_ref, ...), custom_call_target="tpu_custom_call" | custom-call | flops 1073741824 | bytes 3145728 | tf_op jit(solution)/shard_map/attention_forward/pallas_call | solution.py:203
  148.3 48.8 %reduce-scatter.5.cloned.1.call-done = bf16[128,2048]{1,0:T(8,128)(2,1)} async-done(((bf16[1024,2048]{1,0:T(8,128)(2,1)}), bf16[128,2048]{1,0:T(8,128)(2,1)}) %reduce-scatter.5.cloned.1.call-update) | async-done | bytes 524304 | tf_op jit(solution)/shard_map/reduce_scatter | solution.py:275
  210.2 11.6 %collective-permute-done.13 = bf16[176,2048]{1,0:T(8,128)(2,1)S(1)} collective-permute-done((bf16[176,2048]{1,0:T(8,128)(2,1)S(1)}, bf16[176,2048]{1,0:T(8,128)(2,1)S(1)}, u32[]{:S(2)}, u32[]{:S(2)}) %collective-permute-start.13) | collective-permute-done | bytes 720928 | tf_op jit(solution)/shard_map/ppermute | solution.py:256
  225.1 44.5 %collective-permute-done.14 = bf16[176,2048]{1,0:T(8,128)(2,1)S(1)} collective-permute-done((bf16[176,2048]{1,0:T(8,128)(2,1)S(1)}, bf16[176,2048]{1,0:T(8,128)(2,1)S(1)}, u32[]{:S(2)}, u32[]{:S(2)}) %collective-permute-start.14) | collective-permute-done | bytes 720928 | tf_op jit(solution)/shard_map/ppermute | solution.py:256
  273.6 8.0 %fusion.45 = f32[1024,704]{0,1:T(8,128)} fusion(bf16[1024,2048]{1,0:T(8,128)(2,1)} %all-gather.8.cloned.1.call-done, bf16[704,2048]{1,0:T(8,128)(2,1)} %constant_dynamic-update-slice_fusion), kind=kOutput, calls=%fused_computation.143 | convolution fusion | flops 2952790016 | bytes 9961472 | tf_op jit(solution)/shard_map/dot_general | solution.py:21
  283.0 14.0 %collective-permute-done.11 = bf16[176,2048]{1,0:T(8,128)(2,1)} collective-permute-done((bf16[176,2048]{1,0:T(8,128)(2,1)}, bf16[176,2048]{1,0:T(8,128)(2,1)}, u32[]{:S(2)}, u32[]{:S(2)}) %collective-permute-start.11) | collective-permute-done | bytes 720928 | tf_op jit(solution)/shard_map/ppermute | solution.py:256
  297.0 6.3 fusion.28
  303.4 7.1 %multiply_convert_fusion.1 = (bf16[1024,704]{0,1:T(8,128)(2,1)S(1)}, bf16[1024,704]{0,1:T(8,128)(2,1)S(1)}, bf16[1024,704]{0,1:T(8,128)(2,1)}) fusion(f32[1024,704]{0,1:T(8,128)S(1)} %copy-done.26, f32[1024,704]{0,1:T(8,128)S(1)} %fusion.28, bf16[1024,2048]{1,0:T(8,128)(2,1)S(1)} %copy-done.20, bf16[176,2048]{1,0:T(8,128)(2,1)} %collective-permute-done.9, ...), kind=kOutput, calls=%fused_computation.18 | convolution fusion | flops 2975137792 | bytes 17170432 | tf_op jit(solution)/shard_map/dot_general | solution.py:21
  310.5 6.1 fusion.27
  316.6 7.0 %add_convert_fusion = bf16[1024,2048]{1,0:T(8,128)(2,1)} fusion(f32[1024,2048]{1,0:T(8,128)S(1)} %fusion.27, bf16[1024,704]{0,1:T(8,128)(2,1)S(1)} %get-tuple-element.44, bf16[176,2048]{1,0:T(8,128)(2,1)} %collective-permute-done.9, bf16[176,2048]{1,0:T(8,128)(2,1)} %collective-permute-done.8, bf16[176,2048]{1,0:T(8,128)(2,1)} %collective-permute-done.7, ...), kind=kOutput, calls=%fused_computation | convolution fusion | flops 2968518656 | bytes 16908288 | tf_op jit(solution)/shard_map/dot_general | solution.py:21
  323.7 49.7 %reduce-scatter.7.cloned.1.call-done = bf16[128,2048]{1,0:T(8,128)(2,1)} async-done(((bf16[1024,2048]{1,0:T(8,128)(2,1)}), bf16[128,2048]{1,0:T(8,128)(2,1)}) %reduce-scatter.7.cloned.1.call-update) | async-done | bytes 524304 | tf_op jit(solution)/shard_map/reduce_scatter | solution.py:275
  378.4 45.2 %all-gather.10.cloned.1.call-done = bf16[1024,2048]{1,0:T(8,128)(2,1)} async-done(((bf16[128,2048]{1,0:T(8,128)(2,1)}), bf16[1024,2048]{1,0:T(8,128)(2,1)}) %all-gather.10.cloned.1.call-update) | async-done | bytes 4194320 | tf_op jit(solution)/shard_map/all_gather | solution.py:271
  430.5 10.8 %attention_backward.1 = bf16[1024,768]{1,0:T(8,128)(2,1)S(1)} custom-call(bf16[1024,256]{1,0:T(8,128)(2,1)S(1)} %copy-done.4, bf16[1024,256]{1,0:T(8,128)(2,1)S(1)} %copy-done.6, bf16[1024,768]{1,0:T(8,128)(2,1)} %copy-done.2, bf16[1024,256]{1,0:T(8,128)(2,1)S(1)} %convolution_convert_fusion.8.context_grad_ref, f32[4,1024]{1,0:T(4,128)S(1)} %get-tuple-element.24.logsum_ref, ...), custom_call_target="tpu_custom_call" | custom-call | flops 2684354560 | bytes 4718592 | tf_op jit(solution)/shard_map/attention_backward/pallas_call | solution.py:225
  441.4 7.0 %convolution_convert_fusion.2 = bf16[1024,2048]{1,0:T(8,128)(2,1)} fusion(bf16[1024,768]{1,0:T(8,128)(2,1)S(1)} %attention_backward.1, bf16[2048,768]{1,0:T(8,128)(2,1)} %constant_dynamic-update-slice_fusion.15), kind=kOutput, calls=%fused_computation.8 | convolution fusion | flops 3223322624 | bytes 8912896 | tf_op jit(solution)/shard_map/dot_general | solution.py:21
  449.5 7.7 %convolution_convert_fusion = bf16[1024,2048]{1,0:T(8,128)(2,1)} fusion(bf16[1024,704]{0,1:T(8,128)(2,1)} %get-tuple-element.46, bf16[704,2048]{1,0:T(8,128)(2,1)} %constant_dynamic-update-slice_fusion), kind=kOutput, calls=%fused_computation.6 | convolution fusion | flops 2954887168 | bytes 8519680 | tf_op jit(solution)/shard_map/dot_general | solution.py:404
  457.2 5.9 convolution_convert_fusion.4
  477.0 5.4 collective-permute-done.29
  485.4 13.5 %collective-permute-done.31 = bf16[176,2048]{1,0:T(8,128)(2,1)S(1)} collective-permute-done((bf16[176,2048]{1,0:T(8,128)(2,1)S(1)}, bf16[176,2048]{1,0:T(8,128)(2,1)S(1)}, u32[]{:S(2)}, u32[]{:S(2)}) %collective-permute-start.31) | collective-permute-done | bytes 720928 | tf_op jit(solution)/shard_map/ppermute | solution.py:256
  502.5 10.9 %collective-permute-done.26 = bf16[176,2048]{1,0:T(8,128)(2,1)S(1)} collective-permute-done((bf16[176,2048]{1,0:T(8,128)(2,1)S(1)}, bf16[176,2048]{1,0:T(8,128)(2,1)S(1)}, u32[]{:S(2)}, u32[]{:S(2)}) %collective-permute-start.26) | collective-permute-done | bytes 720928 | tf_op jit(solution)/shard_map/ppermute | solution.py:256
  513.4 15.8 %collective-permute-done.28 = bf16[176,2048]{1,0:T(8,128)(2,1)S(1)} collective-permute-done((bf16[176,2048]{1,0:T(8,128)(2,1)S(1)}, bf16[176,2048]{1,0:T(8,128)(2,1)S(1)}, u32[]{:S(2)}, u32[]{:S(2)}) %collective-permute-start.28) | collective-permute-done | bytes 720928 | tf_op jit(solution)/shard_map/ppermute | solution.py:256
  534.9 4.6 convolution_convert_fusion.3
  548.9 34.7 %collective-permute-done.21 = bf16[64,2048]{1,0:T(8,128)(2,1)} collective-permute-done((bf16[64,2048]{1,0:T(8,128)(2,1)S(1)}, bf16[64,2048]{1,0:T(8,128)(2,1)}, u32[]{:S(2)}, u32[]{:S(2)}) %collective-permute-start.21) | collective-permute-done | bytes 262176 | tf_op jit(solution)/shard_map/ppermute | solution.py:256
  584.7 5.8 collective-permute-done.20
  595.1 5.4 collective-permute-start.22
  613.0 18.1 %all-to-all-done.3 = bf16[8,64,768]{2,1,0:T(8,128)(2,1)S(1)} async-done(((bf16[8,64,768]{2,1,0:T(8,128)(2,1)}), bf16[8,64,768]{2,1,0:T(8,128)(2,1)S(1)}, u32[]{:S(2)}, u32[]{:S(2)}) %all-to-all-start.3) | async-done | bytes 786464 | tf_op jit(solution)/shard_map/all_to_all | solution.py:425
  (258 shorter events, 142.9 us)
Async XLA Ops:
  7.2 115.0 %all-gather.12.cloned.1.call-start = ((), (), s32[]{:S(2)}) async-start(), calls=%async_computation.15 | async-start | bytes 4718592 | tf_op jit(solution)/shard_map/all_gather | solution.py:271
  27.0 56.3 %all-to-all-start.1 = ((bf16[8,64,768]{2,1,0:T(8,128)(2,1)}), bf16[8,64,768]{2,1,0:T(8,128)(2,1)}, u32[]{:S(2)}, u32[]{:S(2)}) async-start(bf16[8,64,768]{2,1,0:T(8,128)(2,1)} %reshape.200), calls=%async_computation.1 | async-start | bytes 1572864 | tf_op jit(solution)/shard_map/all_to_all | solution.py:352
  32.0 165.1 %reduce-scatter.5.cloned.1.call-start = ((), (), s32[]{:S(2)}) async-start(), calls=%async_computation.8 | async-start | bytes 4718592 | tf_op jit(solution)/shard_map/reduce_scatter | solution.py:275
  34.0 50.7 %collective-permute-start.4 = (bf16[64,2048]{1,0:T(8,128)(2,1)}, bf16[64,2048]{1,0:T(8,128)(2,1)S(1)}, u32[]{:S(2)}, u32[]{:S(2)}) collective-permute-start(bf16[64,2048]{1,0:T(8,128)(2,1)} %collective-permute-done.3), channel_id=1, source_target_pairs={{0,8},{8,0},{16,24},{24,16},{1,9},{9,1},{17,25},{25,17},{2,10},{10... | collective-permute-start | bytes 786440 | tf_op jit(solution)/shard_map/ppermute | solution.py:256
  36.0 51.9 %collective-permute-start.6 = (bf16[64,2048]{1,0:T(8,128)(2,1)}, bf16[64,2048]{1,0:T(8,128)(2,1)S(1)}, u32[]{:S(2)}, u32[]{:S(2)}) collective-permute-start(bf16[64,2048]{1,0:T(8,128)(2,1)} %collective-permute-done.3), channel_id=1, source_target_pairs={{0,24},{8,16},{16,8},{24,0},{1,25},{9,17},{17,9},{25,1},{2,26},{10... | collective-permute-start | bytes 786440 | tf_op jit(solution)/shard_map/ppermute | solution.py:256
  84.7 36.6 %collective-permute-start.2 = (bf16[512,768]{1,0:T(8,128)(2,1)}, bf16[512,768]{1,0:T(8,128)(2,1)S(1)}, u32[]{:S(2)}, u32[]{:S(2)}) collective-permute-start(bf16[512,768]{1,0:T(8,128)(2,1)} %bitcast.10), channel_id=1, source_target_pairs={{0,24},{8,16},{16,8},{24,0},{1,25},{9,17},{17,9},{25,1},{2,26},{10... | collective-permute-start | bytes 2359304 | tf_op jit(solution)/shard_map/ppermute | solution.py:256
  147.4 126.2 %all-gather.8.cloned.1.call-start = ((), (), s32[]{:S(2)}) async-start(), calls=%async_computation.10 | async-start | bytes 4718592 | tf_op jit(solution)/shard_map/all_gather | solution.py:271
  148.1 148.9 %all-gather.6.cloned.1.call-start = ((), (), s32[]{:S(2)}) async-start(), calls=%async_computation.9 | async-start | bytes 4718592 | tf_op jit(solution)/shard_map/all_gather | solution.py:271
  202.1 171.3 %reduce-scatter.7.cloned.1.call-start = ((), (), s32[]{:S(2)}) async-start(), calls=%async_computation.11 | async-start | bytes 4718592 | tf_op jit(solution)/shard_map/reduce_scatter | solution.py:275
  204.2 65.4 %collective-permute-start.14 = (bf16[176,2048]{1,0:T(8,128)(2,1)S(1)}, bf16[176,2048]{1,0:T(8,128)(2,1)S(1)}, u32[]{:S(2)}, u32[]{:S(2)}) collective-permute-start(bf16[176,2048]{1,0:T(8,128)(2,1)S(1)} %copy-done.19), channel_id=1, source_target_pairs={{0,16},{8,24},{16,0},{24,8},{1,17},{9,25},{17,1},{25,9},{2,18},{10... | collective-permute-start | bytes 2162696 | tf_op jit(solution)/shard_map/ppermute | solution.py:256
  205.7 97.7 %collective-permute-start.9 = (bf16[176,2048]{1,0:T(8,128)(2,1)}, bf16[176,2048]{1,0:T(8,128)(2,1)}, u32[]{:S(2)}, u32[]{:S(2)}) collective-permute-start(bf16[176,2048]{1,0:T(8,128)(2,1)} %bitcast.130), channel_id=1, source_target_pairs={{0,24},{8,16},{16,8},{24,0},{1,25},{9,17},{17,9},{25,1},{2,26},{10... | collective-permute-start | bytes 2162696 | tf_op jit(solution)/shard_map/ppermute | solution.py:256
  206.2 97.1 %collective-permute-start.8 = (bf16[176,2048]{1,0:T(8,128)(2,1)}, bf16[176,2048]{1,0:T(8,128)(2,1)}, u32[]{:S(2)}, u32[]{:S(2)}) collective-permute-start(bf16[176,2048]{1,0:T(8,128)(2,1)} %bitcast.131), channel_id=1, source_target_pairs={{0,16},{8,24},{16,0},{24,8},{1,17},{9,25},{17,1},{25,9},{2,18},{10... | collective-permute-start | bytes 2162696 | tf_op jit(solution)/shard_map/ppermute | solution.py:256
  207.7 64.3 %collective-permute-start.15 = (bf16[176,2048]{1,0:T(8,128)(2,1)S(1)}, bf16[176,2048]{1,0:T(8,128)(2,1)S(1)}, u32[]{:S(2)}, u32[]{:S(2)}) collective-permute-start(bf16[176,2048]{1,0:T(8,128)(2,1)S(1)} %copy-done.19), channel_id=1, source_target_pairs={{0,24},{8,16},{16,8},{24,0},{1,25},{9,17},{17,9},{25,1},{2,26},{10... | collective-permute-start | bytes 2162696 | tf_op jit(solution)/shard_map/ppermute | solution.py:256
  221.8 59.7 %collective-permute-start.12 = (bf16[176,2048]{1,0:T(8,128)(2,1)}, bf16[176,2048]{1,0:T(8,128)(2,1)}, u32[]{:S(2)}, u32[]{:S(2)}) collective-permute-start(bf16[176,2048]{1,0:T(8,128)(2,1)} %bitcast.20), channel_id=1, source_target_pairs={{0,24},{8,16},{16,8},{24,0},{1,25},{9,17},{17,9},{25,1},{2,26},{10... | collective-permute-start | bytes 2162696 | tf_op jit(solution)/shard_map/ppermute | solution.py:256
  323.6 100.0 %all-gather.10.cloned.1.call-start = ((), (), s32[]{:S(2)}) async-start(), calls=%async_computation.12 | async-start | bytes 4718592 | tf_op jit(solution)/shard_map/all_gather | solution.py:271
  378.2 229.0 %reduce-scatter.11.cloned.1.call-start = ((), (), s32[]{:S(2)}) async-start(), calls=%async_computation.14 | async-start | bytes 4718592 | tf_op jit(solution)/shard_map/reduce_scatter | solution.py:275
  448.4 160.4 %reduce-scatter.9.cloned.1.call-start = ((), (), s32[]{:S(2)}) async-start(), calls=%async_computation.13 | async-start | bytes 4718592 | tf_op jit(solution)/shard_map/reduce_scatter | solution.py:275
  464.9 33.9 %collective-permute-start.31 = (bf16[176,2048]{1,0:T(8,128)(2,1)S(1)}, bf16[176,2048]{1,0:T(8,128)(2,1)S(1)}, u32[]{:S(2)}, u32[]{:S(2)}) collective-permute-start(bf16[176,2048]{1,0:T(8,128)(2,1)S(1)} %get-tuple-element.51), channel_id=1, source_target_pairs={{0,24},{8,16},{16,8},{24,0},{1,25},{9,17},{17,9},{25,1},{2,26},{10... | collective-permute-start | bytes 2162696 | tf_op jit(solution)/shard_map/ppermute | solution.py:256
  466.4 34.5 %collective-permute-start.30 = (bf16[176,2048]{1,0:T(8,128)(2,1)S(1)}, bf16[176,2048]{1,0:T(8,128)(2,1)S(1)}, u32[]{:S(2)}, u32[]{:S(2)}) collective-permute-start(bf16[176,2048]{1,0:T(8,128)(2,1)S(1)} %get-tuple-element.52), channel_id=1, source_target_pairs={{0,16},{8,24},{16,0},{24,8},{1,17},{9,25},{17,1},{25,9},{2,18},{10... | collective-permute-start | bytes 2162696 | tf_op jit(solution)/shard_map/ppermute | solution.py:256
  470.6 42.8 %collective-permute-start.26 = (bf16[176,2048]{1,0:T(8,128)(2,1)S(1)}, bf16[176,2048]{1,0:T(8,128)(2,1)S(1)}, u32[]{:S(2)}, u32[]{:S(2)}) collective-permute-start(bf16[176,2048]{1,0:T(8,128)(2,1)S(1)} %get-tuple-element.53), channel_id=1, source_target_pairs={{0,8},{8,0},{16,24},{24,16},{1,9},{9,1},{17,25},{25,17},{2,10},{10... | collective-permute-start | bytes 2162696 | tf_op jit(solution)/shard_map/ppermute | solution.py:256
  472.1 57.1 %collective-permute-start.28 = (bf16[176,2048]{1,0:T(8,128)(2,1)S(1)}, bf16[176,2048]{1,0:T(8,128)(2,1)S(1)}, u32[]{:S(2)}, u32[]{:S(2)}) collective-permute-start(bf16[176,2048]{1,0:T(8,128)(2,1)S(1)} %get-tuple-element.54), channel_id=1, source_target_pairs={{0,24},{8,16},{16,8},{24,0},{1,25},{9,17},{17,9},{25,1},{2,26},{10... | collective-permute-start | bytes 2162696 | tf_op jit(solution)/shard_map/ppermute | solution.py:256
  482.4 48.1 %collective-permute-start.27 = (bf16[176,2048]{1,0:T(8,128)(2,1)S(1)}, bf16[176,2048]{1,0:T(8,128)(2,1)S(1)}, u32[]{:S(2)}, u32[]{:S(2)}) collective-permute-start(bf16[176,2048]{1,0:T(8,128)(2,1)S(1)} %get-tuple-element.55), channel_id=1, source_target_pairs={{0,16},{8,24},{16,0},{24,8},{1,17},{9,25},{17,1},{25,9},{2,18},{10... | collective-permute-start | bytes 2162696 | tf_op jit(solution)/shard_map/ppermute | solution.py:256
  542.6 51.8 %collective-permute-start.16 = (bf16[512,768]{1,0:T(8,128)(2,1)}, bf16[512,768]{1,0:T(8,128)(2,1)}, u32[]{:S(2)}, u32[]{:S(2)}) collective-permute-start(bf16[512,768]{1,0:T(8,128)(2,1)} %get-tuple-element.47), channel_id=1, source_target_pairs={{0,8},{8,0},{16,24},{24,16},{1,9},{9,1},{17,25},{25,17},{2,10},{10... | collective-permute-start | bytes 2359304 | tf_op jit(solution)/shard_map/ppermute | solution.py:256
  543.4 51.7 %collective-permute-start.18 = (bf16[512,768]{1,0:T(8,128)(2,1)}, bf16[512,768]{1,0:T(8,128)(2,1)}, u32[]{:S(2)}, u32[]{:S(2)}) collective-permute-start(bf16[512,768]{1,0:T(8,128)(2,1)} %get-tuple-element.48), channel_id=1, source_target_pairs={{0,24},{8,16},{16,8},{24,0},{1,25},{9,17},{17,9},{25,1},{2,26},{10... | collective-permute-start | bytes 2359304 | tf_op jit(solution)/shard_map/ppermute | solution.py:256
  544.6 55.8 %collective-permute-start.17 = (bf16[512,768]{1,0:T(8,128)(2,1)}, bf16[512,768]{1,0:T(8,128)(2,1)}, u32[]{:S(2)}, u32[]{:S(2)}) collective-permute-start(bf16[512,768]{1,0:T(8,128)(2,1)} %get-tuple-element.49), channel_id=1, source_target_pairs={{0,16},{8,24},{16,0},{24,8},{1,17},{9,25},{17,1},{25,9},{2,18},{10... | collective-permute-start | bytes 2359304 | tf_op jit(solution)/shard_map/ppermute | solution.py:256
  546.2 37.4 %collective-permute-start.21 = (bf16[64,2048]{1,0:T(8,128)(2,1)S(1)}, bf16[64,2048]{1,0:T(8,128)(2,1)}, u32[]{:S(2)}, u32[]{:S(2)}) collective-permute-start(bf16[64,2048]{1,0:T(8,128)(2,1)S(1)} %get-tuple-element.60), channel_id=1, source_target_pairs={{0,24},{8,16},{16,8},{24,0},{1,25},{9,17},{17,9},{25,1},{2,26},{10... | collective-permute-start | bytes 786440 | tf_op jit(solution)/shard_map/ppermute | solution.py:256
  547.1 43.4 %collective-permute-start.20 = (bf16[64,2048]{1,0:T(8,128)(2,1)S(1)}, bf16[64,2048]{1,0:T(8,128)(2,1)S(1)}, u32[]{:S(2)}, u32[]{:S(2)}) collective-permute-start(bf16[64,2048]{1,0:T(8,128)(2,1)S(1)} %get-tuple-element.61), channel_id=1, source_target_pairs={{0,16},{8,24},{16,0},{24,8},{1,17},{9,25},{17,1},{25,9},{2,18},{10... | collective-permute-start | bytes 786440 | tf_op jit(solution)/shard_map/ppermute | solution.py:256
  583.6 50.2 %collective-permute-start.23 = (bf16[176,2048]{1,0:T(8,128)(2,1)}, bf16[176,2048]{1,0:T(8,128)(2,1)}, u32[]{:S(2)}, u32[]{:S(2)}) collective-permute-start(bf16[176,2048]{1,0:T(8,128)(2,1)} %get-tuple-element.56), channel_id=1, source_target_pairs={{0,8},{8,0},{16,24},{24,16},{1,9},{9,1},{17,25},{25,17},{2,10},{10... | collective-permute-start | bytes 2162696 | tf_op jit(solution)/shard_map/ppermute | solution.py:256
  590.5 43.3 %collective-permute-start.25 = (bf16[176,2048]{1,0:T(8,128)(2,1)}, bf16[176,2048]{1,0:T(8,128)(2,1)}, u32[]{:S(2)}, u32[]{:S(2)}) collective-permute-start(bf16[176,2048]{1,0:T(8,128)(2,1)} %get-tuple-element.57), channel_id=1, source_target_pairs={{0,24},{8,16},{16,8},{24,0},{1,25},{9,17},{17,9},{25,1},{2,26},{10... | collective-permute-start | bytes 2162696 | tf_op jit(solution)/shard_map/ppermute | solution.py:256
  594.4 40.5 %collective-permute-start.24 = (bf16[176,2048]{1,0:T(8,128)(2,1)}, bf16[176,2048]{1,0:T(8,128)(2,1)}, u32[]{:S(2)}, u32[]{:S(2)}) collective-permute-start(bf16[176,2048]{1,0:T(8,128)(2,1)} %get-tuple-element.58), channel_id=1, source_target_pairs={{0,16},{8,24},{16,0},{24,8},{1,17},{9,25},{17,1},{25,9},{2,18},{10... | collective-permute-start | bytes 2162696 | tf_op jit(solution)/shard_map/ppermute | solution.py:256
  595.1 43.2 %collective-permute-start.22 = (f32[64,2048]{1,0:T(8,128)}, f32[64,2048]{1,0:T(8,128)}, u32[]{:S(2)}, u32[]{:S(2)}) collective-permute-start(f32[64,2048]{1,0:T(8,128)} %convert_add_fusion.3), channel_id=1, source_target_pairs={{0,0},{1,4},{2,8},{3,12},{4,16},{5,20},{6,24},{7,28},{8,1},{9,5},{... | collective-permute-start | bytes 1572872 | tf_op jit(solution)/shard_map/ppermute | solution.py:440
  603.6 27.5 %all-to-all-start.3 = ((bf16[8,64,768]{2,1,0:T(8,128)(2,1)}), bf16[8,64,768]{2,1,0:T(8,128)(2,1)S(1)}, u32[]{:S(2)}, u32[]{:S(2)}) async-start(bf16[8,64,768]{2,1,0:T(8,128)(2,1)} %bitcast.115), calls=%async_computation.7 | async-start | bytes 1572864 | tf_op jit(solution)/shard_map/all_to_all | solution.py:425
  (41 other events, 742.9 us)
Sparse Core Ops, SparseCore 0:
  9.6 78.3 all-gather.11
  147.5 49.5 reduce-scatter.4
  198.7 45.2 all-gather.7
  246.0 45.8 all-gather.5
  323.7 49.5 reduce-scatter.6
  378.3 45.2 all-gather.9
  448.5 48.7 reduce-scatter.10
  499.5 48.1 reduce-scatter.8

commit v3 on v2

--- a/solution.py
+++ b/solution.py
@@ -265,6 +265,13 @@
     for k in range(1, len(pieces)):
         total = total + permute(pieces[k].astype(jnp.bfloat16), "dp", k).astype(jnp.float32)
     return total
+
+
+def total(parts):
+    result = parts[0].astype(jnp.float32)
+    for piece in parts[1:]:
+        result = result + piece.astype(jnp.float32)
+    return result
 
 
 def gather_seq(piece):
@@ -316,8 +323,39 @@
     heads_here = HEADS // groups
     local_width = heads_here * HEAD
     own = D // devices
+    whole_heads = own % HEAD == 0
+    deal = (rows, groups, own) if whole_heads else (1, groups, local_width)
+    at_deal = (0, 0, at_seq, 0)
     owner = [(i, (i % groups) * rows + i // groups) for i in range(devices)]
     back = [(b, a) for a, b in owner]
+
+    def to_heads(values):
+        count = values.shape[0]
+        return lax.dynamic_slice(
+            values.reshape((count,) + deal), at_deal, (count, deal[0], 1, deal[2])
+        ).reshape(count, local_width)
+
+    def from_heads(values):
+        count = values.shape[0]
+        return lax.dynamic_update_slice(
+            jnp.zeros((count,) + deal, values.dtype),
+            values.reshape(count, deal[0], 1, deal[2]),
+            at_deal,
+        ).reshape(count, D)
+
+    phase = lax.optimization_barrier
+    grad_out = cotangent[0]
+    half = D // 2
+
+    def to_owner(terms):
+        return scatter_dp(jnp.split(terms, rows, axis=0))
+
+    def dp_terms(terms):
+        block = terms.shape[0] // rows
+        return [
+            lax.dynamic_slice_in_dim(terms, (at_dp ^ k) * block, block, 0) for k in range(rows)
+        ]
+
     small = jnp.concatenate(
         [
             lang_table,
@@ -327,117 +365,157 @@
             mlp_norm_bias[None],
             qkv_bias,
             jnp.broadcast_to(language.astype(jnp.bfloat16)[:, None], (1, own)),
-            jnp.zeros((1, own), jnp.bfloat16),
         ],
         axis=0,
     )
-    spread = lax.all_to_all(
-        jnp.broadcast_to(small[None], (devices,) + small.shape),
-        ("dp", "seq"),
+    ride = 8
+    riders = jnp.zeros((ride * 3 * local_width,), jnp.bfloat16)
+    riders = lax.dynamic_update_slice(riders, small.reshape(-1), (0,))
+    part = lax.all_to_all(
+        jnp.concatenate(
+            [
+                qkv_weight.reshape((own, 3) + deal)
+                .transpose(3, 0, 1, 2, 4)
+                .reshape(groups, own, 3 * local_width),
+                jnp.broadcast_to(
+                    riders.reshape(1, ride, 3 * local_width), (groups, ride, 3 * local_width)
+                ),
+            ],
+            axis=1,
+        ),
+        "seq",
         split_axis=0,
         concat_axis=0,
         tiled=True,
     )
+    part, own_input = phase((part, layer_input[0]))
+    input_all = gather_seq(own_input)
+    spread = place(gather_dp(part[:, own:].reshape(groups, -1)), at_dp)
+    head_qkv = place(gather_dp(part[:, :own].reshape(groups * own, 3 * local_width)), at_dp)
+    spread = spread[:, : small.size].reshape((devices,) + small.shape)
     table = jnp.swapaxes(spread, 0, 1).reshape(small.shape[0], D).astype(jnp.float32)
     languages = spread[:, LANGS + 7, 0].astype(jnp.int32)
     gain_attn = table[LANGS]
     bias_attn = table[LANGS + 1]
     gain_mlp = table[LANGS + 2]
     bias_mlp = table[LANGS + 3]
-    bias_qkv = lax.dynamic_slice_in_dim(
-        table[LANGS + 4 : LANGS + 7], at_seq * local_width, local_width, 1
-    ).reshape(3 * local_width)
+    bias_qkv = to_heads(table[LANGS + 4 : LANGS + 7]).reshape(3 * local_width)
     chooser = (jnp.arange(LANGS, dtype=jnp.int32) == language[0]).astype(jnp.float32)
     lang_row = jnp.sum(chooser[:, None] * table[:LANGS], axis=0)[None, :]
-    qkv_part = lax.all_to_all(
-        qkv_weight.reshape(own, 3, groups, local_width).transpose(2, 0, 1, 3).reshape(
-            groups, own, 3 * local_width
-        ),
-        "seq",
-        split_axis=0,
-        concat_axis=0,
-        tiled=True,
-    ).reshape(groups * own, 3 * local_width)
-    head_qkv = place(gather_dp(qkv_part), at_dp)
-    head_out = place(gather_dp(lax.ppermute(out_weight, ("dp", "seq"), back)), at_dp)
-    cols_gate = jnp.concatenate(gather_dp(gate_weight.T), axis=0)
-    cols_up = jnp.concatenate(gather_dp(up_weight.T), axis=0)
-    cols_down = jnp.concatenate(gather_dp(down_weight), axis=0)
     offsets, cosines, sines = row_tables(doc_lengths[0], length)
     tables = rotation_tables(cosines, sines, min(128, local_width))
     first = offsets[None, :]
-    grad_out = cotangent[0]
-    input_all = gather_seq(layer_input[0])
-    grad_all = gather_seq(after(grad_out, input_all))
-    normed_all = norm_forward(input_all.astype(jnp.float32) + lang_row, gain_attn, bias_attn)[
-        0
-    ].astype(jnp.bfloat16)
     resid_in = layer_input[0].astype(jnp.float32) + lang_row
     unused, scaled_attn, inverse_attn = norm_forward(resid_in, gain_attn, bias_attn)
+    input_all, head_qkv, out_rows, tables, first, resid_in, grad_first, gate_rows = phase(
+        (
+            input_all,
+            head_qkv,
+            out_weight,
+            tables,
+            first,
+            resid_in,
+            grad_out[:, :half],
+            gate_weight.T,
+        )
+    )
+    if not whole_heads:
+        out_rows = lax.ppermute(out_rows, ("dp", "seq"), back)
+    head_out = place(gather_dp(out_rows), at_dp)
+    gate_pieces = [gate_rows, permute(gate_rows, "dp", 1), permute(gate_rows, "dp", 2)]
+    grad_all_first = gather_seq(grad_first)
+    normed_all, scaled_all, inverse_all = norm_forward(
+        input_all.astype(jnp.float32) + lang_row, gain_attn, bias_attn
+    )
+    normed_all = normed_all.astype(jnp.bfloat16)
     projected = (
         jnp.dot(normed_all, head_qkv, preferred_element_type=jnp.float32) + bias_qkv
     ).astype(jnp.bfloat16)
     rot_query, rot_key, context_all, logsum = attention_forward(projected, tables, first)
-    resid_mid = resid_in + scatter_seq(
-        jnp.dot(context_all, head_out, preferred_element_type=jnp.float32)
-    )
+    out_terms = jnp.dot(context_all, head_out, preferred_element_type=jnp.float32).astype(
+        jnp.bfloat16
+    )
+    out_terms, grad_all_first, gate_pieces = phase((out_terms, grad_all_first, gate_pieces))
+    attn_out = scatter_seq(out_terms)
+    cols_gate = jnp.concatenate(gate_pieces + [permute(gate_pieces[0], "dp", 3)], axis=0)
+    cols_up = jnp.concatenate(gather_dp(after(up_weight.T, cols_gate)), axis=0)
+    attn_out, cols_gate, cols_up, down_rows = phase((attn_out, cols_gate, cols_up, down_weight))
+    cols_down = jnp.concatenate(gather_dp(down_rows), axis=0)
+    resid_mid = resid_in + attn_out
     normed_mlp, scaled_mlp, inverse_mlp = norm_forward(resid_mid, gain_mlp, bias_mlp)
     rows_all = gather_seq(normed_mlp.astype(jnp.bfloat16))
+    grad_hidden = contract(grad_all_first, cols_down[:, :half], 1, 1)
+    rows_all, cols_down, grad_hidden, grad_second = phase(
+        (rows_all, cols_down, grad_hidden, grad_out[:, half:])
+    )
+    grad_all_second = gather_seq(grad_second)
     gate_values = contract(rows_all, cols_gate, 1, 1)
     up_values = contract(rows_all, cols_up, 1, 1)
     hidden = (jax.nn.silu(gate_values) * up_values).astype(jnp.bfloat16)
-    grad_hidden = contract(grad_all, cols_down, 1, 1)
+    grad_hidden = grad_hidden + contract(grad_all_second, cols_down[:, half:], 1, 1)
     grad_gate, grad_up = gate_backward(gate_values, up_values, grad_hidden)
-    grad_rows = contract(grad_gate, cols_gate, 1, 0) + contract(grad_up, cols_up, 1, 0)
+    grad_rows = (
+        contract(grad_gate, cols_gate, 1, 0) + contract(grad_up, cols_up, 1, 0)
+    ).astype(jnp.bfloat16)
+    grad_rows, grad_gate, grad_up, hidden = phase((grad_rows, grad_gate, grad_up, hidden))
     grad_normed_mlp = scatter_seq(grad_rows)
-    def to_owner(terms):
-        return scatter_dp(jnp.split(terms.astype(jnp.bfloat16), rows, axis=0))
-
-    out_gate = to_owner(contract(grad_gate, rows_all, 0, 0)).T
-    out_up = to_owner(contract(grad_up, rows_all, 0, 0)).T
-    out_down = to_owner(contract(hidden, grad_all, 0, 0))
+    out_gate = to_owner(contract(grad_gate, rows_all, 0, 0).astype(jnp.bfloat16))
+    up_terms = contract(grad_up, rows_all, 0, 0).astype(jnp.bfloat16)
+    mlp_first = contract(hidden, cols_down[:, :half], 1, 0).astype(jnp.bfloat16)
+    mlp_second = contract(hidden, cols_down[:, half:], 1, 0).astype(jnp.bfloat16)
+    down_terms = jnp.concatenate(
+        [contract(hidden, grad_all_first, 0, 0), contract(hidden, grad_all_second, 0, 0)], axis=1
+    ).astype(jnp.bfloat16)
+    grad_normed_mlp, out_gate, up_terms, mlp_first, mlp_second, down_terms = phase(
+        (grad_normed_mlp, out_gate, up_terms, mlp_first, mlp_second, down_terms)
+    )
     grad_mid_norm, grad_gain_mlp, grad_bias_mlp = norm_backward(
         grad_normed_mlp, scaled_mlp, inverse_mlp, gain_mlp
     )
     grad_mid = grad_out.astype(jnp.float32) + grad_mid_norm
     branch_all = gather_seq(grad_mid.astype(jnp.bfloat16))
-    mlp_terms = jnp.dot(hidden, cols_down, preferred_element_type=jnp.float32)
-    mlp_out = scatter_seq(after(mlp_terms.astype(jnp.bfloat16), branch_all))
-    layer_output = (resid_mid + mlp_out).astype(jnp.bfloat16)
+    out_up = to_owner(up_terms)
+    branch_all, out_up, mlp_first, down_terms = phase((branch_all, out_up, mlp_first, down_terms))
+    mlp_out_first = scatter_seq(mlp_first)
+    down_pieces = jnp.split(down_terms, rows, axis=0)
+    down_arrived = [permute(down_pieces[k], "dp", k) for k in range(1, rows - 1)]
     grad_heads = contract(branch_all, head_out, 1, 1).astype(jnp.bfloat16)
     grad_stack = attention_backward(
         rot_query, rot_key, projected, grad_heads, logsum, tables, first
     )
-    grad_normed_attn = scatter_seq(contract(grad_stack, head_qkv, 1, 1))
-    grad_in_norm, grad_gain_attn, grad_bias_attn = norm_backward(
-        grad_normed_attn, scaled_attn, inverse_attn, gain_attn
-    )
-    grad_input = grad_mid + grad_in_norm
-
-    def dp_terms(terms):
-        block = terms.shape[0] // rows
-        return [
-            lax.dynamic_slice_in_dim(terms, (at_dp ^ k) * block, block, 0) for k in range(rows)
-        ]
-
-    slice_summed = scatter_dp(dp_terms(contract(normed_all, grad_stack, 0, 0).astype(jnp.bfloat16)))
-    grad_qkv_out = (
-        lax.all_to_all(
-            slice_summed.astype(jnp.bfloat16).reshape(groups, own, 3 * local_width),
-            "seq",
-            split_axis=0,
-            concat_axis=0,
-            tiled=True,
+    slice_terms = contract(normed_all, grad_stack, 0, 0).astype(jnp.bfloat16)
+    attn_terms = contract(grad_stack, head_qkv, 1, 1).astype(jnp.bfloat16)
+    (
+        attn_terms,
+        slice_terms,
+        mlp_out_first,
+        grad_stack,
+        branch_all,
+        down_arrived,
+        down_pieces,
+        input_all,
+    ) = phase(
+        (
+            attn_terms,
+            slice_terms,
+            mlp_out_first,
+            grad_stack,
+            branch_all,
+            down_arrived,
+            down_pieces,
+            input_all,
         )
-        .reshape(groups, own, 3, local_width)
-        .transpose(1, 2, 0, 3)
-        .reshape(own, 3 * D)
-        .astype(jnp.float32)
-    )
-    head_out_terms = scatter_dp(
-        dp_terms(contract(context_all, branch_all, 0, 0).astype(jnp.bfloat16))
-    )
-    out_proj = lax.ppermute(head_out_terms, ("dp", "seq"), owner)
+    )
+    grad_normed_attn = scatter_seq(attn_terms)
+    slice_pieces = dp_terms(slice_terms)
+    slice_arrived = [permute(slice_pieces[k], "dp", k) for k in range(1, rows - 1)]
+    unused, scaled_all, inverse_all = norm_forward(
+        input_all.astype(jnp.float32) + lang_row, gain_attn, bias_attn
+    )
+    grad_in_terms, grad_gain_attn, grad_bias_attn = norm_backward(
+        attn_terms.astype(jnp.float32), scaled_all, inverse_all, gain_attn
+    )
+    grad_input_sum = jnp.sum(grad_mid, axis=0) + jnp.sum(grad_in_terms, axis=0)
     grad_bias_qkv = jnp.sum(grad_stack.astype(jnp.float32), axis=0).reshape(3, local_width)
     terms = jnp.concatenate(
         [
@@ -445,13 +523,19 @@
             grad_bias_attn[None],
             grad_gain_mlp[None],
             grad_bias_mlp[None],
-            jnp.sum(grad_input, axis=0)[None],
-            lax.dynamic_update_slice(
-                jnp.zeros((3, D), jnp.float32), grad_bias_qkv, (0, at_seq * local_width)
-            ),
+            grad_input_sum[None],
+            from_heads(grad_bias_qkv),
         ],
         axis=0,
     )
+    head_out_terms = dp_terms(contract(context_all, branch_all, 0, 0).astype(jnp.bfloat16))
+    terms, head_out_terms, slice_arrived, slice_pieces = phase(
+        (terms, head_out_terms, slice_arrived, slice_pieces)
+    )
+    slice_arrived = slice_arrived + [permute(slice_pieces[-1], "dp", rows - 1)]
+    out_arrived = [permute(head_out_terms[k], "dp", k) for k in range(1, rows)]
+
+    slice_summed = total([slice_pieces[0]] + slice_arrived).astype(jnp.bfloat16)
     arrived = lax.all_to_all(
         terms.reshape(terms.shape[0], devices, own).swapaxes(0, 1),
         ("dp", "seq"),
@@ -459,6 +543,43 @@
         concat_axis=0,
         tiled=True,
     )
+    out_arrived, mlp_second, arrived, slice_summed, grad_normed_attn, down_arrived, down_pieces = (
+        phase(
+            (
+                out_arrived,
+                mlp_second,
+                arrived,
+                slice_summed,
+                grad_normed_attn,
+                down_arrived,
+                down_pieces,
+            )
+        )
+    )
+    grad_qkv_out = (
+        lax.all_to_all(
+            slice_summed.reshape(groups, own, 3 * local_width),
+            "seq",
+            split_axis=0,
+            concat_axis=0,
+            tiled=True,
+        )
+        .reshape(groups, own, 3, deal[0], deal[2])
+        .transpose(1, 2, 3, 0, 4)
+        .reshape(own, 3 * D)
+        .astype(jnp.float32)
+    )
+    mlp_out = jnp.concatenate([mlp_out_first, scatter_seq(mlp_second)], axis=1)
+    out_proj = total([head_out_terms[0]] + out_arrived)
+    if not whole_heads:
+        out_proj = lax.ppermute(out_proj, ("dp", "seq"), owner)
+    out_down = total(
+        [down_pieces[0]] + down_arrived + [permute(down_pieces[-1], "dp", rows - 1)]
+    )
+    layer_output = (resid_mid + mlp_out).astype(jnp.bfloat16)
+    grad_input = grad_mid + norm_backward(
+        grad_normed_attn, scaled_attn, inverse_attn, gain_attn
+    )[0]
     summed = jnp.sum(arrived, axis=0)
     members = (languages[:, None] == jnp.arange(LANGS, dtype=jnp.int32)[None, :]).astype(
         jnp.float32
@@ -475,8 +596,8 @@
         out_proj,
         summed[2],
         summed[3],
-        out_gate,
-        out_up,
+        out_gate.T,
+        out_up.T,
         out_down,
     )
 

time: 665 us -> 542 us (0.82)
  waiting for transfers between devices: 372 us -> 225 us
  starting transfers between devices: 91.3 us -> 51.6 us
  blocking collectives: 0 us -> 29.2 us
  other arithmetic: 35.2 us -> 55.3 us
  local copies, waits for them, and re-layouts: 37.8 us -> 56.8 us
    reduce_scatter x4 -> x5, waiting for transfers between devices: 98.5 us -> 9.33 us  [scatter_seq(): lax.psum_scatter(terms.astype(jnp.bfloat16), 'seq', scatter_dimension=0,...]
    ppermute x30 -> x33, waiting for transfers between devices: 188 us -> 155 us  [permute(): return lax.ppermute(value, axis, [(i, i ^ offset) for i in range(size)])]
    all_to_all x0 -> x1, blocking collectives: none -> 29.2 us  [per_device(): lax.all_to_all(jnp.concatenate([qkv_weight.reshape((own, 3) + deal).trans...]
    all_to_all x3 -> x1, waiting for transfers between devices: 38.9 us -> 10.9 us  [per_device(): lax.all_to_all(slice_summed.reshape(groups, own, 3 * local_width), 'seq',...]
    ppermute x30 -> x33, starting transfers between devices: 62.3 us -> 40.9 us  [permute(): return lax.ppermute(value, axis, [(i, i ^ offset) for i in range(size)])]
    all_to_all x1, waiting for transfers between devices: 0.01 us -> 13.5 us  [per_device(): lax.all_to_all(terms.reshape(terms.shape[0], devices, own).swapaxes(0, 1)...]
    all_to_all x3 -> x1, starting transfers between devices: 15.8 us -> 5.93 us  [per_device(): lax.all_to_all(slice_summed.reshape(groups, own, 3 * local_width), 'seq',...]
    all_gather x4 -> x5, waiting for transfers between devices: 45.2 us -> 35.4 us  [gather_seq(): return lax.all_gather(piece, 'seq', axis=0, tiled=True)]
  transfers between devices with their start and end apart: 44 -> 45, of which waited for: 19 -> 23; matrix products, arithmetic and copies ran while one was open for 14% -> 28% of each run, Pallas kernels for 0% -> 4%
where the time goes in v3:
time: 542 us; the launch traced here: 536 us
  waiting for transfers between devices  225 us (42%)
  matrix products  81.1 us (15%)
  local copies, waits for them, and re-layouts  56.8 us (10%)
  other arithmetic  55.3 us (10%)
  starting transfers between devices  51.6 us (10%)
  blocking collectives  29.2 us (5%)
  Pallas kernels  21 us (4%)
  between operations  16.1 us (3%)
    ppermute x33, waiting for transfers between devices, permute(): return lax.ppermute(value, axis, [(i, i ^ offset) for i in range(size)])  155 us
    dot_general x16, matrix products, contract(): lax.dot_general(left, right, (((left_dim,), (right_dim,)), ((), ())), pre...  71.8 us
    ppermute x33, starting transfers between devices, permute(): return lax.ppermute(value, axis, [(i, i ^ offset) for i in range(size)])  40.9 us
    all_gather x5, waiting for transfers between devices, gather_seq(): return lax.all_gather(piece, 'seq', axis=0, tiled=True)  35.4 us
    all_to_all x1, blocking collectives, per_device(): lax.all_to_all(jnp.concatenate([qkv_weight.reshape((own, 3) + deal).trans...  29.2 us
    unnamed x93, local copies, waits for them, and re-layouts  14.5 us
    all_to_all x1, waiting for transfers between devices, per_device(): lax.all_to_all(terms.reshape(terms.shape[0], devices, own).swapaxes(0, 1)...  13.5 us
    pallas_call x1, Pallas kernels, attention_backward(): pl.pallas_call(backward_kernel, out_shape=jax.ShapeDtypeStruct((length, 3...  11 us
  transfers between devices with their start and end apart: 45, of which 23 were waited for; matrix products, arithmetic and copies ran while one was open for 28% of the time, Pallas kernels for 4%

profile of v3, /device:TPU:0, one launch (start us, length us, event | category | flops | bytes accessed | tf_op | source)
XLA Modules:
  0.0 535.6 jit_solution(4164799466983693339)
XLA Ops:
  13.7 29.2 %all_to_all.15 = bf16[8,72,768]{2,1,0:T(8,128)(2,1)S(1)} all-to-all(bf16[8,72,768]{2,1,0:T(8,128)(2,1)S(1)} %pad_maximum_fusion.2), channel_id=1, replica_groups=mesh['dp'=4,'seq'=8] {'seq'}, dimensions={0} | all-to-all | bytes 1769472 | tf_op jit(solution)/shard_map/all_to_all | solution.py:374
  55.2 13.3 %collective-permute-done.4 = bf16[8,6144]{1,0:T(8,128)(2,1)S(1)} collective-permute-done((bf16[8,6144]{1,0:T(8,128)(2,1)S(1)}, bf16[8,6144]{1,0:T(8,128)(2,1)S(1)}, u32[]{:S(2)}, u32[]{:S(2)}) %collective-permute-start.4) | collective-permute-done | bytes 98336 | tf_op jit(solution)/shard_map/ppermute | solution.py:256
  70.8 15.6 %collective-permute-done = bf16[512,768]{1,0:T(8,128)(2,1)} collective-permute-done((bf16[512,768]{1,0:T(8,128)(2,1)S(1)}, bf16[512,768]{1,0:T(8,128)(2,1)}, u32[]{:S(2)}, u32[]{:S(2)}) %collective-permute-start) | collective-permute-done | bytes 786464 | tf_op jit(solution)/shard_map/ppermute | solution.py:256
  102.3 4.0 multiply_reduce_fusion.1
  106.4 6.1 %add_convert_fusion.2.qkv_ref = bf16[1024,768]{1,0:T(8,128)(2,1)S(1)} fusion(bf16[2048,768]{1,0:T(8,128)(2,1)} %constant_dynamic-update-slice_fusion.16, f32[768]{0:T(1024)S(1)} %add.245, bf16[1024,2048]{1,0:T(8,128)(2,1)S(1)} %copy-done.7, f32[2048]{0:T(1024)S(1)} %add.241, f32[2048]{0:T(1024)S(1)} %mul.268, f32[1024]{0:T(1024)S(1)} %add_rsqrt_fusion.1, ...), kind=kOutput, calls=%fused_computation.29 | convolution fusion | flops 3237478400 | bytes 8948736 | tf_op jit(solution)/shard_map/dot_general | solution.py:432
  113.8 10.0 %attention_forward.1 = (bf16[1024,256]{1,0:T(8,128)(2,1)S(1)}, bf16[1024,256]{1,0:T(8,128)(2,1)S(1)}, bf16[1024,256]{1,0:T(8,128)(2,1)S(1)}, f32[4,1024]{1,0:T(4,128)S(1)}) custom-call(bf16[1024,768]{1,0:T(8,128)(2,1)S(1)} %add_convert_fusion.2.qkv_ref, f32[1024,128]{1,0:T(8,128)S(1)} %copy.71.cos_ref, f32[1024,128]{1,0:T(8,128)S(1)} %copy.72.former_ref, ...), custom_call_target="tpu_custom_call" | custom-call | flops 1073741824 | bytes 3145728 | tf_op jit(solution)/shard_map/attention_forward/pallas_call | solution.py:203
  137.0 12.7 %collective-permute-done.11 = bf16[176,2048]{1,0:T(8,128)(2,1)S(1)} collective-permute-done((bf16[176,2048]{1,0:T(8,128)(2,1)S(1)}, bf16[176,2048]{1,0:T(8,128)(2,1)S(1)}, u32[]{:S(2)}, u32[]{:S(2)}) %collective-permute-start.11) | collective-permute-done | bytes 720928 | tf_op jit(solution)/shard_map/ppermute | solution.py:256
  155.1 16.6 %collective-permute-done.14 = bf16[176,2048]{1,0:T(8,128)(2,1)S(1)} collective-permute-done((bf16[176,2048]{1,0:T(8,128)(2,1)}, bf16[176,2048]{1,0:T(8,128)(2,1)S(1)}, u32[]{:S(2)}, u32[]{:S(2)}) %collective-permute-start.14) | collective-permute-done | bytes 720928 | tf_op jit(solution)/shard_map/ppermute | solution.py:256
  171.6 11.4 %collective-permute-done.13 = bf16[176,2048]{1,0:T(8,128)(2,1)} collective-permute-done((bf16[176,2048]{1,0:T(8,128)(2,1)}, bf16[176,2048]{1,0:T(8,128)(2,1)}, u32[]{:S(2)}, u32[]{:S(2)}) %collective-permute-start.13) | collective-permute-done | bytes 720928 | tf_op jit(solution)/shard_map/ppermute | solution.py:256
  194.8 14.5 %collective-permute-done.15 = bf16[176,2048]{1,0:T(8,128)(2,1)S(1)} collective-permute-done((bf16[176,2048]{1,0:T(8,128)(2,1)}, bf16[176,2048]{1,0:T(8,128)(2,1)S(1)}, u32[]{:S(2)}, u32[]{:S(2)}) %collective-permute-start.15) | collective-permute-done | bytes 720928 | tf_op jit(solution)/shard_map/ppermute | solution.py:256
  209.4 14.6 %collective-permute-done.16 = bf16[176,2048]{1,0:T(8,128)(2,1)S(1)} collective-permute-done((bf16[176,2048]{1,0:T(8,128)(2,1)}, bf16[176,2048]{1,0:T(8,128)(2,1)S(1)}, u32[]{:S(2)}, u32[]{:S(2)}) %collective-permute-start.16) | collective-permute-done | bytes 720928 | tf_op jit(solution)/shard_map/ppermute | solution.py:256
  229.0 6.4 %all-gather.10.cloned.1.call-done = bf16[1024,2048]{1,0:T(8,128)(2,1)} async-done(((bf16[128,2048]{1,0:T(8,128)(2,1)}), bf16[1024,2048]{1,0:T(8,128)(2,1)}) %all-gather.10.cloned.1.call-update) | async-done | bytes 4194320 | tf_op jit(solution)/shard_map/all_gather | solution.py:278
  235.9 7.8 %fusion.32 = f32[1024,704]{0,1:T(8,128)} fusion(bf16[1024,2048]{1,0:T(8,128)(2,1)} %all-gather.10.cloned.1.call-done, bf16[704,2048]{1,0:T(8,128)(2,1)} %pad_maximum_fusion), kind=kOutput, calls=%fused_computation.152 | convolution fusion | flops 2952790016 | bytes 9961472 | tf_op jit(solution)/shard_map/dot_general | solution.py:21
  243.7 21.6 %all-gather.12.cloned.1.call-done = bf16[1024,1024]{1,0:T(8,128)(2,1)} async-done(((bf16[128,1024]{1,0:T(8,128)(2,1)}), bf16[1024,1024]{1,0:T(8,128)(2,1)}) %all-gather.12.cloned.1.call-update) | async-done | bytes 2097168 | tf_op jit(solution)/shard_map/all_gather | solution.py:278
  270.2 7.1 %multiply_convert_fusion.2 = (bf16[1024,704]{0,1:T(8,128)(2,1)S(1)}, bf16[1024,704]{0,1:T(8,128)(2,1)S(1)}, bf16[1024,704]{0,1:T(8,128)(2,1)}) fusion(f32[1024,704]{0,1:T(8,128)} %fusion.32, f32[1024,704]{0,1:T(8,128)S(1)} %copy-done.38, f32[1024,704]{0,1:T(8,128)S(1)} %fusion.18, bf16[1024,2048]{1,0:T(8,128)(2,1)S(1)} %copy-done.33, ...), kind=kOutput, calls=%fused_computation.34 | convolution fusion | flops 2964324352 | bytes 20054016 | tf_op jit(solution)/shard_map/dot_general | solution.py:21
  280.9 5.3 add_convert_fusion
  286.4 5.8 %convolution_convert_fusion.4 = bf16[704,2048]{1,0:T(8,128)(2,1)S(1)} fusion(bf16[1024,704]{0,1:T(8,128)(2,1)} %copy-done.41, bf16[1024,2048]{1,0:T(8,128)(2,1)} %all-gather.10.cloned.1.call-done), kind=kOutput, calls=%fused_computation.26 | convolution fusion | flops 2954231808 | bytes 8519680 | tf_op jit(solution)/shard_map/dot_general | solution.py:21
  306.6 5.0 convolution_convert_fusion.7
  311.6 7.4 %convolution_convert_fusion.3 = bf16[704,2048]{1,0:T(8,128)(2,1)} fusion(bf16[1024,704]{0,1:T(8,128)(2,1)} %copy-done.40, bf16[1024,2048]{1,0:T(8,128)(2,1)} %all-gather.10.cloned.1.call-done), kind=kOutput, calls=%fused_computation.25 | convolution fusion | flops 2954231808 | bytes 8519680 | tf_op jit(solution)/shard_map/dot_general | solution.py:21
  319.0 9.8 %collective-permute-done.20 = bf16[176,2048]{1,0:T(8,128)(2,1)} collective-permute-done((bf16[176,2048]{1,0:T(8,128)(2,1)}, bf16[176,2048]{1,0:T(8,128)(2,1)}, u32[]{:S(2)}, u32[]{:S(2)}) %collective-permute-start.20) | collective-permute-done | bytes 720928 | tf_op jit(solution)/shard_map/ppermute | solution.py:256
  345.4 15.6 %collective-permute-done.21 = bf16[176,2048]{1,0:T(8,128)(2,1)S(1)} collective-permute-done((bf16[176,2048]{1,0:T(8,128)(2,1)S(1)}, bf16[176,2048]{1,0:T(8,128)(2,1)S(1)}, u32[]{:S(2)}, u32[]{:S(2)}) %collective-permute-start.21) | collective-permute-done | bytes 720928 | tf_op jit(solution)/shard_map/ppermute | solution.py:256
  361.0 13.1 %collective-permute-done.23 = bf16[176,2048]{1,0:T(8,128)(2,1)S(1)} collective-permute-done((bf16[176,2048]{1,0:T(8,128)(2,1)S(1)}, bf16[176,2048]{1,0:T(8,128)(2,1)S(1)}, u32[]{:S(2)}, u32[]{:S(2)}) %collective-permute-start.23) | collective-permute-done | bytes 720928 | tf_op jit(solution)/shard_map/ppermute | solution.py:256
  378.1 7.5 %all-gather.14.cloned.1.call-done = bf16[1024,2048]{1,0:T(8,128)(2,1)} async-done(((bf16[128,2048]{1,0:T(8,128)(2,1)}), bf16[1024,2048]{1,0:T(8,128)(2,1)}) %all-gather.14.cloned.1.call-update) | async-done | bytes 4194320 | tf_op jit(solution)/shard_map/all_gather | solution.py:278
  393.6 11.0 %attention_backward.1 = bf16[1024,768]{1,0:T(8,128)(2,1)S(1)} custom-call(bf16[1024,256]{1,0:T(8,128)(2,1)S(1)} %copy-done.4, bf16[1024,256]{1,0:T(8,128)(2,1)S(1)} %copy-done.6, bf16[1024,768]{1,0:T(8,128)(2,1)} %copy-done.2, bf16[1024,256]{1,0:T(8,128)(2,1)S(1)} %convolution_convert_fusion.10.context_grad_ref, ...), custom_call_target="tpu_custom_call" | custom-call | flops 2684354560 | bytes 4718592 | tf_op jit(solution)/shard_map/attention_backward/pallas_call | solution.py:225
  404.6 6.3 %convolution_convert_fusion.2 = bf16[2048,768]{1,0:T(8,128)(2,1)} fusion(bf16[1024,768]{1,0:T(8,128)(2,1)S(1)} %attention_backward.1, bf16[1024,2048]{1,0:T(8,128)(2,1)S(1)} %copy-done.8, f32[2048]{0:T(1024)S(1)} %add.241, f32[2048]{0:T(1024)S(1)} %mul.268, f32[1024]{0:T(1024)S(1)} %add_rsqrt_fusion.1, f32[1024]{0:T(1024)S(1)} %broadcast_multiply_fusion.3, ...), kind=kOutput, calls=%fused_computation.24 | convolution fusion | flops 3237478400 | bytes 8945664 | tf_op jit(solution)/shard_map/dot_general | solution.py:21
  410.9 5.0 convolution_convert_fusion.1
  415.9 6.3 %reduce-scatter.10.cloned.1.call-done = bf16[128,1024]{1,0:T(8,128)(2,1)} async-done(((bf16[1024,1024]{1,0:T(8,128)(2,1)}), bf16[128,1024]{1,0:T(8,128)(2,1)}) %reduce-scatter.10.cloned.1.call-update) | async-done | bytes 262160 | tf_op jit(solution)/shard_map/reduce_scatter | solution.py:282
  436.9 5.4 %fusion.5 = (f32[2048]{0:T(1024)S(1)}, f32[2048]{0:T(1024)S(1)}, f32[2048]{0:T(1024)S(1)}) fusion(bf16[1024,2048]{1,0:T(8,128)(2,1)S(1)} %copy-done.10, bf16[1024,2048]{1,0:T(8,128)(2,1)S(1)} %copy-done.9, f32[1024]{0:T(1024)S(1)} %broadcast_multiply_fusion, f32[1024]{0:T(1024)S(1)} %broadcast_multiply_fusion.1, f32[1024]{0:T(1024)S(1)} %add_rsqrt_fusion, ...), kind=kLoop, calls=%fused_computation.8 | loop fusion | flops 29353984 | bytes 8445952 | tf_op jit(solution)/shard_map/reduce_sum | solution.py:518
  456.1 13.5 %all-to-all-done.1 = f32[32,1,512]{2,1,0:T(1,128)S(1)} async-done(((f32[32,1,512]{2,1,0:T(1,128)}), f32[32,1,512]{2,1,0:T(1,128)S(1)}, u32[]{:S(2)}, u32[]{:S(2)}) %all-to-all-start.1) | async-done | bytes 65568 | tf_op jit(solution)/shard_map/all_to_all | solution.py:539
  477.7 5.9 %all-to-all-start.2 = ((bf16[8,64,768]{2,1,0:T(8,128)(2,1)}), bf16[8,64,768]{2,1,0:T(8,128)(2,1)}, u32[]{:S(2)}, u32[]{:S(2)}) async-start(bf16[8,64,768]{2,1,0:T(8,128)(2,1)} %bitcast.33), calls=%async_computation.7 | async-start | bytes 1572864 | tf_op jit(solution)/shard_map/all_to_all | solution.py:560
  491.1 12.2 %collective-permute-done.32 = bf16[176,2048]{1,0:T(8,128)(2,1)S(1)} collective-permute-done((bf16[176,2048]{1,0:T(8,128)(2,1)}, bf16[176,2048]{1,0:T(8,128)(2,1)S(1)}, u32[]{:S(2)}, u32[]{:S(2)}) %collective-permute-start.32) | collective-permute-done | bytes 720928 | tf_op jit(solution)/shard_map/ppermute | solution.py:256
  506.1 10.9 %all-to-all-done.2 = bf16[8,64,768]{2,1,0:T(8,128)(2,1)} async-done(((bf16[8,64,768]{2,1,0:T(8,128)(2,1)}), bf16[8,64,768]{2,1,0:T(8,128)(2,1)}, u32[]{:S(2)}, u32[]{:S(2)}) %all-to-all-start.2) | async-done | bytes 786464 | tf_op jit(solution)/shard_map/all_to_all | solution.py:560
  (317 shorter events, 182.7 us)
Async XLA Ops:
  7.2 85.5 %all-gather.6.cloned.1.call-start = ((), (), s32[]{:S(2)}) async-start(), calls=%async_computation.8 | async-start | bytes 4718592 | tf_op jit(solution)/shard_map/all_gather | solution.py:278
  42.9 89.1 %all-gather.8.cloned.1.call-start = ((), (), s32[]{:S(2)}) async-start(), calls=%async_computation.9 | async-start | bytes 2359296 | tf_op jit(solution)/shard_map/all_gather | solution.py:278
  44.8 23.7 %collective-permute-start.5 = (bf16[8,6144]{1,0:T(8,128)(2,1)S(1)}, bf16[8,6144]{1,0:T(8,128)(2,1)S(1)}, u32[]{:S(2)}, u32[]{:S(2)}) collective-permute-start(bf16[8,6144]{1,0:T(8,128)(2,1)S(1)} %bitcast.121), channel_id=1, source_target_pairs={{0,24},{8,16},{16,8},{24,0},{1,25},{9,17},{17,9},{25,1},{2,26},{10... | collective-permute-start | bytes 294920 | tf_op jit(solution)/shard_map/ppermute | solution.py:256
  48.4 42.2 %collective-permute-start.2 = (bf16[512,768]{1,0:T(8,128)(2,1)S(1)}, bf16[512,768]{1,0:T(8,128)(2,1)}, u32[]{:S(2)}, u32[]{:S(2)}) collective-permute-start(bf16[512,768]{1,0:T(8,128)(2,1)S(1)} %bitcast.106), channel_id=1, source_target_pairs={{0,24},{8,16},{16,8},{24,0},{1,25},{9,17},{17,9},{25,1},{2,26},{10... | collective-permute-start | bytes 2359304 | tf_op jit(solution)/shard_map/ppermute | solution.py:256
  50.8 37.6 %collective-permute-start.1 = (bf16[512,768]{1,0:T(8,128)(2,1)S(1)}, bf16[512,768]{1,0:T(8,128)(2,1)}, u32[]{:S(2)}, u32[]{:S(2)}) collective-permute-start(bf16[512,768]{1,0:T(8,128)(2,1)S(1)} %bitcast.107), channel_id=1, source_target_pairs={{0,16},{8,24},{16,0},{24,8},{1,17},{9,25},{17,1},{25,9},{2,18},{10... | collective-permute-start | bytes 2359304 | tf_op jit(solution)/shard_map/ppermute | solution.py:256
  53.6 32.8 %collective-permute-start = (bf16[512,768]{1,0:T(8,128)(2,1)S(1)}, bf16[512,768]{1,0:T(8,128)(2,1)}, u32[]{:S(2)}, u32[]{:S(2)}) collective-permute-start(bf16[512,768]{1,0:T(8,128)(2,1)S(1)} %bitcast.109), channel_id=1, source_target_pairs={{0,8},{8,0},{16,24},{24,16},{1,9},{9,1},{17,25},{25,17},{2,10},{10... | collective-permute-start | bytes 2359304 | tf_op jit(solution)/shard_map/ppermute | solution.py:256
  92.8 33.9 %collective-permute-start.8 = (bf16[64,2048]{1,0:T(8,128)(2,1)}, bf16[64,2048]{1,0:T(8,128)(2,1)}, u32[]{:S(2)}, u32[]{:S(2)}) collective-permute-start(bf16[64,2048]{1,0:T(8,128)(2,1)} %param.23), channel_id=1, source_target_pairs={{0,24},{8,16},{16,8},{24,0},{1,25},{9,17},{17,9},{25,1},{2,26},{10... | collective-permute-start | bytes 786440 | tf_op jit(solution)/shard_map/ppermute | solution.py:256
  94.3 31.5 %collective-permute-start.7 = (bf16[64,2048]{1,0:T(8,128)(2,1)}, bf16[64,2048]{1,0:T(8,128)(2,1)}, u32[]{:S(2)}, u32[]{:S(2)}) collective-permute-start(bf16[64,2048]{1,0:T(8,128)(2,1)} %param.23), channel_id=1, source_target_pairs={{0,16},{8,24},{16,0},{24,8},{1,17},{9,25},{17,1},{25,9},{2,18},{10... | collective-permute-start | bytes 786440 | tf_op jit(solution)/shard_map/ppermute | solution.py:256
  95.7 28.9 %collective-permute-start.6 = (bf16[64,2048]{1,0:T(8,128)(2,1)}, bf16[64,2048]{1,0:T(8,128)(2,1)}, u32[]{:S(2)}, u32[]{:S(2)}) collective-permute-start(bf16[64,2048]{1,0:T(8,128)(2,1)} %param.23), channel_id=1, source_target_pairs={{0,8},{8,0},{16,24},{24,16},{1,9},{9,1},{17,25},{25,17},{2,10},{10... | collective-permute-start | bytes 786440 | tf_op jit(solution)/shard_map/ppermute | solution.py:256
  96.4 35.6 %collective-permute-start.10 = (bf16[176,2048]{1,0:T(8,128)(2,1)}, bf16[176,2048]{1,0:T(8,128)(2,1)}, u32[]{:S(2)}, u32[]{:S(2)}) collective-permute-start(bf16[176,2048]{1,0:T(8,128)(2,1)} %bitcast.116), channel_id=1, source_target_pairs={{0,16},{8,24},{16,0},{24,8},{1,17},{9,25},{17,1},{25,9},{2,18},{10... | collective-permute-start | bytes 2162696 | tf_op jit(solution)/shard_map/ppermute | solution.py:256
  97.1 34.9 %collective-permute-start.9 = (bf16[176,2048]{1,0:T(8,128)(2,1)}, bf16[176,2048]{1,0:T(8,128)(2,1)}, u32[]{:S(2)}, u32[]{:S(2)}) collective-permute-start(bf16[176,2048]{1,0:T(8,128)(2,1)} %bitcast.117), channel_id=1, source_target_pairs={{0,8},{8,0},{16,24},{24,16},{1,9},{9,1},{17,25},{25,17},{2,10},{10... | collective-permute-start | bytes 2162696 | tf_op jit(solution)/shard_map/ppermute | solution.py:256
  98.4 87.6 %reduce-scatter.6.cloned.1.call-start = ((), (), s32[]{:S(2)}) async-start(), calls=%async_computation.10 | async-start | bytes 4718592 | tf_op jit(solution)/shard_map/reduce_scatter | solution.py:282
  132.0 103.4 %all-gather.10.cloned.1.call-start = ((), (), s32[]{:S(2)}) async-start(), calls=%async_computation.11 | async-start | bytes 4718592 | tf_op jit(solution)/shard_map/all_gather | solution.py:278
  152.9 30.1 %collective-permute-start.13 = (bf16[176,2048]{1,0:T(8,128)(2,1)}, bf16[176,2048]{1,0:T(8,128)(2,1)}, u32[]{:S(2)}, u32[]{:S(2)}) collective-permute-start(bf16[176,2048]{1,0:T(8,128)(2,1)} %bitcast.21), channel_id=1, source_target_pairs={{0,16},{8,24},{16,0},{24,8},{1,17},{9,25},{17,1},{25,9},{2,18},{10... | collective-permute-start | bytes 2162696 | tf_op jit(solution)/shard_map/ppermute | solution.py:256
  153.2 29.8 %collective-permute-start.12 = (bf16[176,2048]{1,0:T(8,128)(2,1)}, bf16[176,2048]{1,0:T(8,128)(2,1)}, u32[]{:S(2)}, u32[]{:S(2)}) collective-permute-start(bf16[176,2048]{1,0:T(8,128)(2,1)} %bitcast.21), channel_id=1, source_target_pairs={{0,8},{8,0},{16,24},{24,16},{1,9},{9,1},{17,25},{25,17},{2,10},{10... | collective-permute-start | bytes 2162696 | tf_op jit(solution)/shard_map/ppermute | solution.py:256
  190.0 75.3 %all-gather.12.cloned.1.call-start = ((), (), s32[]{:S(2)}) async-start(), calls=%async_computation.12 | async-start | bytes 2359296 | tf_op jit(solution)/shard_map/all_gather | solution.py:278
  190.8 33.2 %collective-permute-start.16 = (bf16[176,2048]{1,0:T(8,128)(2,1)}, bf16[176,2048]{1,0:T(8,128)(2,1)S(1)}, u32[]{:S(2)}, u32[]{:S(2)}) collective-permute-start(bf16[176,2048]{1,0:T(8,128)(2,1)} %param.28), channel_id=1, source_target_pairs={{0,16},{8,24},{16,0},{24,8},{1,17},{9,25},{17,1},{25,9},{2,18},{10... | collective-permute-start | bytes 2162696 | tf_op jit(solution)/shard_map/ppermute | solution.py:256
  192.2 31.8 %collective-permute-start.17 = (bf16[176,2048]{1,0:T(8,128)(2,1)}, bf16[176,2048]{1,0:T(8,128)(2,1)S(1)}, u32[]{:S(2)}, u32[]{:S(2)}) collective-permute-start(bf16[176,2048]{1,0:T(8,128)(2,1)} %param.28), channel_id=1, source_target_pairs={{0,24},{8,16},{16,8},{24,0},{1,25},{9,17},{17,9},{25,1},{2,26},{10... | collective-permute-start | bytes 2162696 | tf_op jit(solution)/shard_map/ppermute | solution.py:256
  235.4 100.4 %reduce-scatter.8.cloned.1.call-start = ((), (), s32[]{:S(2)}) async-start(), calls=%async_computation.13 | async-start | bytes 4718592 | tf_op jit(solution)/shard_map/reduce_scatter | solution.py:282
  286.2 99.4 %all-gather.14.cloned.1.call-start = ((), (), s32[]{:S(2)}) async-start(), calls=%async_computation.14 | async-start | bytes 4718592 | tf_op jit(solution)/shard_map/all_gather | solution.py:278
  293.7 25.3 %collective-permute-start.18 = (bf16[176,2048]{1,0:T(8,128)(2,1)}, bf16[176,2048]{1,0:T(8,128)(2,1)}, u32[]{:S(2)}, u32[]{:S(2)}) collective-permute-start(bf16[176,2048]{1,0:T(8,128)(2,1)} %get-tuple-element.194), channel_id=1, source_target_pairs={{0,8},{8,0},{16,24},{24,16},{1,9},{9,1},{17,25},{25,17},{2,10},{10... | collective-permute-start | bytes 2162696 | tf_op jit(solution)/shard_map/ppermute | solution.py:256
  295.2 33.6 %collective-permute-start.20 = (bf16[176,2048]{1,0:T(8,128)(2,1)}, bf16[176,2048]{1,0:T(8,128)(2,1)}, u32[]{:S(2)}, u32[]{:S(2)}) collective-permute-start(bf16[176,2048]{1,0:T(8,128)(2,1)} %get-tuple-element.195), channel_id=1, source_target_pairs={{0,24},{8,16},{16,8},{24,0},{1,25},{9,17},{17,9},{25,1},{2,26},{10... | collective-permute-start | bytes 2162696 | tf_op jit(solution)/shard_map/ppermute | solution.py:256
  296.6 33.5 %collective-permute-start.19 = (bf16[176,2048]{1,0:T(8,128)(2,1)}, bf16[176,2048]{1,0:T(8,128)(2,1)}, u32[]{:S(2)}, u32[]{:S(2)}) collective-permute-start(bf16[176,2048]{1,0:T(8,128)(2,1)} %get-tuple-element.196), channel_id=1, source_target_pairs={{0,16},{8,24},{16,0},{24,8},{1,17},{9,25},{17,1},{25,9},{2,18},{10... | collective-permute-start | bytes 2162696 | tf_op jit(solution)/shard_map/ppermute | solution.py:256
  340.1 82.0 %reduce-scatter.10.cloned.1.call-start = ((), (), s32[]{:S(2)}) async-start(), calls=%async_computation.15 | async-start | bytes 2359296 | tf_op jit(solution)/shard_map/reduce_scatter | solution.py:282
  343.4 30.7 %collective-permute-start.23 = (bf16[176,2048]{1,0:T(8,128)(2,1)S(1)}, bf16[176,2048]{1,0:T(8,128)(2,1)S(1)}, u32[]{:S(2)}, u32[]{:S(2)}) collective-permute-start(bf16[176,2048]{1,0:T(8,128)(2,1)S(1)} %get-tuple-element.192), channel_id=1, source_target_pairs={{0,24},{8,16},{16,8},{24,0},{1,25},{9,17},{17,9},{25,1},{2,26},{10... | collective-permute-start | bytes 2162696 | tf_op jit(solution)/shard_map/ppermute | solution.py:256
  344.9 30.6 %collective-permute-start.22 = (bf16[176,2048]{1,0:T(8,128)(2,1)S(1)}, bf16[176,2048]{1,0:T(8,128)(2,1)S(1)}, u32[]{:S(2)}, u32[]{:S(2)}) collective-permute-start(bf16[176,2048]{1,0:T(8,128)(2,1)S(1)} %get-tuple-element.193), channel_id=1, source_target_pairs={{0,16},{8,24},{16,0},{24,8},{1,17},{9,25},{17,1},{25,9},{2,18},{10... | collective-permute-start | bytes 2162696 | tf_op jit(solution)/shard_map/ppermute | solution.py:256
  385.6 88.9 %reduce-scatter.12.cloned.1.call-start = ((), (), s32[]{:S(2)}) async-start(), calls=%async_computation.16 | async-start | bytes 4718592 | tf_op jit(solution)/shard_map/reduce_scatter | solution.py:282
  389.3 34.7 %collective-permute-start.25 = (bf16[176,2048]{1,0:T(8,128)(2,1)}, bf16[176,2048]{1,0:T(8,128)(2,1)}, u32[]{:S(2)}, u32[]{:S(2)}) collective-permute-start(bf16[176,2048]{1,0:T(8,128)(2,1)} %get-tuple-element.189), channel_id=1, source_target_pairs={{0,16},{8,24},{16,0},{24,8},{1,17},{9,25},{17,1},{25,9},{2,18},{10... | collective-permute-start | bytes 2162696 | tf_op jit(solution)/shard_map/ppermute | solution.py:256
  390.7 33.2 %collective-permute-start.24 = (bf16[176,2048]{1,0:T(8,128)(2,1)}, bf16[176,2048]{1,0:T(8,128)(2,1)}, u32[]{:S(2)}, u32[]{:S(2)}) collective-permute-start(bf16[176,2048]{1,0:T(8,128)(2,1)} %get-tuple-element.190), channel_id=1, source_target_pairs={{0,8},{8,0},{16,24},{24,16},{1,9},{9,1},{17,25},{25,17},{2,10},{10... | collective-permute-start | bytes 2162696 | tf_op jit(solution)/shard_map/ppermute | solution.py:256
  447.3 23.7 %collective-permute-start.31 = (bf16[512,768]{1,0:T(8,128)(2,1)S(1)}, bf16[512,768]{1,0:T(8,128)(2,1)}, u32[]{:S(2)}, u32[]{:S(2)}) collective-permute-start(bf16[512,768]{1,0:T(8,128)(2,1)S(1)} %copy-done.26), channel_id=1, source_target_pairs={{0,24},{8,16},{16,8},{24,0},{1,25},{9,17},{17,9},{25,1},{2,26},{10... | collective-permute-start | bytes 2359304 | tf_op jit(solution)/shard_map/ppermute | solution.py:256
  452.3 74.4 %reduce-scatter.14.cloned.1.call-start = ((), (), s32[]{:S(2)}) async-start(), calls=%async_computation.17 | async-start | bytes 2359296 | tf_op jit(solution)/shard_map/reduce_scatter | solution.py:282
  477.7 39.3 %all-to-all-start.2 = ((bf16[8,64,768]{2,1,0:T(8,128)(2,1)}), bf16[8,64,768]{2,1,0:T(8,128)(2,1)}, u32[]{:S(2)}, u32[]{:S(2)}) async-start(bf16[8,64,768]{2,1,0:T(8,128)(2,1)} %bitcast.33), calls=%async_computation.7 | async-start | bytes 1572864 | tf_op jit(solution)/shard_map/all_to_all | solution.py:560
  (55 other events, 705.9 us)
Sparse Core Ops, SparseCore 0:
  43.0 46.0 all-gather.5
  98.5 27.3 all-gather.7
  132.1 48.2 reduce-scatter.5
  190.1 45.2 all-gather.9
  237.4 27.8 all-gather.11
  286.3 49.4 reduce-scatter.7
  340.2 45.2 all-gather.13
  387.9 34.2 reduce-scatter.9
  424.5 50.0 reduce-scatter.11
  477.1 47.2 reduce-scatter.13

commit v4 on v3

--- a/solution.py
+++ b/solution.py
@@ -181,6 +181,79 @@
         grad_ref[:, value_part] = grad_value[...].astype(jnp.bfloat16)
 
 
+def columns_kernel(part_refs, out_ref, deal, width):
+    row = 0
+    for ref in part_refs:
+        groups, rows = ref.shape[0], ref.shape[1]
+        for c in range(3):
+            for d in range(0, deal, 2):
+                for s in range(0, groups, 2):
+                    begin = c * deal * HEAD + d * HEAD
+                    left = ref[s, :, begin : begin + 2 * HEAD].astype(jnp.float32)
+                    right = ref[s + 1, :, begin : begin + 2 * HEAD].astype(jnp.float32)
+                    lower = lax.broadcasted_iota(jnp.int32, left.shape, 1) < HEAD
+                    out = c * width + d * groups * HEAD + s * HEAD
+                    out_ref[row : row + rows, out : out + 2 * HEAD] = jnp.where(
+                        lower, left, pltpu.roll(right, HEAD, 1)
+                    )
+                    out = out + groups * HEAD
+                    out_ref[row : row + rows, out : out + 2 * HEAD] = jnp.where(
+                        lower, pltpu.roll(left, HEAD, 1), right
+                    )
+        row += rows
+
+
+def columns_in_place(parts, deal):
+    rows = sum(part.shape[1] for part in parts)
+    width = parts[0].shape[0] * deal * HEAD
+
+    def kernel(*refs):
+        columns_kernel(refs[:-1], refs[-1], deal, width)
+
+    return pl.pallas_call(
+        kernel,
+        out_shape=jax.ShapeDtypeStruct((rows, 3 * width), jnp.float32),
+        compiler_params=pltpu.CompilerParams(vmem_limit_bytes=VMEM_BYTES),
+        name="columns_in_place",
+    )(*parts)
+
+
+def deal_kernel(weight_ref, riders_ref, out_ref, deal):
+    groups = out_ref.shape[0]
+    rows, width = weight_ref.shape[0], weight_ref.shape[1] // 3
+    for c in range(3):
+        for d in range(0, deal, 2):
+            for s in range(0, groups, 2):
+                begin = c * width + d * groups * HEAD + s * HEAD
+                upper = weight_ref[:, begin : begin + 2 * HEAD].astype(jnp.float32)
+                begin = begin + groups * HEAD
+                after = weight_ref[:, begin : begin + 2 * HEAD].astype(jnp.float32)
+                lower = lax.broadcasted_iota(jnp.int32, upper.shape, 1) < HEAD
+                out = c * deal * HEAD + d * HEAD
+                out_ref[s, 0:rows, out : out + 2 * HEAD] = jnp.where(
+                    lower, upper, pltpu.roll(after, HEAD, 1)
+                ).astype(jnp.bfloat16)
+                out_ref[s + 1, 0:rows, out : out + 2 * HEAD] = jnp.where(
+                    lower, pltpu.roll(upper, HEAD, 1), after
+                ).astype(jnp.bfloat16)
+    for s in range(groups):
+        out_ref[s, rows:, :] = riders_ref[...]
+
+
+def deal_columns(weight, riders, groups, deal):
+    def kernel(*refs):
+        deal_kernel(*refs, deal)
+
+    return pl.pallas_call(
+        kernel,
+        out_shape=jax.ShapeDtypeStruct(
+            (groups, weight.shape[0] + riders.shape[0], riders.shape[1]), jnp.bfloat16
+        ),
+        compiler_params=pltpu.CompilerParams(vmem_limit_bytes=VMEM_BYTES),
+        name="deal_columns",
+    )(weight, riders)
+
+
 def rotation_tables(cosines, sines, lanes):
     length = cosines.shape[0]
     rest = jnp.ones((length, HEAD - ROT), jnp.float32)
@@ -210,11 +283,7 @@
         ),
         scratch_shapes=[pltpu.VMEM((lanes, length), jnp.bfloat16)],
         compiler_params=pltpu.CompilerParams(vmem_limit_bytes=VMEM_BYTES),
-        cost_estimate=pl.CostEstimate(
-            flops=4 * length * length * width,
-            bytes_accessed=12 * length * width,
-            transcendentals=length * length * width // HEAD,
-        ),
+        cost_estimate=pl.CostEstimate(flops=1, bytes_accessed=1, transcendentals=1),
         name="attention_forward",
     )(projected, *tables, first)
 
@@ -232,11 +301,7 @@
             pltpu.VMEM((length, lanes), jnp.float32),
         ],
         compiler_params=pltpu.CompilerParams(vmem_limit_bytes=VMEM_BYTES),
-        cost_estimate=pl.CostEstimate(
-            flops=10 * length * length * width,
-            bytes_accessed=18 * length * width,
-            transcendentals=length * length * width // HEAD,
-        ),
+        cost_estimate=pl.CostEstimate(flops=1, bytes_accessed=1, transcendentals=1),
         name="attention_backward",
     )(queries, key_heads, projected, grad_context, logsum, *tables, first)
 
@@ -260,11 +325,35 @@
     return [piece] + [permute(piece, "dp", k) for k in range(1, lax.axis_size("dp"))]
 
 
-def scatter_dp(pieces):
-    total = pieces[0].astype(jnp.float32)
-    for k in range(1, len(pieces)):
-        total = total + permute(pieces[k].astype(jnp.bfloat16), "dp", k).astype(jnp.float32)
-    return total
+def near_dp(piece):
+    return [piece, permute(piece, "dp", 1), permute(piece, "dp", 2)]
+
+
+def corner_dp(pieces):
+    middle = pieces[0].shape[0] // 2
+    return jnp.concatenate(
+        [permute(pieces[2][:middle], "dp", 1), permute(pieces[1][middle:], "dp", 2)], axis=0
+    )
+
+
+def send_corner(pieces):
+    middle = pieces[0].shape[0] // 2
+    return (permute(pieces[3][:middle], "dp", 2), permute(pieces[3][middle:], "dp", 1))
+
+
+def add_corner(pieces, corner):
+    middle = pieces[0].shape[0] // 2
+    first = total([pieces[1][:middle], corner[0]]).astype(jnp.bfloat16)
+    second = total([pieces[2][middle:], corner[1]]).astype(jnp.bfloat16)
+    return [
+        jnp.concatenate([first, pieces[1][middle:]], axis=0),
+        jnp.concatenate([pieces[2][:middle], second], axis=0),
+    ]
+
+
+def send_near(pieces, corner):
+    first, second = add_corner(pieces, corner)
+    return [permute(first, "dp", 1), permute(second, "dp", 2)]
 
 
 def total(parts):
@@ -345,10 +434,6 @@
 
     phase = lax.optimization_barrier
     grad_out = cotangent[0]
-    half = D // 2
-
-    def to_owner(terms):
-        return scatter_dp(jnp.split(terms, rows, axis=0))
 
     def dp_terms(terms):
         block = terms.shape[0] // rows
@@ -368,30 +453,29 @@
         ],
         axis=0,
     )
-    ride = 8
+    ride = 16
     riders = jnp.zeros((ride * 3 * local_width,), jnp.bfloat16)
     riders = lax.dynamic_update_slice(riders, small.reshape(-1), (0,))
-    part = lax.all_to_all(
-        jnp.concatenate(
+    riders = riders.reshape(ride, 3 * local_width)
+    if whole_heads and rows % 2 == 0:
+        dealt = deal_columns(qkv_weight, riders, groups, rows)
+    else:
+        dealt = jnp.concatenate(
             [
                 qkv_weight.reshape((own, 3) + deal)
                 .transpose(3, 0, 1, 2, 4)
                 .reshape(groups, own, 3 * local_width),
-                jnp.broadcast_to(
-                    riders.reshape(1, ride, 3 * local_width), (groups, ride, 3 * local_width)
-                ),
+                jnp.broadcast_to(riders[None], (groups,) + riders.shape),
             ],
             axis=1,
-        ),
-        "seq",
-        split_axis=0,
-        concat_axis=0,
-        tiled=True,
-    )
-    part, own_input = phase((part, layer_input[0]))
-    input_all = gather_seq(own_input)
+        )
+    part = lax.all_to_all(dealt, "seq", split_axis=0, concat_axis=0, tiled=True)
+    chips = groups // 2
+    input_all = gather_seq(layer_input[0])
     spread = place(gather_dp(part[:, own:].reshape(groups, -1)), at_dp)
-    head_qkv = place(gather_dp(part[:, :own].reshape(groups * own, 3 * local_width)), at_dp)
+    qkv_pieces = near_dp(part[:, :own].reshape(groups * own, 3 * local_width))
+    input_all, spread, grad_far = phase((input_all, spread, grad_out))
+    grad_pieces = [grad_out] + [permute(grad_far, "seq", 2 * k) for k in range(1, chips)]
     spread = spread[:, : small.size].reshape((devices,) + small.shape)
     table = jnp.swapaxes(spread, 0, 1).reshape(small.shape[0], D).astype(jnp.float32)
     languages = spread[:, LANGS + 7, 0].astype(jnp.int32)
@@ -407,27 +491,18 @@
     first = offsets[None, :]
     resid_in = layer_input[0].astype(jnp.float32) + lang_row
     unused, scaled_attn, inverse_attn = norm_forward(resid_in, gain_attn, bias_attn)
-    input_all, head_qkv, out_rows, tables, first, resid_in, grad_first, gate_rows = phase(
-        (
-            input_all,
-            head_qkv,
-            out_weight,
-            tables,
-            first,
-            resid_in,
-            grad_out[:, :half],
-            gate_weight.T,
-        )
+    normed_all = norm_forward(input_all.astype(jnp.float32) + lang_row, gain_attn, bias_attn)[
+        0
+    ].astype(jnp.bfloat16)
+    qkv_pieces, tables, first, resid_in = phase((qkv_pieces, tables, first, resid_in))
+    head_qkv = place(qkv_pieces + [corner_dp(qkv_pieces)], at_dp)
+    head_qkv, normed_all, out_rows, gate_rows = phase(
+        (head_qkv, normed_all, out_weight, gate_weight.T)
     )
     if not whole_heads:
         out_rows = lax.ppermute(out_rows, ("dp", "seq"), back)
     head_out = place(gather_dp(out_rows), at_dp)
-    gate_pieces = [gate_rows, permute(gate_rows, "dp", 1), permute(gate_rows, "dp", 2)]
-    grad_all_first = gather_seq(grad_first)
-    normed_all, scaled_all, inverse_all = norm_forward(
-        input_all.astype(jnp.float32) + lang_row, gain_attn, bias_attn
-    )
-    normed_all = normed_all.astype(jnp.bfloat16)
+    gate_pieces = near_dp(gate_rows)
     projected = (
         jnp.dot(normed_all, head_qkv, preferred_element_type=jnp.float32) + bias_qkv
     ).astype(jnp.bfloat16)
@@ -435,80 +510,102 @@
     out_terms = jnp.dot(context_all, head_out, preferred_element_type=jnp.float32).astype(
         jnp.bfloat16
     )
-    out_terms, grad_all_first, gate_pieces = phase((out_terms, grad_all_first, gate_pieces))
+    out_terms, grad_pieces, gate_pieces, up_rows = phase(
+        (out_terms, grad_pieces, gate_pieces, up_weight.T)
+    )
     attn_out = scatter_seq(out_terms)
-    cols_gate = jnp.concatenate(gate_pieces + [permute(gate_pieces[0], "dp", 3)], axis=0)
-    cols_up = jnp.concatenate(gather_dp(after(up_weight.T, cols_gate)), axis=0)
-    attn_out, cols_gate, cols_up, down_rows = phase((attn_out, cols_gate, cols_up, down_weight))
-    cols_down = jnp.concatenate(gather_dp(down_rows), axis=0)
+    gate_pieces = gate_pieces + [corner_dp(gate_pieces)]
+    up_pieces = near_dp(up_rows)
+    mates = permute(jnp.concatenate(grad_pieces, axis=0), "seq", 1)
+    gate_pieces, up_pieces, mates = phase((gate_pieces, up_pieces, mates))
+    up_pieces = up_pieces + [corner_dp(up_pieces)]
+    mates = jnp.split(mates, chips, axis=0)
+    grad_all = place([piece for pair in zip(grad_pieces, mates) for piece in pair], at_seq)
+    attn_out, up_pieces, grad_all, down_rows = phase((attn_out, up_pieces, grad_all, down_weight))
     resid_mid = resid_in + attn_out
     normed_mlp, scaled_mlp, inverse_mlp = norm_forward(resid_mid, gain_mlp, bias_mlp)
     rows_all = gather_seq(normed_mlp.astype(jnp.bfloat16))
-    grad_hidden = contract(grad_all_first, cols_down[:, :half], 1, 1)
-    rows_all, cols_down, grad_hidden, grad_second = phase(
-        (rows_all, cols_down, grad_hidden, grad_out[:, half:])
-    )
-    grad_all_second = gather_seq(grad_second)
+    down_pieces = near_dp(down_rows)
+    down_pieces = phase(down_pieces)
+    cols_down = jnp.concatenate(down_pieces + [corner_dp(down_pieces)], axis=0)
+    cols_gate = jnp.concatenate(gate_pieces, axis=0)
+    cols_up = jnp.concatenate(up_pieces, axis=0)
+    grad_hidden = contract(grad_all, cols_down, 1, 1)
+    rows_all, cols_down, cols_gate, cols_up, grad_hidden = phase(
+        (rows_all, cols_down, cols_gate, cols_up, grad_hidden)
+    )
     gate_values = contract(rows_all, cols_gate, 1, 1)
     up_values = contract(rows_all, cols_up, 1, 1)
     hidden = (jax.nn.silu(gate_values) * up_values).astype(jnp.bfloat16)
-    grad_hidden = grad_hidden + contract(grad_all_second, cols_down[:, half:], 1, 1)
     grad_gate, grad_up = gate_backward(gate_values, up_values, grad_hidden)
     grad_rows = (
         contract(grad_gate, cols_gate, 1, 0) + contract(grad_up, cols_up, 1, 0)
     ).astype(jnp.bfloat16)
     grad_rows, grad_gate, grad_up, hidden = phase((grad_rows, grad_gate, grad_up, hidden))
     grad_normed_mlp = scatter_seq(grad_rows)
-    out_gate = to_owner(contract(grad_gate, rows_all, 0, 0).astype(jnp.bfloat16))
+    gate_terms = jnp.split(
+        contract(grad_gate, rows_all, 0, 0).astype(jnp.bfloat16), rows, axis=0
+    )
+    gate_corner = send_corner(gate_terms)
+    mlp_terms = (
+        contract(hidden, cols_down, 1, 0).astype(jnp.bfloat16).reshape(chips, 2, tokens, D)
+    )
+    mlp_other = permute(
+        lax.dynamic_index_in_dim(mlp_terms, 1 - at_seq % 2, 1, keepdims=False), "seq", 1
+    )
     up_terms = contract(grad_up, rows_all, 0, 0).astype(jnp.bfloat16)
-    mlp_first = contract(hidden, cols_down[:, :half], 1, 0).astype(jnp.bfloat16)
-    mlp_second = contract(hidden, cols_down[:, half:], 1, 0).astype(jnp.bfloat16)
-    down_terms = jnp.concatenate(
-        [contract(hidden, grad_all_first, 0, 0), contract(hidden, grad_all_second, 0, 0)], axis=1
+    gate_corner, gate_terms, mlp_terms, mlp_other, up_terms = phase(
+        (gate_corner, gate_terms, mlp_terms, mlp_other, up_terms)
+    )
+    gate_near = send_near(gate_terms, gate_corner)
+    mlp_pairs = total(
+        [lax.dynamic_index_in_dim(mlp_terms, at_seq % 2, 1, keepdims=False), mlp_other]
     ).astype(jnp.bfloat16)
-    grad_normed_mlp, out_gate, up_terms, mlp_first, mlp_second, down_terms = phase(
-        (grad_normed_mlp, out_gate, up_terms, mlp_first, mlp_second, down_terms)
-    )
+    down_terms = contract(hidden, grad_all, 0, 0).astype(jnp.bfloat16)
+    mlp_pieces = [
+        lax.dynamic_index_in_dim(mlp_pairs, (at_seq // 2) ^ k, 0, keepdims=False)
+        for k in range(chips)
+    ]
+    grad_normed_mlp, gate_near, up_terms, mlp_pieces, down_terms = phase(
+        (grad_normed_mlp, gate_near, up_terms, mlp_pieces, down_terms)
+    )
+    out_gate = total([gate_terms[0], *gate_near])
     grad_mid_norm, grad_gain_mlp, grad_bias_mlp = norm_backward(
         grad_normed_mlp, scaled_mlp, inverse_mlp, gain_mlp
     )
     grad_mid = grad_out.astype(jnp.float32) + grad_mid_norm
     branch_all = gather_seq(grad_mid.astype(jnp.bfloat16))
-    out_up = to_owner(up_terms)
-    branch_all, out_up, mlp_first, down_terms = phase((branch_all, out_up, mlp_first, down_terms))
-    mlp_out_first = scatter_seq(mlp_first)
-    down_pieces = jnp.split(down_terms, rows, axis=0)
-    down_arrived = [permute(down_pieces[k], "dp", k) for k in range(1, rows - 1)]
+    up_terms = jnp.split(up_terms, rows, axis=0)
+    down_terms = jnp.split(down_terms, rows, axis=0)
+    up_corner = send_corner(up_terms)
+    mlp_sums = [permute(mlp_pieces[1], "seq", 2)]
+    up_corner, up_terms, down_terms = phase((up_corner, up_terms, down_terms))
+    up_near = send_near(up_terms, up_corner)
+    down_corner = send_corner(down_terms)
+    down_terms = down_terms[:1] + add_corner(down_terms, down_corner)
+    branch_all, up_near, mlp_sums, mlp_pieces, down_terms = phase(
+        (branch_all, up_near, mlp_sums, mlp_pieces, down_terms)
+    )
+    out_up = total([up_terms[0], *up_near])
+    mlp_sums = mlp_sums + [permute(mlp_pieces[k], "seq", 2 * k) for k in range(2, chips - 1)]
+    down_near = [permute(down_terms[1], "dp", 1), permute(down_terms[2], "dp", 2)]
     grad_heads = contract(branch_all, head_out, 1, 1).astype(jnp.bfloat16)
     grad_stack = attention_backward(
         rot_query, rot_key, projected, grad_heads, logsum, tables, first
     )
+    grad_stack, down_near = phase((grad_stack, down_near))
     slice_terms = contract(normed_all, grad_stack, 0, 0).astype(jnp.bfloat16)
     attn_terms = contract(grad_stack, head_qkv, 1, 1).astype(jnp.bfloat16)
-    (
-        attn_terms,
-        slice_terms,
-        mlp_out_first,
-        grad_stack,
-        branch_all,
-        down_arrived,
-        down_pieces,
-        input_all,
-    ) = phase(
-        (
-            attn_terms,
-            slice_terms,
-            mlp_out_first,
-            grad_stack,
-            branch_all,
-            down_arrived,
-            down_pieces,
-            input_all,
-        )
-    )
-    grad_normed_attn = scatter_seq(attn_terms)
     slice_pieces = dp_terms(slice_terms)
-    slice_arrived = [permute(slice_pieces[k], "dp", k) for k in range(1, rows - 1)]
+    attn_terms, slice_pieces, grad_stack, branch_all, mlp_sums, mlp_pieces, input_all = phase(
+        (attn_terms, slice_pieces, grad_stack, branch_all, mlp_sums, mlp_pieces, input_all)
+    )
+    mlp_sums = mlp_sums + [permute(mlp_pieces[-1], "seq", 2 * (chips - 1))]
+    out_down = total([down_terms[0], *down_near])
+    half = D // 2
+    attn_first = scatter_seq(attn_terms[:, :half])
+    attn_second = scatter_seq(attn_terms[:, half:])
+    slice_corner = send_corner(slice_pieces)
     unused, scaled_all, inverse_all = norm_forward(
         input_all.astype(jnp.float32) + lang_row, gain_attn, bias_attn
     )
@@ -529,13 +626,10 @@
         axis=0,
     )
     head_out_terms = dp_terms(contract(context_all, branch_all, 0, 0).astype(jnp.bfloat16))
-    terms, head_out_terms, slice_arrived, slice_pieces = phase(
-        (terms, head_out_terms, slice_arrived, slice_pieces)
-    )
-    slice_arrived = slice_arrived + [permute(slice_pieces[-1], "dp", rows - 1)]
-    out_arrived = [permute(head_out_terms[k], "dp", k) for k in range(1, rows)]
-
-    slice_summed = total([slice_pieces[0]] + slice_arrived).astype(jnp.bfloat16)
+    terms, head_out_terms, slice_corner, slice_pieces, mlp_sums = phase(
+        (terms, head_out_terms, slice_corner, slice_pieces, mlp_sums)
+    )
+    slice_near = send_near(slice_pieces, slice_corner)
     arrived = lax.all_to_all(
         terms.reshape(terms.shape[0], devices, own).swapaxes(0, 1),
         ("dp", "seq"),
@@ -543,39 +637,34 @@
         concat_axis=0,
         tiled=True,
     )
-    out_arrived, mlp_second, arrived, slice_summed, grad_normed_attn, down_arrived, down_pieces = (
-        phase(
-            (
-                out_arrived,
-                mlp_second,
-                arrived,
-                slice_summed,
-                grad_normed_attn,
-                down_arrived,
-                down_pieces,
-            )
+    attn_first, arrived, slice_near, head_out_terms = phase(
+        (attn_first, arrived, slice_near, head_out_terms)
+    )
+    home = lax.all_to_all(
+        total([slice_pieces[0], *slice_near])
+        .astype(jnp.bfloat16)
+        .reshape(groups, own, 3 * local_width),
+        "seq",
+        split_axis=0,
+        concat_axis=0,
+        tiled=True,
+    )
+    out_arrived = [permute(head_out_terms[k], "dp", k) for k in range(1, rows)]
+    home, out_arrived, attn_second = phase((home, out_arrived, attn_second))
+    grad_normed_attn = jnp.concatenate([attn_first, attn_second], axis=1)
+    if whole_heads and rows % 2 == 0:
+        grad_qkv_out = columns_in_place([home], rows)
+    else:
+        grad_qkv_out = (
+            home.reshape(groups, own, 3, deal[0], deal[2])
+            .transpose(1, 2, 3, 0, 4)
+            .reshape(own, 3 * D)
+            .astype(jnp.float32)
         )
-    )
-    grad_qkv_out = (
-        lax.all_to_all(
-            slice_summed.reshape(groups, own, 3 * local_width),
-            "seq",
-            split_axis=0,
-            concat_axis=0,
-            tiled=True,
-        )
-        .reshape(groups, own, 3, deal[0], deal[2])
-        .transpose(1, 2, 3, 0, 4)
-        .reshape(own, 3 * D)
-        .astype(jnp.float32)
-    )
-    mlp_out = jnp.concatenate([mlp_out_first, scatter_seq(mlp_second)], axis=1)
     out_proj = total([head_out_terms[0]] + out_arrived)
     if not whole_heads:
         out_proj = lax.ppermute(out_proj, ("dp", "seq"), owner)
-    out_down = total(
-        [down_pieces[0]] + down_arrived + [permute(down_pieces[-1], "dp", rows - 1)]
-    )
+    mlp_out = total([mlp_pieces[0]] + mlp_sums)
     layer_output = (resid_mid + mlp_out).astype(jnp.bfloat16)
     grad_input = grad_mid + norm_backward(
         grad_normed_attn, scaled_attn, inverse_attn, gain_attn

time: 542 us -> 519 us (0.958)
  waiting for transfers between devices: 225 us -> 169 us
  starting transfers between devices: 51.6 us -> 83.6 us
  blocking collectives: 29.2 us -> 0 us
  other arithmetic: 55.3 us -> 79.3 us
  local copies, waits for them, and re-layouts: 56.8 us -> 71.5 us
  matrix products: 81.1 us -> 67.6 us
    ppermute x33 -> x49, waiting for transfers between devices: 155 us -> 68.4 us  [permute(): return lax.ppermute(value, axis, [(i, i ^ offset) for i in range(size)])]
    all_to_all x1 -> x2, waiting for transfers between devices: 10.9 us -> 40.5 us  [the longest x1 37.3 us: per_device(): part = lax.all_to_all(dealt, 'seq', split_axis=0, concat_axis=0, tiled=True)]
    all_to_all x1 -> x0, blocking collectives: 29.2 us -> none  [per_device(): lax.all_to_all(jnp.concatenate([qkv_weight.reshape((own, 3) + deal).trans...]
    reduce_scatter x5 -> x4, waiting for transfers between devices: 9.33 us -> 28.3 us  [scatter_seq(): lax.psum_scatter(terms.astype(jnp.bfloat16), 'seq', scatter_dimension=0,...]
    ppermute x33 -> x49, starting transfers between devices: 40.9 us -> 56.7 us  [permute(): return lax.ppermute(value, axis, [(i, i ^ offset) for i in range(size)])]
    slice x2 -> x22, local copies, waits for them, and re-layouts: 0.88 us -> 13.6 us  [the longest x4 4.85 us: corner_dp(): pieces[1][middle:]]
    all_to_all x1, starting transfers between devices: 3.38 us -> 15.2 us  [per_device(): lax.all_to_all(terms.reshape(terms.shape[0], devices, own).swapaxes(0, 1)...]
    concatenate x3 -> x13, other arithmetic: 4.9 us -> 16.7 us  [the longest x1 3.06 us: per_device(): cols_up = jnp.concatenate(up_pieces, axis=0)]
  transfers between devices with their start and end apart: 45 -> 59, of which waited for: 23 -> 25; matrix products, arithmetic and copies ran while one was open for 28% -> 34% of each run, Pallas kernels for 4% -> 4%
where the time goes in v4:
time: 519 us; the launch traced here: 512 us
  waiting for transfers between devices  169 us (33%)
  starting transfers between devices  83.6 us (16%)
  other arithmetic  79.3 us (15%)
  local copies, waits for them, and re-layouts  71.5 us (14%)
  matrix products  67.6 us (13%)
  Pallas kernels  23.6 us (5%)
  between operations  16.6 us (3%)
    ppermute x49, waiting for transfers between devices, permute(): return lax.ppermute(value, axis, [(i, i ^ offset) for i in range(size)])  68.4 us
    dot_general x13, matrix products, contract(): lax.dot_general(left, right, (((left_dim,), (right_dim,)), ((), ())), pre...  60.9 us
    ppermute x49, starting transfers between devices, permute(): return lax.ppermute(value, axis, [(i, i ^ offset) for i in range(size)])  56.7 us
    all_to_all x1, waiting for transfers between devices, per_device(): part = lax.all_to_all(dealt, 'seq', split_axis=0, concat_axis=0, tiled=True)  37.3 us
    reduce_scatter x4, waiting for transfers between devices, scatter_seq(): lax.psum_scatter(terms.astype(jnp.bfloat16), 'seq', scatter_dimension=0,...  28.3 us
    all_gather x3, waiting for transfers between devices, gather_seq(): return lax.all_gather(piece, 'seq', axis=0, tiled=True)  26.8 us
    dynamic_update_slice x19, local copies, waits for them, and re-layouts, place(): lax.dynamic_update_slice_in_dim(result, piece, (index ^ k) * block, 0)  20.1 us
    all_to_all x1, starting transfers between devices, per_device(): lax.all_to_all(terms.reshape(terms.shape[0], devices, own).swapaxes(0, 1)...  15.2 us
  transfers between devices with their start and end apart: 59, of which 25 were waited for; matrix products, arithmetic and copies ran while one was open for 34% of the time, Pallas kernels for 4%

profile of v4, /device:TPU:0, one launch (start us, length us, event | category | flops | bytes accessed | tf_op | source)
XLA Modules:
  0.0 511.7 jit_solution(117956428386631739)
XLA Ops:
  11.9 6.3 %all-to-all-start = ((bf16[8,80,768]{2,1,0:T(8,128)(2,1)}), bf16[8,80,768]{2,1,0:T(8,128)(2,1)S(1)}, u32[]{:S(2)}, u32[]{:S(2)}) async-start(bf16[8,80,768]{2,1,0:T(8,128)(2,1)} %deal_columns.1), calls=%async_computation | async-start | bytes 1966080 | tf_op jit(solution)/shard_map/all_to_all | solution.py:472
  20.7 37.3 %all-to-all-done = bf16[8,80,768]{2,1,0:T(8,128)(2,1)S(1)} async-done(((bf16[8,80,768]{2,1,0:T(8,128)(2,1)}), bf16[8,80,768]{2,1,0:T(8,128)(2,1)S(1)}, u32[]{:S(2)}, u32[]{:S(2)}) %all-to-all-start) | async-done | bytes 983072 | tf_op jit(solution)/shard_map/all_to_all | solution.py:472
  66.4 4.8 collective-permute-done.2
  73.3 5.7 %all-gather.9.cloned.1.call-done = bf16[1,1024,2048]{2,1,0:T(8,128)(2,1)} async-done(((bf16[1,128,2048]{2,1,0:T(8,128)(2,1)}), bf16[1,1024,2048]{2,1,0:T(8,128)(2,1)}) %all-gather.9.cloned.1.call-update) | async-done | bytes 4194320 | tf_op jit(solution)/shard_map/all_gather | solution.py:367
  99.7 4.0 add_convert_fusion.1
  115.9 9.8 %attention_forward.1 = (bf16[1024,256]{1,0:T(8,128)(2,1)S(1)}, bf16[1024,256]{1,0:T(8,128)(2,1)S(1)}, bf16[1024,256]{1,0:T(8,128)(2,1)S(1)}, f32[4,1024]{1,0:T(4,128)S(1)}) custom-call(bf16[1024,768]{1,0:T(8,128)(2,1)S(1)} %add_convert_fusion.2.qkv_ref, f32[1024,128]{1,0:T(8,128)S(1)} %copy.70.cos_ref, f32[1024,128]{1,0:T(8,128)S(1)} %copy.71.former_ref, ...), custom_call_target="tpu_custom_call" | custom-call | flops 1 | bytes 1 | tf_op jit(solution)/shard_map/attention_forward/pallas_call | solution.py:276
  134.6 5.9 %collective-permute-done.10 = bf16[128,2048]{1,0:T(8,128)(2,1)} collective-permute-done((bf16[128,2048]{1,0:T(8,128)(2,1)S(1)}, bf16[128,2048]{1,0:T(8,128)(2,1)}, u32[]{:S(2)}, u32[]{:S(2)}) %collective-permute-start.10) | collective-permute-done | bytes 524320 | tf_op jit(solution)/shard_map/ppermute | solution.py:321
  157.5 15.7 %collective-permute-done.15 = bf16[88,2048]{1,0:T(8,128)(2,1)} collective-permute-done((bf16[88,2048]{1,0:T(8,128)(2,1)}, bf16[88,2048]{1,0:T(8,128)(2,1)}, u32[]{:S(2)}, u32[]{:S(2)}) %collective-permute-start.15) | collective-permute-done | bytes 360480 | tf_op jit(solution)/shard_map/ppermute | solution.py:321
  205.1 9.0 %collective-permute-done.23 = bf16[176,2048]{1,0:T(8,128)(2,1)S(1)} collective-permute-done((bf16[176,2048]{1,0:T(8,128)(2,1)}, bf16[176,2048]{1,0:T(8,128)(2,1)S(1)}, u32[]{:S(2)}, u32[]{:S(2)}) %collective-permute-start.23) | collective-permute-done | bytes 720928 | tf_op jit(solution)/shard_map/ppermute | solution.py:321
  217.6 5.1 collective-permute-done.24
  225.5 7.1 %fusion.32 = f32[1024,704]{0,1:T(8,128)} fusion(bf16[1024,2048]{1,0:T(8,128)(2,1)} %slice_dynamic-update-slice_fusion, bf16[704,2048]{1,0:T(8,128)(2,1)S(1)} %constant_dynamic-update-slice_fusion), kind=kOutput, calls=%fused_computation.177 | convolution fusion | flops 2952790016 | bytes 9961472 | tf_op jit(solution)/shard_map/dot_general | solution.py:21
  232.6 10.8 %all-gather.5.cloned.1.call-done = bf16[1024,2048]{1,0:T(8,128)(2,1)} async-done(((bf16[128,2048]{1,0:T(8,128)(2,1)}), bf16[1024,2048]{1,0:T(8,128)(2,1)}) %all-gather.5.cloned.1.call-update) | async-done | bytes 4194320 | tf_op jit(solution)/shard_map/all_gather | solution.py:367
  243.4 6.0 %fusion.33 = f32[1024,704]{0,1:T(8,128)S(1)} fusion(bf16[1024,2048]{1,0:T(8,128)(2,1)} %all-gather.5.cloned.1.call-done, bf16[704,2048]{1,0:T(8,128)(2,1)} %pad_maximum_fusion), kind=kOutput, calls=%fused_computation.178 | convolution fusion | flops 2952790016 | bytes 9961472 | tf_op jit(solution)/shard_map/dot_general | solution.py:21
  249.4 5.4 %multiply_convert_fusion = (bf16[1024,704]{0,1:T(8,128)(2,1)}, bf16[1024,704]{0,1:T(8,128)(2,1)S(1)}, bf16[1024,704]{0,1:T(8,128)(2,1)S(1)}) fusion(f32[1024,704]{0,1:T(8,128)S(1)} %fusion.33, f32[1024,704]{0,1:T(8,128)S(1)} %copy-done.61, bf16[1024,2048]{1,0:T(8,128)(2,1)S(1)} %copy-done.56, bf16[704,2048]{1,0:T(8,128)(2,1)S(1)} %copy-done.29), kind=kOutput, calls=%fused_computation.35 | convolution fusion | flops 2963603456 | bytes 17170432 | tf_op jit(solution)/shard_map/dot_general | solution.py:21
  254.8 3.5 fusion.34
  258.4 5.3 %add_convert_fusion = bf16[1024,2048]{1,0:T(8,128)(2,1)} fusion(f32[1024,2048]{1,0:T(8,128)S(1)} %fusion.34, bf16[1024,704]{0,1:T(8,128)(2,1)S(1)} %get-tuple-element.195, bf16[704,2048]{1,0:T(8,128)(2,1)S(1)} %copy-done.28), kind=kOutput, calls=%fused_computation.16 | convolution fusion | flops 2956984320 | bytes 16908288 | tf_op jit(solution)/shard_map/dot_general | solution.py:21
  264.0 5.8 %convolution_convert_fusion = bf16[1024,2048]{1,0:T(8,128)(2,1)S(1)} fusion(bf16[1024,704]{0,1:T(8,128)(2,1)} %get-tuple-element.196, bf16[704,2048]{1,0:T(8,128)(2,1)} %copy-done.47), kind=kOutput, calls=%fused_computation.24 | convolution fusion | flops 2954887168 | bytes 8519680 | tf_op jit(solution)/shard_map/dot_general | solution.py:21
  278.5 6.7 %convolution_convert_fusion.4 = bf16[704,2048]{1,0:T(8,128)(2,1)} fusion(bf16[1024,704]{0,1:T(8,128)(2,1)S(1)} %copy-done.64, bf16[1024,2048]{1,0:T(8,128)(2,1)} %slice_dynamic-update-slice_fusion), kind=kOutput, calls=%fused_computation.28 | convolution fusion | flops 2954231808 | bytes 8519680 | tf_op jit(solution)/shard_map/dot_general | solution.py:21
  285.2 4.5 convolution_convert_fusion.5
  296.3 16.4 %reduce-scatter.7.cloned.1.call-done = bf16[128,2048]{1,0:T(8,128)(2,1)} async-done(((bf16[1024,2048]{1,0:T(8,128)(2,1)}), bf16[128,2048]{1,0:T(8,128)(2,1)}) %reduce-scatter.7.cloned.1.call-update) | async-done | bytes 524304 | tf_op jit(solution)/shard_map/reduce_scatter | solution.py:371
  334.3 6.8 %collective-permute-done.37 = bf16[88,2048]{1,0:T(8,128)(2,1)S(1)} collective-permute-done((bf16[88,2048]{1,0:T(8,128)(2,1)S(1)}, bf16[88,2048]{1,0:T(8,128)(2,1)S(1)}, u32[]{:S(2)}, u32[]{:S(2)}) %collective-permute-start.37) | collective-permute-done | bytes 360480 | tf_op jit(solution)/shard_map/ppermute | solution.py:321
  347.1 7.4 %collective-permute-done.34 = bf16[176,2048]{1,0:T(8,128)(2,1)S(1)} collective-permute-done((bf16[176,2048]{1,0:T(8,128)(2,1)S(1)}, bf16[176,2048]{1,0:T(8,128)(2,1)S(1)}, u32[]{:S(2)}, u32[]{:S(2)}) %collective-permute-start.34) | collective-permute-done | bytes 720928 | tf_op jit(solution)/shard_map/ppermute | solution.py:321
  354.5 10.3 %all-gather.7.cloned.1.call-done = bf16[1024,2048]{1,0:T(8,128)(2,1)} async-done(((bf16[128,2048]{1,0:T(8,128)(2,1)}), bf16[1024,2048]{1,0:T(8,128)(2,1)}) %all-gather.7.cloned.1.call-update) | async-done | bytes 4194320 | tf_op jit(solution)/shard_map/all_gather | solution.py:367
  369.9 3.5 convolution_convert_fusion.8.context_grad_ref
  375.5 11.1 %attention_backward.1 = bf16[1024,768]{1,0:T(8,128)(2,1)S(1)} custom-call(bf16[1024,256]{1,0:T(8,128)(2,1)S(1)} %copy-done.5, bf16[1024,256]{1,0:T(8,128)(2,1)S(1)} %copy-done.7, bf16[1024,768]{1,0:T(8,128)(2,1)} %copy-done, bf16[1024,256]{1,0:T(8,128)(2,1)S(1)} %convolution_convert_fusion.8.context_grad_ref, f32[4,1024]{1,0:T(4,128)S(1)} %get-tuple-element.222.logsum_ref, ...), custom_call_target="tpu_custom_call" | custom-call | flops 1 | bytes 1 | tf_op jit(solution)/shard_map/attention_backward/pallas_call | solution.py:294
  387.5 3.8 convolution_convert_fusion.3
  393.8 3.7 convolution_convert_fusion.2
  417.9 7.1 %fusion.5 = (f32[2048]{0:T(1024)S(1)}, f32[2048]{0:T(1024)S(1)}, f32[2048]{0:T(1024)S(1)}) fusion(bf16[1024,2048]{1,0:T(8,128)(2,1)} %copy-done.10, bf16[1024,2048]{1,0:T(8,128)(2,1)} %bitcast.116, f32[1024]{0:T(1024)S(1)} %broadcast_multiply_fusion, f32[1024]{0:T(1024)S(1)} %broadcast_multiply_fusion.1, f32[1024]{0:T(1024)S(1)} %add_rsqrt_fusion, ...), kind=kLoop, calls=%fused_computation.8 | loop fusion | flops 29353984 | bytes 8445952 | tf_op jit(solution)/shard_map/reduce_sum | solution.py:615
  437.7 15.2 %all-to-all-start.1 = ((f32[32,1,512]{2,1,0:T(1,128)}), f32[32,1,512]{2,1,0:T(1,128)S(1)}, u32[]{:S(2)}, u32[]{:S(2)}) async-start(f32[32,1,512]{2,1,0:T(1,128)} %reshape.274), calls=%async_computation.4 | async-start | bytes 131072 | tf_op jit(solution)/shard_map/all_to_all | solution.py:633
  455.5 4.8 all-to-all-done.1
  465.3 4.6 all-to-all-start.2
  480.4 11.9 %reduce-scatter.11.cloned.1.call-done = bf16[128,1024]{1,0:T(8,128)(2,1)} async-done(((bf16[1024,1024]{1,0:T(8,128)(2,1)}), bf16[128,1024]{1,0:T(8,128)(2,1)}) %reduce-scatter.11.cloned.1.call-update) | async-done | bytes 262160 | tf_op jit(solution)/shard_map/reduce_scatter | solution.py:371
  (426 shorter events, 229.9 us)
Async XLA Ops:
  11.9 46.2 %all-to-all-start = ((bf16[8,80,768]{2,1,0:T(8,128)(2,1)}), bf16[8,80,768]{2,1,0:T(8,128)(2,1)S(1)}, u32[]{:S(2)}, u32[]{:S(2)}) async-start(bf16[8,80,768]{2,1,0:T(8,128)(2,1)} %deal_columns.1), calls=%async_computation | async-start | bytes 1966080 | tf_op jit(solution)/shard_map/all_to_all | solution.py:472
  18.2 60.7 %all-gather.9.cloned.1.call-start = ((), (), s32[]{:S(2)}) async-start(), calls=%async_computation.13 | async-start | bytes 4718592 | tf_op jit(solution)/shard_map/all_gather | solution.py:367
  18.9 174.0 %reduce-scatter.5.cloned.1.call-start = ((), (), s32[]{:S(2)}) async-start(), calls=%async_computation.7 | async-start | bytes 4718592 | tf_op jit(solution)/shard_map/reduce_scatter | solution.py:371
  61.7 27.7 %collective-permute-start.1 = (bf16[512,768]{1,0:T(8,128)(2,1)S(1)}, bf16[512,768]{1,0:T(8,128)(2,1)S(1)}, u32[]{:S(2)}, u32[]{:S(2)}) collective-permute-start(bf16[512,768]{1,0:T(8,128)(2,1)S(1)} %bitcast.127), channel_id=1, source_target_pairs={{0,16},{8,24},{16,0},{24,8},{1,17},{9,25},{17,1},{25,9},{2,18},{10... | collective-permute-start | bytes 2359304 | tf_op jit(solution)/shard_map/ppermute | solution.py:321
  63.3 26.1 %collective-permute-start = (bf16[512,768]{1,0:T(8,128)(2,1)S(1)}, bf16[512,768]{1,0:T(8,128)(2,1)}, u32[]{:S(2)}, u32[]{:S(2)}) collective-permute-start(bf16[512,768]{1,0:T(8,128)(2,1)S(1)} %bitcast.128), channel_id=1, source_target_pairs={{0,8},{8,0},{16,24},{24,16},{1,9},{9,1},{17,25},{25,17},{2,10},{10... | collective-permute-start | bytes 2359304 | tf_op jit(solution)/shard_map/ppermute | solution.py:321
  80.8 53.8 %collective-permute-start.12 = (bf16[128,2048]{1,0:T(8,128)(2,1)S(1)}, bf16[128,2048]{1,0:T(8,128)(2,1)}, u32[]{:S(2)}, u32[]{:S(2)}) collective-permute-start(bf16[128,2048]{1,0:T(8,128)(2,1)S(1)} %bitcast.120), channel_id=1, source_target_pairs={{0,6},{1,7},{2,4},{3,5},{4,2},{5,3},{6,0},{7,1},{8,14},{9,15},{10,... | collective-permute-start | bytes 1572872 | tf_op jit(solution)/shard_map/ppermute | solution.py:321
  82.1 52.5 %collective-permute-start.11 = (bf16[128,2048]{1,0:T(8,128)(2,1)S(1)}, bf16[128,2048]{1,0:T(8,128)(2,1)}, u32[]{:S(2)}, u32[]{:S(2)}) collective-permute-start(bf16[128,2048]{1,0:T(8,128)(2,1)S(1)} %bitcast.121), channel_id=1, source_target_pairs={{0,4},{1,5},{2,6},{3,7},{4,0},{5,1},{6,2},{7,3},{8,12},{9,13},{10,... | collective-permute-start | bytes 1572872 | tf_op jit(solution)/shard_map/ppermute | solution.py:321
  143.5 99.9 %all-gather.5.cloned.1.call-start = ((), (), s32[]{:S(2)}) async-start(), calls=%async_computation.8 | async-start | bytes 4718592 | tf_op jit(solution)/shard_map/all_gather | solution.py:367
  146.4 28.9 %collective-permute-start.19 = (bf16[512,2048]{1,0:T(8,128)(2,1)}, bf16[512,2048]{1,0:T(8,128)(2,1)}, u32[]{:S(2)}, u32[]{:S(2)}) collective-permute-start(bf16[512,2048]{1,0:T(8,128)(2,1)} %pad_maximum_fusion.2), channel_id=1, source_target_pairs={{0,1},{1,0},{2,3},{3,2},{4,5},{5,4},{6,7},{7,6},{8,9},{9,8},{10,11... | collective-permute-start | bytes 6291464 | tf_op jit(solution)/shard_map/ppermute | solution.py:321
  146.4 28.9 %collective-permute-start.18 = (bf16[176,2048]{1,0:T(8,128)(2,1)}, bf16[176,2048]{1,0:T(8,128)(2,1)S(1)}, u32[]{:S(2)}, u32[]{:S(2)}) collective-permute-start(bf16[176,2048]{1,0:T(8,128)(2,1)} %bitcast.21), channel_id=1, source_target_pairs={{0,16},{8,24},{16,0},{24,8},{1,17},{9,25},{17,1},{25,9},{2,18},{10... | collective-permute-start | bytes 2162696 | tf_op jit(solution)/shard_map/ppermute | solution.py:321
  146.9 28.4 %collective-permute-start.17 = (bf16[176,2048]{1,0:T(8,128)(2,1)}, bf16[176,2048]{1,0:T(8,128)(2,1)}, u32[]{:S(2)}, u32[]{:S(2)}) collective-permute-start(bf16[176,2048]{1,0:T(8,128)(2,1)} %bitcast.21), channel_id=1, source_target_pairs={{0,8},{8,0},{16,24},{24,16},{1,9},{9,1},{17,25},{25,17},{2,10},{10... | collective-permute-start | bytes 2162696 | tf_op jit(solution)/shard_map/ppermute | solution.py:321
  151.1 22.2 %collective-permute-start.15 = (bf16[88,2048]{1,0:T(8,128)(2,1)}, bf16[88,2048]{1,0:T(8,128)(2,1)}, u32[]{:S(2)}, u32[]{:S(2)}) collective-permute-start(bf16[88,2048]{1,0:T(8,128)(2,1)} %slice.172), channel_id=1, source_target_pairs={{0,8},{8,0},{16,24},{24,16},{1,9},{9,1},{17,25},{25,17},{2,10},{10... | collective-permute-start | bytes 1081352 | tf_op jit(solution)/shard_map/ppermute | solution.py:321
  152.5 20.7 %collective-permute-start.16 = (bf16[88,2048]{1,0:T(8,128)(2,1)}, bf16[88,2048]{1,0:T(8,128)(2,1)}, u32[]{:S(2)}, u32[]{:S(2)}) collective-permute-start(bf16[88,2048]{1,0:T(8,128)(2,1)} %slice.173), channel_id=1, source_target_pairs={{0,16},{8,24},{16,0},{24,8},{1,17},{9,25},{17,1},{25,9},{2,18},{10... | collective-permute-start | bytes 1081352 | tf_op jit(solution)/shard_map/ppermute | solution.py:321
  196.9 115.7 %reduce-scatter.7.cloned.1.call-start = ((), (), s32[]{:S(2)}) async-start(), calls=%async_computation.9 | async-start | bytes 4718592 | tf_op jit(solution)/shard_map/reduce_scatter | solution.py:371
  263.7 101.1 %all-gather.7.cloned.1.call-start = ((), (), s32[]{:S(2)}) async-start(), calls=%async_computation.10 | async-start | bytes 4718592 | tf_op jit(solution)/shard_map/all_gather | solution.py:367
  270.2 20.6 %collective-permute-start.28 = (bf16[4,128,2048]{2,1,0:T(8,128)(2,1)S(1)}, bf16[4,128,2048]{2,1,0:T(8,128)(2,1)S(1)}, u32[]{:S(2)}, u32[]{:S(2)}) collective-permute-start(bf16[4,128,2048]{2,1,0:T(8,128)(2,1)S(1)} %dynamic-slice_bitcast_fusion), channel_id=1, source_target_pairs={{0,1},{1,0},{2,3},{3,2},{4,5},{5,4},{6,7},{7,6},{8,9},{9,8},{10,11... | collective-permute-start | bytes 6291464 | tf_op jit(solution)/shard_map/ppermute | solution.py:321
  291.8 21.9 %collective-permute-start.30 = (bf16[176,2048]{1,0:T(8,128)(2,1)}, bf16[176,2048]{1,0:T(8,128)(2,1)}, u32[]{:S(2)}, u32[]{:S(2)}) collective-permute-start(bf16[176,2048]{1,0:T(8,128)(2,1)} %pad_maximum_fusion.8), channel_id=1, source_target_pairs={{0,16},{8,24},{16,0},{24,8},{1,17},{9,25},{17,1},{25,9},{2,18},{10... | collective-permute-start | bytes 2162696 | tf_op jit(solution)/shard_map/ppermute | solution.py:321
  316.7 145.0 %reduce-scatter.9.cloned.1.call-start = ((), (), s32[]{:S(2)}) async-start(), calls=%async_computation.11 | async-start | bytes 2359296 | tf_op jit(solution)/shard_map/reduce_scatter | solution.py:371
  317.2 29.9 %collective-permute-start.35 = (bf16[128,2048]{1,0:T(8,128)(2,1)}, bf16[128,2048]{1,0:T(8,128)(2,1)S(1)}, u32[]{:S(2)}, u32[]{:S(2)}) collective-permute-start(bf16[128,2048]{1,0:T(8,128)(2,1)} %get-tuple-element.213), channel_id=1, source_target_pairs={{0,2},{1,3},{2,0},{3,1},{4,6},{5,7},{6,4},{7,5},{8,10},{9,11},{10,... | collective-permute-start | bytes 1572872 | tf_op jit(solution)/shard_map/ppermute | solution.py:321
  332.1 22.4 %collective-permute-start.34 = (bf16[176,2048]{1,0:T(8,128)(2,1)S(1)}, bf16[176,2048]{1,0:T(8,128)(2,1)S(1)}, u32[]{:S(2)}, u32[]{:S(2)}) collective-permute-start(bf16[176,2048]{1,0:T(8,128)(2,1)S(1)} %pad_maximum_fusion.10), channel_id=1, source_target_pairs={{0,16},{8,24},{16,0},{24,8},{1,17},{9,25},{17,1},{25,9},{2,18},{10... | collective-permute-start | bytes 2162696 | tf_op jit(solution)/shard_map/ppermute | solution.py:321
  332.9 21.6 %collective-permute-start.33 = (bf16[176,2048]{1,0:T(8,128)(2,1)S(1)}, bf16[176,2048]{1,0:T(8,128)(2,1)}, u32[]{:S(2)}, u32[]{:S(2)}) collective-permute-start(bf16[176,2048]{1,0:T(8,128)(2,1)S(1)} %pad_maximum_fusion.9), channel_id=1, source_target_pairs={{0,8},{8,0},{16,24},{24,16},{1,9},{9,1},{17,25},{25,17},{2,10},{10... | collective-permute-start | bytes 2162696 | tf_op jit(solution)/shard_map/ppermute | solution.py:321
  364.9 21.8 %collective-permute-start.38 = (bf16[176,2048]{1,0:T(8,128)(2,1)}, bf16[176,2048]{1,0:T(8,128)(2,1)S(1)}, u32[]{:S(2)}, u32[]{:S(2)}) collective-permute-start(bf16[176,2048]{1,0:T(8,128)(2,1)} %pad_maximum_fusion.11), channel_id=1, source_target_pairs={{0,8},{8,0},{16,24},{24,16},{1,9},{9,1},{17,25},{25,17},{2,10},{10... | collective-permute-start | bytes 2162696 | tf_op jit(solution)/shard_map/ppermute | solution.py:321
  366.2 21.3 %collective-permute-start.39 = (bf16[176,2048]{1,0:T(8,128)(2,1)}, bf16[176,2048]{1,0:T(8,128)(2,1)}, u32[]{:S(2)}, u32[]{:S(2)}) collective-permute-start(bf16[176,2048]{1,0:T(8,128)(2,1)} %pad_maximum_fusion.12), channel_id=1, source_target_pairs={{0,16},{8,24},{16,0},{24,8},{1,17},{9,25},{17,1},{25,9},{2,18},{10... | collective-permute-start | bytes 2162696 | tf_op jit(solution)/shard_map/ppermute | solution.py:321
  367.7 29.8 %collective-permute-start.40 = (bf16[128,2048]{1,0:T(8,128)(2,1)}, bf16[128,2048]{1,0:T(8,128)(2,1)S(1)}, u32[]{:S(2)}, u32[]{:S(2)}) collective-permute-start(bf16[128,2048]{1,0:T(8,128)(2,1)} %get-tuple-element.227), channel_id=1, source_target_pairs={{0,4},{1,5},{2,6},{3,7},{4,0},{5,1},{6,2},{7,3},{8,12},{9,13},{10,... | collective-permute-start | bytes 1572872 | tf_op jit(solution)/shard_map/ppermute | solution.py:321
  400.9 91.4 %reduce-scatter.11.cloned.1.call-start = ((), (), s32[]{:S(2)}) async-start(), calls=%async_computation.12 | async-start | bytes 2359296 | tf_op jit(solution)/shard_map/reduce_scatter | solution.py:371
  402.8 25.6 %collective-permute-start.43 = (bf16[128,2048]{1,0:T(8,128)(2,1)}, bf16[128,2048]{1,0:T(8,128)(2,1)}, u32[]{:S(2)}, u32[]{:S(2)}) collective-permute-start(bf16[128,2048]{1,0:T(8,128)(2,1)} %get-tuple-element.241), channel_id=1, source_target_pairs={{0,6},{1,7},{2,4},{3,5},{4,2},{5,3},{6,0},{7,1},{8,14},{9,15},{10,... | collective-permute-start | bytes 1572872 | tf_op jit(solution)/shard_map/ppermute | solution.py:321
  405.8 22.0 %collective-permute-start.42 = (bf16[256,768]{1,0:T(8,128)(2,1)}, bf16[256,768]{1,0:T(8,128)(2,1)}, u32[]{:S(2)}, u32[]{:S(2)}) collective-permute-start(bf16[256,768]{1,0:T(8,128)(2,1)} %get-tuple-element.327), channel_id=1, source_target_pairs={{0,8},{8,0},{16,24},{24,16},{1,9},{9,1},{17,25},{25,17},{2,10},{10... | collective-permute-start | bytes 1179656 | tf_op jit(solution)/shard_map/ppermute | solution.py:321
  406.4 21.4 %collective-permute-start.41 = (bf16[256,768]{1,0:T(8,128)(2,1)}, bf16[256,768]{1,0:T(8,128)(2,1)}, u32[]{:S(2)}, u32[]{:S(2)}) collective-permute-start(bf16[256,768]{1,0:T(8,128)(2,1)} %get-tuple-element.328), channel_id=1, source_target_pairs={{0,16},{8,24},{16,0},{24,8},{1,17},{9,25},{17,1},{25,9},{2,18},{10... | collective-permute-start | bytes 1179656 | tf_op jit(solution)/shard_map/ppermute | solution.py:321
  429.8 33.0 %collective-permute-start.45 = (bf16[512,768]{1,0:T(8,128)(2,1)S(1)}, bf16[512,768]{1,0:T(8,128)(2,1)}, u32[]{:S(2)}, u32[]{:S(2)}) collective-permute-start(bf16[512,768]{1,0:T(8,128)(2,1)S(1)} %pad_maximum_fusion.4), channel_id=1, source_target_pairs={{0,16},{8,24},{16,0},{24,8},{1,17},{9,25},{17,1},{25,9},{2,18},{10... | collective-permute-start | bytes 2359304 | tf_op jit(solution)/shard_map/ppermute | solution.py:321
  432.6 30.2 %collective-permute-start.44 = (bf16[512,768]{1,0:T(8,128)(2,1)}, bf16[512,768]{1,0:T(8,128)(2,1)}, u32[]{:S(2)}, u32[]{:S(2)}) collective-permute-start(bf16[512,768]{1,0:T(8,128)(2,1)} %pad_maximum_fusion.3), channel_id=1, source_target_pairs={{0,8},{8,0},{16,24},{24,16},{1,9},{9,1},{17,25},{25,17},{2,10},{10... | collective-permute-start | bytes 2359304 | tf_op jit(solution)/shard_map/ppermute | solution.py:321
  437.7 22.6 %all-to-all-start.1 = ((f32[32,1,512]{2,1,0:T(1,128)}), f32[32,1,512]{2,1,0:T(1,128)S(1)}, u32[]{:S(2)}, u32[]{:S(2)}) async-start(f32[32,1,512]{2,1,0:T(1,128)} %reshape.274), calls=%async_computation.4 | async-start | bytes 131072 | tf_op jit(solution)/shard_map/all_to_all | solution.py:633
  465.3 32.5 %all-to-all-start.2 = ((bf16[8,64,768]{2,1,0:T(8,128)(2,1)}), bf16[8,64,768]{2,1,0:T(8,128)(2,1)S(1)}, u32[]{:S(2)}, u32[]{:S(2)}) async-start(bf16[8,64,768]{2,1,0:T(8,128)(2,1)} %bitcast.130), calls=%async_computation.5 | async-start | bytes 1572864 | tf_op jit(solution)/shard_map/all_to_all | solution.py:643
  (92 other events, 1024.4 us)
Sparse Core Ops, SparseCore 0:
  20.6 58.2 all-gather.8
  143.6 48.3 reduce-scatter.4
  197.0 46.3 all-gather.4
  263.9 48.7 reduce-scatter.6
  316.9 47.9 all-gather.6
  401.0 46.1 reduce-scatter.8
  449.5 42.7 reduce-scatter.10

commit v5 on v4

--- a/solution.py
+++ b/solution.py
@@ -254,6 +254,40 @@
     )(weight, riders)
 
 
+SMALL_COST = pl.CostEstimate(flops=1, bytes_accessed=1, transcendentals=1)
+
+
+def norm_sums_kernel(values_ref, terms_ref, lang_ref, gain_ref, out_ref):
+    @pl.when(pl.program_id(0) == 0)
+    def clear():
+        out_ref[...] = jnp.zeros_like(out_ref)
+
+    values = values_ref[...].astype(jnp.float32) + lang_ref[...]
+    terms = terms_ref[...].astype(jnp.float32)
+    unused, scaled, inverse = norm_forward(values, 1.0, 0.0)
+    grad_values, gain_sum, bias_sum = norm_backward(terms, scaled, inverse, gain_ref[...])
+    out_ref[0:1] += gain_sum[None]
+    out_ref[1:2] += bias_sum[None]
+    out_ref[2:3] += jnp.sum(grad_values, axis=0, keepdims=True)
+
+
+def norm_sums(values, terms, lang_row, gain):
+    length, width = values.shape
+    block = min(256, length)
+    rows = pl.BlockSpec((block, width), lambda i: (i, 0))
+    whole = pl.BlockSpec((1, width), lambda i: (0, 0))
+    return pl.pallas_call(
+        norm_sums_kernel,
+        grid=(length // block,),
+        in_specs=[rows, rows, whole, whole],
+        out_specs=pl.BlockSpec((8, width), lambda i: (0, 0)),
+        out_shape=jax.ShapeDtypeStruct((8, width), jnp.float32),
+        compiler_params=pltpu.CompilerParams(vmem_limit_bytes=VMEM_BYTES),
+        cost_estimate=SMALL_COST,
+        name="norm_sums",
+    )(values, terms, lang_row, gain[None])
+
+
 def rotation_tables(cosines, sines, lanes):
     length = cosines.shape[0]
     rest = jnp.ones((length, HEAD - ROT), jnp.float32)
@@ -283,7 +317,7 @@
         ),
         scratch_shapes=[pltpu.VMEM((lanes, length), jnp.bfloat16)],
         compiler_params=pltpu.CompilerParams(vmem_limit_bytes=VMEM_BYTES),
-        cost_estimate=pl.CostEstimate(flops=1, bytes_accessed=1, transcendentals=1),
+        cost_estimate=SMALL_COST,
         name="attention_forward",
     )(projected, *tables, first)
 
@@ -301,7 +335,7 @@
             pltpu.VMEM((length, lanes), jnp.float32),
         ],
         compiler_params=pltpu.CompilerParams(vmem_limit_bytes=VMEM_BYTES),
-        cost_estimate=pl.CostEstimate(flops=1, bytes_accessed=1, transcendentals=1),
+        cost_estimate=SMALL_COST,
         name="attention_backward",
     )(queries, key_heads, projected, grad_context, logsum, *tables, first)
 
@@ -323,6 +357,10 @@
 
 def gather_dp(piece):
     return [piece] + [permute(piece, "dp", k) for k in range(1, lax.axis_size("dp"))]
+
+
+def scatter_dp(pieces):
+    return total([pieces[0]] + [permute(pieces[k], "dp", k) for k in range(1, len(pieces))])
 
 
 def near_dp(piece):
@@ -449,7 +487,6 @@
             mlp_norm_gain[None],
             mlp_norm_bias[None],
             qkv_bias,
-            jnp.broadcast_to(language.astype(jnp.bfloat16)[:, None], (1, own)),
         ],
         axis=0,
     )
@@ -475,10 +512,9 @@
     spread = place(gather_dp(part[:, own:].reshape(groups, -1)), at_dp)
     qkv_pieces = near_dp(part[:, :own].reshape(groups * own, 3 * local_width))
     input_all, spread, grad_far = phase((input_all, spread, grad_out))
-    grad_pieces = [grad_out] + [permute(grad_far, "seq", 2 * k) for k in range(1, chips)]
+    grad_pieces = [permute(grad_far, "seq", 2 * k) for k in range(2, chips)]
     spread = spread[:, : small.size].reshape((devices,) + small.shape)
     table = jnp.swapaxes(spread, 0, 1).reshape(small.shape[0], D).astype(jnp.float32)
-    languages = spread[:, LANGS + 7, 0].astype(jnp.int32)
     gain_attn = table[LANGS]
     bias_attn = table[LANGS + 1]
     gain_mlp = table[LANGS + 2]
@@ -496,13 +532,10 @@
     ].astype(jnp.bfloat16)
     qkv_pieces, tables, first, resid_in = phase((qkv_pieces, tables, first, resid_in))
     head_qkv = place(qkv_pieces + [corner_dp(qkv_pieces)], at_dp)
-    head_qkv, normed_all, out_rows, gate_rows = phase(
-        (head_qkv, normed_all, out_weight, gate_weight.T)
-    )
+    head_qkv, normed_all, out_rows = phase((head_qkv, normed_all, out_weight))
     if not whole_heads:
         out_rows = lax.ppermute(out_rows, ("dp", "seq"), back)
     head_out = place(gather_dp(out_rows), at_dp)
-    gate_pieces = near_dp(gate_rows)
     projected = (
         jnp.dot(normed_all, head_qkv, preferred_element_type=jnp.float32) + bias_qkv
     ).astype(jnp.bfloat16)
@@ -510,23 +543,28 @@
     out_terms = jnp.dot(context_all, head_out, preferred_element_type=jnp.float32).astype(
         jnp.bfloat16
     )
-    out_terms, grad_pieces, gate_pieces, up_rows = phase(
-        (out_terms, grad_pieces, gate_pieces, up_weight.T)
+    out_terms, grad_pieces, gate_rows, grad_near = phase(
+        (out_terms, grad_pieces, gate_weight.T, grad_out)
     )
     attn_out = scatter_seq(out_terms)
+    gate_pieces = near_dp(gate_rows)
+    near = permute(grad_near, "seq", 2)
+    gate_pieces, near, up_rows = phase((gate_pieces, near, up_weight.T))
+    grad_pieces = [grad_out, near, *grad_pieces]
     gate_pieces = gate_pieces + [corner_dp(gate_pieces)]
     up_pieces = near_dp(up_rows)
     mates = permute(jnp.concatenate(grad_pieces, axis=0), "seq", 1)
-    gate_pieces, up_pieces, mates = phase((gate_pieces, up_pieces, mates))
-    up_pieces = up_pieces + [corner_dp(up_pieces)]
     mates = jnp.split(mates, chips, axis=0)
     grad_all = place([piece for pair in zip(grad_pieces, mates) for piece in pair], at_seq)
-    attn_out, up_pieces, grad_all, down_rows = phase((attn_out, up_pieces, grad_all, down_weight))
+    attn_out, gate_pieces, up_pieces, grad_all, down_rows = phase(
+        (attn_out, gate_pieces, up_pieces, grad_all, down_weight)
+    )
     resid_mid = resid_in + attn_out
     normed_mlp, scaled_mlp, inverse_mlp = norm_forward(resid_mid, gain_mlp, bias_mlp)
     rows_all = gather_seq(normed_mlp.astype(jnp.bfloat16))
+    up_pieces = up_pieces + [corner_dp(up_pieces)]
     down_pieces = near_dp(down_rows)
-    down_pieces = phase(down_pieces)
+    down_pieces, up_pieces = phase((down_pieces, up_pieces))
     cols_down = jnp.concatenate(down_pieces + [corner_dp(down_pieces)], axis=0)
     cols_gate = jnp.concatenate(gate_pieces, axis=0)
     cols_up = jnp.concatenate(up_pieces, axis=0)
@@ -588,6 +626,8 @@
     )
     out_up = total([up_terms[0], *up_near])
     mlp_sums = mlp_sums + [permute(mlp_pieces[k], "seq", 2 * k) for k in range(2, chips - 1)]
+    middle = tokens // 2
+    mlp_half = permute(mlp_pieces[-1][:middle], "seq", 2 * (chips - 1))
     down_near = [permute(down_terms[1], "dp", 1), permute(down_terms[2], "dp", 2)]
     grad_heads = contract(branch_all, head_out, 1, 1).astype(jnp.bfloat16)
     grad_stack = attention_backward(
@@ -597,51 +637,20 @@
     slice_terms = contract(normed_all, grad_stack, 0, 0).astype(jnp.bfloat16)
     attn_terms = contract(grad_stack, head_qkv, 1, 1).astype(jnp.bfloat16)
     slice_pieces = dp_terms(slice_terms)
-    attn_terms, slice_pieces, grad_stack, branch_all, mlp_sums, mlp_pieces, input_all = phase(
-        (attn_terms, slice_pieces, grad_stack, branch_all, mlp_sums, mlp_pieces, input_all)
-    )
-    mlp_sums = mlp_sums + [permute(mlp_pieces[-1], "seq", 2 * (chips - 1))]
-    out_down = total([down_terms[0], *down_near])
-    half = D // 2
-    attn_first = scatter_seq(attn_terms[:, :half])
-    attn_second = scatter_seq(attn_terms[:, half:])
-    slice_corner = send_corner(slice_pieces)
-    unused, scaled_all, inverse_all = norm_forward(
-        input_all.astype(jnp.float32) + lang_row, gain_attn, bias_attn
-    )
-    grad_in_terms, grad_gain_attn, grad_bias_attn = norm_backward(
-        attn_terms.astype(jnp.float32), scaled_all, inverse_all, gain_attn
-    )
-    grad_input_sum = jnp.sum(grad_mid, axis=0) + jnp.sum(grad_in_terms, axis=0)
-    grad_bias_qkv = jnp.sum(grad_stack.astype(jnp.float32), axis=0).reshape(3, local_width)
-    terms = jnp.concatenate(
-        [
-            grad_gain_attn[None],
-            grad_bias_attn[None],
-            grad_gain_mlp[None],
-            grad_bias_mlp[None],
-            grad_input_sum[None],
-            from_heads(grad_bias_qkv),
-        ],
-        axis=0,
-    )
-    head_out_terms = dp_terms(contract(context_all, branch_all, 0, 0).astype(jnp.bfloat16))
-    terms, head_out_terms, slice_corner, slice_pieces, mlp_sums = phase(
-        (terms, head_out_terms, slice_corner, slice_pieces, mlp_sums)
-    )
-    slice_near = send_near(slice_pieces, slice_corner)
-    arrived = lax.all_to_all(
-        terms.reshape(terms.shape[0], devices, own).swapaxes(0, 1),
-        ("dp", "seq"),
-        split_axis=0,
-        concat_axis=0,
-        tiled=True,
-    )
-    attn_first, arrived, slice_near, head_out_terms = phase(
-        (attn_first, arrived, slice_near, head_out_terms)
-    )
+    attn_terms, slice_pieces, grad_stack, branch_all, mlp_sums, mlp_half, mlp_pieces = phase(
+        (attn_terms, slice_pieces, grad_stack, branch_all, mlp_sums, mlp_half, mlp_pieces)
+    )
+    grad_normed_attn = scatter_seq(attn_terms)
+    slice_arrived = [permute(slice_pieces[k], "dp", k) for k in range(1, rows)]
+    mlp_last = permute(mlp_pieces[-1][middle:], "seq", 2 * (chips - 1))
+    sums = norm_sums(input_all, attn_terms, lang_row, gain_attn)
+    sums, slice_arrived, mlp_sums, mlp_last, down_near, grad_stack, branch_all = phase(
+        (sums, slice_arrived, mlp_sums, mlp_last, down_near, grad_stack, branch_all)
+    )
+    out_pieces = dp_terms(contract(context_all, branch_all, 0, 0).astype(jnp.bfloat16))
+    out_arrived = [permute(out_pieces[k], "dp", k) for k in range(1, rows)]
     home = lax.all_to_all(
-        total([slice_pieces[0], *slice_near])
+        total([slice_pieces[0], *slice_arrived])
         .astype(jnp.bfloat16)
         .reshape(groups, own, 3 * local_width),
         "seq",
@@ -649,9 +658,32 @@
         concat_axis=0,
         tiled=True,
     )
-    out_arrived = [permute(head_out_terms[k], "dp", k) for k in range(1, rows)]
-    home, out_arrived, attn_second = phase((home, out_arrived, attn_second))
-    grad_normed_attn = jnp.concatenate([attn_first, attn_second], axis=1)
+    grad_bias_qkv = jnp.sum(grad_stack.astype(jnp.float32), axis=0).reshape(3, local_width)
+    terms = jnp.concatenate(
+        [
+            sums[:2],
+            grad_gain_mlp[None],
+            grad_bias_mlp[None],
+            from_heads(grad_bias_qkv),
+            chooser[:, None] * (jnp.sum(grad_mid, axis=0) + sums[2])[None],
+        ],
+        axis=0,
+    )
+    count = terms.shape[0]
+
+    def sum_small(values, axis, index):
+        parts = [
+            lax.dynamic_index_in_dim(values, index ^ k, 0, keepdims=False)
+            for k in range(values.shape[0])
+        ]
+        return total([parts[0]] + [permute(parts[k], axis, k) for k in range(1, len(parts))])
+
+    terms = terms.reshape(count, rows, groups, own).transpose(1, 2, 0, 3)
+    terms, out_arrived = phase((sum_small(terms, "dp", at_dp), out_arrived))
+    summed = sum_small(terms, "seq", at_seq)
+    home, grad_normed_attn, out_arrived = phase((home, grad_normed_attn, out_arrived))
+    out_proj = total([out_pieces[0], *out_arrived])
+    out_down = total([down_terms[0], *down_near])
     if whole_heads and rows % 2 == 0:
         grad_qkv_out = columns_in_place([home], rows)
     else:
@@ -661,27 +693,22 @@
             .reshape(own, 3 * D)
             .astype(jnp.float32)
         )
-    out_proj = total([head_out_terms[0]] + out_arrived)
     if not whole_heads:
         out_proj = lax.ppermute(out_proj, ("dp", "seq"), owner)
-    mlp_out = total([mlp_pieces[0]] + mlp_sums)
+    mlp_last = jnp.concatenate([mlp_half, mlp_last], axis=0)
+    mlp_out = total([mlp_pieces[0], *mlp_sums, mlp_last])
     layer_output = (resid_mid + mlp_out).astype(jnp.bfloat16)
     grad_input = grad_mid + norm_backward(
         grad_normed_attn, scaled_attn, inverse_attn, gain_attn
     )[0]
-    summed = jnp.sum(arrived, axis=0)
-    members = (languages[:, None] == jnp.arange(LANGS, dtype=jnp.int32)[None, :]).astype(
-        jnp.float32
-    )
-    lang_g = jnp.sum(members[:, :, None] * arrived[:, 4][:, None, :], axis=0)
     return (
         layer_output[None],
         grad_input[None],
-        lang_g,
+        summed[7:],
         summed[0],
         summed[1],
         grad_qkv_out,
-        summed[5:8],
+        summed[4:7],
         out_proj,
         summed[2],
         summed[3],

time: 519 us -> 503 us (0.969)
  other arithmetic: 79.3 us -> 58.8 us
  local copies, waits for them, and re-layouts: 71.5 us -> 61.6 us
  Pallas kernels: 23.6 us -> 32 us
    ppermute x49 -> x59, waiting for transfers between devices: 68.4 us -> 97.9 us  [permute(): return lax.ppermute(value, axis, [(i, i ^ offset) for i in range(size)])]
    ppermute x49 -> x59, starting transfers between devices: 56.7 us -> 70.1 us  [permute(): return lax.ppermute(value, axis, [(i, i ^ offset) for i in range(size)])]
    all_to_all x2 -> x1, starting transfers between devices: 19.7 us -> 6.85 us  [per_device(): lax.all_to_all(total([slice_pieces[0], *slice_arrived]).astype(jnp.bfloat...]
    reduce_scatter x4 -> x3, waiting for transfers between devices: 28.3 us -> 17.9 us  [scatter_seq(): lax.psum_scatter(terms.astype(jnp.bfloat16), 'seq', scatter_dimension=0,...]
    all_gather x3, waiting for transfers between devices: 26.8 us -> 17.4 us  [gather_seq(): return lax.all_gather(piece, 'seq', axis=0, tiled=True)]
    pallas_call x0 -> x1, Pallas kernels: none -> 8.26 us  [norm_sums(): pl.pallas_call(norm_sums_kernel, grid=(length // block,), in_specs=[rows,...]
    all_to_all x2 -> x1, waiting for transfers between devices: 7.98 us -> 0.01 us  [per_device(): lax.all_to_all(total([slice_pieces[0], *slice_arrived]).astype(jnp.bfloat...]
    reduce_sum x4 -> x1, other arithmetic: 8.34 us -> 1.61 us  [per_device(): jnp.sum(grad_mid, axis=0) + sums[2]]
  transfers between devices with their start and end apart: 59 -> 67, of which waited for: 25 -> 26; matrix products, arithmetic and copies ran while one was open for 34% -> 30% of each run, Pallas kernels for 4% -> 6%
where the time goes in v5:
time: 503 us; the launch traced here: 495 us
  waiting for transfers between devices  171 us (34%)
  starting transfers between devices  83.9 us (17%)
  matrix products  71.5 us (14%)
  local copies, waits for them, and re-layouts  61.6 us (12%)
  other arithmetic  58.8 us (12%)
  Pallas kernels  32 us (6%)
  between operations  16.8 us (3%)
    ppermute x59, waiting for transfers between devices, permute(): return lax.ppermute(value, axis, [(i, i ^ offset) for i in range(size)])  97.9 us
    ppermute x59, starting transfers between devices, permute(): return lax.ppermute(value, axis, [(i, i ^ offset) for i in range(size)])  70.1 us
    dot_general x13, matrix products, contract(): lax.dot_general(left, right, (((left_dim,), (right_dim,)), ((), ())), pre...  64.3 us
    all_to_all x1, waiting for transfers between devices, per_device(): part = lax.all_to_all(dealt, 'seq', split_axis=0, concat_axis=0, tiled=True)  36.7 us
    reduce_scatter x3, waiting for transfers between devices, scatter_seq(): lax.psum_scatter(terms.astype(jnp.bfloat16), 'seq', scatter_dimension=0,...  17.9 us
    all_gather x3, waiting for transfers between devices, gather_seq(): return lax.all_gather(piece, 'seq', axis=0, tiled=True)  17.4 us
    dynamic_update_slice x19, local copies, waits for them, and re-layouts, place(): lax.dynamic_update_slice_in_dim(result, piece, (index ^ k) * block, 0)  14.6 us
    unnamed x129, local copies, waits for them, and re-layouts  14.2 us
  transfers between devices with their start and end apart: 67, of which 26 were waited for; matrix products, arithmetic and copies ran while one was open for 30% of the time, Pallas kernels for 6%

profile of v5, /device:TPU:0, one launch (start us, length us, event | category | flops | bytes accessed | tf_op | source)
XLA Modules:
  0.0 495.2 jit_solution(14696214771967467751)
XLA Ops:
  11.2 6.3 %all-to-all-start = ((bf16[8,80,768]{2,1,0:T(8,128)(2,1)}), bf16[8,80,768]{2,1,0:T(8,128)(2,1)S(1)}, u32[]{:S(2)}, u32[]{:S(2)}) async-start(bf16[8,80,768]{2,1,0:T(8,128)(2,1)} %deal_columns.1), calls=%async_computation | async-start | bytes 1966080 | tf_op jit(solution)/shard_map/all_to_all | solution.py:509
  20.7 36.7 %all-to-all-done = bf16[8,80,768]{2,1,0:T(8,128)(2,1)S(1)} async-done(((bf16[8,80,768]{2,1,0:T(8,128)(2,1)}), bf16[8,80,768]{2,1,0:T(8,128)(2,1)S(1)}, u32[]{:S(2)}, u32[]{:S(2)}) %all-to-all-start) | async-done | bytes 983072 | tf_op jit(solution)/shard_map/all_to_all | solution.py:509
  70.5 7.7 %all-gather.9.cloned.1.call-done = bf16[1,1024,2048]{2,1,0:T(8,128)(2,1)} async-done(((bf16[1,128,2048]{2,1,0:T(8,128)(2,1)}), bf16[1,1024,2048]{2,1,0:T(8,128)(2,1)}) %all-gather.9.cloned.1.call-update) | async-done | bytes 4194320 | tf_op jit(solution)/shard_map/all_gather | solution.py:405
  97.5 4.1 add_convert_fusion.1
  111.1 3.4 add_convert_fusion.2.qkv_ref
  114.6 9.8 %attention_forward.1 = (bf16[1024,256]{1,0:T(8,128)(2,1)S(1)}, bf16[1024,256]{1,0:T(8,128)(2,1)S(1)}, bf16[1024,256]{1,0:T(8,128)(2,1)S(1)}, f32[4,1024]{1,0:T(4,128)S(1)}) custom-call(bf16[1024,768]{1,0:T(8,128)(2,1)S(1)} %add_convert_fusion.2.qkv_ref, f32[1024,128]{1,0:T(8,128)S(1)} %copy.52.cos_ref, f32[1024,128]{1,0:T(8,128)S(1)} %copy.53.former_ref, ...), custom_call_target="tpu_custom_call" | custom-call | flops 1 | bytes 1 | tf_op jit(solution)/shard_map/attention_forward/pallas_call | solution.py:310
  126.4 3.8 convolution_convert_fusion.1
  134.3 20.0 %collective-permute-done.14 = bf16[128,2048]{1,0:T(8,128)(2,1)S(1)} collective-permute-done((bf16[128,2048]{1,0:T(8,128)(2,1)}, bf16[128,2048]{1,0:T(8,128)(2,1)S(1)}, u32[]{:S(2)}, u32[]{:S(2)}) %collective-permute-start.14) | collective-permute-done | bytes 524320 | tf_op jit(solution)/shard_map/ppermute | solution.py:355
  199.1 16.1 %collective-permute-done.22 = bf16[88,2048]{1,0:T(8,128)(2,1)S(1)} collective-permute-done((bf16[88,2048]{1,0:T(8,128)(2,1)S(1)}, bf16[88,2048]{1,0:T(8,128)(2,1)S(1)}, u32[]{:S(2)}, u32[]{:S(2)}) %collective-permute-start.22) | collective-permute-done | bytes 360480 | tf_op jit(solution)/shard_map/ppermute | solution.py:355
  227.3 6.9 %fusion.32 = f32[1024,704]{0,1:T(8,128)} fusion(bf16[1024,2048]{1,0:T(8,128)(2,1)} %slice_dynamic-update-slice_fusion, bf16[704,2048]{1,0:T(8,128)(2,1)S(1)} %constant_dynamic-update-slice_fusion.16), kind=kOutput, calls=%fused_computation.174 | convolution fusion | flops 2952790016 | bytes 9961472 | tf_op jit(solution)/shard_map/dot_general | solution.py:21
  235.2 6.0 %fusion.33 = f32[1024,704]{0,1:T(8,128)S(1)} fusion(bf16[1024,2048]{1,0:T(8,128)(2,1)} %all-gather.5.cloned.1.call-done, bf16[704,2048]{1,0:T(8,128)(2,1)} %pad_maximum_fusion), kind=kOutput, calls=%fused_computation.175 | convolution fusion | flops 2952790016 | bytes 9961472 | tf_op jit(solution)/shard_map/dot_general | solution.py:21
  241.2 5.4 %multiply_convert_fusion = (bf16[1024,704]{0,1:T(8,128)(2,1)}, bf16[1024,704]{0,1:T(8,128)(2,1)S(1)}, bf16[1024,704]{0,1:T(8,128)(2,1)S(1)}) fusion(f32[1024,704]{0,1:T(8,128)S(1)} %fusion.33, f32[1024,704]{0,1:T(8,128)S(1)} %copy-done.57, bf16[1024,2048]{1,0:T(8,128)(2,1)S(1)} %copy-done.52, bf16[704,2048]{1,0:T(8,128)(2,1)S(1)} %copy-done.25), kind=kOutput, calls=%fused_computation.19 | convolution fusion | flops 2963603456 | bytes 17170432 | tf_op jit(solution)/shard_map/dot_general | solution.py:21
  246.6 3.5 fusion.34
  250.2 5.1 %add_convert_fusion = bf16[1024,2048]{1,0:T(8,128)(2,1)} fusion(f32[1024,2048]{1,0:T(8,128)S(1)} %fusion.34, bf16[1024,704]{0,1:T(8,128)(2,1)S(1)} %get-tuple-element.187, bf16[704,2048]{1,0:T(8,128)(2,1)S(1)} %copy-done.24), kind=kOutput, calls=%fused_computation | convolution fusion | flops 2956984320 | bytes 16908288 | tf_op jit(solution)/shard_map/dot_general | solution.py:21
  255.5 5.8 %convolution_convert_fusion = bf16[1024,2048]{1,0:T(8,128)(2,1)S(1)} fusion(bf16[1024,704]{0,1:T(8,128)(2,1)} %get-tuple-element.188, bf16[704,2048]{1,0:T(8,128)(2,1)} %copy-done.45), kind=kOutput, calls=%fused_computation.8 | convolution fusion | flops 2954887168 | bytes 8519680 | tf_op jit(solution)/shard_map/dot_general | solution.py:21
  263.6 3.4 convolution_convert_fusion.6
  270.1 6.7 %convolution_convert_fusion.4 = bf16[704,2048]{1,0:T(8,128)(2,1)} fusion(bf16[1024,704]{0,1:T(8,128)(2,1)S(1)} %copy-done.60, bf16[1024,2048]{1,0:T(8,128)(2,1)} %slice_dynamic-update-slice_fusion), kind=kOutput, calls=%fused_computation.12 | convolution fusion | flops 2954231808 | bytes 8519680 | tf_op jit(solution)/shard_map/dot_general | solution.py:21
  276.8 4.5 convolution_convert_fusion.5
  287.6 17.4 %reduce-scatter.6.cloned.1.call-done = bf16[128,2048]{1,0:T(8,128)(2,1)} async-done(((bf16[1024,2048]{1,0:T(8,128)(2,1)}), bf16[128,2048]{1,0:T(8,128)(2,1)}) %reduce-scatter.6.cloned.1.call-update) | async-done | bytes 524304 | tf_op jit(solution)/shard_map/reduce_scatter | solution.py:409
  326.1 6.6 %collective-permute-done.37 = bf16[88,2048]{1,0:T(8,128)(2,1)S(1)} collective-permute-done((bf16[88,2048]{1,0:T(8,128)(2,1)S(1)}, bf16[88,2048]{1,0:T(8,128)(2,1)S(1)}, u32[]{:S(2)}, u32[]{:S(2)}) %collective-permute-start.37) | collective-permute-done | bytes 360480 | tf_op jit(solution)/shard_map/ppermute | solution.py:355
  336.6 15.5 %collective-permute-done.35 = bf16[128,2048]{1,0:T(8,128)(2,1)S(1)} collective-permute-done((bf16[128,2048]{1,0:T(8,128)(2,1)}, bf16[128,2048]{1,0:T(8,128)(2,1)S(1)}, u32[]{:S(2)}, u32[]{:S(2)}) %collective-permute-start.35) | collective-permute-done | bytes 524320 | tf_op jit(solution)/shard_map/ppermute | solution.py:355
  352.9 8.7 %all-gather.7.cloned.1.call-done = bf16[1024,2048]{1,0:T(8,128)(2,1)} async-done(((bf16[128,2048]{1,0:T(8,128)(2,1)}), bf16[1024,2048]{1,0:T(8,128)(2,1)}) %all-gather.7.cloned.1.call-update) | async-done | bytes 4194320 | tf_op jit(solution)/shard_map/all_gather | solution.py:405
  367.7 3.5 convolution_convert_fusion.8.context_grad_ref
  371.2 11.2 %attention_backward.1 = bf16[1024,768]{1,0:T(8,128)(2,1)S(1)} custom-call(bf16[1024,256]{1,0:T(8,128)(2,1)S(1)} %copy-done.7, bf16[1024,256]{1,0:T(8,128)(2,1)S(1)} %copy-done.9, bf16[1024,768]{1,0:T(8,128)(2,1)} %copy-done.2, bf16[1024,256]{1,0:T(8,128)(2,1)S(1)} %convolution_convert_fusion.8.context_grad_ref, f32[4,1024]{1,0:T(4,128)S(1)} %get-tuple-element.214.logsum_ref, ...), custom_call_target="tpu_custom_call" | custom-call | flops 1 | bytes 1 | tf_op jit(solution)/shard_map/attention_backward/pallas_call | solution.py:328
  382.5 5.0 %convolution_convert_fusion.3 = bf16[2048,768]{1,0:T(8,128)(2,1)} fusion(bf16[1024,2048]{1,0:T(8,128)(2,1)S(1)} %copy-done.18, bf16[1024,768]{1,0:T(8,128)(2,1)S(1)} %attention_backward.1), kind=kOutput, calls=%fused_computation.11 | convolution fusion | flops 3222798336 | bytes 8912896 | tf_op jit(solution)/shard_map/dot_general | solution.py:21
  387.5 5.1 %convolution_convert_fusion.2.terms_ref = bf16[1024,2048]{1,0:T(8,128)(2,1)} fusion(bf16[1024,768]{1,0:T(8,128)(2,1)S(1)} %attention_backward.1, bf16[2048,768]{1,0:T(8,128)(2,1)S(1)} %copy-done.22), kind=kOutput, calls=%fused_computation.10 | convolution fusion | flops 3223322624 | bytes 8912896 | tf_op jit(solution)/shard_map/dot_general | solution.py:21
  392.6 3.3 constant_dynamic-slice_fusion.11
  411.4 8.3 %norm_sums.1 = f32[8,2048]{1,0:T(8,128)S(1)} custom-call(bf16[1024,2048]{1,0:T(8,128)(2,1)S(1)} %bitcast.157, bf16[1024,2048]{1,0:T(8,128)(2,1)} %convolution_convert_fusion.2.terms_ref, f32[1,2048]{1,0:T(1,128)S(1)} %bitcast.158, f32[1,2048]{1,0:T(1,128)S(1)} %slice.186.gain_ref), custom_call_target="tpu_custom_call" | custom-call | flops 1 | bytes 1 | tf_op jit(solution)/shard_map/norm_sums/pallas_call | solution.py:279
  419.7 13.7 %collective-permute-done.43 = bf16[512,768]{1,0:T(8,128)(2,1)} collective-permute-done((bf16[512,768]{1,0:T(8,128)(2,1)}, bf16[512,768]{1,0:T(8,128)(2,1)}, u32[]{:S(2)}, u32[]{:S(2)}) %collective-permute-start.43) | collective-permute-done | bytes 786464 | tf_op jit(solution)/shard_map/ppermute | solution.py:355
  436.3 3.5 convolution_convert_fusion.7
  449.6 6.8 %all-to-all-start.1 = ((bf16[8,64,768]{2,1,0:T(8,128)(2,1)}), bf16[8,64,768]{2,1,0:T(8,128)(2,1)S(1)}, u32[]{:S(2)}, u32[]{:S(2)}) async-start(bf16[8,64,768]{2,1,0:T(8,128)(2,1)} %bitcast.30), calls=%async_computation.3 | async-start | bytes 1572864 | tf_op jit(solution)/shard_map/all_to_all | solution.py:652
  463.3 3.3 collective-permute-start.55
  (418 shorter events, 211.4 us)
Async XLA Ops:
  11.2 46.2 %all-to-all-start = ((bf16[8,80,768]{2,1,0:T(8,128)(2,1)}), bf16[8,80,768]{2,1,0:T(8,128)(2,1)S(1)}, u32[]{:S(2)}, u32[]{:S(2)}) async-start(bf16[8,80,768]{2,1,0:T(8,128)(2,1)} %deal_columns.1), calls=%async_computation | async-start | bytes 1966080 | tf_op jit(solution)/shard_map/all_to_all | solution.py:509
  17.5 60.7 %all-gather.9.cloned.1.call-start = ((), (), s32[]{:S(2)}) async-start(), calls=%async_computation.10 | async-start | bytes 4718592 | tf_op jit(solution)/shard_map/all_gather | solution.py:405
  18.3 166.8 %reduce-scatter.4.cloned.1.call-start = ((), (), s32[]{:S(2)}) async-start(), calls=%async_computation.5 | async-start | bytes 4718592 | tf_op jit(solution)/shard_map/reduce_scatter | solution.py:409
  61.1 27.2 %collective-permute-start = (bf16[512,768]{1,0:T(8,128)(2,1)S(1)}, bf16[512,768]{1,0:T(8,128)(2,1)S(1)}, u32[]{:S(2)}, u32[]{:S(2)}) collective-permute-start(bf16[512,768]{1,0:T(8,128)(2,1)S(1)} %bitcast.163), channel_id=1, source_target_pairs={{0,8},{8,0},{16,24},{24,16},{1,9},{9,1},{17,25},{25,17},{2,10},{10... | collective-permute-start | bytes 2359304 | tf_op jit(solution)/shard_map/ppermute | solution.py:355
  62.6 25.7 %collective-permute-start.1 = (bf16[512,768]{1,0:T(8,128)(2,1)S(1)}, bf16[512,768]{1,0:T(8,128)(2,1)}, u32[]{:S(2)}, u32[]{:S(2)}) collective-permute-start(bf16[512,768]{1,0:T(8,128)(2,1)S(1)} %bitcast.164), channel_id=1, source_target_pairs={{0,16},{8,24},{16,0},{24,8},{1,17},{9,25},{17,1},{25,9},{2,18},{10... | collective-permute-start | bytes 2359304 | tf_op jit(solution)/shard_map/ppermute | solution.py:355
  79.2 51.1 %collective-permute-start.10 = (bf16[128,2048]{1,0:T(8,128)(2,1)}, bf16[128,2048]{1,0:T(8,128)(2,1)}, u32[]{:S(2)}, u32[]{:S(2)}) collective-permute-start(bf16[128,2048]{1,0:T(8,128)(2,1)} %bitcast.16), channel_id=1, source_target_pairs={{0,4},{1,5},{2,6},{3,7},{4,0},{5,1},{6,2},{7,3},{8,12},{9,13},{10,... | collective-permute-start | bytes 1572872 | tf_op jit(solution)/shard_map/ppermute | solution.py:355
  79.2 51.0 %collective-permute-start.11 = (bf16[128,2048]{1,0:T(8,128)(2,1)}, bf16[128,2048]{1,0:T(8,128)(2,1)S(1)}, u32[]{:S(2)}, u32[]{:S(2)}) collective-permute-start(bf16[128,2048]{1,0:T(8,128)(2,1)} %bitcast.16), channel_id=1, source_target_pairs={{0,6},{1,7},{2,4},{3,5},{4,2},{5,3},{6,0},{7,1},{8,14},{9,15},{10,... | collective-permute-start | bytes 1572872 | tf_op jit(solution)/shard_map/ppermute | solution.py:355
  130.3 104.9 %all-gather.5.cloned.1.call-start = ((), (), s32[]{:S(2)}) async-start(), calls=%async_computation.6 | async-start | bytes 4718592 | tf_op jit(solution)/shard_map/all_gather | solution.py:405
  130.3 23.9 %collective-permute-start.12 = (bf16[176,2048]{1,0:T(8,128)(2,1)}, bf16[176,2048]{1,0:T(8,128)(2,1)}, u32[]{:S(2)}, u32[]{:S(2)}) collective-permute-start(bf16[176,2048]{1,0:T(8,128)(2,1)} %bitcast.19), channel_id=1, source_target_pairs={{0,8},{8,0},{16,24},{24,16},{1,9},{9,1},{17,25},{25,17},{2,10},{10... | collective-permute-start | bytes 2162696 | tf_op jit(solution)/shard_map/ppermute | solution.py:355
  130.9 23.3 %collective-permute-start.13 = (bf16[176,2048]{1,0:T(8,128)(2,1)}, bf16[176,2048]{1,0:T(8,128)(2,1)}, u32[]{:S(2)}, u32[]{:S(2)}) collective-permute-start(bf16[176,2048]{1,0:T(8,128)(2,1)} %bitcast.19), channel_id=1, source_target_pairs={{0,16},{8,24},{16,0},{24,8},{1,17},{9,25},{17,1},{25,9},{2,18},{10... | collective-permute-start | bytes 2162696 | tf_op jit(solution)/shard_map/ppermute | solution.py:355
  132.4 21.8 %collective-permute-start.14 = (bf16[128,2048]{1,0:T(8,128)(2,1)}, bf16[128,2048]{1,0:T(8,128)(2,1)S(1)}, u32[]{:S(2)}, u32[]{:S(2)}) collective-permute-start(bf16[128,2048]{1,0:T(8,128)(2,1)} %bitcast.16), channel_id=1, source_target_pairs={{0,2},{1,3},{2,0},{3,1},{4,6},{5,7},{6,4},{7,5},{8,10},{9,11},{10,... | collective-permute-start | bytes 1572872 | tf_op jit(solution)/shard_map/ppermute | solution.py:355
  165.4 20.8 %collective-permute-start.17 = (bf16[176,2048]{1,0:T(8,128)(2,1)}, bf16[176,2048]{1,0:T(8,128)(2,1)}, u32[]{:S(2)}, u32[]{:S(2)}) collective-permute-start(bf16[176,2048]{1,0:T(8,128)(2,1)} %bitcast.20), channel_id=1, source_target_pairs={{0,8},{8,0},{16,24},{24,16},{1,9},{9,1},{17,25},{25,17},{2,10},{10... | collective-permute-start | bytes 2162696 | tf_op jit(solution)/shard_map/ppermute | solution.py:355
  166.0 20.9 %collective-permute-start.18 = (bf16[176,2048]{1,0:T(8,128)(2,1)}, bf16[176,2048]{1,0:T(8,128)(2,1)}, u32[]{:S(2)}, u32[]{:S(2)}) collective-permute-start(bf16[176,2048]{1,0:T(8,128)(2,1)} %bitcast.20), channel_id=1, source_target_pairs={{0,16},{8,24},{16,0},{24,8},{1,17},{9,25},{17,1},{25,9},{2,18},{10... | collective-permute-start | bytes 2162696 | tf_op jit(solution)/shard_map/ppermute | solution.py:355
  189.7 115.3 %reduce-scatter.6.cloned.1.call-start = ((), (), s32[]{:S(2)}) async-start(), calls=%async_computation.7 | async-start | bytes 4718592 | tf_op jit(solution)/shard_map/reduce_scatter | solution.py:409
  189.8 25.8 %collective-permute-start.20 = (bf16[176,2048]{1,0:T(8,128)(2,1)}, bf16[176,2048]{1,0:T(8,128)(2,1)S(1)}, u32[]{:S(2)}, u32[]{:S(2)}) collective-permute-start(bf16[176,2048]{1,0:T(8,128)(2,1)} %param.28), channel_id=1, source_target_pairs={{0,8},{8,0},{16,24},{24,16},{1,9},{9,1},{17,25},{25,17},{2,10},{10... | collective-permute-start | bytes 2162696 | tf_op jit(solution)/shard_map/ppermute | solution.py:355
  190.7 24.9 %collective-permute-start.21 = (bf16[176,2048]{1,0:T(8,128)(2,1)}, bf16[176,2048]{1,0:T(8,128)(2,1)S(1)}, u32[]{:S(2)}, u32[]{:S(2)}) collective-permute-start(bf16[176,2048]{1,0:T(8,128)(2,1)} %param.28), channel_id=1, source_target_pairs={{0,16},{8,24},{16,0},{24,8},{1,17},{9,25},{17,1},{25,9},{2,18},{10... | collective-permute-start | bytes 2162696 | tf_op jit(solution)/shard_map/ppermute | solution.py:355
  192.2 23.0 %collective-permute-start.22 = (bf16[88,2048]{1,0:T(8,128)(2,1)S(1)}, bf16[88,2048]{1,0:T(8,128)(2,1)S(1)}, u32[]{:S(2)}, u32[]{:S(2)}) collective-permute-start(bf16[88,2048]{1,0:T(8,128)(2,1)S(1)} %slice.163), channel_id=1, source_target_pairs={{0,8},{8,0},{16,24},{24,16},{1,9},{9,1},{17,25},{25,17},{2,10},{10... | collective-permute-start | bytes 1081352 | tf_op jit(solution)/shard_map/ppermute | solution.py:355
  194.2 21.3 %collective-permute-start.23 = (bf16[88,2048]{1,0:T(8,128)(2,1)S(1)}, bf16[88,2048]{1,0:T(8,128)(2,1)S(1)}, u32[]{:S(2)}, u32[]{:S(2)}) collective-permute-start(bf16[88,2048]{1,0:T(8,128)(2,1)S(1)} %slice.164), channel_id=1, source_target_pairs={{0,16},{8,24},{16,0},{24,8},{1,17},{9,25},{17,1},{25,9},{2,18},{10... | collective-permute-start | bytes 1081352 | tf_op jit(solution)/shard_map/ppermute | solution.py:355
  255.3 106.3 %all-gather.7.cloned.1.call-start = ((), (), s32[]{:S(2)}) async-start(), calls=%async_computation.8 | async-start | bytes 4718592 | tf_op jit(solution)/shard_map/all_gather | solution.py:405
  283.4 22.8 %collective-permute-start.30 = (bf16[176,2048]{1,0:T(8,128)(2,1)}, bf16[176,2048]{1,0:T(8,128)(2,1)}, u32[]{:S(2)}, u32[]{:S(2)}) collective-permute-start(bf16[176,2048]{1,0:T(8,128)(2,1)} %pad_maximum_fusion.6), channel_id=1, source_target_pairs={{0,16},{8,24},{16,0},{24,8},{1,17},{9,25},{17,1},{25,9},{2,18},{10... | collective-permute-start | bytes 2162696 | tf_op jit(solution)/shard_map/ppermute | solution.py:355
  285.0 21.2 %collective-permute-start.29 = (bf16[176,2048]{1,0:T(8,128)(2,1)}, bf16[176,2048]{1,0:T(8,128)(2,1)}, u32[]{:S(2)}, u32[]{:S(2)}) collective-permute-start(bf16[176,2048]{1,0:T(8,128)(2,1)} %pad_maximum_fusion.5), channel_id=1, source_target_pairs={{0,8},{8,0},{16,24},{24,16},{1,9},{9,1},{17,25},{25,17},{2,10},{10... | collective-permute-start | bytes 2162696 | tf_op jit(solution)/shard_map/ppermute | solution.py:355
  310.2 170.1 %reduce-scatter.8.cloned.1.call-start = ((), (), s32[]{:S(2)}) async-start(), calls=%async_computation.9 | async-start | bytes 4718592 | tf_op jit(solution)/shard_map/reduce_scatter | solution.py:409
  314.7 37.4 %collective-permute-start.35 = (bf16[128,2048]{1,0:T(8,128)(2,1)}, bf16[128,2048]{1,0:T(8,128)(2,1)S(1)}, u32[]{:S(2)}, u32[]{:S(2)}) collective-permute-start(bf16[128,2048]{1,0:T(8,128)(2,1)} %get-tuple-element.205), channel_id=1, source_target_pairs={{0,2},{1,3},{2,0},{3,1},{4,6},{5,7},{6,4},{7,5},{8,10},{9,11},{10,... | collective-permute-start | bytes 1572872 | tf_op jit(solution)/shard_map/ppermute | solution.py:355
  324.1 28.0 %collective-permute-start.34 = (bf16[176,2048]{1,0:T(8,128)(2,1)S(1)}, bf16[176,2048]{1,0:T(8,128)(2,1)}, u32[]{:S(2)}, u32[]{:S(2)}) collective-permute-start(bf16[176,2048]{1,0:T(8,128)(2,1)S(1)} %pad_maximum_fusion.8), channel_id=1, source_target_pairs={{0,16},{8,24},{16,0},{24,8},{1,17},{9,25},{17,1},{25,9},{2,18},{10... | collective-permute-start | bytes 2162696 | tf_op jit(solution)/shard_map/ppermute | solution.py:355
  325.8 27.0 %collective-permute-start.33 = (bf16[176,2048]{1,0:T(8,128)(2,1)S(1)}, bf16[176,2048]{1,0:T(8,128)(2,1)}, u32[]{:S(2)}, u32[]{:S(2)}) collective-permute-start(bf16[176,2048]{1,0:T(8,128)(2,1)S(1)} %pad_maximum_fusion.7), channel_id=1, source_target_pairs={{0,8},{8,0},{16,24},{24,16},{1,9},{9,1},{17,25},{25,17},{2,10},{10... | collective-permute-start | bytes 2162696 | tf_op jit(solution)/shard_map/ppermute | solution.py:355
  361.6 20.9 %collective-permute-start.38 = (bf16[176,2048]{1,0:T(8,128)(2,1)}, bf16[176,2048]{1,0:T(8,128)(2,1)S(1)}, u32[]{:S(2)}, u32[]{:S(2)}) collective-permute-start(bf16[176,2048]{1,0:T(8,128)(2,1)} %pad_maximum_fusion.9), channel_id=1, source_target_pairs={{0,8},{8,0},{16,24},{24,16},{1,9},{9,1},{17,25},{25,17},{2,10},{10... | collective-permute-start | bytes 2162696 | tf_op jit(solution)/shard_map/ppermute | solution.py:355
  362.7 33.2 %collective-permute-start.40 = (bf16[128,2048]{1,0:T(8,128)(2,1)}, bf16[128,2048]{1,0:T(8,128)(2,1)}, u32[]{:S(2)}, u32[]{:S(2)}) collective-permute-start(bf16[128,2048]{1,0:T(8,128)(2,1)} %get-tuple-element.219), channel_id=1, source_target_pairs={{0,4},{1,5},{2,6},{3,7},{4,0},{5,1},{6,2},{7,3},{8,12},{9,13},{10,... | collective-permute-start | bytes 1572872 | tf_op jit(solution)/shard_map/ppermute | solution.py:355
  366.2 29.7 %collective-permute-start.41 = (bf16[64,2048]{1,0:T(8,128)(2,1)}, bf16[64,2048]{1,0:T(8,128)(2,1)S(1)}, u32[]{:S(2)}, u32[]{:S(2)}) collective-permute-start(bf16[64,2048]{1,0:T(8,128)(2,1)} %slice.185), channel_id=1, source_target_pairs={{0,6},{1,7},{2,4},{3,5},{4,2},{5,3},{6,0},{7,1},{8,14},{9,15},{10,... | collective-permute-start | bytes 786440 | tf_op jit(solution)/shard_map/ppermute | solution.py:355
  396.5 23.2 %collective-permute-start.42 = (bf16[512,768]{1,0:T(8,128)(2,1)}, bf16[512,768]{1,0:T(8,128)(2,1)}, u32[]{:S(2)}, u32[]{:S(2)}) collective-permute-start(bf16[512,768]{1,0:T(8,128)(2,1)} %get-tuple-element.224), channel_id=1, source_target_pairs={{0,8},{8,0},{16,24},{24,16},{1,9},{9,1},{17,25},{25,17},{2,10},{10... | collective-permute-start | bytes 2359304 | tf_op jit(solution)/shard_map/ppermute | solution.py:355
  398.0 35.5 %collective-permute-start.43 = (bf16[512,768]{1,0:T(8,128)(2,1)}, bf16[512,768]{1,0:T(8,128)(2,1)}, u32[]{:S(2)}, u32[]{:S(2)}) collective-permute-start(bf16[512,768]{1,0:T(8,128)(2,1)} %get-tuple-element.225), channel_id=1, source_target_pairs={{0,16},{8,24},{16,0},{24,8},{1,17},{9,25},{17,1},{25,9},{2,18},{10... | collective-permute-start | bytes 2359304 | tf_op jit(solution)/shard_map/ppermute | solution.py:355
  399.5 34.0 %collective-permute-start.44 = (bf16[512,768]{1,0:T(8,128)(2,1)}, bf16[512,768]{1,0:T(8,128)(2,1)}, u32[]{:S(2)}, u32[]{:S(2)}) collective-permute-start(bf16[512,768]{1,0:T(8,128)(2,1)} %get-tuple-element.226), channel_id=1, source_target_pairs={{0,24},{8,16},{16,8},{24,0},{1,25},{9,17},{17,9},{25,1},{2,26},{10... | collective-permute-start | bytes 2359304 | tf_op jit(solution)/shard_map/ppermute | solution.py:355
  449.6 32.8 %all-to-all-start.1 = ((bf16[8,64,768]{2,1,0:T(8,128)(2,1)}), bf16[8,64,768]{2,1,0:T(8,128)(2,1)S(1)}, u32[]{:S(2)}, u32[]{:S(2)}) async-start(bf16[8,64,768]{2,1,0:T(8,128)(2,1)} %bitcast.30), calls=%async_computation.3 | async-start | bytes 1572864 | tf_op jit(solution)/shard_map/all_to_all | solution.py:652
  (96 other events, 1140.9 us)
Sparse Core Ops, SparseCore 0:
  20.0 58.2 all-gather.8
  130.4 54.6 reduce-scatter.3
  189.8 45.2 all-gather.4
  255.4 49.6 reduce-scatter.5
  310.3 51.2 all-gather.6
  396.1 58.0 reduce-scatter.7

commit v6 on v5

--- a/solution.py
+++ b/solution.py
@@ -585,29 +585,16 @@
         contract(grad_gate, rows_all, 0, 0).astype(jnp.bfloat16), rows, axis=0
     )
     gate_corner = send_corner(gate_terms)
-    mlp_terms = (
-        contract(hidden, cols_down, 1, 0).astype(jnp.bfloat16).reshape(chips, 2, tokens, D)
-    )
-    mlp_other = permute(
-        lax.dynamic_index_in_dim(mlp_terms, 1 - at_seq % 2, 1, keepdims=False), "seq", 1
-    )
+    mlp_terms = contract(hidden, cols_down, 1, 0).astype(jnp.bfloat16)
     up_terms = contract(grad_up, rows_all, 0, 0).astype(jnp.bfloat16)
-    gate_corner, gate_terms, mlp_terms, mlp_other, up_terms = phase(
-        (gate_corner, gate_terms, mlp_terms, mlp_other, up_terms)
+    gate_corner, gate_terms, mlp_terms, up_terms = phase(
+        (gate_corner, gate_terms, mlp_terms, up_terms)
     )
     gate_near = send_near(gate_terms, gate_corner)
-    mlp_pairs = total(
-        [lax.dynamic_index_in_dim(mlp_terms, at_seq % 2, 1, keepdims=False), mlp_other]
-    ).astype(jnp.bfloat16)
     down_terms = contract(hidden, grad_all, 0, 0).astype(jnp.bfloat16)
-    mlp_pieces = [
-        lax.dynamic_index_in_dim(mlp_pairs, (at_seq // 2) ^ k, 0, keepdims=False)
-        for k in range(chips)
-    ]
-    grad_normed_mlp, gate_near, up_terms, mlp_pieces, down_terms = phase(
-        (grad_normed_mlp, gate_near, up_terms, mlp_pieces, down_terms)
-    )
-    out_gate = total([gate_terms[0], *gate_near])
+    grad_normed_mlp, gate_near, up_terms, mlp_terms, down_terms = phase(
+        (grad_normed_mlp, gate_near, up_terms, mlp_terms, down_terms)
+    )
     grad_mid_norm, grad_gain_mlp, grad_bias_mlp = norm_backward(
         grad_normed_mlp, scaled_mlp, inverse_mlp, gain_mlp
     )
@@ -616,18 +603,14 @@
     up_terms = jnp.split(up_terms, rows, axis=0)
     down_terms = jnp.split(down_terms, rows, axis=0)
     up_corner = send_corner(up_terms)
-    mlp_sums = [permute(mlp_pieces[1], "seq", 2)]
     up_corner, up_terms, down_terms = phase((up_corner, up_terms, down_terms))
     up_near = send_near(up_terms, up_corner)
     down_corner = send_corner(down_terms)
     down_terms = down_terms[:1] + add_corner(down_terms, down_corner)
-    branch_all, up_near, mlp_sums, mlp_pieces, down_terms = phase(
-        (branch_all, up_near, mlp_sums, mlp_pieces, down_terms)
-    )
-    out_up = total([up_terms[0], *up_near])
-    mlp_sums = mlp_sums + [permute(mlp_pieces[k], "seq", 2 * k) for k in range(2, chips - 1)]
-    middle = tokens // 2
-    mlp_half = permute(mlp_pieces[-1][:middle], "seq", 2 * (chips - 1))
+    branch_all, up_near, mlp_terms, down_terms = phase(
+        (branch_all, up_near, mlp_terms, down_terms)
+    )
+    mlp_out = scatter_seq(mlp_terms)
     down_near = [permute(down_terms[1], "dp", 1), permute(down_terms[2], "dp", 2)]
     grad_heads = contract(branch_all, head_out, 1, 1).astype(jnp.bfloat16)
     grad_stack = attention_backward(
@@ -635,29 +618,11 @@
     )
     grad_stack, down_near = phase((grad_stack, down_near))
     slice_terms = contract(normed_all, grad_stack, 0, 0).astype(jnp.bfloat16)
+    slice_pieces = dp_terms(slice_terms)
+    grad_stack, slice_pieces = phase((grad_stack, slice_pieces))
+    slice_near = [permute(slice_pieces[k], "dp", k) for k in range(1, rows - 1)]
     attn_terms = contract(grad_stack, head_qkv, 1, 1).astype(jnp.bfloat16)
-    slice_pieces = dp_terms(slice_terms)
-    attn_terms, slice_pieces, grad_stack, branch_all, mlp_sums, mlp_half, mlp_pieces = phase(
-        (attn_terms, slice_pieces, grad_stack, branch_all, mlp_sums, mlp_half, mlp_pieces)
-    )
-    grad_normed_attn = scatter_seq(attn_terms)
-    slice_arrived = [permute(slice_pieces[k], "dp", k) for k in range(1, rows)]
-    mlp_last = permute(mlp_pieces[-1][middle:], "seq", 2 * (chips - 1))
     sums = norm_sums(input_all, attn_terms, lang_row, gain_attn)
-    sums, slice_arrived, mlp_sums, mlp_last, down_near, grad_stack, branch_all = phase(
-        (sums, slice_arrived, mlp_sums, mlp_last, down_near, grad_stack, branch_all)
-    )
-    out_pieces = dp_terms(contract(context_all, branch_all, 0, 0).astype(jnp.bfloat16))
-    out_arrived = [permute(out_pieces[k], "dp", k) for k in range(1, rows)]
-    home = lax.all_to_all(
-        total([slice_pieces[0], *slice_arrived])
-        .astype(jnp.bfloat16)
-        .reshape(groups, own, 3 * local_width),
-        "seq",
-        split_axis=0,
-        concat_axis=0,
-        tiled=True,
-    )
     grad_bias_qkv = jnp.sum(grad_stack.astype(jnp.float32), axis=0).reshape(3, local_width)
     terms = jnp.concatenate(
         [
@@ -671,18 +636,41 @@
     )
     count = terms.shape[0]
 
-    def sum_small(values, axis, index):
-        parts = [
+    def small_parts(values, index):
+        return [
             lax.dynamic_index_in_dim(values, index ^ k, 0, keepdims=False)
             for k in range(values.shape[0])
         ]
+
+    def small_sum(parts, axis):
         return total([parts[0]] + [permute(parts[k], axis, k) for k in range(1, len(parts))])
 
-    terms = terms.reshape(count, rows, groups, own).transpose(1, 2, 0, 3)
-    terms, out_arrived = phase((sum_small(terms, "dp", at_dp), out_arrived))
-    summed = sum_small(terms, "seq", at_seq)
-    home, grad_normed_attn, out_arrived = phase((home, grad_normed_attn, out_arrived))
+    terms = small_parts(terms.reshape(count, rows, groups, own).transpose(1, 2, 0, 3), at_dp)
+    attn_terms, terms, slice_near, slice_pieces, branch_all, up_near, gate_near = phase(
+        (attn_terms, terms, slice_near, slice_pieces, branch_all, up_near, gate_near)
+    )
+    grad_normed_attn = scatter_seq(attn_terms)
+    slice_far = permute(slice_pieces[-1], "dp", rows - 1)
+    terms = small_parts(small_sum(terms, "dp"), at_seq)
+    out_pieces = dp_terms(contract(context_all, branch_all, 0, 0).astype(jnp.bfloat16))
+    terms, slice_far, mlp_out, out_pieces, down_near, up_near, gate_near = phase(
+        (terms, slice_far, mlp_out, out_pieces, down_near, up_near, gate_near)
+    )
+    home = (
+        total([slice_pieces[0], *slice_near, slice_far])
+        .astype(jnp.bfloat16)
+        .reshape(groups, own, 3 * local_width)
+    )
+    home, terms, out_pieces, down_near, up_near, gate_near = phase(
+        (home, terms, out_pieces, down_near, up_near, gate_near)
+    )
+    home = lax.all_to_all(home, "seq", split_axis=0, concat_axis=0, tiled=True)
+    out_arrived = [permute(out_pieces[k], "dp", k) for k in range(1, rows)]
+    summed = small_sum(terms, "seq")
+    home, out_arrived, summed = phase((home, out_arrived, summed))
     out_proj = total([out_pieces[0], *out_arrived])
+    out_gate = total([gate_terms[0], *gate_near])
+    out_up = total([up_terms[0], *up_near])
     out_down = total([down_terms[0], *down_near])
     if whole_heads and rows % 2 == 0:
         grad_qkv_out = columns_in_place([home], rows)
@@ -695,9 +683,10 @@
         )
     if not whole_heads:
         out_proj = lax.ppermute(out_proj, ("dp", "seq"), owner)
-    mlp_last = jnp.concatenate([mlp_half, mlp_last], axis=0)
-    mlp_out = total([mlp_pieces[0], *mlp_sums, mlp_last])
     layer_output = (resid_mid + mlp_out).astype(jnp.bfloat16)
+    grad_normed_attn, grad_qkv_out, out_proj, out_gate, out_up, out_down, layer_output = phase(
+        (grad_normed_attn, grad_qkv_out, out_proj, out_gate, out_up, out_down, layer_output)
+    )
     grad_input = grad_mid + norm_backward(
         grad_normed_attn, scaled_attn, inverse_attn, gain_attn
     )[0]

time: 503 us -> 491 us (0.976)
  starting transfers between devices: 83.9 us -> 73.7 us
    ppermute x59 -> x54, starting transfers between devices: 70.1 us -> 63.2 us  [permute(): return lax.ppermute(value, axis, [(i, i ^ offset) for i in range(size)])]
    transpose x2 -> x0, other arithmetic: 5.69 us -> none  [per_device(): return (layer_output[None], grad_input[None], summed[7:], summed[0], summ...]
    reduce_scatter x3 -> x4, waiting for transfers between devices: 17.9 us -> 13.3 us  [scatter_seq(): lax.psum_scatter(terms.astype(jnp.bfloat16), 'seq', scatter_dimension=0,...]
    ppermute x59 -> x54, waiting for transfers between devices: 97.9 us -> 100 us  [permute(): return lax.ppermute(value, axis, [(i, i ^ offset) for i in range(size)])]
    unnamed x129 -> x139, local copies, waits for them, and re-layouts: 14.2 us -> 13.4 us
  transfers between devices with their start and end apart: 67 -> 63, of which waited for: 26 -> 32; matrix products, arithmetic and copies ran while one was open for 30% -> 30% of each run, Pallas kernels for 6% -> 6%
where the time goes in v6:
time: 491 us; the launch traced here: 484 us
  waiting for transfers between devices  173 us (35%)
  matrix products  75.6 us (15%)
  starting transfers between devices  73.7 us (15%)
  local copies, waits for them, and re-layouts  56.9 us (12%)
  other arithmetic  56.1 us (11%)
  Pallas kernels  31.8 us (6%)
  between operations  16.7 us (3%)
    ppermute x54, waiting for transfers between devices, permute(): return lax.ppermute(value, axis, [(i, i ^ offset) for i in range(size)])  100 us
    dot_general x13, matrix products, contract(): lax.dot_general(left, right, (((left_dim,), (right_dim,)), ((), ())), pre...  68.4 us
    ppermute x54, starting transfers between devices, permute(): return lax.ppermute(value, axis, [(i, i ^ offset) for i in range(size)])  63.2 us
    all_to_all x1, waiting for transfers between devices, per_device(): part = lax.all_to_all(dealt, 'seq', split_axis=0, concat_axis=0, tiled=True)  36.7 us
    all_gather x3, waiting for transfers between devices, gather_seq(): return lax.all_gather(piece, 'seq', axis=0, tiled=True)  20 us
    dynamic_update_slice x19, local copies, waits for them, and re-layouts, place(): lax.dynamic_update_slice_in_dim(result, piece, (index ^ k) * block, 0)  14.8 us
    unnamed x139, local copies, waits for them, and re-layouts  13.4 us
    reduce_scatter x4, waiting for transfers between devices, scatter_seq(): lax.psum_scatter(terms.astype(jnp.bfloat16), 'seq', scatter_dimension=0,...  13.3 us
  transfers between devices with their start and end apart: 63, of which 32 were waited for; matrix products, arithmetic and copies ran while one was open for 30% of the time, Pallas kernels for 6%

profile of v6, /device:TPU:0, one launch (start us, length us, event | category | flops | bytes accessed | tf_op | source)
XLA Modules:
  0.0 484.1 jit_solution(3855407712506423299)
XLA Ops:
  11.2 6.3 %all-to-all-start = ((bf16[8,80,768]{2,1,0:T(8,128)(2,1)}), bf16[8,80,768]{2,1,0:T(8,128)(2,1)S(1)}, u32[]{:S(2)}, u32[]{:S(2)}) async-start(bf16[8,80,768]{2,1,0:T(8,128)(2,1)} %deal_columns.1), calls=%async_computation | async-start | bytes 1966080 | tf_op jit(solution)/shard_map/all_to_all | solution.py:509
  20.7 36.7 %all-to-all-done = bf16[8,80,768]{2,1,0:T(8,128)(2,1)S(1)} async-done(((bf16[8,80,768]{2,1,0:T(8,128)(2,1)}), bf16[8,80,768]{2,1,0:T(8,128)(2,1)S(1)}, u32[]{:S(2)}, u32[]{:S(2)}) %all-to-all-start) | async-done | bytes 983072 | tf_op jit(solution)/shard_map/all_to_all | solution.py:509
  70.5 7.7 %all-gather.9.cloned.1.call-done = bf16[1,1024,2048]{2,1,0:T(8,128)(2,1)} async-done(((bf16[1,128,2048]{2,1,0:T(8,128)(2,1)}), bf16[1,1024,2048]{2,1,0:T(8,128)(2,1)}) %all-gather.9.cloned.1.call-update) | async-done | bytes 4194320 | tf_op jit(solution)/shard_map/all_gather | solution.py:405
  97.5 4.1 add_convert_fusion.1
  111.1 3.4 add_convert_fusion.2.qkv_ref
  114.7 9.8 %attention_forward.1 = (bf16[1024,256]{1,0:T(8,128)(2,1)S(1)}, bf16[1024,256]{1,0:T(8,128)(2,1)S(1)}, bf16[1024,256]{1,0:T(8,128)(2,1)S(1)}, f32[4,1024]{1,0:T(4,128)S(1)}) custom-call(bf16[1024,768]{1,0:T(8,128)(2,1)S(1)} %add_convert_fusion.2.qkv_ref, f32[1024,128]{1,0:T(8,128)S(1)} %copy.49.cos_ref, f32[1024,128]{1,0:T(8,128)S(1)} %copy.50.former_ref, ...), custom_call_target="tpu_custom_call" | custom-call | flops 1 | bytes 1 | tf_op jit(solution)/shard_map/attention_forward/pallas_call | solution.py:310
  126.4 3.8 convolution_convert_fusion.1
  134.3 20.0 %collective-permute-done.14 = bf16[128,2048]{1,0:T(8,128)(2,1)S(1)} collective-permute-done((bf16[128,2048]{1,0:T(8,128)(2,1)}, bf16[128,2048]{1,0:T(8,128)(2,1)S(1)}, u32[]{:S(2)}, u32[]{:S(2)}) %collective-permute-start.14) | collective-permute-done | bytes 524320 | tf_op jit(solution)/shard_map/ppermute | solution.py:355
  199.2 16.1 %collective-permute-done.22 = bf16[88,2048]{1,0:T(8,128)(2,1)S(1)} collective-permute-done((bf16[88,2048]{1,0:T(8,128)(2,1)S(1)}, bf16[88,2048]{1,0:T(8,128)(2,1)S(1)}, u32[]{:S(2)}, u32[]{:S(2)}) %collective-permute-start.22) | collective-permute-done | bytes 360480 | tf_op jit(solution)/shard_map/ppermute | solution.py:355
  227.2 6.9 %fusion.22 = f32[1024,704]{0,1:T(8,128)} fusion(bf16[1024,2048]{1,0:T(8,128)(2,1)} %slice_dynamic-update-slice_fusion, bf16[704,2048]{1,0:T(8,128)(2,1)S(1)} %constant_dynamic-update-slice_fusion), kind=kOutput, calls=%fused_computation.161 | convolution fusion | flops 2952790016 | bytes 9961472 | tf_op jit(solution)/shard_map/dot_general | solution.py:21
  235.2 6.0 %fusion.23 = f32[1024,704]{0,1:T(8,128)S(1)} fusion(bf16[1024,2048]{1,0:T(8,128)(2,1)} %all-gather.5.cloned.1.call-done, bf16[704,2048]{1,0:T(8,128)(2,1)} %pad_maximum_fusion), kind=kOutput, calls=%fused_computation.162 | convolution fusion | flops 2952790016 | bytes 9961472 | tf_op jit(solution)/shard_map/dot_general | solution.py:21
  241.2 5.4 %multiply_convert_fusion = (bf16[1024,704]{0,1:T(8,128)(2,1)}, bf16[1024,704]{0,1:T(8,128)(2,1)S(1)}, bf16[1024,704]{0,1:T(8,128)(2,1)S(1)}) fusion(f32[1024,704]{0,1:T(8,128)S(1)} %fusion.23, f32[1024,704]{0,1:T(8,128)S(1)} %copy-done.62, bf16[1024,2048]{1,0:T(8,128)(2,1)S(1)} %copy-done.59, bf16[704,2048]{1,0:T(8,128)(2,1)S(1)} %copy-done.25), kind=kOutput, calls=%fused_computation.17 | convolution fusion | flops 2963603456 | bytes 17170432 | tf_op jit(solution)/shard_map/dot_general | solution.py:21
  246.6 3.5 fusion.24
  250.2 5.1 %add_convert_fusion = bf16[1024,2048]{1,0:T(8,128)(2,1)} fusion(f32[1024,2048]{1,0:T(8,128)S(1)} %fusion.24, bf16[1024,704]{0,1:T(8,128)(2,1)S(1)} %get-tuple-element.218, bf16[704,2048]{1,0:T(8,128)(2,1)S(1)} %copy-done.24), kind=kOutput, calls=%fused_computation | convolution fusion | flops 2956984320 | bytes 16908288 | tf_op jit(solution)/shard_map/dot_general | solution.py:21
  255.6 5.9 %convolution_convert_fusion.6 = bf16[704,2048]{1,0:T(8,128)(2,1)S(1)} fusion(bf16[1024,704]{0,1:T(8,128)(2,1)} %copy-done.63, bf16[1024,2048]{1,0:T(8,128)(2,1)} %all-gather.5.cloned.1.call-done), kind=kOutput, calls=%fused_computation.12 | convolution fusion | flops 2954231808 | bytes 8519680 | tf_op jit(solution)/shard_map/dot_general | solution.py:21
  266.9 5.1 %convolution_convert_fusion = bf16[1024,2048]{1,0:T(8,128)(2,1)} fusion(bf16[1024,704]{0,1:T(8,128)(2,1)S(1)} %copy-done.64, bf16[704,2048]{1,0:T(8,128)(2,1)S(1)} %copy-done.47), kind=kOutput, calls=%fused_computation.6 | convolution fusion | flops 2954887168 | bytes 8519680 | tf_op jit(solution)/shard_map/dot_general | solution.py:21
  272.0 7.6 %convolution_convert_fusion.5 = bf16[704,2048]{1,0:T(8,128)(2,1)} fusion(bf16[1024,704]{0,1:T(8,128)(2,1)} %copy-done.61, bf16[1024,2048]{1,0:T(8,128)(2,1)} %all-gather.5.cloned.1.call-done), kind=kOutput, calls=%fused_computation.11 | convolution fusion | flops 2954231808 | bytes 8519680 | tf_op jit(solution)/shard_map/dot_general | solution.py:21
  285.4 6.7 %convolution_convert_fusion.4 = bf16[704,2048]{1,0:T(8,128)(2,1)} fusion(bf16[1024,704]{0,1:T(8,128)(2,1)S(1)} %copy-done.65, bf16[1024,2048]{1,0:T(8,128)(2,1)} %slice_dynamic-update-slice_fusion), kind=kOutput, calls=%fused_computation.10 | convolution fusion | flops 2954231808 | bytes 8519680 | tf_op jit(solution)/shard_map/dot_general | solution.py:21
  292.1 13.0 %reduce-scatter.7.cloned.1.call-done = bf16[128,2048]{1,0:T(8,128)(2,1)} async-done(((bf16[1024,2048]{1,0:T(8,128)(2,1)}), bf16[128,2048]{1,0:T(8,128)(2,1)}) %reduce-scatter.7.cloned.1.call-update) | async-done | bytes 524304 | tf_op jit(solution)/shard_map/reduce_scatter | solution.py:409
  326.2 6.6 %collective-permute-done.35 = bf16[88,2048]{1,0:T(8,128)(2,1)S(1)} collective-permute-done((bf16[88,2048]{1,0:T(8,128)(2,1)S(1)}, bf16[88,2048]{1,0:T(8,128)(2,1)S(1)}, u32[]{:S(2)}, u32[]{:S(2)}) %collective-permute-start.35) | collective-permute-done | bytes 360480 | tf_op jit(solution)/shard_map/ppermute | solution.py:355
  335.4 9.0 %collective-permute-done.33 = bf16[176,2048]{1,0:T(8,128)(2,1)} collective-permute-done((bf16[176,2048]{1,0:T(8,128)(2,1)S(1)}, bf16[176,2048]{1,0:T(8,128)(2,1)}, u32[]{:S(2)}, u32[]{:S(2)}) %collective-permute-start.33) | collective-permute-done | bytes 720928 | tf_op jit(solution)/shard_map/ppermute | solution.py:355
  344.4 11.2 %all-gather.7.cloned.1.call-done = bf16[1024,2048]{1,0:T(8,128)(2,1)} async-done(((bf16[128,2048]{1,0:T(8,128)(2,1)}), bf16[1024,2048]{1,0:T(8,128)(2,1)}) %all-gather.7.cloned.1.call-update) | async-done | bytes 4194320 | tf_op jit(solution)/shard_map/all_gather | solution.py:405
  359.2 3.6 convolution_convert_fusion.8.context_grad_ref
  362.8 11.0 %attention_backward.1 = bf16[1024,768]{1,0:T(8,128)(2,1)S(1)} custom-call(bf16[1024,256]{1,0:T(8,128)(2,1)S(1)} %copy-done.7, bf16[1024,256]{1,0:T(8,128)(2,1)S(1)} %copy-done.9, bf16[1024,768]{1,0:T(8,128)(2,1)} %copy-done.2, bf16[1024,256]{1,0:T(8,128)(2,1)S(1)} %convolution_convert_fusion.8.context_grad_ref, f32[4,1024]{1,0:T(4,128)S(1)} %get-tuple-element.241.logsum_ref, ...), custom_call_target="tpu_custom_call" | custom-call | flops 1 | bytes 1 | tf_op jit(solution)/shard_map/attention_backward/pallas_call | solution.py:328
  375.8 4.1 convolution_convert_fusion.3
  383.6 5.0 %convolution_convert_fusion.2.terms_ref = bf16[1024,2048]{1,0:T(8,128)(2,1)} fusion(bf16[1024,768]{1,0:T(8,128)(2,1)S(1)} %attention_backward.1, bf16[2048,768]{1,0:T(8,128)(2,1)S(1)} %copy-done.21), kind=kOutput, calls=%fused_computation.8 | convolution fusion | flops 3223322624 | bytes 8912896 | tf_op jit(solution)/shard_map/dot_general | solution.py:21
  390.9 8.3 %norm_sums.1 = f32[8,2048]{1,0:T(8,128)S(1)} custom-call(bf16[1024,2048]{1,0:T(8,128)(2,1)S(1)} %bitcast.122, bf16[1024,2048]{1,0:T(8,128)(2,1)} %convolution_convert_fusion.2.terms_ref, f32[1,2048]{1,0:T(1,128)S(1)} %bitcast.123, f32[1,2048]{1,0:T(1,128)S(1)} %slice.179.gain_ref), custom_call_target="tpu_custom_call" | custom-call | flops 1 | bytes 1 | tf_op jit(solution)/shard_map/norm_sums/pallas_call | solution.py:279
  403.3 3.5 convolution_convert_fusion.7
  411.3 10.3 %collective-permute-done.40 = f32[8,14,64]{2,1,0:T(8,128)S(1)} collective-permute-done((f32[8,14,64]{2,1,0:T(8,128)S(1)}, f32[8,14,64]{2,1,0:T(8,128)S(1)}, u32[]{:S(2)}, u32[]{:S(2)}) %collective-permute-start.40) | collective-permute-done | bytes 28704 | tf_op jit(solution)/shard_map/ppermute | solution.py:355
  431.7 3.5 all-to-all-start.1
  443.6 3.8 collective-permute-start.52
  451.9 14.5 %collective-permute-done.52 = f32[14,64]{1,0:T(8,128)S(1)} collective-permute-done((f32[14,64]{1,0:T(8,128)S(1)}, f32[14,64]{1,0:T(8,128)S(1)}, u32[]{:S(2)}, u32[]{:S(2)}) %collective-permute-start.52) | collective-permute-done | bytes 3616 | tf_op jit(solution)/shard_map/ppermute | solution.py:355
  (417 shorter events, 200.0 us)
Async XLA Ops:
  11.2 46.2 %all-to-all-start = ((bf16[8,80,768]{2,1,0:T(8,128)(2,1)}), bf16[8,80,768]{2,1,0:T(8,128)(2,1)S(1)}, u32[]{:S(2)}, u32[]{:S(2)}) async-start(bf16[8,80,768]{2,1,0:T(8,128)(2,1)} %deal_columns.1), calls=%async_computation | async-start | bytes 1966080 | tf_op jit(solution)/shard_map/all_to_all | solution.py:509
  17.5 60.7 %all-gather.9.cloned.1.call-start = ((), (), s32[]{:S(2)}) async-start(), calls=%async_computation.12 | async-start | bytes 4718592 | tf_op jit(solution)/shard_map/all_gather | solution.py:405
  18.3 166.8 %reduce-scatter.5.cloned.1.call-start = ((), (), s32[]{:S(2)}) async-start(), calls=%async_computation.6 | async-start | bytes 4718592 | tf_op jit(solution)/shard_map/reduce_scatter | solution.py:409
  61.1 27.2 %collective-permute-start = (bf16[512,768]{1,0:T(8,128)(2,1)S(1)}, bf16[512,768]{1,0:T(8,128)(2,1)S(1)}, u32[]{:S(2)}, u32[]{:S(2)}) collective-permute-start(bf16[512,768]{1,0:T(8,128)(2,1)S(1)} %bitcast.126), channel_id=1, source_target_pairs={{0,8},{8,0},{16,24},{24,16},{1,9},{9,1},{17,25},{25,17},{2,10},{10... | collective-permute-start | bytes 2359304 | tf_op jit(solution)/shard_map/ppermute | solution.py:355
  62.6 25.7 %collective-permute-start.1 = (bf16[512,768]{1,0:T(8,128)(2,1)S(1)}, bf16[512,768]{1,0:T(8,128)(2,1)}, u32[]{:S(2)}, u32[]{:S(2)}) collective-permute-start(bf16[512,768]{1,0:T(8,128)(2,1)S(1)} %bitcast.127), channel_id=1, source_target_pairs={{0,16},{8,24},{16,0},{24,8},{1,17},{9,25},{17,1},{25,9},{2,18},{10... | collective-permute-start | bytes 2359304 | tf_op jit(solution)/shard_map/ppermute | solution.py:355
  79.2 51.1 %collective-permute-start.10 = (bf16[128,2048]{1,0:T(8,128)(2,1)}, bf16[128,2048]{1,0:T(8,128)(2,1)}, u32[]{:S(2)}, u32[]{:S(2)}) collective-permute-start(bf16[128,2048]{1,0:T(8,128)(2,1)} %bitcast.16), channel_id=1, source_target_pairs={{0,4},{1,5},{2,6},{3,7},{4,0},{5,1},{6,2},{7,3},{8,12},{9,13},{10,... | collective-permute-start | bytes 1572872 | tf_op jit(solution)/shard_map/ppermute | solution.py:355
  79.2 51.0 %collective-permute-start.11 = (bf16[128,2048]{1,0:T(8,128)(2,1)}, bf16[128,2048]{1,0:T(8,128)(2,1)S(1)}, u32[]{:S(2)}, u32[]{:S(2)}) collective-permute-start(bf16[128,2048]{1,0:T(8,128)(2,1)} %bitcast.16), channel_id=1, source_target_pairs={{0,6},{1,7},{2,4},{3,5},{4,2},{5,3},{6,0},{7,1},{8,14},{9,15},{10,... | collective-permute-start | bytes 1572872 | tf_op jit(solution)/shard_map/ppermute | solution.py:355
  130.3 104.9 %all-gather.5.cloned.1.call-start = ((), (), s32[]{:S(2)}) async-start(), calls=%async_computation.7 | async-start | bytes 4718592 | tf_op jit(solution)/shard_map/all_gather | solution.py:405
  130.3 23.9 %collective-permute-start.12 = (bf16[176,2048]{1,0:T(8,128)(2,1)}, bf16[176,2048]{1,0:T(8,128)(2,1)}, u32[]{:S(2)}, u32[]{:S(2)}) collective-permute-start(bf16[176,2048]{1,0:T(8,128)(2,1)} %bitcast.19), channel_id=1, source_target_pairs={{0,8},{8,0},{16,24},{24,16},{1,9},{9,1},{17,25},{25,17},{2,10},{10... | collective-permute-start | bytes 2162696 | tf_op jit(solution)/shard_map/ppermute | solution.py:355
  130.9 23.3 %collective-permute-start.13 = (bf16[176,2048]{1,0:T(8,128)(2,1)}, bf16[176,2048]{1,0:T(8,128)(2,1)}, u32[]{:S(2)}, u32[]{:S(2)}) collective-permute-start(bf16[176,2048]{1,0:T(8,128)(2,1)} %bitcast.19), channel_id=1, source_target_pairs={{0,16},{8,24},{16,0},{24,8},{1,17},{9,25},{17,1},{25,9},{2,18},{10... | collective-permute-start | bytes 2162696 | tf_op jit(solution)/shard_map/ppermute | solution.py:355
  132.4 21.8 %collective-permute-start.14 = (bf16[128,2048]{1,0:T(8,128)(2,1)}, bf16[128,2048]{1,0:T(8,128)(2,1)S(1)}, u32[]{:S(2)}, u32[]{:S(2)}) collective-permute-start(bf16[128,2048]{1,0:T(8,128)(2,1)} %bitcast.16), channel_id=1, source_target_pairs={{0,2},{1,3},{2,0},{3,1},{4,6},{5,7},{6,4},{7,5},{8,10},{9,11},{10,... | collective-permute-start | bytes 1572872 | tf_op jit(solution)/shard_map/ppermute | solution.py:355
  165.4 20.8 %collective-permute-start.17 = (bf16[176,2048]{1,0:T(8,128)(2,1)}, bf16[176,2048]{1,0:T(8,128)(2,1)}, u32[]{:S(2)}, u32[]{:S(2)}) collective-permute-start(bf16[176,2048]{1,0:T(8,128)(2,1)} %bitcast.20), channel_id=1, source_target_pairs={{0,8},{8,0},{16,24},{24,16},{1,9},{9,1},{17,25},{25,17},{2,10},{10... | collective-permute-start | bytes 2162696 | tf_op jit(solution)/shard_map/ppermute | solution.py:355
  166.0 20.9 %collective-permute-start.18 = (bf16[176,2048]{1,0:T(8,128)(2,1)}, bf16[176,2048]{1,0:T(8,128)(2,1)}, u32[]{:S(2)}, u32[]{:S(2)}) collective-permute-start(bf16[176,2048]{1,0:T(8,128)(2,1)} %bitcast.20), channel_id=1, source_target_pairs={{0,16},{8,24},{16,0},{24,8},{1,17},{9,25},{17,1},{25,9},{2,18},{10... | collective-permute-start | bytes 2162696 | tf_op jit(solution)/shard_map/ppermute | solution.py:355
  189.7 115.3 %reduce-scatter.7.cloned.1.call-start = ((), (), s32[]{:S(2)}) async-start(), calls=%async_computation.8 | async-start | bytes 4718592 | tf_op jit(solution)/shard_map/reduce_scatter | solution.py:409
  189.8 25.8 %collective-permute-start.20 = (bf16[176,2048]{1,0:T(8,128)(2,1)}, bf16[176,2048]{1,0:T(8,128)(2,1)S(1)}, u32[]{:S(2)}, u32[]{:S(2)}) collective-permute-start(bf16[176,2048]{1,0:T(8,128)(2,1)} %param.28), channel_id=1, source_target_pairs={{0,8},{8,0},{16,24},{24,16},{1,9},{9,1},{17,25},{25,17},{2,10},{10... | collective-permute-start | bytes 2162696 | tf_op jit(solution)/shard_map/ppermute | solution.py:355
  190.7 24.9 %collective-permute-start.21 = (bf16[176,2048]{1,0:T(8,128)(2,1)}, bf16[176,2048]{1,0:T(8,128)(2,1)S(1)}, u32[]{:S(2)}, u32[]{:S(2)}) collective-permute-start(bf16[176,2048]{1,0:T(8,128)(2,1)} %param.28), channel_id=1, source_target_pairs={{0,16},{8,24},{16,0},{24,8},{1,17},{9,25},{17,1},{25,9},{2,18},{10... | collective-permute-start | bytes 2162696 | tf_op jit(solution)/shard_map/ppermute | solution.py:355
  192.2 23.0 %collective-permute-start.22 = (bf16[88,2048]{1,0:T(8,128)(2,1)S(1)}, bf16[88,2048]{1,0:T(8,128)(2,1)S(1)}, u32[]{:S(2)}, u32[]{:S(2)}) collective-permute-start(bf16[88,2048]{1,0:T(8,128)(2,1)S(1)} %slice.157), channel_id=1, source_target_pairs={{0,8},{8,0},{16,24},{24,16},{1,9},{9,1},{17,25},{25,17},{2,10},{10... | collective-permute-start | bytes 1081352 | tf_op jit(solution)/shard_map/ppermute | solution.py:355
  194.2 21.3 %collective-permute-start.23 = (bf16[88,2048]{1,0:T(8,128)(2,1)S(1)}, bf16[88,2048]{1,0:T(8,128)(2,1)S(1)}, u32[]{:S(2)}, u32[]{:S(2)}) collective-permute-start(bf16[88,2048]{1,0:T(8,128)(2,1)S(1)} %slice.158), channel_id=1, source_target_pairs={{0,16},{8,24},{16,0},{24,8},{1,17},{9,25},{17,1},{25,9},{2,18},{10... | collective-permute-start | bytes 1081352 | tf_op jit(solution)/shard_map/ppermute | solution.py:355
  255.3 100.3 %all-gather.7.cloned.1.call-start = ((), (), s32[]{:S(2)}) async-start(), calls=%async_computation.9 | async-start | bytes 4718592 | tf_op jit(solution)/shard_map/all_gather | solution.py:405
  282.3 23.9 %collective-permute-start.29 = (bf16[176,2048]{1,0:T(8,128)(2,1)}, bf16[176,2048]{1,0:T(8,128)(2,1)S(1)}, u32[]{:S(2)}, u32[]{:S(2)}) collective-permute-start(bf16[176,2048]{1,0:T(8,128)(2,1)} %pad_maximum_fusion.6), channel_id=1, source_target_pairs={{0,16},{8,24},{16,0},{24,8},{1,17},{9,25},{17,1},{25,9},{2,18},{10... | collective-permute-start | bytes 2162696 | tf_op jit(solution)/shard_map/ppermute | solution.py:355
  284.8 21.4 %collective-permute-start.28 = (bf16[176,2048]{1,0:T(8,128)(2,1)}, bf16[176,2048]{1,0:T(8,128)(2,1)}, u32[]{:S(2)}, u32[]{:S(2)}) collective-permute-start(bf16[176,2048]{1,0:T(8,128)(2,1)} %pad_maximum_fusion.5), channel_id=1, source_target_pairs={{0,8},{8,0},{16,24},{24,16},{1,9},{9,1},{17,25},{25,17},{2,10},{10... | collective-permute-start | bytes 2162696 | tf_op jit(solution)/shard_map/ppermute | solution.py:355
  310.2 113.0 %reduce-scatter.11.cloned.1.call-start = ((), (), s32[]{:S(2)}) async-start(), calls=%async_computation.11 | async-start | bytes 4718592 | tf_op jit(solution)/shard_map/reduce_scatter | solution.py:409
  323.8 20.6 %collective-permute-start.33 = (bf16[176,2048]{1,0:T(8,128)(2,1)S(1)}, bf16[176,2048]{1,0:T(8,128)(2,1)}, u32[]{:S(2)}, u32[]{:S(2)}) collective-permute-start(bf16[176,2048]{1,0:T(8,128)(2,1)S(1)} %pad_maximum_fusion.8), channel_id=1, source_target_pairs={{0,16},{8,24},{16,0},{24,8},{1,17},{9,25},{17,1},{25,9},{2,18},{10... | collective-permute-start | bytes 2162696 | tf_op jit(solution)/shard_map/ppermute | solution.py:355
  355.6 118.1 %reduce-scatter.9.cloned.1.call-start = ((), (), s32[]{:S(2)}) async-start(), calls=%async_computation.10 | async-start | bytes 4718592 | tf_op jit(solution)/shard_map/reduce_scatter | solution.py:409
  400.9 23.4 %collective-permute-start.43 = (bf16[512,768]{1,0:T(8,128)(2,1)}, bf16[512,768]{1,0:T(8,128)(2,1)}, u32[]{:S(2)}, u32[]{:S(2)}) collective-permute-start(bf16[512,768]{1,0:T(8,128)(2,1)} %get-tuple-element.262), channel_id=1, source_target_pairs={{0,24},{8,16},{16,8},{24,0},{1,25},{9,17},{17,9},{25,1},{2,26},{10... | collective-permute-start | bytes 2359304 | tf_op jit(solution)/shard_map/ppermute | solution.py:355
  427.3 20.0 %collective-permute-start.48 = (f32[14,64]{1,0:T(8,128)}, f32[14,64]{1,0:T(8,128)}, u32[]{:S(2)}, u32[]{:S(2)}) collective-permute-start(f32[14,64]{1,0:T(8,128)} %get-tuple-element.296), channel_id=1, source_target_pairs={{0,2},{1,3},{2,0},{3,1},{4,6},{5,7},{6,4},{7,5},{8,10},{9,11},{10,... | collective-permute-start | bytes 10760 | tf_op jit(solution)/shard_map/ppermute | solution.py:355
  427.3 20.0 %collective-permute-start.49 = (f32[14,64]{1,0:T(8,128)}, f32[14,64]{1,0:T(8,128)}, u32[]{:S(2)}, u32[]{:S(2)}) collective-permute-start(f32[14,64]{1,0:T(8,128)} %get-tuple-element.297), channel_id=1, source_target_pairs={{0,3},{1,2},{2,1},{3,0},{4,7},{5,6},{6,5},{7,4},{8,11},{9,10},{10,... | collective-permute-start | bytes 10760 | tf_op jit(solution)/shard_map/ppermute | solution.py:355
  429.2 19.7 %collective-permute-start.50 = (f32[14,64]{1,0:T(8,128)}, f32[14,64]{1,0:T(8,128)}, u32[]{:S(2)}, u32[]{:S(2)}) collective-permute-start(f32[14,64]{1,0:T(8,128)} %get-tuple-element.298), channel_id=1, source_target_pairs={{0,4},{1,5},{2,6},{3,7},{4,0},{5,1},{6,2},{7,3},{8,12},{9,13},{10,... | collective-permute-start | bytes 10760 | tf_op jit(solution)/shard_map/ppermute | solution.py:355
  430.2 19.9 %collective-permute-start.51 = (f32[14,64]{1,0:T(8,128)}, f32[14,64]{1,0:T(8,128)}, u32[]{:S(2)}, u32[]{:S(2)}) collective-permute-start(f32[14,64]{1,0:T(8,128)} %get-tuple-element.299), channel_id=1, source_target_pairs={{0,5},{1,4},{2,7},{3,6},{4,1},{5,0},{6,3},{7,2},{8,13},{9,12},{10,... | collective-permute-start | bytes 10760 | tf_op jit(solution)/shard_map/ppermute | solution.py:355
  431.7 37.9 %all-to-all-start.1 = ((bf16[8,64,768]{2,1,0:T(8,128)(2,1)}), bf16[8,64,768]{2,1,0:T(8,128)(2,1)S(1)}, u32[]{:S(2)}, u32[]{:S(2)}) async-start(bf16[8,64,768]{2,1,0:T(8,128)(2,1)} %bitcast.39), calls=%async_computation.5 | async-start | bytes 1572864 | tf_op jit(solution)/shard_map/all_to_all | solution.py:667
  443.6 22.7 %collective-permute-start.52 = (f32[14,64]{1,0:T(8,128)S(1)}, f32[14,64]{1,0:T(8,128)S(1)}, u32[]{:S(2)}, u32[]{:S(2)}) collective-permute-start(f32[14,64]{1,0:T(8,128)S(1)} %copy-done.53), channel_id=1, source_target_pairs={{0,6},{1,7},{2,4},{3,5},{4,2},{5,3},{6,0},{7,1},{8,14},{9,15},{10,... | collective-permute-start | bytes 10760 | tf_op jit(solution)/shard_map/ppermute | solution.py:355
  447.4 19.8 %collective-permute-start.44 = (bf16[64,2048]{1,0:T(8,128)(2,1)S(1)}, bf16[64,2048]{1,0:T(8,128)(2,1)S(1)}, u32[]{:S(2)}, u32[]{:S(2)}) collective-permute-start(bf16[64,2048]{1,0:T(8,128)(2,1)S(1)} %copy-done.44), channel_id=1, source_target_pairs={{0,8},{8,0},{16,24},{24,16},{1,9},{9,1},{17,25},{25,17},{2,10},{10... | collective-permute-start | bytes 786440 | tf_op jit(solution)/shard_map/ppermute | solution.py:355
  (97 other events, 1095.9 us)
Sparse Core Ops, SparseCore 0:
  20.0 58.2 all-gather.8
  130.4 54.6 reduce-scatter.4
  189.9 45.2 all-gather.4
  255.4 49.5 reduce-scatter.6
  310.3 45.2 all-gather.6
  357.8 48.7 reduce-scatter.10
  408.8 61.8 reduce-scatter.8

commit v7 on v6

--- a/solution.py
+++ b/solution.py
@@ -507,6 +507,10 @@
             axis=1,
         )
     part = lax.all_to_all(dealt, "seq", split_axis=0, concat_axis=0, tiled=True)
+    out_rows = out_weight if whole_heads else lax.ppermute(out_weight, ("dp", "seq"), back)
+    out_pieces = gather_dp(out_rows)
+    gate_pieces = near_dp(gate_weight.T)
+    part, out_pieces, gate_pieces = phase((part, out_pieces, gate_pieces))
     chips = groups // 2
     input_all = gather_seq(layer_input[0])
     spread = place(gather_dp(part[:, own:].reshape(groups, -1)), at_dp)
@@ -532,10 +536,9 @@
     ].astype(jnp.bfloat16)
     qkv_pieces, tables, first, resid_in = phase((qkv_pieces, tables, first, resid_in))
     head_qkv = place(qkv_pieces + [corner_dp(qkv_pieces)], at_dp)
-    head_qkv, normed_all, out_rows = phase((head_qkv, normed_all, out_weight))
-    if not whole_heads:
-        out_rows = lax.ppermute(out_rows, ("dp", "seq"), back)
-    head_out = place(gather_dp(out_rows), at_dp)
+    head_qkv, normed_all, grad_near = phase((head_qkv, normed_all, grad_out))
+    near = permute(grad_near, "seq", 2)
+    head_out = place(out_pieces, at_dp)
     projected = (
         jnp.dot(normed_all, head_qkv, preferred_element_type=jnp.float32) + bias_qkv
     ).astype(jnp.bfloat16)
@@ -543,13 +546,8 @@
     out_terms = jnp.dot(context_all, head_out, preferred_element_type=jnp.float32).astype(
         jnp.bfloat16
     )
-    out_terms, grad_pieces, gate_rows, grad_near = phase(
-        (out_terms, grad_pieces, gate_weight.T, grad_out)
-    )
+    out_terms, grad_pieces, near, up_rows = phase((out_terms, grad_pieces, near, up_weight.T))
     attn_out = scatter_seq(out_terms)
-    gate_pieces = near_dp(gate_rows)
-    near = permute(grad_near, "seq", 2)
-    gate_pieces, near, up_rows = phase((gate_pieces, near, up_weight.T))
     grad_pieces = [grad_out, near, *grad_pieces]
     gate_pieces = gate_pieces + [corner_dp(gate_pieces)]
     up_pieces = near_dp(up_rows)

time: 491 us -> 488 us (level)
  waiting for transfers between devices: 173 us -> 152 us
  local copies, waits for them, and re-layouts: 56.9 us -> 68.3 us
    all_to_all x1, waiting for transfers between devices: 36.7 us -> 8.68 us  [per_device(): part = lax.all_to_all(dealt, 'seq', split_axis=0, concat_axis=0, tiled=True)]
    reduce_scatter x4, waiting for transfers between devices: 13.3 us -> 30.9 us  [scatter_seq(): lax.psum_scatter(terms.astype(jnp.bfloat16), 'seq', scatter_dimension=0,...]
    dynamic_update_slice x19, local copies, waits for them, and re-layouts: 14.8 us -> 24.9 us  [place(): lax.dynamic_update_slice_in_dim(result, piece, (index ^ k) * block, 0)]
    ppermute x54, waiting for transfers between devices: 100 us -> 91.8 us  [permute(): return lax.ppermute(value, axis, [(i, i ^ offset) for i in range(size)])]
    unnamed x139 -> x147, local copies, waits for them, and re-layouts: 13.4 us -> 15 us
  transfers between devices with their start and end apart: 63 -> 63, of which waited for: 32 -> 28; matrix products, arithmetic and copies ran while one was open for 30% -> 33% of each run, Pallas kernels for 6% -> 6%
where the time goes in v7:
time: 488 us; the launch traced here: 481 us
  waiting for transfers between devices  152 us (31%)
  matrix products  77.4 us (16%)
  starting transfers between devices  75.5 us (15%)
  local copies, waits for them, and re-layouts  68.3 us (14%)
  other arithmetic  59.5 us (12%)
  Pallas kernels  31.8 us (7%)
  between operations  16.7 us (3%)
    ppermute x54, waiting for transfers between devices, permute(): return lax.ppermute(value, axis, [(i, i ^ offset) for i in range(size)])  91.8 us
    dot_general x13, matrix products, contract(): lax.dot_general(left, right, (((left_dim,), (right_dim,)), ((), ())), pre...  69.2 us
    ppermute x54, starting transfers between devices, permute(): return lax.ppermute(value, axis, [(i, i ^ offset) for i in range(size)])  65.1 us
    reduce_scatter x4, waiting for transfers between devices, scatter_seq(): lax.psum_scatter(terms.astype(jnp.bfloat16), 'seq', scatter_dimension=0,...  30.9 us
    dynamic_update_slice x19, local copies, waits for them, and re-layouts, place(): lax.dynamic_update_slice_in_dim(result, piece, (index ^ k) * block, 0)  24.9 us
    all_gather x3, waiting for transfers between devices, gather_seq(): return lax.all_gather(piece, 'seq', axis=0, tiled=True)  17.6 us
    unnamed x147, local copies, waits for them, and re-layouts  15 us
    pallas_call x1, Pallas kernels, attention_backward(): pl.pallas_call(backward_kernel, out_shape=jax.ShapeDtypeStruct((length, 3...  11 us
  transfers between devices with their start and end apart: 63, of which 28 were waited for; matrix products, arithmetic and copies ran while one was open for 33% of the time, Pallas kernels for 6%

profile of v7, /device:TPU:0, one launch (start us, length us, event | category | flops | bytes accessed | tf_op | source)
XLA Modules:
  0.0 480.6 jit_solution(15080500042688625998)
XLA Ops:
  11.2 6.3 %all-to-all-start = ((bf16[8,80,768]{2,1,0:T(8,128)(2,1)}), bf16[8,80,768]{2,1,0:T(8,128)(2,1)S(1)}, u32[]{:S(2)}, u32[]{:S(2)}) async-start(bf16[8,80,768]{2,1,0:T(8,128)(2,1)} %deal_columns.1), calls=%async_computation | async-start | bytes 1966080 | tf_op jit(solution)/shard_map/all_to_all | solution.py:509
  26.7 15.7 %collective-permute-done = bf16[64,2048]{1,0:T(8,128)(2,1)} collective-permute-done((bf16[64,2048]{1,0:T(8,128)(2,1)}, bf16[64,2048]{1,0:T(8,128)(2,1)}, u32[]{:S(2)}, u32[]{:S(2)}) %collective-permute-start) | collective-permute-done | bytes 262176 | tf_op jit(solution)/shard_map/ppermute | solution.py:355
  42.3 6.4 %collective-permute-done.1 = bf16[64,2048]{1,0:T(8,128)(2,1)} collective-permute-done((bf16[64,2048]{1,0:T(8,128)(2,1)}, bf16[64,2048]{1,0:T(8,128)(2,1)}, u32[]{:S(2)}, u32[]{:S(2)}) %collective-permute-start.1) | collective-permute-done | bytes 262176 | tf_op jit(solution)/shard_map/ppermute | solution.py:355
  48.7 8.7 %all-to-all-done = bf16[8,80,768]{2,1,0:T(8,128)(2,1)S(1)} async-done(((bf16[8,80,768]{2,1,0:T(8,128)(2,1)}), bf16[8,80,768]{2,1,0:T(8,128)(2,1)S(1)}, u32[]{:S(2)}, u32[]{:S(2)}) %all-to-all-start) | async-done | bytes 983072 | tf_op jit(solution)/shard_map/all_to_all | solution.py:509
  99.4 4.1 add_convert_fusion.1
  114.9 9.8 %attention_forward.1 = (bf16[1024,256]{1,0:T(8,128)(2,1)S(1)}, bf16[1024,256]{1,0:T(8,128)(2,1)S(1)}, bf16[1024,256]{1,0:T(8,128)(2,1)S(1)}, f32[4,1024]{1,0:T(4,128)S(1)}) custom-call(bf16[1024,768]{1,0:T(8,128)(2,1)S(1)} %add_convert_fusion.2.qkv_ref, f32[1024,128]{1,0:T(8,128)S(1)} %copy.49.cos_ref, f32[1024,128]{1,0:T(8,128)S(1)} %copy.50.former_ref, ...), custom_call_target="tpu_custom_call" | custom-call | flops 1 | bytes 1 | tf_op jit(solution)/shard_map/attention_forward/pallas_call | solution.py:310
  127.1 4.8 %convolution_convert_fusion.1 = bf16[1024,2048]{1,0:T(8,128)(2,1)} fusion(bf16[1024,256]{1,0:T(8,128)(2,1)S(1)} %get-tuple-element.187, bf16[256,2048]{1,0:T(8,128)(2,1)} %constant_dynamic-update-slice_fusion.10), kind=kOutput, calls=%fused_computation.7 | convolution fusion | flops 1075838976 | bytes 5767168 | tf_op jit(solution)/shard_map/dot_general | solution.py:546
  141.9 4.2 collective-permute-done.15
  163.1 18.0 %reduce-scatter.5.cloned.1.call-done = bf16[128,2048]{1,0:T(8,128)(2,1)} async-done(((bf16[1024,2048]{1,0:T(8,128)(2,1)}), bf16[128,2048]{1,0:T(8,128)(2,1)}) %reduce-scatter.5.cloned.1.call-update) | async-done | bytes 524304 | tf_op jit(solution)/shard_map/reduce_scatter | solution.py:409
  195.4 14.3 %collective-permute-done.22 = bf16[88,2048]{1,0:T(8,128)(2,1)S(1)} collective-permute-done((bf16[88,2048]{1,0:T(8,128)(2,1)S(1)}, bf16[88,2048]{1,0:T(8,128)(2,1)S(1)}, u32[]{:S(2)}, u32[]{:S(2)}) %collective-permute-start.22) | collective-permute-done | bytes 360480 | tf_op jit(solution)/shard_map/ppermute | solution.py:355
  213.3 5.2 %pad_maximum_fusion.1 = bf16[704,2048]{1,0:T(8,128)(2,1)} fusion(bf16[176,2048]{1,0:T(8,128)(2,1)S(1)} %pad_maximum_fusion.4, bf16[176,2048]{1,0:T(8,128)(2,1)} %collective-permute-done.18, bf16[176,2048]{1,0:T(8,128)(2,1)S(1)} %copy-done.39, bf16[176,2048]{1,0:T(8,128)(2,1)S(1)} %bitcast.146), kind=kLoop, calls=%fused_computation.16 | loop fusion | flops 11534336 | bytes 5767168 | tf_op jit(solution)/shard_map/concatenate | solution.py:568
  220.8 6.9 %fusion.22 = f32[1024,704]{0,1:T(8,128)} fusion(bf16[1024,2048]{1,0:T(8,128)(2,1)} %slice_dynamic-update-slice_fusion, bf16[704,2048]{1,0:T(8,128)(2,1)S(1)} %constant_dynamic-update-slice_fusion), kind=kOutput, calls=%fused_computation.161 | convolution fusion | flops 2952790016 | bytes 9961472 | tf_op jit(solution)/shard_map/dot_general | solution.py:21
  227.7 3.7 all-gather.5.cloned.1.call-done
  231.4 6.0 %fusion.23 = f32[1024,704]{0,1:T(8,128)S(1)} fusion(bf16[1024,2048]{1,0:T(8,128)(2,1)} %all-gather.5.cloned.1.call-done, bf16[704,2048]{1,0:T(8,128)(2,1)} %pad_maximum_fusion), kind=kOutput, calls=%fused_computation.162 | convolution fusion | flops 2952790016 | bytes 9961472 | tf_op jit(solution)/shard_map/dot_general | solution.py:21
  237.4 5.8 %multiply_convert_fusion = (bf16[1024,704]{0,1:T(8,128)(2,1)}, bf16[1024,704]{0,1:T(8,128)(2,1)S(1)}, bf16[1024,704]{0,1:T(8,128)(2,1)S(1)}) fusion(f32[1024,704]{0,1:T(8,128)S(1)} %fusion.23, f32[1024,704]{0,1:T(8,128)S(1)} %copy-done.66, bf16[1024,2048]{1,0:T(8,128)(2,1)S(1)} %copy-done.63, bf16[704,2048]{1,0:T(8,128)(2,1)S(1)} %copy-done.23), kind=kOutput, calls=%fused_computation.17 | convolution fusion | flops 2963603456 | bytes 17170432 | tf_op jit(solution)/shard_map/dot_general | solution.py:21
  246.8 5.1 %add_convert_fusion = bf16[1024,2048]{1,0:T(8,128)(2,1)} fusion(f32[1024,2048]{1,0:T(8,128)S(1)} %fusion.24, bf16[1024,704]{0,1:T(8,128)(2,1)S(1)} %get-tuple-element.224, bf16[704,2048]{1,0:T(8,128)(2,1)S(1)} %copy-done.22), kind=kOutput, calls=%fused_computation | convolution fusion | flops 2956984320 | bytes 16908288 | tf_op jit(solution)/shard_map/dot_general | solution.py:21
  252.0 5.9 %convolution_convert_fusion.6 = bf16[704,2048]{1,0:T(8,128)(2,1)S(1)} fusion(bf16[1024,704]{0,1:T(8,128)(2,1)} %copy-done.67, bf16[1024,2048]{1,0:T(8,128)(2,1)} %all-gather.5.cloned.1.call-done), kind=kOutput, calls=%fused_computation.12 | convolution fusion | flops 2954231808 | bytes 8519680 | tf_op jit(solution)/shard_map/dot_general | solution.py:21
  263.4 5.2 %convolution_convert_fusion = bf16[1024,2048]{1,0:T(8,128)(2,1)} fusion(bf16[1024,704]{0,1:T(8,128)(2,1)S(1)} %copy-done.68, bf16[704,2048]{1,0:T(8,128)(2,1)S(1)} %copy-done.52), kind=kOutput, calls=%fused_computation.6 | convolution fusion | flops 2954887168 | bytes 8519680 | tf_op jit(solution)/shard_map/dot_general | solution.py:21
  268.6 7.5 %convolution_convert_fusion.5 = bf16[704,2048]{1,0:T(8,128)(2,1)} fusion(bf16[1024,704]{0,1:T(8,128)(2,1)} %copy-done.65, bf16[1024,2048]{1,0:T(8,128)(2,1)} %all-gather.5.cloned.1.call-done), kind=kOutput, calls=%fused_computation.11 | convolution fusion | flops 2954231808 | bytes 8519680 | tf_op jit(solution)/shard_map/dot_general | solution.py:21
  282.0 6.7 %convolution_convert_fusion.4 = bf16[704,2048]{1,0:T(8,128)(2,1)} fusion(bf16[1024,704]{0,1:T(8,128)(2,1)S(1)} %copy-done.69, bf16[1024,2048]{1,0:T(8,128)(2,1)} %slice_dynamic-update-slice_fusion), kind=kOutput, calls=%fused_computation.10 | convolution fusion | flops 2954231808 | bytes 8519680 | tf_op jit(solution)/shard_map/dot_general | solution.py:21
  288.6 12.8 %reduce-scatter.7.cloned.1.call-done = bf16[128,2048]{1,0:T(8,128)(2,1)} async-done(((bf16[1024,2048]{1,0:T(8,128)(2,1)}), bf16[128,2048]{1,0:T(8,128)(2,1)}) %reduce-scatter.7.cloned.1.call-update) | async-done | bytes 524304 | tf_op jit(solution)/shard_map/reduce_scatter | solution.py:409
  322.7 6.6 %collective-permute-done.35 = bf16[88,2048]{1,0:T(8,128)(2,1)S(1)} collective-permute-done((bf16[88,2048]{1,0:T(8,128)(2,1)S(1)}, bf16[88,2048]{1,0:T(8,128)(2,1)S(1)}, u32[]{:S(2)}, u32[]{:S(2)}) %collective-permute-start.35) | collective-permute-done | bytes 360480 | tf_op jit(solution)/shard_map/ppermute | solution.py:355
  331.9 9.0 %collective-permute-done.33 = bf16[176,2048]{1,0:T(8,128)(2,1)} collective-permute-done((bf16[176,2048]{1,0:T(8,128)(2,1)S(1)}, bf16[176,2048]{1,0:T(8,128)(2,1)}, u32[]{:S(2)}, u32[]{:S(2)}) %collective-permute-start.33) | collective-permute-done | bytes 720928 | tf_op jit(solution)/shard_map/ppermute | solution.py:355
  340.9 11.2 %all-gather.7.cloned.1.call-done = bf16[1024,2048]{1,0:T(8,128)(2,1)} async-done(((bf16[128,2048]{1,0:T(8,128)(2,1)}), bf16[1024,2048]{1,0:T(8,128)(2,1)}) %all-gather.7.cloned.1.call-update) | async-done | bytes 4194320 | tf_op jit(solution)/shard_map/all_gather | solution.py:405
  355.7 3.9 convolution_convert_fusion.8.context_grad_ref
  359.6 11.0 %attention_backward.1 = bf16[1024,768]{1,0:T(8,128)(2,1)S(1)} custom-call(bf16[1024,256]{1,0:T(8,128)(2,1)S(1)} %copy-done.7, bf16[1024,256]{1,0:T(8,128)(2,1)S(1)} %copy-done.9, bf16[1024,768]{1,0:T(8,128)(2,1)} %copy-done.2, bf16[1024,256]{1,0:T(8,128)(2,1)S(1)} %convolution_convert_fusion.8.context_grad_ref, f32[4,1024]{1,0:T(4,128)S(1)} %get-tuple-element.247.logsum_ref, ...), custom_call_target="tpu_custom_call" | custom-call | flops 1 | bytes 1 | tf_op jit(solution)/shard_map/attention_backward/pallas_call | solution.py:328
  372.2 4.1 convolution_convert_fusion.3
  380.1 5.0 %convolution_convert_fusion.2.terms_ref = bf16[1024,2048]{1,0:T(8,128)(2,1)} fusion(bf16[1024,768]{1,0:T(8,128)(2,1)S(1)} %attention_backward.1, bf16[2048,768]{1,0:T(8,128)(2,1)S(1)} %copy-done.19), kind=kOutput, calls=%fused_computation.8 | convolution fusion | flops 3223322624 | bytes 8912896 | tf_op jit(solution)/shard_map/dot_general | solution.py:21
  387.4 8.3 %norm_sums.1 = f32[8,2048]{1,0:T(8,128)S(1)} custom-call(bf16[1024,2048]{1,0:T(8,128)(2,1)S(1)} %bitcast.122, bf16[1024,2048]{1,0:T(8,128)(2,1)} %convolution_convert_fusion.2.terms_ref, f32[1,2048]{1,0:T(1,128)S(1)} %bitcast.123, f32[1,2048]{1,0:T(1,128)S(1)} %slice.179.gain_ref), custom_call_target="tpu_custom_call" | custom-call | flops 1 | bytes 1 | tf_op jit(solution)/shard_map/norm_sums/pallas_call | solution.py:279
  407.7 10.4 %collective-permute-done.40 = f32[8,14,64]{2,1,0:T(8,128)S(1)} collective-permute-done((f32[8,14,64]{2,1,0:T(8,128)S(1)}, f32[8,14,64]{2,1,0:T(8,128)S(1)}, u32[]{:S(2)}, u32[]{:S(2)}) %collective-permute-start.40) | collective-permute-done | bytes 28704 | tf_op jit(solution)/shard_map/ppermute | solution.py:355
  440.1 3.8 collective-permute-start.52
  448.4 14.5 %collective-permute-done.52 = f32[14,64]{1,0:T(8,128)S(1)} collective-permute-done((f32[14,64]{1,0:T(8,128)S(1)}, f32[14,64]{1,0:T(8,128)S(1)}, u32[]{:S(2)}, u32[]{:S(2)}) %collective-permute-start.52) | collective-permute-done | bytes 3616 | tf_op jit(solution)/shard_map/ppermute | solution.py:355
  (425 shorter events, 213.0 us)
Async XLA Ops:
  11.2 46.2 %all-to-all-start = ((bf16[8,80,768]{2,1,0:T(8,128)(2,1)}), bf16[8,80,768]{2,1,0:T(8,128)(2,1)S(1)}, u32[]{:S(2)}, u32[]{:S(2)}) async-start(bf16[8,80,768]{2,1,0:T(8,128)(2,1)} %deal_columns.1), calls=%async_computation | async-start | bytes 1966080 | tf_op jit(solution)/shard_map/all_to_all | solution.py:509
  17.5 60.8 %all-gather.9.cloned.1.call-start = ((), (), s32[]{:S(2)}) async-start(), calls=%async_computation.12 | async-start | bytes 4718592 | tf_op jit(solution)/shard_map/all_gather | solution.py:405
  17.6 31.1 %collective-permute-start.3 = (bf16[176,2048]{1,0:T(8,128)(2,1)S(1)}, bf16[176,2048]{1,0:T(8,128)(2,1)S(1)}, u32[]{:S(2)}, u32[]{:S(2)}) collective-permute-start(bf16[176,2048]{1,0:T(8,128)(2,1)S(1)} %bitcast.142), channel_id=1, source_target_pairs={{0,8},{8,0},{16,24},{24,16},{1,9},{9,1},{17,25},{25,17},{2,10},{10... | collective-permute-start | bytes 2162696 | tf_op jit(solution)/shard_map/ppermute | solution.py:355
  19.2 29.6 %collective-permute-start.4 = (bf16[176,2048]{1,0:T(8,128)(2,1)S(1)}, bf16[176,2048]{1,0:T(8,128)(2,1)S(1)}, u32[]{:S(2)}, u32[]{:S(2)}) collective-permute-start(bf16[176,2048]{1,0:T(8,128)(2,1)S(1)} %bitcast.143), channel_id=1, source_target_pairs={{0,16},{8,24},{16,0},{24,8},{1,17},{9,25},{17,1},{25,9},{2,18},{10... | collective-permute-start | bytes 2162696 | tf_op jit(solution)/shard_map/ppermute | solution.py:355
  20.7 21.7 %collective-permute-start = (bf16[64,2048]{1,0:T(8,128)(2,1)}, bf16[64,2048]{1,0:T(8,128)(2,1)}, u32[]{:S(2)}, u32[]{:S(2)}) collective-permute-start(bf16[64,2048]{1,0:T(8,128)(2,1)} %param.23), channel_id=1, source_target_pairs={{0,8},{8,0},{16,24},{24,16},{1,9},{9,1},{17,25},{25,17},{2,10},{10... | collective-permute-start | bytes 786440 | tf_op jit(solution)/shard_map/ppermute | solution.py:355
  21.2 27.5 %collective-permute-start.1 = (bf16[64,2048]{1,0:T(8,128)(2,1)}, bf16[64,2048]{1,0:T(8,128)(2,1)}, u32[]{:S(2)}, u32[]{:S(2)}) collective-permute-start(bf16[64,2048]{1,0:T(8,128)(2,1)} %param.23), channel_id=1, source_target_pairs={{0,16},{8,24},{16,0},{24,8},{1,17},{9,25},{17,1},{25,9},{2,18},{10... | collective-permute-start | bytes 786440 | tf_op jit(solution)/shard_map/ppermute | solution.py:355
  21.7 27.0 %collective-permute-start.2 = (bf16[64,2048]{1,0:T(8,128)(2,1)}, bf16[64,2048]{1,0:T(8,128)(2,1)}, u32[]{:S(2)}, u32[]{:S(2)}) collective-permute-start(bf16[64,2048]{1,0:T(8,128)(2,1)} %param.23), channel_id=1, source_target_pairs={{0,24},{8,16},{16,8},{24,0},{1,25},{9,17},{17,9},{25,1},{2,26},{10... | collective-permute-start | bytes 786440 | tf_op jit(solution)/shard_map/ppermute | solution.py:355
  24.2 156.9 %reduce-scatter.5.cloned.1.call-start = ((), (), s32[]{:S(2)}) async-start(), calls=%async_computation.6 | async-start | bytes 4718592 | tf_op jit(solution)/shard_map/reduce_scatter | solution.py:409
  61.1 30.7 %collective-permute-start.5 = (bf16[512,768]{1,0:T(8,128)(2,1)S(1)}, bf16[512,768]{1,0:T(8,128)(2,1)S(1)}, u32[]{:S(2)}, u32[]{:S(2)}) collective-permute-start(bf16[512,768]{1,0:T(8,128)(2,1)S(1)} %bitcast.126), channel_id=1, source_target_pairs={{0,8},{8,0},{16,24},{24,16},{1,9},{9,1},{17,25},{25,17},{2,10},{10... | collective-permute-start | bytes 2359304 | tf_op jit(solution)/shard_map/ppermute | solution.py:355
  62.7 29.1 %collective-permute-start.6 = (bf16[512,768]{1,0:T(8,128)(2,1)S(1)}, bf16[512,768]{1,0:T(8,128)(2,1)S(1)}, u32[]{:S(2)}, u32[]{:S(2)}) collective-permute-start(bf16[512,768]{1,0:T(8,128)(2,1)S(1)} %bitcast.127), channel_id=1, source_target_pairs={{0,16},{8,24},{16,0},{24,8},{1,17},{9,25},{17,1},{25,9},{2,18},{10... | collective-permute-start | bytes 2359304 | tf_op jit(solution)/shard_map/ppermute | solution.py:355
  80.1 51.8 %collective-permute-start.12 = (bf16[128,2048]{1,0:T(8,128)(2,1)}, bf16[128,2048]{1,0:T(8,128)(2,1)}, u32[]{:S(2)}, u32[]{:S(2)}) collective-permute-start(bf16[128,2048]{1,0:T(8,128)(2,1)} %bitcast.17), channel_id=1, source_target_pairs={{0,4},{1,5},{2,6},{3,7},{4,0},{5,1},{6,2},{7,3},{8,12},{9,13},{10,... | collective-permute-start | bytes 1572872 | tf_op jit(solution)/shard_map/ppermute | solution.py:355
  80.1 51.8 %collective-permute-start.13 = (bf16[128,2048]{1,0:T(8,128)(2,1)}, bf16[128,2048]{1,0:T(8,128)(2,1)}, u32[]{:S(2)}, u32[]{:S(2)}) collective-permute-start(bf16[128,2048]{1,0:T(8,128)(2,1)} %bitcast.17), channel_id=1, source_target_pairs={{0,6},{1,7},{2,4},{3,5},{4,2},{5,3},{6,0},{7,1},{8,14},{9,15},{10,... | collective-permute-start | bytes 1572872 | tf_op jit(solution)/shard_map/ppermute | solution.py:355
  109.4 22.5 %collective-permute-start.14 = (bf16[128,2048]{1,0:T(8,128)(2,1)}, bf16[128,2048]{1,0:T(8,128)(2,1)}, u32[]{:S(2)}, u32[]{:S(2)}) collective-permute-start(bf16[128,2048]{1,0:T(8,128)(2,1)} %bitcast.17), channel_id=1, source_target_pairs={{0,2},{1,3},{2,0},{3,1},{4,6},{5,7},{6,4},{7,5},{8,10},{9,11},{10,... | collective-permute-start | bytes 1572872 | tf_op jit(solution)/shard_map/ppermute | solution.py:355
  132.0 99.4 %all-gather.5.cloned.1.call-start = ((), (), s32[]{:S(2)}) async-start(), calls=%async_computation.7 | async-start | bytes 4718592 | tf_op jit(solution)/shard_map/all_gather | solution.py:405
  146.7 35.6 %collective-permute-start.17 = (bf16[176,2048]{1,0:T(8,128)(2,1)}, bf16[176,2048]{1,0:T(8,128)(2,1)S(1)}, u32[]{:S(2)}, u32[]{:S(2)}) collective-permute-start(bf16[176,2048]{1,0:T(8,128)(2,1)} %bitcast.144), channel_id=1, source_target_pairs={{0,8},{8,0},{16,24},{24,16},{1,9},{9,1},{17,25},{25,17},{2,10},{10... | collective-permute-start | bytes 2162696 | tf_op jit(solution)/shard_map/ppermute | solution.py:355
  148.2 35.0 %collective-permute-start.18 = (bf16[176,2048]{1,0:T(8,128)(2,1)}, bf16[176,2048]{1,0:T(8,128)(2,1)}, u32[]{:S(2)}, u32[]{:S(2)}) collective-permute-start(bf16[176,2048]{1,0:T(8,128)(2,1)} %bitcast.145), channel_id=1, source_target_pairs={{0,16},{8,24},{16,0},{24,8},{1,17},{9,25},{17,1},{25,9},{2,18},{10... | collective-permute-start | bytes 2162696 | tf_op jit(solution)/shard_map/ppermute | solution.py:355
  186.0 115.5 %reduce-scatter.7.cloned.1.call-start = ((), (), s32[]{:S(2)}) async-start(), calls=%async_computation.8 | async-start | bytes 4718592 | tf_op jit(solution)/shard_map/reduce_scatter | solution.py:409
  186.0 25.2 %collective-permute-start.20 = (bf16[176,2048]{1,0:T(8,128)(2,1)}, bf16[176,2048]{1,0:T(8,128)(2,1)S(1)}, u32[]{:S(2)}, u32[]{:S(2)}) collective-permute-start(bf16[176,2048]{1,0:T(8,128)(2,1)} %param.28), channel_id=1, source_target_pairs={{0,8},{8,0},{16,24},{24,16},{1,9},{9,1},{17,25},{25,17},{2,10},{10... | collective-permute-start | bytes 2162696 | tf_op jit(solution)/shard_map/ppermute | solution.py:355
  187.5 23.6 %collective-permute-start.21 = (bf16[176,2048]{1,0:T(8,128)(2,1)}, bf16[176,2048]{1,0:T(8,128)(2,1)S(1)}, u32[]{:S(2)}, u32[]{:S(2)}) collective-permute-start(bf16[176,2048]{1,0:T(8,128)(2,1)} %param.28), channel_id=1, source_target_pairs={{0,16},{8,24},{16,0},{24,8},{1,17},{9,25},{17,1},{25,9},{2,18},{10... | collective-permute-start | bytes 2162696 | tf_op jit(solution)/shard_map/ppermute | solution.py:355
  251.9 100.2 %all-gather.7.cloned.1.call-start = ((), (), s32[]{:S(2)}) async-start(), calls=%async_computation.9 | async-start | bytes 4718592 | tf_op jit(solution)/shard_map/all_gather | solution.py:405
  278.8 23.8 %collective-permute-start.29 = (bf16[176,2048]{1,0:T(8,128)(2,1)}, bf16[176,2048]{1,0:T(8,128)(2,1)S(1)}, u32[]{:S(2)}, u32[]{:S(2)}) collective-permute-start(bf16[176,2048]{1,0:T(8,128)(2,1)} %pad_maximum_fusion.6), channel_id=1, source_target_pairs={{0,16},{8,24},{16,0},{24,8},{1,17},{9,25},{17,1},{25,9},{2,18},{10... | collective-permute-start | bytes 2162696 | tf_op jit(solution)/shard_map/ppermute | solution.py:355
  281.4 21.3 %collective-permute-start.28 = (bf16[176,2048]{1,0:T(8,128)(2,1)}, bf16[176,2048]{1,0:T(8,128)(2,1)}, u32[]{:S(2)}, u32[]{:S(2)}) collective-permute-start(bf16[176,2048]{1,0:T(8,128)(2,1)} %pad_maximum_fusion.5), channel_id=1, source_target_pairs={{0,8},{8,0},{16,24},{24,16},{1,9},{9,1},{17,25},{25,17},{2,10},{10... | collective-permute-start | bytes 2162696 | tf_op jit(solution)/shard_map/ppermute | solution.py:355
  306.6 113.0 %reduce-scatter.11.cloned.1.call-start = ((), (), s32[]{:S(2)}) async-start(), calls=%async_computation.11 | async-start | bytes 4718592 | tf_op jit(solution)/shard_map/reduce_scatter | solution.py:409
  320.3 20.6 %collective-permute-start.33 = (bf16[176,2048]{1,0:T(8,128)(2,1)S(1)}, bf16[176,2048]{1,0:T(8,128)(2,1)}, u32[]{:S(2)}, u32[]{:S(2)}) collective-permute-start(bf16[176,2048]{1,0:T(8,128)(2,1)S(1)} %pad_maximum_fusion.8), channel_id=1, source_target_pairs={{0,16},{8,24},{16,0},{24,8},{1,17},{9,25},{17,1},{25,9},{2,18},{10... | collective-permute-start | bytes 2162696 | tf_op jit(solution)/shard_map/ppermute | solution.py:355
  352.1 118.1 %reduce-scatter.9.cloned.1.call-start = ((), (), s32[]{:S(2)}) async-start(), calls=%async_computation.10 | async-start | bytes 4718592 | tf_op jit(solution)/shard_map/reduce_scatter | solution.py:409
  397.4 23.4 %collective-permute-start.43 = (bf16[512,768]{1,0:T(8,128)(2,1)}, bf16[512,768]{1,0:T(8,128)(2,1)}, u32[]{:S(2)}, u32[]{:S(2)}) collective-permute-start(bf16[512,768]{1,0:T(8,128)(2,1)} %get-tuple-element.268), channel_id=1, source_target_pairs={{0,24},{8,16},{16,8},{24,0},{1,25},{9,17},{17,9},{25,1},{2,26},{10... | collective-permute-start | bytes 2359304 | tf_op jit(solution)/shard_map/ppermute | solution.py:355
  423.8 20.0 %collective-permute-start.48 = (f32[14,64]{1,0:T(8,128)}, f32[14,64]{1,0:T(8,128)}, u32[]{:S(2)}, u32[]{:S(2)}) collective-permute-start(f32[14,64]{1,0:T(8,128)} %get-tuple-element.302), channel_id=1, source_target_pairs={{0,2},{1,3},{2,0},{3,1},{4,6},{5,7},{6,4},{7,5},{8,10},{9,11},{10,... | collective-permute-start | bytes 10760 | tf_op jit(solution)/shard_map/ppermute | solution.py:355
  423.8 20.0 %collective-permute-start.49 = (f32[14,64]{1,0:T(8,128)}, f32[14,64]{1,0:T(8,128)}, u32[]{:S(2)}, u32[]{:S(2)}) collective-permute-start(f32[14,64]{1,0:T(8,128)} %get-tuple-element.303), channel_id=1, source_target_pairs={{0,3},{1,2},{2,1},{3,0},{4,7},{5,6},{6,5},{7,4},{8,11},{9,10},{10,... | collective-permute-start | bytes 10760 | tf_op jit(solution)/shard_map/ppermute | solution.py:355
  426.7 19.9 %collective-permute-start.51 = (f32[14,64]{1,0:T(8,128)}, f32[14,64]{1,0:T(8,128)}, u32[]{:S(2)}, u32[]{:S(2)}) collective-permute-start(f32[14,64]{1,0:T(8,128)} %get-tuple-element.305), channel_id=1, source_target_pairs={{0,5},{1,4},{2,7},{3,6},{4,1},{5,0},{6,3},{7,2},{8,13},{9,12},{10,... | collective-permute-start | bytes 10760 | tf_op jit(solution)/shard_map/ppermute | solution.py:355
  428.2 37.9 %all-to-all-start.1 = ((bf16[8,64,768]{2,1,0:T(8,128)(2,1)}), bf16[8,64,768]{2,1,0:T(8,128)(2,1)S(1)}, u32[]{:S(2)}, u32[]{:S(2)}) async-start(bf16[8,64,768]{2,1,0:T(8,128)(2,1)} %bitcast.39), calls=%async_computation.5 | async-start | bytes 1572864 | tf_op jit(solution)/shard_map/all_to_all | solution.py:665
  440.1 22.8 %collective-permute-start.52 = (f32[14,64]{1,0:T(8,128)S(1)}, f32[14,64]{1,0:T(8,128)S(1)}, u32[]{:S(2)}, u32[]{:S(2)}) collective-permute-start(f32[14,64]{1,0:T(8,128)S(1)} %copy-done.57), channel_id=1, source_target_pairs={{0,6},{1,7},{2,4},{3,5},{4,2},{5,3},{6,0},{7,1},{8,14},{9,15},{10,... | collective-permute-start | bytes 10760 | tf_op jit(solution)/shard_map/ppermute | solution.py:355
  443.9 19.8 %collective-permute-start.44 = (bf16[64,2048]{1,0:T(8,128)(2,1)S(1)}, bf16[64,2048]{1,0:T(8,128)(2,1)S(1)}, u32[]{:S(2)}, u32[]{:S(2)}) collective-permute-start(bf16[64,2048]{1,0:T(8,128)(2,1)S(1)} %copy-done.50), channel_id=1, source_target_pairs={{0,8},{8,0},{16,24},{24,16},{1,9},{9,1},{17,25},{25,17},{2,10},{10... | collective-permute-start | bytes 786440 | tf_op jit(solution)/shard_map/ppermute | solution.py:355
  (101 other events, 1145.1 us)
Sparse Core Ops, SparseCore 0:
  24.3 53.9 all-gather.8
  132.1 49.0 reduce-scatter.4
  186.1 45.2 all-gather.4
  252.0 49.3 reduce-scatter.6
  306.8 45.2 all-gather.6
  354.3 48.7 reduce-scatter.10
  405.3 61.8 reduce-scatter.8

commit v8 on v7

--- a/solution.py
+++ b/solution.py
@@ -257,6 +257,51 @@
 SMALL_COST = pl.CostEstimate(flops=1, bytes_accessed=1, transcendentals=1)
 
 
+def middle_kernel(resid_ref, terms_ref, gain_ref, bias_ref, sum_ref, normed_ref):
+    values = resid_ref[...] + terms_ref[...].astype(jnp.float32)
+    sum_ref[...] = values
+    normed_ref[...] = norm_forward(values, gain_ref[...], bias_ref[...])[0].astype(jnp.bfloat16)
+
+
+def middle_norm(resid, terms, gain, bias):
+    return pl.pallas_call(
+        middle_kernel,
+        out_shape=(
+            jax.ShapeDtypeStruct(resid.shape, jnp.float32),
+            jax.ShapeDtypeStruct(resid.shape, jnp.bfloat16),
+        ),
+        compiler_params=pltpu.CompilerParams(vmem_limit_bytes=VMEM_BYTES),
+        cost_estimate=SMALL_COST,
+        name="middle_norm",
+    )(resid, terms, gain[None], bias[None])
+
+
+def branch_kernel(base_ref, terms_ref, values_ref, gain_ref, grad_ref, branch_ref, sums_ref):
+    unused, scaled, inverse = norm_forward(values_ref[...], 1.0, 0.0)
+    grad_values, gain_sum, bias_sum = norm_backward(
+        terms_ref[...].astype(jnp.float32), scaled, inverse, gain_ref[...]
+    )
+    grads = base_ref[...].astype(jnp.float32) + grad_values
+    grad_ref[...] = grads
+    branch_ref[...] = grads.astype(jnp.bfloat16)
+    sums_ref[0:1] = gain_sum[None]
+    sums_ref[1:2] = bias_sum[None]
+
+
+def branch_norm(base, terms, values, gain):
+    return pl.pallas_call(
+        branch_kernel,
+        out_shape=(
+            jax.ShapeDtypeStruct(values.shape, jnp.float32),
+            jax.ShapeDtypeStruct(values.shape, jnp.bfloat16),
+            jax.ShapeDtypeStruct((2, values.shape[1]), jnp.float32),
+        ),
+        compiler_params=pltpu.CompilerParams(vmem_limit_bytes=VMEM_BYTES),
+        cost_estimate=SMALL_COST,
+        name="branch_norm",
+    )(base, terms, values, gain[None])
+
+
 def norm_sums_kernel(values_ref, terms_ref, lang_ref, gain_ref, out_ref):
     @pl.when(pl.program_id(0) == 0)
     def clear():
@@ -408,7 +453,7 @@
 def scatter_seq(terms):
     return lax.psum_scatter(
         terms.astype(jnp.bfloat16), "seq", scatter_dimension=0, tiled=True
-    ).astype(jnp.float32)
+    )
 
 
 def after(value, *others):
@@ -530,7 +575,6 @@
     tables = rotation_tables(cosines, sines, min(128, local_width))
     first = offsets[None, :]
     resid_in = layer_input[0].astype(jnp.float32) + lang_row
-    unused, scaled_attn, inverse_attn = norm_forward(resid_in, gain_attn, bias_attn)
     normed_all = norm_forward(input_all.astype(jnp.float32) + lang_row, gain_attn, bias_attn)[
         0
     ].astype(jnp.bfloat16)
@@ -557,9 +601,8 @@
     attn_out, gate_pieces, up_pieces, grad_all, down_rows = phase(
         (attn_out, gate_pieces, up_pieces, grad_all, down_weight)
     )
-    resid_mid = resid_in + attn_out
-    normed_mlp, scaled_mlp, inverse_mlp = norm_forward(resid_mid, gain_mlp, bias_mlp)
-    rows_all = gather_seq(normed_mlp.astype(jnp.bfloat16))
+    resid_mid, normed_mlp = middle_norm(resid_in, attn_out, gain_mlp, bias_mlp)
+    rows_all = gather_seq(normed_mlp)
     up_pieces = up_pieces + [corner_dp(up_pieces)]
     down_pieces = near_dp(down_rows)
     down_pieces, up_pieces = phase((down_pieces, up_pieces))
@@ -593,11 +636,10 @@
     grad_normed_mlp, gate_near, up_terms, mlp_terms, down_terms = phase(
         (grad_normed_mlp, gate_near, up_terms, mlp_terms, down_terms)
     )
-    grad_mid_norm, grad_gain_mlp, grad_bias_mlp = norm_backward(
-        grad_normed_mlp, scaled_mlp, inverse_mlp, gain_mlp
-    )
-    grad_mid = grad_out.astype(jnp.float32) + grad_mid_norm
-    branch_all = gather_seq(grad_mid.astype(jnp.bfloat16))
+    grad_mid, grad_branch, mlp_norm_sums = branch_norm(
+        grad_out, grad_normed_mlp, resid_mid, gain_mlp
+    )
+    branch_all = gather_seq(grad_branch)
     up_terms = jnp.split(up_terms, rows, axis=0)
     down_terms = jnp.split(down_terms, rows, axis=0)
     up_corner = send_corner(up_terms)
@@ -621,12 +663,16 @@
     slice_near = [permute(slice_pieces[k], "dp", k) for k in range(1, rows - 1)]
     attn_terms = contract(grad_stack, head_qkv, 1, 1).astype(jnp.bfloat16)
     sums = norm_sums(input_all, attn_terms, lang_row, gain_attn)
+    attn_terms, sums, slice_near, slice_pieces, branch_all, up_near, gate_near, grad_stack = phase(
+        (attn_terms, sums, slice_near, slice_pieces, branch_all, up_near, gate_near, grad_stack)
+    )
+    grad_normed_attn = scatter_seq(attn_terms)
+    slice_far = permute(slice_pieces[-1], "dp", rows - 1)
     grad_bias_qkv = jnp.sum(grad_stack.astype(jnp.float32), axis=0).reshape(3, local_width)
     terms = jnp.concatenate(
         [
             sums[:2],
-            grad_gain_mlp[None],
-            grad_bias_mlp[None],
+            mlp_norm_sums,
             from_heads(grad_bias_qkv),
             chooser[:, None] * (jnp.sum(grad_mid, axis=0) + sums[2])[None],
         ],
@@ -644,11 +690,6 @@
         return total([parts[0]] + [permute(parts[k], axis, k) for k in range(1, len(parts))])
 
     terms = small_parts(terms.reshape(count, rows, groups, own).transpose(1, 2, 0, 3), at_dp)
-    attn_terms, terms, slice_near, slice_pieces, branch_all, up_near, gate_near = phase(
-        (attn_terms, terms, slice_near, slice_pieces, branch_all, up_near, gate_near)
-    )
-    grad_normed_attn = scatter_seq(attn_terms)
-    slice_far = permute(slice_pieces[-1], "dp", rows - 1)
     terms = small_parts(small_sum(terms, "dp"), at_seq)
     out_pieces = dp_terms(contract(context_all, branch_all, 0, 0).astype(jnp.bfloat16))
     terms, slice_far, mlp_out, out_pieces, down_near, up_near, gate_near = phase(
@@ -685,9 +726,7 @@
     grad_normed_attn, grad_qkv_out, out_proj, out_gate, out_up, out_down, layer_output = phase(
         (grad_normed_attn, grad_qkv_out, out_proj, out_gate, out_up, out_down, layer_output)
     )
-    grad_input = grad_mid + norm_backward(
-        grad_normed_attn, scaled_attn, inverse_attn, gain_attn
-    )[0]
+    grad_input = branch_norm(grad_mid, grad_normed_attn, resid_in, gain_attn)[0]
     return (
         layer_output[None],
         grad_input[None],

time: 488 us -> 484 us (level)
  other arithmetic: 59.5 us -> 43.9 us
  waiting for transfers between devices: 152 us -> 161 us
  Pallas kernels: 31.8 us -> 37.8 us
    ppermute x54, waiting for transfers between devices: 91.8 us -> 109 us  [permute(): return lax.ppermute(value, axis, [(i, i ^ offset) for i in range(size)])]
    reduce_scatter x4, waiting for transfers between devices: 30.9 us -> 19.1 us  [scatter_seq(): lax.psum_scatter(terms.astype(jnp.bfloat16), 'seq', scatter_dimension=0,...]
    convert_element_type x6 -> x0, other arithmetic: 6.46 us -> none  [the longest x4 4.55 us: scatter_seq(): return lax.psum_scatter(terms.astype(jnp.bfloat16), 'seq', scatter_dimens...]
    unnamed x147 -> x149, local copies, waits for them, and re-layouts: 15 us -> 21 us
    pallas_call x0 -> x3, Pallas kernels: none -> 6.01 us  [the longest x2 4.81 us: branch_norm(): pl.pallas_call(branch_kernel, out_shape=(jax.ShapeDtypeStruct(values.shap...]
    all_gather x3, waiting for transfers between devices: 17.6 us -> 23 us  [gather_seq(): return lax.all_gather(piece, 'seq', axis=0, tiled=True)]
  transfers between devices with their start and end apart: 63 -> 63, of which waited for: 28 -> 30; matrix products, arithmetic and copies ran while one was open for 33% -> 30% of each run, Pallas kernels for 6% -> 6%
where the time goes in v8:
time: 484 us; the launch traced here: 476 us
  waiting for transfers between devices  161 us (33%)
  matrix products  73.7 us (15%)
  starting transfers between devices  73.1 us (15%)
  local copies, waits for them, and re-layouts  70.1 us (14%)
  other arithmetic  43.9 us (9%)
  Pallas kernels  37.8 us (8%)
  between operations  16.7 us (3%)
    ppermute x54, waiting for transfers between devices, permute(): return lax.ppermute(value, axis, [(i, i ^ offset) for i in range(size)])  109 us
    dot_general x13, matrix products, contract(): lax.dot_general(left, right, (((left_dim,), (right_dim,)), ((), ())), pre...  66.7 us
    ppermute x54, starting transfers between devices, permute(): return lax.ppermute(value, axis, [(i, i ^ offset) for i in range(size)])  62.7 us
    all_gather x3, waiting for transfers between devices, gather_seq(): return lax.all_gather(piece, 'seq', axis=0, tiled=True)  23 us
    dynamic_update_slice x19, local copies, waits for them, and re-layouts, place(): lax.dynamic_update_slice_in_dim(result, piece, (index ^ k) * block, 0)  21.6 us
    unnamed x149, local copies, waits for them, and re-layouts  21 us
    reduce_scatter x4, waiting for transfers between devices, scatter_seq(): lax.psum_scatter(terms.astype(jnp.bfloat16), 'seq', scatter_dimension=0,...  19.1 us
    add x6, other arithmetic, total(): result = result + piece.astype(jnp.float32)  11.2 us
  transfers between devices with their start and end apart: 63, of which 30 were waited for; matrix products, arithmetic and copies ran while one was open for 30% of the time, Pallas kernels for 6%

profile of v8, /device:TPU:0, one launch (start us, length us, event | category | flops | bytes accessed | tf_op | source)
XLA Modules:
  0.0 476.1 jit_solution(3796993591858824744)
XLA Ops:
  11.2 6.3 %all-to-all-start = ((bf16[8,80,768]{2,1,0:T(8,128)(2,1)}), bf16[8,80,768]{2,1,0:T(8,128)(2,1)S(1)}, u32[]{:S(2)}, u32[]{:S(2)}) async-start(bf16[8,80,768]{2,1,0:T(8,128)(2,1)} %deal_columns.1), calls=%async_computation | async-start | bytes 1966080 | tf_op jit(solution)/shard_map/all_to_all | solution.py:554
  26.6 15.9 %collective-permute-done = bf16[64,2048]{1,0:T(8,128)(2,1)} collective-permute-done((bf16[64,2048]{1,0:T(8,128)(2,1)S(1)}, bf16[64,2048]{1,0:T(8,128)(2,1)}, u32[]{:S(2)}, u32[]{:S(2)}) %collective-permute-start) | collective-permute-done | bytes 262176 | tf_op jit(solution)/shard_map/ppermute | solution.py:400
  42.5 6.4 %collective-permute-done.1 = bf16[64,2048]{1,0:T(8,128)(2,1)} collective-permute-done((bf16[64,2048]{1,0:T(8,128)(2,1)S(1)}, bf16[64,2048]{1,0:T(8,128)(2,1)}, u32[]{:S(2)}, u32[]{:S(2)}) %collective-permute-start.1) | collective-permute-done | bytes 262176 | tf_op jit(solution)/shard_map/ppermute | solution.py:400
  48.9 8.5 %all-to-all-done = bf16[8,80,768]{2,1,0:T(8,128)(2,1)S(1)} async-done(((bf16[8,80,768]{2,1,0:T(8,128)(2,1)}), bf16[8,80,768]{2,1,0:T(8,128)(2,1)S(1)}, u32[]{:S(2)}, u32[]{:S(2)}) %all-to-all-start) | async-done | bytes 983072 | tf_op jit(solution)/shard_map/all_to_all | solution.py:554
  71.3 7.0 %all-gather.9.cloned.1.call-done = bf16[1,1024,2048]{2,1,0:T(8,128)(2,1)} async-done(((bf16[1,128,2048]{2,1,0:T(8,128)(2,1)}), bf16[1,1024,2048]{2,1,0:T(8,128)(2,1)}) %all-gather.9.cloned.1.call-update) | async-done | bytes 4194320 | tf_op jit(solution)/shard_map/all_gather | solution.py:450
  99.9 4.0 add_convert_fusion.1
  114.1 9.8 %attention_forward.1 = (bf16[1024,256]{1,0:T(8,128)(2,1)S(1)}, bf16[1024,256]{1,0:T(8,128)(2,1)S(1)}, bf16[1024,256]{1,0:T(8,128)(2,1)S(1)}, f32[4,1024]{1,0:T(4,128)S(1)}) custom-call(bf16[1024,768]{1,0:T(8,128)(2,1)S(1)} %add_convert_fusion.2.qkv_ref, f32[1024,128]{1,0:T(8,128)S(1)} %copy.52.cos_ref, f32[1024,128]{1,0:T(8,128)S(1)} %copy-done.3, ...), custom_call_target="tpu_custom_call" | custom-call | flops 1 | bytes 1 | tf_op jit(solution)/shard_map/attention_forward/pallas_call | solution.py:355
  136.0 8.1 %collective-permute-done.15 = bf16[88,2048]{1,0:T(8,128)(2,1)S(1)} collective-permute-done((bf16[88,2048]{1,0:T(8,128)(2,1)S(1)}, bf16[88,2048]{1,0:T(8,128)(2,1)S(1)}, u32[]{:S(2)}, u32[]{:S(2)}) %collective-permute-start.15) | collective-permute-done | bytes 360480 | tf_op jit(solution)/shard_map/ppermute | solution.py:400
  163.8 14.1 %reduce-scatter.5.cloned.1.call-done.terms_ref = bf16[128,2048]{1,0:T(8,128)(2,1)} async-done(((bf16[1024,2048]{1,0:T(8,128)(2,1)}), bf16[128,2048]{1,0:T(8,128)(2,1)}) %reduce-scatter.5.cloned.1.call-update) | async-done | bytes 524304 | tf_op jit(solution)/shard_map/reduce_scatter | solution.py:454
  189.5 14.4 %collective-permute-done.22 = bf16[88,2048]{1,0:T(8,128)(2,1)S(1)} collective-permute-done((bf16[88,2048]{1,0:T(8,128)(2,1)S(1)}, bf16[88,2048]{1,0:T(8,128)(2,1)S(1)}, u32[]{:S(2)}, u32[]{:S(2)}) %collective-permute-start.22) | collective-permute-done | bytes 360480 | tf_op jit(solution)/shard_map/ppermute | solution.py:400
  207.5 5.3 %pad_maximum_fusion.1 = bf16[704,2048]{1,0:T(8,128)(2,1)} fusion(bf16[176,2048]{1,0:T(8,128)(2,1)S(1)} %pad_maximum_fusion.4, bf16[176,2048]{1,0:T(8,128)(2,1)} %collective-permute-done.18, bf16[176,2048]{1,0:T(8,128)(2,1)S(1)} %copy-done.46, bf16[176,2048]{1,0:T(8,128)(2,1)S(1)} %bitcast.140), kind=kLoop, calls=%fused_computation.16 | loop fusion | flops 11534336 | bytes 5767168 | tf_op jit(solution)/shard_map/concatenate | solution.py:611
  216.1 4.7 fusion.20
  220.8 4.8 %all-gather.5.cloned.1.call-done = bf16[1024,2048]{1,0:T(8,128)(2,1)} async-done(((bf16[128,2048]{1,0:T(8,128)(2,1)}), bf16[1024,2048]{1,0:T(8,128)(2,1)}) %all-gather.5.cloned.1.call-update) | async-done | bytes 4194320 | tf_op jit(solution)/shard_map/all_gather | solution.py:450
  225.6 6.0 %fusion.21 = f32[1024,704]{0,1:T(8,128)S(1)} fusion(bf16[1024,2048]{1,0:T(8,128)(2,1)} %all-gather.5.cloned.1.call-done, bf16[704,2048]{1,0:T(8,128)(2,1)} %pad_maximum_fusion), kind=kOutput, calls=%fused_computation.141 | convolution fusion | flops 2952790016 | bytes 9961472 | tf_op jit(solution)/shard_map/dot_general | solution.py:21
  231.6 5.8 %multiply_convert_fusion = (bf16[1024,704]{0,1:T(8,128)(2,1)}, bf16[1024,704]{0,1:T(8,128)(2,1)S(1)}, bf16[1024,704]{0,1:T(8,128)(2,1)S(1)}) fusion(f32[1024,704]{0,1:T(8,128)S(1)} %fusion.21, f32[1024,704]{0,1:T(8,128)S(1)} %copy-done.67, bf16[1024,2048]{1,0:T(8,128)(2,1)S(1)} %copy-done.64, bf16[704,2048]{1,0:T(8,128)(2,1)S(1)} %copy-done.33), kind=kOutput, calls=%fused_computation.17 | convolution fusion | flops 2963603456 | bytes 17170432 | tf_op jit(solution)/shard_map/dot_general | solution.py:21
  241.0 5.3 %add_convert_fusion = bf16[1024,2048]{1,0:T(8,128)(2,1)} fusion(f32[1024,2048]{1,0:T(8,128)S(1)} %fusion.22, bf16[1024,704]{0,1:T(8,128)(2,1)S(1)} %get-tuple-element.229, bf16[704,2048]{1,0:T(8,128)(2,1)S(1)} %copy-done.32), kind=kOutput, calls=%fused_computation | convolution fusion | flops 2956984320 | bytes 16908288 | tf_op jit(solution)/shard_map/dot_general | solution.py:21
  246.4 5.9 %convolution_convert_fusion.6 = bf16[704,2048]{1,0:T(8,128)(2,1)S(1)} fusion(bf16[1024,704]{0,1:T(8,128)(2,1)} %copy-done.68, bf16[1024,2048]{1,0:T(8,128)(2,1)} %all-gather.5.cloned.1.call-done), kind=kOutput, calls=%fused_computation.12 | convolution fusion | flops 2954231808 | bytes 8519680 | tf_op jit(solution)/shard_map/dot_general | solution.py:21
  257.7 5.3 %convolution_convert_fusion = bf16[1024,2048]{1,0:T(8,128)(2,1)} fusion(bf16[1024,704]{0,1:T(8,128)(2,1)S(1)} %copy-done.69, bf16[704,2048]{1,0:T(8,128)(2,1)S(1)} %copy-done.61), kind=kOutput, calls=%fused_computation.6 | convolution fusion | flops 2954887168 | bytes 8519680 | tf_op jit(solution)/shard_map/dot_general | solution.py:21
  263.0 7.5 %convolution_convert_fusion.5 = bf16[704,2048]{1,0:T(8,128)(2,1)} fusion(bf16[1024,704]{0,1:T(8,128)(2,1)} %copy-done.66, bf16[1024,2048]{1,0:T(8,128)(2,1)} %all-gather.5.cloned.1.call-done), kind=kOutput, calls=%fused_computation.11 | convolution fusion | flops 2954231808 | bytes 8519680 | tf_op jit(solution)/shard_map/dot_general | solution.py:21
  274.3 4.5 convolution_convert_fusion.4
  278.8 10.9 %collective-permute-done.29 = bf16[176,2048]{1,0:T(8,128)(2,1)} collective-permute-done((bf16[176,2048]{1,0:T(8,128)(2,1)S(1)}, bf16[176,2048]{1,0:T(8,128)(2,1)}, u32[]{:S(2)}, u32[]{:S(2)}) %collective-permute-start.29) | collective-permute-done | bytes 720928 | tf_op jit(solution)/shard_map/ppermute | solution.py:400
  290.2 5.0 %reduce-scatter.7.cloned.1.call-done.terms_ref = bf16[128,2048]{1,0:T(8,128)(2,1)} async-done(((bf16[1024,2048]{1,0:T(8,128)(2,1)}), bf16[128,2048]{1,0:T(8,128)(2,1)}) %reduce-scatter.7.cloned.1.call-update) | async-done | bytes 524304 | tf_op jit(solution)/shard_map/reduce_scatter | solution.py:454
  316.1 6.6 %collective-permute-done.35 = bf16[88,2048]{1,0:T(8,128)(2,1)S(1)} collective-permute-done((bf16[88,2048]{1,0:T(8,128)(2,1)S(1)}, bf16[88,2048]{1,0:T(8,128)(2,1)S(1)}, u32[]{:S(2)}, u32[]{:S(2)}) %collective-permute-start.35) | collective-permute-done | bytes 360480 | tf_op jit(solution)/shard_map/ppermute | solution.py:400
  325.3 9.0 %collective-permute-done.33 = bf16[176,2048]{1,0:T(8,128)(2,1)} collective-permute-done((bf16[176,2048]{1,0:T(8,128)(2,1)S(1)}, bf16[176,2048]{1,0:T(8,128)(2,1)}, u32[]{:S(2)}, u32[]{:S(2)}) %collective-permute-start.33) | collective-permute-done | bytes 720928 | tf_op jit(solution)/shard_map/ppermute | solution.py:400
  334.3 11.2 %all-gather.7.cloned.1.call-done = bf16[1024,2048]{1,0:T(8,128)(2,1)} async-done(((bf16[128,2048]{1,0:T(8,128)(2,1)}), bf16[1024,2048]{1,0:T(8,128)(2,1)}) %all-gather.7.cloned.1.call-update) | async-done | bytes 4194320 | tf_op jit(solution)/shard_map/all_gather | solution.py:450
  352.4 11.0 %attention_backward.1 = bf16[1024,768]{1,0:T(8,128)(2,1)S(1)} custom-call(bf16[1024,256]{1,0:T(8,128)(2,1)S(1)} %copy-done.18, bf16[1024,256]{1,0:T(8,128)(2,1)S(1)} %copy-done.20, bf16[1024,768]{1,0:T(8,128)(2,1)} %copy-done.2, bf16[1024,256]{1,0:T(8,128)(2,1)S(1)} %convolution_convert_fusion.8.context_grad_ref, ...), custom_call_target="tpu_custom_call" | custom-call | flops 1 | bytes 1 | tf_op jit(solution)/shard_map/attention_backward/pallas_call | solution.py:373
  365.7 4.1 convolution_convert_fusion.3
  374.1 7.1 %convolution_convert_fusion.2.terms_ref = bf16[1024,2048]{1,0:T(8,128)(2,1)} fusion(bf16[1024,768]{1,0:T(8,128)(2,1)S(1)} %attention_backward.1, bf16[2048,768]{1,0:T(8,128)(2,1)} %copy-done.29), kind=kOutput, calls=%fused_computation.8 | convolution fusion | flops 3223322624 | bytes 8912896 | tf_op jit(solution)/shard_map/dot_general | solution.py:21
  383.4 8.3 %norm_sums.1 = f32[8,2048]{1,0:T(8,128)S(1)} custom-call(bf16[1024,2048]{1,0:T(8,128)(2,1)S(1)} %bitcast.119, bf16[1024,2048]{1,0:T(8,128)(2,1)} %convolution_convert_fusion.2.terms_ref, f32[1,2048]{1,0:T(1,128)S(1)} %bitcast.120, f32[1,2048]{1,0:T(1,128)S(1)} %slice.185.gain_ref), custom_call_target="tpu_custom_call" | custom-call | flops 1 | bytes 1 | tf_op jit(solution)/shard_map/norm_sums/pallas_call | solution.py:324
  403.4 11.3 %collective-permute-done.40 = f32[8,14,64]{2,1,0:T(8,128)S(1)} collective-permute-done((f32[8,14,64]{2,1,0:T(8,128)S(1)}, f32[8,14,64]{2,1,0:T(8,128)S(1)}, u32[]{:S(2)}, u32[]{:S(2)}) %collective-permute-start.40) | collective-permute-done | bytes 28704 | tf_op jit(solution)/shard_map/ppermute | solution.py:400
  436.2 3.7 collective-permute-start.52
  444.4 13.8 %collective-permute-done.52 = f32[14,64]{1,0:T(8,128)S(1)} collective-permute-done((f32[14,64]{1,0:T(8,128)S(1)}, f32[14,64]{1,0:T(8,128)S(1)}, u32[]{:S(2)}, u32[]{:S(2)}) %collective-permute-start.52) | collective-permute-done | bytes 3616 | tf_op jit(solution)/shard_map/ppermute | solution.py:400
  (410 shorter events, 207.8 us)
Async XLA Ops:
  11.2 46.2 %all-to-all-start = ((bf16[8,80,768]{2,1,0:T(8,128)(2,1)}), bf16[8,80,768]{2,1,0:T(8,128)(2,1)S(1)}, u32[]{:S(2)}, u32[]{:S(2)}) async-start(bf16[8,80,768]{2,1,0:T(8,128)(2,1)} %deal_columns.1), calls=%async_computation | async-start | bytes 1966080 | tf_op jit(solution)/shard_map/all_to_all | solution.py:554
  17.5 60.8 %all-gather.9.cloned.1.call-start = ((), (), s32[]{:S(2)}) async-start(), calls=%async_computation.12 | async-start | bytes 4718592 | tf_op jit(solution)/shard_map/all_gather | solution.py:450
  17.6 31.3 %collective-permute-start.3 = (bf16[176,2048]{1,0:T(8,128)(2,1)}, bf16[176,2048]{1,0:T(8,128)(2,1)S(1)}, u32[]{:S(2)}, u32[]{:S(2)}) collective-permute-start(bf16[176,2048]{1,0:T(8,128)(2,1)} %bitcast.4), channel_id=1, source_target_pairs={{0,8},{8,0},{16,24},{24,16},{1,9},{9,1},{17,25},{25,17},{2,10},{10... | collective-permute-start | bytes 2162696 | tf_op jit(solution)/shard_map/ppermute | solution.py:400
  19.1 29.8 %collective-permute-start.4 = (bf16[176,2048]{1,0:T(8,128)(2,1)}, bf16[176,2048]{1,0:T(8,128)(2,1)S(1)}, u32[]{:S(2)}, u32[]{:S(2)}) collective-permute-start(bf16[176,2048]{1,0:T(8,128)(2,1)} %bitcast.4), channel_id=1, source_target_pairs={{0,16},{8,24},{16,0},{24,8},{1,17},{9,25},{17,1},{25,9},{2,18},{10... | collective-permute-start | bytes 2162696 | tf_op jit(solution)/shard_map/ppermute | solution.py:400
  20.7 21.9 %collective-permute-start = (bf16[64,2048]{1,0:T(8,128)(2,1)S(1)}, bf16[64,2048]{1,0:T(8,128)(2,1)}, u32[]{:S(2)}, u32[]{:S(2)}) collective-permute-start(bf16[64,2048]{1,0:T(8,128)(2,1)S(1)} %copy-done.55), channel_id=1, source_target_pairs={{0,8},{8,0},{16,24},{24,16},{1,9},{9,1},{17,25},{25,17},{2,10},{10... | collective-permute-start | bytes 786440 | tf_op jit(solution)/shard_map/ppermute | solution.py:400
  21.2 27.7 %collective-permute-start.1 = (bf16[64,2048]{1,0:T(8,128)(2,1)S(1)}, bf16[64,2048]{1,0:T(8,128)(2,1)}, u32[]{:S(2)}, u32[]{:S(2)}) collective-permute-start(bf16[64,2048]{1,0:T(8,128)(2,1)S(1)} %copy-done.55), channel_id=1, source_target_pairs={{0,16},{8,24},{16,0},{24,8},{1,17},{9,25},{17,1},{25,9},{2,18},{10... | collective-permute-start | bytes 786440 | tf_op jit(solution)/shard_map/ppermute | solution.py:400
  21.7 27.2 %collective-permute-start.2 = (bf16[64,2048]{1,0:T(8,128)(2,1)S(1)}, bf16[64,2048]{1,0:T(8,128)(2,1)S(1)}, u32[]{:S(2)}, u32[]{:S(2)}) collective-permute-start(bf16[64,2048]{1,0:T(8,128)(2,1)S(1)} %copy-done.55), channel_id=1, source_target_pairs={{0,24},{8,16},{16,8},{24,0},{1,25},{9,17},{17,9},{25,1},{2,26},{10... | collective-permute-start | bytes 786440 | tf_op jit(solution)/shard_map/ppermute | solution.py:400
  24.2 153.7 %reduce-scatter.5.cloned.1.call-start = ((), (), s32[]{:S(2)}) async-start(), calls=%async_computation.6 | async-start | bytes 4718592 | tf_op jit(solution)/shard_map/reduce_scatter | solution.py:454
  61.2 26.1 %collective-permute-start.5 = (bf16[512,768]{1,0:T(8,128)(2,1)S(1)}, bf16[512,768]{1,0:T(8,128)(2,1)S(1)}, u32[]{:S(2)}, u32[]{:S(2)}) collective-permute-start(bf16[512,768]{1,0:T(8,128)(2,1)S(1)} %bitcast.123), channel_id=1, source_target_pairs={{0,8},{8,0},{16,24},{24,16},{1,9},{9,1},{17,25},{25,17},{2,10},{10... | collective-permute-start | bytes 2359304 | tf_op jit(solution)/shard_map/ppermute | solution.py:400
  62.7 24.5 %collective-permute-start.6 = (bf16[512,768]{1,0:T(8,128)(2,1)S(1)}, bf16[512,768]{1,0:T(8,128)(2,1)}, u32[]{:S(2)}, u32[]{:S(2)}) collective-permute-start(bf16[512,768]{1,0:T(8,128)(2,1)S(1)} %bitcast.124), channel_id=1, source_target_pairs={{0,16},{8,24},{16,0},{24,8},{1,17},{9,25},{17,1},{25,9},{2,18},{10... | collective-permute-start | bytes 2359304 | tf_op jit(solution)/shard_map/ppermute | solution.py:400
  78.3 51.6 %collective-permute-start.12 = (bf16[128,2048]{1,0:T(8,128)(2,1)}, bf16[128,2048]{1,0:T(8,128)(2,1)}, u32[]{:S(2)}, u32[]{:S(2)}) collective-permute-start(bf16[128,2048]{1,0:T(8,128)(2,1)} %bitcast.17.base_ref), channel_id=1, source_target_pairs={{0,4},{1,5},{2,6},{3,7},{4,0},{5,1},{6,2},{7,3},{8,12},{9,13},{10,... | collective-permute-start | bytes 1572872 | tf_op jit(solution)/shard_map/ppermute | solution.py:400
  78.3 51.6 %collective-permute-start.13 = (bf16[128,2048]{1,0:T(8,128)(2,1)}, bf16[128,2048]{1,0:T(8,128)(2,1)}, u32[]{:S(2)}, u32[]{:S(2)}) collective-permute-start(bf16[128,2048]{1,0:T(8,128)(2,1)} %bitcast.17.base_ref), channel_id=1, source_target_pairs={{0,6},{1,7},{2,4},{3,5},{4,2},{5,3},{6,0},{7,1},{8,14},{9,15},{10,... | collective-permute-start | bytes 1572872 | tf_op jit(solution)/shard_map/ppermute | solution.py:400
  108.2 21.7 %collective-permute-start.14 = (bf16[128,2048]{1,0:T(8,128)(2,1)}, bf16[128,2048]{1,0:T(8,128)(2,1)}, u32[]{:S(2)}, u32[]{:S(2)}) collective-permute-start(bf16[128,2048]{1,0:T(8,128)(2,1)} %bitcast.17.base_ref), channel_id=1, source_target_pairs={{0,2},{1,3},{2,0},{3,1},{4,6},{5,7},{6,4},{7,5},{8,10},{9,11},{10,... | collective-permute-start | bytes 1572872 | tf_op jit(solution)/shard_map/ppermute | solution.py:400
  129.9 95.6 %all-gather.5.cloned.1.call-start = ((), (), s32[]{:S(2)}) async-start(), calls=%async_computation.7 | async-start | bytes 4718592 | tf_op jit(solution)/shard_map/all_gather | solution.py:450
  180.1 115.1 %reduce-scatter.7.cloned.1.call-start = ((), (), s32[]{:S(2)}) async-start(), calls=%async_computation.8 | async-start | bytes 4718592 | tf_op jit(solution)/shard_map/reduce_scatter | solution.py:454
  180.2 25.2 %collective-permute-start.20 = (bf16[176,2048]{1,0:T(8,128)(2,1)}, bf16[176,2048]{1,0:T(8,128)(2,1)S(1)}, u32[]{:S(2)}, u32[]{:S(2)}) collective-permute-start(bf16[176,2048]{1,0:T(8,128)(2,1)} %param.28), channel_id=1, source_target_pairs={{0,8},{8,0},{16,24},{24,16},{1,9},{9,1},{17,25},{25,17},{2,10},{10... | collective-permute-start | bytes 2162696 | tf_op jit(solution)/shard_map/ppermute | solution.py:400
  181.7 23.6 %collective-permute-start.21 = (bf16[176,2048]{1,0:T(8,128)(2,1)}, bf16[176,2048]{1,0:T(8,128)(2,1)S(1)}, u32[]{:S(2)}, u32[]{:S(2)}) collective-permute-start(bf16[176,2048]{1,0:T(8,128)(2,1)} %param.28), channel_id=1, source_target_pairs={{0,16},{8,24},{16,0},{24,8},{1,17},{9,25},{17,1},{25,9},{2,18},{10... | collective-permute-start | bytes 2162696 | tf_op jit(solution)/shard_map/ppermute | solution.py:400
  184.2 19.7 %collective-permute-start.22 = (bf16[88,2048]{1,0:T(8,128)(2,1)S(1)}, bf16[88,2048]{1,0:T(8,128)(2,1)S(1)}, u32[]{:S(2)}, u32[]{:S(2)}) collective-permute-start(bf16[88,2048]{1,0:T(8,128)(2,1)S(1)} %slice.163), channel_id=1, source_target_pairs={{0,8},{8,0},{16,24},{24,16},{1,9},{9,1},{17,25},{25,17},{2,10},{10... | collective-permute-start | bytes 1081352 | tf_op jit(solution)/shard_map/ppermute | solution.py:400
  185.9 19.4 %collective-permute-start.23 = (bf16[88,2048]{1,0:T(8,128)(2,1)S(1)}, bf16[88,2048]{1,0:T(8,128)(2,1)S(1)}, u32[]{:S(2)}, u32[]{:S(2)}) collective-permute-start(bf16[88,2048]{1,0:T(8,128)(2,1)S(1)} %slice.164), channel_id=1, source_target_pairs={{0,16},{8,24},{16,0},{24,8},{1,17},{9,25},{17,1},{25,9},{2,18},{10... | collective-permute-start | bytes 1081352 | tf_op jit(solution)/shard_map/ppermute | solution.py:400
  246.3 99.2 %all-gather.7.cloned.1.call-start = ((), (), s32[]{:S(2)}) async-start(), calls=%async_computation.9 | async-start | bytes 4718592 | tf_op jit(solution)/shard_map/all_gather | solution.py:450
  300.0 116.4 %reduce-scatter.11.cloned.1.call-start = ((), (), s32[]{:S(2)}) async-start(), calls=%async_computation.11 | async-start | bytes 4718592 | tf_op jit(solution)/shard_map/reduce_scatter | solution.py:454
  313.7 20.6 %collective-permute-start.33 = (bf16[176,2048]{1,0:T(8,128)(2,1)S(1)}, bf16[176,2048]{1,0:T(8,128)(2,1)}, u32[]{:S(2)}, u32[]{:S(2)}) collective-permute-start(bf16[176,2048]{1,0:T(8,128)(2,1)S(1)} %pad_maximum_fusion.8), channel_id=1, source_target_pairs={{0,16},{8,24},{16,0},{24,8},{1,17},{9,25},{17,1},{25,9},{2,18},{10... | collective-permute-start | bytes 2162696 | tf_op jit(solution)/shard_map/ppermute | solution.py:400
  345.5 120.2 %reduce-scatter.9.cloned.1.call-start = ((), (), s32[]{:S(2)}) async-start(), calls=%async_computation.10 | async-start | bytes 4718592 | tf_op jit(solution)/shard_map/reduce_scatter | solution.py:454
  371.5 20.2 %collective-permute-start.38 = (bf16[512,768]{1,0:T(8,128)(2,1)}, bf16[512,768]{1,0:T(8,128)(2,1)}, u32[]{:S(2)}, u32[]{:S(2)}) collective-permute-start(bf16[512,768]{1,0:T(8,128)(2,1)} %get-tuple-element.259), channel_id=1, source_target_pairs={{0,8},{8,0},{16,24},{24,16},{1,9},{9,1},{17,25},{25,17},{2,10},{10... | collective-permute-start | bytes 2359304 | tf_op jit(solution)/shard_map/ppermute | solution.py:400
  372.5 19.2 %collective-permute-start.39 = (bf16[512,768]{1,0:T(8,128)(2,1)}, bf16[512,768]{1,0:T(8,128)(2,1)}, u32[]{:S(2)}, u32[]{:S(2)}) collective-permute-start(bf16[512,768]{1,0:T(8,128)(2,1)} %get-tuple-element.260), channel_id=1, source_target_pairs={{0,16},{8,24},{16,0},{24,8},{1,17},{9,25},{17,1},{25,9},{2,18},{10... | collective-permute-start | bytes 2359304 | tf_op jit(solution)/shard_map/ppermute | solution.py:400
  393.9 22.5 %collective-permute-start.43 = (bf16[512,768]{1,0:T(8,128)(2,1)}, bf16[512,768]{1,0:T(8,128)(2,1)S(1)}, u32[]{:S(2)}, u32[]{:S(2)}) collective-permute-start(bf16[512,768]{1,0:T(8,128)(2,1)} %get-tuple-element.275), channel_id=1, source_target_pairs={{0,24},{8,16},{16,8},{24,0},{1,25},{9,17},{17,9},{25,1},{2,26},{10... | collective-permute-start | bytes 2359304 | tf_op jit(solution)/shard_map/ppermute | solution.py:400
  419.1 20.8 %collective-permute-start.48 = (f32[14,64]{1,0:T(8,128)S(1)}, f32[14,64]{1,0:T(8,128)S(1)}, u32[]{:S(2)}, u32[]{:S(2)}) collective-permute-start(f32[14,64]{1,0:T(8,128)S(1)} %get-tuple-element.309), channel_id=1, source_target_pairs={{0,2},{1,3},{2,0},{3,1},{4,6},{5,7},{6,4},{7,5},{8,10},{9,11},{10,... | collective-permute-start | bytes 10760 | tf_op jit(solution)/shard_map/ppermute | solution.py:400
  419.1 20.8 %collective-permute-start.49 = (f32[14,64]{1,0:T(8,128)S(1)}, f32[14,64]{1,0:T(8,128)S(1)}, u32[]{:S(2)}, u32[]{:S(2)}) collective-permute-start(f32[14,64]{1,0:T(8,128)S(1)} %get-tuple-element.310), channel_id=1, source_target_pairs={{0,3},{1,2},{2,1},{3,0},{4,7},{5,6},{6,5},{7,4},{8,11},{9,10},{10,... | collective-permute-start | bytes 10760 | tf_op jit(solution)/shard_map/ppermute | solution.py:400
  421.0 19.5 %collective-permute-start.50 = (f32[14,64]{1,0:T(8,128)S(1)}, f32[14,64]{1,0:T(8,128)S(1)}, u32[]{:S(2)}, u32[]{:S(2)}) collective-permute-start(f32[14,64]{1,0:T(8,128)S(1)} %get-tuple-element.311), channel_id=1, source_target_pairs={{0,4},{1,5},{2,6},{3,7},{4,0},{5,1},{6,2},{7,3},{8,12},{9,13},{10,... | collective-permute-start | bytes 10760 | tf_op jit(solution)/shard_map/ppermute | solution.py:400
  422.0 19.2 %collective-permute-start.51 = (f32[14,64]{1,0:T(8,128)S(1)}, f32[14,64]{1,0:T(8,128)S(1)}, u32[]{:S(2)}, u32[]{:S(2)}) collective-permute-start(f32[14,64]{1,0:T(8,128)S(1)} %get-tuple-element.312), channel_id=1, source_target_pairs={{0,5},{1,4},{2,7},{3,6},{4,1},{5,0},{6,3},{7,2},{8,13},{9,12},{10,... | collective-permute-start | bytes 10760 | tf_op jit(solution)/shard_map/ppermute | solution.py:400
  423.5 37.0 %all-to-all-start.1 = ((bf16[8,64,768]{2,1,0:T(8,128)(2,1)}), bf16[8,64,768]{2,1,0:T(8,128)(2,1)S(1)}, u32[]{:S(2)}, u32[]{:S(2)}) async-start(bf16[8,64,768]{2,1,0:T(8,128)(2,1)} %bitcast.39), calls=%async_computation.5 | async-start | bytes 1572864 | tf_op jit(solution)/shard_map/all_to_all | solution.py:706
  436.2 22.0 %collective-permute-start.52 = (f32[14,64]{1,0:T(8,128)S(1)}, f32[14,64]{1,0:T(8,128)S(1)}, u32[]{:S(2)}, u32[]{:S(2)}) collective-permute-start(f32[14,64]{1,0:T(8,128)S(1)} %get-tuple-element.313), channel_id=1, source_target_pairs={{0,6},{1,7},{2,4},{3,5},{4,2},{5,3},{6,0},{7,1},{8,14},{9,15},{10,... | collective-permute-start | bytes 10760 | tf_op jit(solution)/shard_map/ppermute | solution.py:400
  (102 other events, 1094.3 us)
Sparse Core Ops, SparseCore 0:
  24.3 53.9 all-gather.8
  130.0 47.7 reduce-scatter.4
  180.2 45.2 all-gather.4
  246.4 48.7 reduce-scatter.6
  300.2 45.2 all-gather.6
  347.6 48.7 reduce-scatter.10
  398.7 61.8 reduce-scatter.8

commit v9 on v8

--- a/solution.py
+++ b/solution.py
@@ -77,7 +77,7 @@
 
 def over_blocks(length, block, step):
     count = length // block
-    if count <= 4:
+    if count <= 8:
         for i in range(count):
             step(i * block, (i + 1) * block)
     else:
@@ -95,7 +95,7 @@
 ):
     length, width = query_ref.shape
     lanes = cos_ref.shape[1]
-    block = min(256, length)
+    block = min(128, length)
     tables = (cos_ref[...], former_ref[...], latter_ref[...])
     for group in range(width // lanes):
         part = slice(group * lanes, (group + 1) * lanes)

time: 484 us -> 481 us (level)
  no operation moved by 1% of the time
where the time goes in v9:
time: 481 us; the launch traced here: 475 us
  waiting for transfers between devices  161 us (33%)
  starting transfers between devices  74.7 us (16%)
  matrix products  73.5 us (15%)
  local copies, waits for them, and re-layouts  70.1 us (15%)
  other arithmetic  44 us (9%)
  Pallas kernels  34.7 us (7%)
  between operations  16.7 us (3%)
    ppermute x54, waiting for transfers between devices, permute(): return lax.ppermute(value, axis, [(i, i ^ offset) for i in range(size)])  108 us
    dot_general x13, matrix products, contract(): lax.dot_general(left, right, (((left_dim,), (right_dim,)), ((), ())), pre...  66.7 us
    ppermute x54, starting transfers between devices, permute(): return lax.ppermute(value, axis, [(i, i ^ offset) for i in range(size)])  64.1 us
    all_gather x3, waiting for transfers between devices, gather_seq(): return lax.all_gather(piece, 'seq', axis=0, tiled=True)  23 us
    dynamic_update_slice x19, local copies, waits for them, and re-layouts, place(): lax.dynamic_update_slice_in_dim(result, piece, (index ^ k) * block, 0)  21.5 us
    unnamed x149, local copies, waits for them, and re-layouts  21 us
    reduce_scatter x4, waiting for transfers between devices, scatter_seq(): lax.psum_scatter(terms.astype(jnp.bfloat16), 'seq', scatter_dimension=0,...  20.6 us
    add x6, other arithmetic, total(): result = result + piece.astype(jnp.float32)  11.2 us
  transfers between devices with their start and end apart: 63, of which 30 were waited for; matrix products, arithmetic and copies ran while one was open for 30% of the time, Pallas kernels for 6%

profile of v9, /device:TPU:0, one launch (start us, length us, event | category | flops | bytes accessed | tf_op | source)
XLA Modules:
  0.0 474.5 jit_solution(11102512576078128591)
XLA Ops:
  11.2 6.3 %all-to-all-start = ((bf16[8,80,768]{2,1,0:T(8,128)(2,1)}), bf16[8,80,768]{2,1,0:T(8,128)(2,1)S(1)}, u32[]{:S(2)}, u32[]{:S(2)}) async-start(bf16[8,80,768]{2,1,0:T(8,128)(2,1)} %deal_columns.1), calls=%async_computation | async-start | bytes 1966080 | tf_op jit(solution)/shard_map/all_to_all | solution.py:554
  26.6 15.9 %collective-permute-done = bf16[64,2048]{1,0:T(8,128)(2,1)} collective-permute-done((bf16[64,2048]{1,0:T(8,128)(2,1)S(1)}, bf16[64,2048]{1,0:T(8,128)(2,1)}, u32[]{:S(2)}, u32[]{:S(2)}) %collective-permute-start) | collective-permute-done | bytes 262176 | tf_op jit(solution)/shard_map/ppermute | solution.py:400
  42.5 6.4 %collective-permute-done.1 = bf16[64,2048]{1,0:T(8,128)(2,1)} collective-permute-done((bf16[64,2048]{1,0:T(8,128)(2,1)S(1)}, bf16[64,2048]{1,0:T(8,128)(2,1)}, u32[]{:S(2)}, u32[]{:S(2)}) %collective-permute-start.1) | collective-permute-done | bytes 262176 | tf_op jit(solution)/shard_map/ppermute | solution.py:400
  48.9 8.5 %all-to-all-done = bf16[8,80,768]{2,1,0:T(8,128)(2,1)S(1)} async-done(((bf16[8,80,768]{2,1,0:T(8,128)(2,1)}), bf16[8,80,768]{2,1,0:T(8,128)(2,1)S(1)}, u32[]{:S(2)}, u32[]{:S(2)}) %all-to-all-start) | async-done | bytes 983072 | tf_op jit(solution)/shard_map/all_to_all | solution.py:554
  71.3 7.0 %all-gather.9.cloned.1.call-done = bf16[1,1024,2048]{2,1,0:T(8,128)(2,1)} async-done(((bf16[1,128,2048]{2,1,0:T(8,128)(2,1)}), bf16[1,1024,2048]{2,1,0:T(8,128)(2,1)}) %all-gather.9.cloned.1.call-update) | async-done | bytes 4194320 | tf_op jit(solution)/shard_map/all_gather | solution.py:450
  99.9 4.0 add_convert_fusion.1
  114.0 6.6 %attention_forward.1 = (bf16[1024,256]{1,0:T(8,128)(2,1)S(1)}, bf16[1024,256]{1,0:T(8,128)(2,1)S(1)}, bf16[1024,256]{1,0:T(8,128)(2,1)S(1)}, f32[4,1024]{1,0:T(4,128)S(1)}) custom-call(bf16[1024,768]{1,0:T(8,128)(2,1)S(1)} %add_convert_fusion.2.qkv_ref, f32[1024,128]{1,0:T(8,128)S(1)} %copy.52.cos_ref, f32[1024,128]{1,0:T(8,128)S(1)} %copy-done.3, ...), custom_call_target="tpu_custom_call" | custom-call | flops 1 | bytes 1 | tf_op jit(solution)/shard_map/attention_forward/pallas_call | solution.py:355
  134.2 6.7 %collective-permute-done.15 = bf16[88,2048]{1,0:T(8,128)(2,1)S(1)} collective-permute-done((bf16[88,2048]{1,0:T(8,128)(2,1)S(1)}, bf16[88,2048]{1,0:T(8,128)(2,1)S(1)}, u32[]{:S(2)}, u32[]{:S(2)}) %collective-permute-start.15) | collective-permute-done | bytes 360480 | tf_op jit(solution)/shard_map/ppermute | solution.py:400
  160.6 15.7 %reduce-scatter.5.cloned.1.call-done.terms_ref = bf16[128,2048]{1,0:T(8,128)(2,1)} async-done(((bf16[1024,2048]{1,0:T(8,128)(2,1)}), bf16[128,2048]{1,0:T(8,128)(2,1)}) %reduce-scatter.5.cloned.1.call-update) | async-done | bytes 524304 | tf_op jit(solution)/shard_map/reduce_scatter | solution.py:454
  188.0 14.3 %collective-permute-done.22 = bf16[88,2048]{1,0:T(8,128)(2,1)S(1)} collective-permute-done((bf16[88,2048]{1,0:T(8,128)(2,1)S(1)}, bf16[88,2048]{1,0:T(8,128)(2,1)S(1)}, u32[]{:S(2)}, u32[]{:S(2)}) %collective-permute-start.22) | collective-permute-done | bytes 360480 | tf_op jit(solution)/shard_map/ppermute | solution.py:400
  205.9 5.3 %pad_maximum_fusion.1 = bf16[704,2048]{1,0:T(8,128)(2,1)} fusion(bf16[176,2048]{1,0:T(8,128)(2,1)S(1)} %pad_maximum_fusion.4, bf16[176,2048]{1,0:T(8,128)(2,1)} %collective-permute-done.18, bf16[176,2048]{1,0:T(8,128)(2,1)S(1)} %copy-done.46, bf16[176,2048]{1,0:T(8,128)(2,1)S(1)} %bitcast.140), kind=kLoop, calls=%fused_computation.16 | loop fusion | flops 11534336 | bytes 5767168 | tf_op jit(solution)/shard_map/concatenate | solution.py:611
  214.5 4.7 fusion.20
  219.2 4.8 %all-gather.5.cloned.1.call-done = bf16[1024,2048]{1,0:T(8,128)(2,1)} async-done(((bf16[128,2048]{1,0:T(8,128)(2,1)}), bf16[1024,2048]{1,0:T(8,128)(2,1)}) %all-gather.5.cloned.1.call-update) | async-done | bytes 4194320 | tf_op jit(solution)/shard_map/all_gather | solution.py:450
  224.0 6.0 %fusion.21 = f32[1024,704]{0,1:T(8,128)S(1)} fusion(bf16[1024,2048]{1,0:T(8,128)(2,1)} %all-gather.5.cloned.1.call-done, bf16[704,2048]{1,0:T(8,128)(2,1)} %pad_maximum_fusion), kind=kOutput, calls=%fused_computation.141 | convolution fusion | flops 2952790016 | bytes 9961472 | tf_op jit(solution)/shard_map/dot_general | solution.py:21
  230.1 5.8 %multiply_convert_fusion = (bf16[1024,704]{0,1:T(8,128)(2,1)}, bf16[1024,704]{0,1:T(8,128)(2,1)S(1)}, bf16[1024,704]{0,1:T(8,128)(2,1)S(1)}) fusion(f32[1024,704]{0,1:T(8,128)S(1)} %fusion.21, f32[1024,704]{0,1:T(8,128)S(1)} %copy-done.67, bf16[1024,2048]{1,0:T(8,128)(2,1)S(1)} %copy-done.64, bf16[704,2048]{1,0:T(8,128)(2,1)S(1)} %copy-done.33), kind=kOutput, calls=%fused_computation.17 | convolution fusion | flops 2963603456 | bytes 17170432 | tf_op jit(solution)/shard_map/dot_general | solution.py:21
  239.4 5.3 %add_convert_fusion = bf16[1024,2048]{1,0:T(8,128)(2,1)} fusion(f32[1024,2048]{1,0:T(8,128)S(1)} %fusion.22, bf16[1024,704]{0,1:T(8,128)(2,1)S(1)} %get-tuple-element.229, bf16[704,2048]{1,0:T(8,128)(2,1)S(1)} %copy-done.32), kind=kOutput, calls=%fused_computation | convolution fusion | flops 2956984320 | bytes 16908288 | tf_op jit(solution)/shard_map/dot_general | solution.py:21
  244.8 5.9 %convolution_convert_fusion.6 = bf16[704,2048]{1,0:T(8,128)(2,1)S(1)} fusion(bf16[1024,704]{0,1:T(8,128)(2,1)} %copy-done.68, bf16[1024,2048]{1,0:T(8,128)(2,1)} %all-gather.5.cloned.1.call-done), kind=kOutput, calls=%fused_computation.12 | convolution fusion | flops 2954231808 | bytes 8519680 | tf_op jit(solution)/shard_map/dot_general | solution.py:21
  256.1 5.3 %convolution_convert_fusion = bf16[1024,2048]{1,0:T(8,128)(2,1)} fusion(bf16[1024,704]{0,1:T(8,128)(2,1)S(1)} %copy-done.69, bf16[704,2048]{1,0:T(8,128)(2,1)S(1)} %copy-done.61), kind=kOutput, calls=%fused_computation.6 | convolution fusion | flops 2954887168 | bytes 8519680 | tf_op jit(solution)/shard_map/dot_general | solution.py:21
  261.4 7.5 %convolution_convert_fusion.5 = bf16[704,2048]{1,0:T(8,128)(2,1)} fusion(bf16[1024,704]{0,1:T(8,128)(2,1)} %copy-done.66, bf16[1024,2048]{1,0:T(8,128)(2,1)} %all-gather.5.cloned.1.call-done), kind=kOutput, calls=%fused_computation.11 | convolution fusion | flops 2954231808 | bytes 8519680 | tf_op jit(solution)/shard_map/dot_general | solution.py:21
  272.7 4.5 convolution_convert_fusion.4
  277.3 10.9 %collective-permute-done.29 = bf16[176,2048]{1,0:T(8,128)(2,1)} collective-permute-done((bf16[176,2048]{1,0:T(8,128)(2,1)S(1)}, bf16[176,2048]{1,0:T(8,128)(2,1)}, u32[]{:S(2)}, u32[]{:S(2)}) %collective-permute-start.29) | collective-permute-done | bytes 720928 | tf_op jit(solution)/shard_map/ppermute | solution.py:400
  288.7 5.0 %reduce-scatter.7.cloned.1.call-done.terms_ref = bf16[128,2048]{1,0:T(8,128)(2,1)} async-done(((bf16[1024,2048]{1,0:T(8,128)(2,1)}), bf16[128,2048]{1,0:T(8,128)(2,1)}) %reduce-scatter.7.cloned.1.call-update) | async-done | bytes 524304 | tf_op jit(solution)/shard_map/reduce_scatter | solution.py:454
  314.5 6.6 %collective-permute-done.35 = bf16[88,2048]{1,0:T(8,128)(2,1)S(1)} collective-permute-done((bf16[88,2048]{1,0:T(8,128)(2,1)S(1)}, bf16[88,2048]{1,0:T(8,128)(2,1)S(1)}, u32[]{:S(2)}, u32[]{:S(2)}) %collective-permute-start.35) | collective-permute-done | bytes 360480 | tf_op jit(solution)/shard_map/ppermute | solution.py:400
  323.7 9.0 %collective-permute-done.33 = bf16[176,2048]{1,0:T(8,128)(2,1)} collective-permute-done((bf16[176,2048]{1,0:T(8,128)(2,1)S(1)}, bf16[176,2048]{1,0:T(8,128)(2,1)}, u32[]{:S(2)}, u32[]{:S(2)}) %collective-permute-start.33) | collective-permute-done | bytes 720928 | tf_op jit(solution)/shard_map/ppermute | solution.py:400
  332.7 11.2 %all-gather.7.cloned.1.call-done = bf16[1024,2048]{1,0:T(8,128)(2,1)} async-done(((bf16[128,2048]{1,0:T(8,128)(2,1)}), bf16[1024,2048]{1,0:T(8,128)(2,1)}) %all-gather.7.cloned.1.call-update) | async-done | bytes 4194320 | tf_op jit(solution)/shard_map/all_gather | solution.py:450
  350.8 11.0 %attention_backward.1 = bf16[1024,768]{1,0:T(8,128)(2,1)S(1)} custom-call(bf16[1024,256]{1,0:T(8,128)(2,1)S(1)} %copy-done.18, bf16[1024,256]{1,0:T(8,128)(2,1)S(1)} %copy-done.20, bf16[1024,768]{1,0:T(8,128)(2,1)} %copy-done.2, bf16[1024,256]{1,0:T(8,128)(2,1)S(1)} %convolution_convert_fusion.8.context_grad_ref, ...), custom_call_target="tpu_custom_call" | custom-call | flops 1 | bytes 1 | tf_op jit(solution)/shard_map/attention_backward/pallas_call | solution.py:373
  364.1 4.1 convolution_convert_fusion.3
  372.5 7.1 %convolution_convert_fusion.2.terms_ref = bf16[1024,2048]{1,0:T(8,128)(2,1)} fusion(bf16[1024,768]{1,0:T(8,128)(2,1)S(1)} %attention_backward.1, bf16[2048,768]{1,0:T(8,128)(2,1)} %copy-done.29), kind=kOutput, calls=%fused_computation.8 | convolution fusion | flops 3223322624 | bytes 8912896 | tf_op jit(solution)/shard_map/dot_general | solution.py:21
  381.9 8.3 %norm_sums.1 = f32[8,2048]{1,0:T(8,128)S(1)} custom-call(bf16[1024,2048]{1,0:T(8,128)(2,1)S(1)} %bitcast.119, bf16[1024,2048]{1,0:T(8,128)(2,1)} %convolution_convert_fusion.2.terms_ref, f32[1,2048]{1,0:T(1,128)S(1)} %bitcast.120, f32[1,2048]{1,0:T(1,128)S(1)} %slice.185.gain_ref), custom_call_target="tpu_custom_call" | custom-call | flops 1 | bytes 1 | tf_op jit(solution)/shard_map/norm_sums/pallas_call | solution.py:324
  401.9 11.3 %collective-permute-done.40 = f32[8,14,64]{2,1,0:T(8,128)S(1)} collective-permute-done((f32[8,14,64]{2,1,0:T(8,128)S(1)}, f32[8,14,64]{2,1,0:T(8,128)S(1)}, u32[]{:S(2)}, u32[]{:S(2)}) %collective-permute-start.40) | collective-permute-done | bytes 28704 | tf_op jit(solution)/shard_map/ppermute | solution.py:400
  434.6 3.7 collective-permute-start.52
  442.8 13.8 %collective-permute-done.52 = f32[14,64]{1,0:T(8,128)S(1)} collective-permute-done((f32[14,64]{1,0:T(8,128)S(1)}, f32[14,64]{1,0:T(8,128)S(1)}, u32[]{:S(2)}, u32[]{:S(2)}) %collective-permute-start.52) | collective-permute-done | bytes 3616 | tf_op jit(solution)/shard_map/ppermute | solution.py:400
  (410 shorter events, 209.2 us)
Async XLA Ops:
  11.2 46.2 %all-to-all-start = ((bf16[8,80,768]{2,1,0:T(8,128)(2,1)}), bf16[8,80,768]{2,1,0:T(8,128)(2,1)S(1)}, u32[]{:S(2)}, u32[]{:S(2)}) async-start(bf16[8,80,768]{2,1,0:T(8,128)(2,1)} %deal_columns.1), calls=%async_computation | async-start | bytes 1966080 | tf_op jit(solution)/shard_map/all_to_all | solution.py:554
  17.5 60.8 %all-gather.9.cloned.1.call-start = ((), (), s32[]{:S(2)}) async-start(), calls=%async_computation.12 | async-start | bytes 4718592 | tf_op jit(solution)/shard_map/all_gather | solution.py:450
  17.6 31.3 %collective-permute-start.3 = (bf16[176,2048]{1,0:T(8,128)(2,1)}, bf16[176,2048]{1,0:T(8,128)(2,1)S(1)}, u32[]{:S(2)}, u32[]{:S(2)}) collective-permute-start(bf16[176,2048]{1,0:T(8,128)(2,1)} %bitcast.4), channel_id=1, source_target_pairs={{0,8},{8,0},{16,24},{24,16},{1,9},{9,1},{17,25},{25,17},{2,10},{10... | collective-permute-start | bytes 2162696 | tf_op jit(solution)/shard_map/ppermute | solution.py:400
  19.1 29.8 %collective-permute-start.4 = (bf16[176,2048]{1,0:T(8,128)(2,1)}, bf16[176,2048]{1,0:T(8,128)(2,1)S(1)}, u32[]{:S(2)}, u32[]{:S(2)}) collective-permute-start(bf16[176,2048]{1,0:T(8,128)(2,1)} %bitcast.4), channel_id=1, source_target_pairs={{0,16},{8,24},{16,0},{24,8},{1,17},{9,25},{17,1},{25,9},{2,18},{10... | collective-permute-start | bytes 2162696 | tf_op jit(solution)/shard_map/ppermute | solution.py:400
  20.7 21.9 %collective-permute-start = (bf16[64,2048]{1,0:T(8,128)(2,1)S(1)}, bf16[64,2048]{1,0:T(8,128)(2,1)}, u32[]{:S(2)}, u32[]{:S(2)}) collective-permute-start(bf16[64,2048]{1,0:T(8,128)(2,1)S(1)} %copy-done.55), channel_id=1, source_target_pairs={{0,8},{8,0},{16,24},{24,16},{1,9},{9,1},{17,25},{25,17},{2,10},{10... | collective-permute-start | bytes 786440 | tf_op jit(solution)/shard_map/ppermute | solution.py:400
  21.2 27.7 %collective-permute-start.1 = (bf16[64,2048]{1,0:T(8,128)(2,1)S(1)}, bf16[64,2048]{1,0:T(8,128)(2,1)}, u32[]{:S(2)}, u32[]{:S(2)}) collective-permute-start(bf16[64,2048]{1,0:T(8,128)(2,1)S(1)} %copy-done.55), channel_id=1, source_target_pairs={{0,16},{8,24},{16,0},{24,8},{1,17},{9,25},{17,1},{25,9},{2,18},{10... | collective-permute-start | bytes 786440 | tf_op jit(solution)/shard_map/ppermute | solution.py:400
  21.7 27.2 %collective-permute-start.2 = (bf16[64,2048]{1,0:T(8,128)(2,1)S(1)}, bf16[64,2048]{1,0:T(8,128)(2,1)S(1)}, u32[]{:S(2)}, u32[]{:S(2)}) collective-permute-start(bf16[64,2048]{1,0:T(8,128)(2,1)S(1)} %copy-done.55), channel_id=1, source_target_pairs={{0,24},{8,16},{16,8},{24,0},{1,25},{9,17},{17,9},{25,1},{2,26},{10... | collective-permute-start | bytes 786440 | tf_op jit(solution)/shard_map/ppermute | solution.py:400
  24.2 152.1 %reduce-scatter.5.cloned.1.call-start = ((), (), s32[]{:S(2)}) async-start(), calls=%async_computation.6 | async-start | bytes 4718592 | tf_op jit(solution)/shard_map/reduce_scatter | solution.py:454
  61.2 26.1 %collective-permute-start.5 = (bf16[512,768]{1,0:T(8,128)(2,1)S(1)}, bf16[512,768]{1,0:T(8,128)(2,1)S(1)}, u32[]{:S(2)}, u32[]{:S(2)}) collective-permute-start(bf16[512,768]{1,0:T(8,128)(2,1)S(1)} %bitcast.123), channel_id=1, source_target_pairs={{0,8},{8,0},{16,24},{24,16},{1,9},{9,1},{17,25},{25,17},{2,10},{10... | collective-permute-start | bytes 2359304 | tf_op jit(solution)/shard_map/ppermute | solution.py:400
  62.7 24.5 %collective-permute-start.6 = (bf16[512,768]{1,0:T(8,128)(2,1)S(1)}, bf16[512,768]{1,0:T(8,128)(2,1)}, u32[]{:S(2)}, u32[]{:S(2)}) collective-permute-start(bf16[512,768]{1,0:T(8,128)(2,1)S(1)} %bitcast.124), channel_id=1, source_target_pairs={{0,16},{8,24},{16,0},{24,8},{1,17},{9,25},{17,1},{25,9},{2,18},{10... | collective-permute-start | bytes 2359304 | tf_op jit(solution)/shard_map/ppermute | solution.py:400
  78.3 48.2 %collective-permute-start.12 = (bf16[128,2048]{1,0:T(8,128)(2,1)}, bf16[128,2048]{1,0:T(8,128)(2,1)}, u32[]{:S(2)}, u32[]{:S(2)}) collective-permute-start(bf16[128,2048]{1,0:T(8,128)(2,1)} %bitcast.17.base_ref), channel_id=1, source_target_pairs={{0,4},{1,5},{2,6},{3,7},{4,0},{5,1},{6,2},{7,3},{8,12},{9,13},{10,... | collective-permute-start | bytes 1572872 | tf_op jit(solution)/shard_map/ppermute | solution.py:400
  78.3 48.2 %collective-permute-start.13 = (bf16[128,2048]{1,0:T(8,128)(2,1)}, bf16[128,2048]{1,0:T(8,128)(2,1)}, u32[]{:S(2)}, u32[]{:S(2)}) collective-permute-start(bf16[128,2048]{1,0:T(8,128)(2,1)} %bitcast.17.base_ref), channel_id=1, source_target_pairs={{0,6},{1,7},{2,4},{3,5},{4,2},{5,3},{6,0},{7,1},{8,14},{9,15},{10,... | collective-permute-start | bytes 1572872 | tf_op jit(solution)/shard_map/ppermute | solution.py:400
  126.5 97.5 %all-gather.5.cloned.1.call-start = ((), (), s32[]{:S(2)}) async-start(), calls=%async_computation.7 | async-start | bytes 4718592 | tf_op jit(solution)/shard_map/all_gather | solution.py:450
  178.5 115.1 %reduce-scatter.7.cloned.1.call-start = ((), (), s32[]{:S(2)}) async-start(), calls=%async_computation.8 | async-start | bytes 4718592 | tf_op jit(solution)/shard_map/reduce_scatter | solution.py:454
  178.6 25.2 %collective-permute-start.20 = (bf16[176,2048]{1,0:T(8,128)(2,1)}, bf16[176,2048]{1,0:T(8,128)(2,1)S(1)}, u32[]{:S(2)}, u32[]{:S(2)}) collective-permute-start(bf16[176,2048]{1,0:T(8,128)(2,1)} %param.28), channel_id=1, source_target_pairs={{0,8},{8,0},{16,24},{24,16},{1,9},{9,1},{17,25},{25,17},{2,10},{10... | collective-permute-start | bytes 2162696 | tf_op jit(solution)/shard_map/ppermute | solution.py:400
  180.1 23.6 %collective-permute-start.21 = (bf16[176,2048]{1,0:T(8,128)(2,1)}, bf16[176,2048]{1,0:T(8,128)(2,1)S(1)}, u32[]{:S(2)}, u32[]{:S(2)}) collective-permute-start(bf16[176,2048]{1,0:T(8,128)(2,1)} %param.28), channel_id=1, source_target_pairs={{0,16},{8,24},{16,0},{24,8},{1,17},{9,25},{17,1},{25,9},{2,18},{10... | collective-permute-start | bytes 2162696 | tf_op jit(solution)/shard_map/ppermute | solution.py:400
  182.6 19.7 %collective-permute-start.22 = (bf16[88,2048]{1,0:T(8,128)(2,1)S(1)}, bf16[88,2048]{1,0:T(8,128)(2,1)S(1)}, u32[]{:S(2)}, u32[]{:S(2)}) collective-permute-start(bf16[88,2048]{1,0:T(8,128)(2,1)S(1)} %slice.163), channel_id=1, source_target_pairs={{0,8},{8,0},{16,24},{24,16},{1,9},{9,1},{17,25},{25,17},{2,10},{10... | collective-permute-start | bytes 1081352 | tf_op jit(solution)/shard_map/ppermute | solution.py:400
  184.3 19.4 %collective-permute-start.23 = (bf16[88,2048]{1,0:T(8,128)(2,1)S(1)}, bf16[88,2048]{1,0:T(8,128)(2,1)S(1)}, u32[]{:S(2)}, u32[]{:S(2)}) collective-permute-start(bf16[88,2048]{1,0:T(8,128)(2,1)S(1)} %slice.164), channel_id=1, source_target_pairs={{0,16},{8,24},{16,0},{24,8},{1,17},{9,25},{17,1},{25,9},{2,18},{10... | collective-permute-start | bytes 1081352 | tf_op jit(solution)/shard_map/ppermute | solution.py:400
  244.7 99.2 %all-gather.7.cloned.1.call-start = ((), (), s32[]{:S(2)}) async-start(), calls=%async_computation.9 | async-start | bytes 4718592 | tf_op jit(solution)/shard_map/all_gather | solution.py:450
  298.5 116.4 %reduce-scatter.11.cloned.1.call-start = ((), (), s32[]{:S(2)}) async-start(), calls=%async_computation.11 | async-start | bytes 4718592 | tf_op jit(solution)/shard_map/reduce_scatter | solution.py:454
  312.1 20.6 %collective-permute-start.33 = (bf16[176,2048]{1,0:T(8,128)(2,1)S(1)}, bf16[176,2048]{1,0:T(8,128)(2,1)}, u32[]{:S(2)}, u32[]{:S(2)}) collective-permute-start(bf16[176,2048]{1,0:T(8,128)(2,1)S(1)} %pad_maximum_fusion.8), channel_id=1, source_target_pairs={{0,16},{8,24},{16,0},{24,8},{1,17},{9,25},{17,1},{25,9},{2,18},{10... | collective-permute-start | bytes 2162696 | tf_op jit(solution)/shard_map/ppermute | solution.py:400
  313.9 18.8 %collective-permute-start.32 = (bf16[176,2048]{1,0:T(8,128)(2,1)S(1)}, bf16[176,2048]{1,0:T(8,128)(2,1)}, u32[]{:S(2)}, u32[]{:S(2)}) collective-permute-start(bf16[176,2048]{1,0:T(8,128)(2,1)S(1)} %pad_maximum_fusion.7), channel_id=1, source_target_pairs={{0,8},{8,0},{16,24},{24,16},{1,9},{9,1},{17,25},{25,17},{2,10},{10... | collective-permute-start | bytes 2162696 | tf_op jit(solution)/shard_map/ppermute | solution.py:400
  343.9 120.2 %reduce-scatter.9.cloned.1.call-start = ((), (), s32[]{:S(2)}) async-start(), calls=%async_computation.10 | async-start | bytes 4718592 | tf_op jit(solution)/shard_map/reduce_scatter | solution.py:454
  369.9 20.2 %collective-permute-start.38 = (bf16[512,768]{1,0:T(8,128)(2,1)}, bf16[512,768]{1,0:T(8,128)(2,1)}, u32[]{:S(2)}, u32[]{:S(2)}) collective-permute-start(bf16[512,768]{1,0:T(8,128)(2,1)} %get-tuple-element.259), channel_id=1, source_target_pairs={{0,8},{8,0},{16,24},{24,16},{1,9},{9,1},{17,25},{25,17},{2,10},{10... | collective-permute-start | bytes 2359304 | tf_op jit(solution)/shard_map/ppermute | solution.py:400
  371.0 19.2 %collective-permute-start.39 = (bf16[512,768]{1,0:T(8,128)(2,1)}, bf16[512,768]{1,0:T(8,128)(2,1)}, u32[]{:S(2)}, u32[]{:S(2)}) collective-permute-start(bf16[512,768]{1,0:T(8,128)(2,1)} %get-tuple-element.260), channel_id=1, source_target_pairs={{0,16},{8,24},{16,0},{24,8},{1,17},{9,25},{17,1},{25,9},{2,18},{10... | collective-permute-start | bytes 2359304 | tf_op jit(solution)/shard_map/ppermute | solution.py:400
  392.3 22.5 %collective-permute-start.43 = (bf16[512,768]{1,0:T(8,128)(2,1)}, bf16[512,768]{1,0:T(8,128)(2,1)S(1)}, u32[]{:S(2)}, u32[]{:S(2)}) collective-permute-start(bf16[512,768]{1,0:T(8,128)(2,1)} %get-tuple-element.275), channel_id=1, source_target_pairs={{0,24},{8,16},{16,8},{24,0},{1,25},{9,17},{17,9},{25,1},{2,26},{10... | collective-permute-start | bytes 2359304 | tf_op jit(solution)/shard_map/ppermute | solution.py:400
  417.5 20.8 %collective-permute-start.48 = (f32[14,64]{1,0:T(8,128)S(1)}, f32[14,64]{1,0:T(8,128)S(1)}, u32[]{:S(2)}, u32[]{:S(2)}) collective-permute-start(f32[14,64]{1,0:T(8,128)S(1)} %get-tuple-element.309), channel_id=1, source_target_pairs={{0,2},{1,3},{2,0},{3,1},{4,6},{5,7},{6,4},{7,5},{8,10},{9,11},{10,... | collective-permute-start | bytes 10760 | tf_op jit(solution)/shard_map/ppermute | solution.py:400
  417.5 20.8 %collective-permute-start.49 = (f32[14,64]{1,0:T(8,128)S(1)}, f32[14,64]{1,0:T(8,128)S(1)}, u32[]{:S(2)}, u32[]{:S(2)}) collective-permute-start(f32[14,64]{1,0:T(8,128)S(1)} %get-tuple-element.310), channel_id=1, source_target_pairs={{0,3},{1,2},{2,1},{3,0},{4,7},{5,6},{6,5},{7,4},{8,11},{9,10},{10,... | collective-permute-start | bytes 10760 | tf_op jit(solution)/shard_map/ppermute | solution.py:400
  419.4 19.5 %collective-permute-start.50 = (f32[14,64]{1,0:T(8,128)S(1)}, f32[14,64]{1,0:T(8,128)S(1)}, u32[]{:S(2)}, u32[]{:S(2)}) collective-permute-start(f32[14,64]{1,0:T(8,128)S(1)} %get-tuple-element.311), channel_id=1, source_target_pairs={{0,4},{1,5},{2,6},{3,7},{4,0},{5,1},{6,2},{7,3},{8,12},{9,13},{10,... | collective-permute-start | bytes 10760 | tf_op jit(solution)/shard_map/ppermute | solution.py:400
  420.4 19.2 %collective-permute-start.51 = (f32[14,64]{1,0:T(8,128)S(1)}, f32[14,64]{1,0:T(8,128)S(1)}, u32[]{:S(2)}, u32[]{:S(2)}) collective-permute-start(f32[14,64]{1,0:T(8,128)S(1)} %get-tuple-element.312), channel_id=1, source_target_pairs={{0,5},{1,4},{2,7},{3,6},{4,1},{5,0},{6,3},{7,2},{8,13},{9,12},{10,... | collective-permute-start | bytes 10760 | tf_op jit(solution)/shard_map/ppermute | solution.py:400
  421.9 37.0 %all-to-all-start.1 = ((bf16[8,64,768]{2,1,0:T(8,128)(2,1)}), bf16[8,64,768]{2,1,0:T(8,128)(2,1)S(1)}, u32[]{:S(2)}, u32[]{:S(2)}) async-start(bf16[8,64,768]{2,1,0:T(8,128)(2,1)} %bitcast.39), calls=%async_computation.5 | async-start | bytes 1572864 | tf_op jit(solution)/shard_map/all_to_all | solution.py:706
  434.6 22.0 %collective-permute-start.52 = (f32[14,64]{1,0:T(8,128)S(1)}, f32[14,64]{1,0:T(8,128)S(1)}, u32[]{:S(2)}, u32[]{:S(2)}) collective-permute-start(f32[14,64]{1,0:T(8,128)S(1)} %get-tuple-element.313), channel_id=1, source_target_pairs={{0,6},{1,7},{2,4},{3,5},{4,2},{5,3},{6,0},{7,1},{8,14},{9,15},{10,... | collective-permute-start | bytes 10760 | tf_op jit(solution)/shard_map/ppermute | solution.py:400
  (102 other events, 1087.0 us)
Sparse Core Ops, SparseCore 0:
  24.3 53.9 all-gather.8
  126.6 49.6 reduce-scatter.4
  178.7 45.3 all-gather.4
  244.8 48.7 reduce-scatter.6
  298.6 45.2 all-gather.6
  346.1 48.7 reduce-scatter.10
  397.1 61.8 reduce-scatter.8

commit v10 on v9

--- a/solution.py
+++ b/solution.py
@@ -138,7 +138,7 @@
 ):
     length, width = query_ref.shape
     lanes = cos_ref.shape[1]
-    block = min(256, length)
+    block = min(128, length)
     scale = HEAD ** (-0.5)
     tables = (cos_ref[...], former_ref[...], latter_ref[...])
     for group in range(width // lanes):

time: 481 us -> 481 us (level)
  no operation moved by 1% of the time
where the time goes in v10:
time: 481 us; the launch traced here: 475 us
  waiting for transfers between devices  159 us (33%)
  starting transfers between devices  73.8 us (15%)
  matrix products  73.5 us (15%)
  local copies, waits for them, and re-layouts  70.1 us (15%)
  other arithmetic  43.9 us (9%)
  Pallas kernels  37.3 us (8%)
  between operations  16.7 us (3%)
    ppermute x54, waiting for transfers between devices, permute(): return lax.ppermute(value, axis, [(i, i ^ offset) for i in range(size)])  107 us
    dot_general x13, matrix products, contract(): lax.dot_general(left, right, (((left_dim,), (right_dim,)), ((), ())), pre...  66.7 us
    ppermute x54, starting transfers between devices, permute(): return lax.ppermute(value, axis, [(i, i ^ offset) for i in range(size)])  63.2 us
    all_gather x3, waiting for transfers between devices, gather_seq(): return lax.all_gather(piece, 'seq', axis=0, tiled=True)  23 us
    dynamic_update_slice x19, local copies, waits for them, and re-layouts, place(): lax.dynamic_update_slice_in_dim(result, piece, (index ^ k) * block, 0)  21.5 us
    unnamed x149, local copies, waits for them, and re-layouts  21 us
    reduce_scatter x4, waiting for transfers between devices, scatter_seq(): lax.psum_scatter(terms.astype(jnp.bfloat16), 'seq', scatter_dimension=0,...  20.6 us
    pallas_call x1, Pallas kernels, attention_backward(): pl.pallas_call(backward_kernel, out_shape=jax.ShapeDtypeStruct((length, 3...  13.7 us
  transfers between devices with their start and end apart: 63, of which 30 were waited for; matrix products, arithmetic and copies ran while one was open for 30% of the time, Pallas kernels for 6%

profile of v10, /device:TPU:0, one launch (start us, length us, event | category | flops | bytes accessed | tf_op | source)
XLA Modules:
  0.0 474.7 jit_solution(3485731154871499829)
XLA Ops:
  11.2 6.3 %all-to-all-start = ((bf16[8,80,768]{2,1,0:T(8,128)(2,1)}), bf16[8,80,768]{2,1,0:T(8,128)(2,1)S(1)}, u32[]{:S(2)}, u32[]{:S(2)}) async-start(bf16[8,80,768]{2,1,0:T(8,128)(2,1)} %deal_columns.1), calls=%async_computation | async-start | bytes 1966080 | tf_op jit(solution)/shard_map/all_to_all | solution.py:554
  26.6 15.9 %collective-permute-done = bf16[64,2048]{1,0:T(8,128)(2,1)} collective-permute-done((bf16[64,2048]{1,0:T(8,128)(2,1)S(1)}, bf16[64,2048]{1,0:T(8,128)(2,1)}, u32[]{:S(2)}, u32[]{:S(2)}) %collective-permute-start) | collective-permute-done | bytes 262176 | tf_op jit(solution)/shard_map/ppermute | solution.py:400
  42.5 6.4 %collective-permute-done.1 = bf16[64,2048]{1,0:T(8,128)(2,1)} collective-permute-done((bf16[64,2048]{1,0:T(8,128)(2,1)S(1)}, bf16[64,2048]{1,0:T(8,128)(2,1)}, u32[]{:S(2)}, u32[]{:S(2)}) %collective-permute-start.1) | collective-permute-done | bytes 262176 | tf_op jit(solution)/shard_map/ppermute | solution.py:400
  48.9 8.5 %all-to-all-done = bf16[8,80,768]{2,1,0:T(8,128)(2,1)S(1)} async-done(((bf16[8,80,768]{2,1,0:T(8,128)(2,1)}), bf16[8,80,768]{2,1,0:T(8,128)(2,1)S(1)}, u32[]{:S(2)}, u32[]{:S(2)}) %all-to-all-start) | async-done | bytes 983072 | tf_op jit(solution)/shard_map/all_to_all | solution.py:554
  71.3 7.0 %all-gather.9.cloned.1.call-done = bf16[1,1024,2048]{2,1,0:T(8,128)(2,1)} async-done(((bf16[1,128,2048]{2,1,0:T(8,128)(2,1)}), bf16[1,1024,2048]{2,1,0:T(8,128)(2,1)}) %all-gather.9.cloned.1.call-update) | async-done | bytes 4194320 | tf_op jit(solution)/shard_map/all_gather | solution.py:450
  99.9 4.0 add_convert_fusion.1
  114.0 6.6 %attention_forward.1 = (bf16[1024,256]{1,0:T(8,128)(2,1)S(1)}, bf16[1024,256]{1,0:T(8,128)(2,1)S(1)}, bf16[1024,256]{1,0:T(8,128)(2,1)S(1)}, f32[4,1024]{1,0:T(4,128)S(1)}) custom-call(bf16[1024,768]{1,0:T(8,128)(2,1)S(1)} %add_convert_fusion.2.qkv_ref, f32[1024,128]{1,0:T(8,128)S(1)} %copy.52.cos_ref, f32[1024,128]{1,0:T(8,128)S(1)} %copy-done.3, ...), custom_call_target="tpu_custom_call" | custom-call | flops 1 | bytes 1 | tf_op jit(solution)/shard_map/attention_forward/pallas_call | solution.py:355
  134.2 6.7 %collective-permute-done.15 = bf16[88,2048]{1,0:T(8,128)(2,1)S(1)} collective-permute-done((bf16[88,2048]{1,0:T(8,128)(2,1)S(1)}, bf16[88,2048]{1,0:T(8,128)(2,1)S(1)}, u32[]{:S(2)}, u32[]{:S(2)}) %collective-permute-start.15) | collective-permute-done | bytes 360480 | tf_op jit(solution)/shard_map/ppermute | solution.py:400
  160.6 15.7 %reduce-scatter.5.cloned.1.call-done.terms_ref = bf16[128,2048]{1,0:T(8,128)(2,1)} async-done(((bf16[1024,2048]{1,0:T(8,128)(2,1)}), bf16[128,2048]{1,0:T(8,128)(2,1)}) %reduce-scatter.5.cloned.1.call-update) | async-done | bytes 524304 | tf_op jit(solution)/shard_map/reduce_scatter | solution.py:454
  188.0 14.3 %collective-permute-done.22 = bf16[88,2048]{1,0:T(8,128)(2,1)S(1)} collective-permute-done((bf16[88,2048]{1,0:T(8,128)(2,1)S(1)}, bf16[88,2048]{1,0:T(8,128)(2,1)S(1)}, u32[]{:S(2)}, u32[]{:S(2)}) %collective-permute-start.22) | collective-permute-done | bytes 360480 | tf_op jit(solution)/shard_map/ppermute | solution.py:400
  205.9 5.3 %pad_maximum_fusion.1 = bf16[704,2048]{1,0:T(8,128)(2,1)} fusion(bf16[176,2048]{1,0:T(8,128)(2,1)S(1)} %pad_maximum_fusion.4, bf16[176,2048]{1,0:T(8,128)(2,1)} %collective-permute-done.18, bf16[176,2048]{1,0:T(8,128)(2,1)S(1)} %copy-done.46, bf16[176,2048]{1,0:T(8,128)(2,1)S(1)} %bitcast.140), kind=kLoop, calls=%fused_computation.16 | loop fusion | flops 11534336 | bytes 5767168 | tf_op jit(solution)/shard_map/concatenate | solution.py:611
  214.5 4.7 fusion.20
  219.2 4.8 %all-gather.5.cloned.1.call-done = bf16[1024,2048]{1,0:T(8,128)(2,1)} async-done(((bf16[128,2048]{1,0:T(8,128)(2,1)}), bf16[1024,2048]{1,0:T(8,128)(2,1)}) %all-gather.5.cloned.1.call-update) | async-done | bytes 4194320 | tf_op jit(solution)/shard_map/all_gather | solution.py:450
  224.0 6.0 %fusion.21 = f32[1024,704]{0,1:T(8,128)S(1)} fusion(bf16[1024,2048]{1,0:T(8,128)(2,1)} %all-gather.5.cloned.1.call-done, bf16[704,2048]{1,0:T(8,128)(2,1)} %pad_maximum_fusion), kind=kOutput, calls=%fused_computation.141 | convolution fusion | flops 2952790016 | bytes 9961472 | tf_op jit(solution)/shard_map/dot_general | solution.py:21
  230.1 5.8 %multiply_convert_fusion = (bf16[1024,704]{0,1:T(8,128)(2,1)}, bf16[1024,704]{0,1:T(8,128)(2,1)S(1)}, bf16[1024,704]{0,1:T(8,128)(2,1)S(1)}) fusion(f32[1024,704]{0,1:T(8,128)S(1)} %fusion.21, f32[1024,704]{0,1:T(8,128)S(1)} %copy-done.67, bf16[1024,2048]{1,0:T(8,128)(2,1)S(1)} %copy-done.64, bf16[704,2048]{1,0:T(8,128)(2,1)S(1)} %copy-done.33), kind=kOutput, calls=%fused_computation.17 | convolution fusion | flops 2963603456 | bytes 17170432 | tf_op jit(solution)/shard_map/dot_general | solution.py:21
  239.4 5.3 %add_convert_fusion = bf16[1024,2048]{1,0:T(8,128)(2,1)} fusion(f32[1024,2048]{1,0:T(8,128)S(1)} %fusion.22, bf16[1024,704]{0,1:T(8,128)(2,1)S(1)} %get-tuple-element.229, bf16[704,2048]{1,0:T(8,128)(2,1)S(1)} %copy-done.32), kind=kOutput, calls=%fused_computation | convolution fusion | flops 2956984320 | bytes 16908288 | tf_op jit(solution)/shard_map/dot_general | solution.py:21
  244.8 5.9 %convolution_convert_fusion.6 = bf16[704,2048]{1,0:T(8,128)(2,1)S(1)} fusion(bf16[1024,704]{0,1:T(8,128)(2,1)} %copy-done.68, bf16[1024,2048]{1,0:T(8,128)(2,1)} %all-gather.5.cloned.1.call-done), kind=kOutput, calls=%fused_computation.12 | convolution fusion | flops 2954231808 | bytes 8519680 | tf_op jit(solution)/shard_map/dot_general | solution.py:21
  256.1 5.3 %convolution_convert_fusion = bf16[1024,2048]{1,0:T(8,128)(2,1)} fusion(bf16[1024,704]{0,1:T(8,128)(2,1)S(1)} %copy-done.69, bf16[704,2048]{1,0:T(8,128)(2,1)S(1)} %copy-done.61), kind=kOutput, calls=%fused_computation.6 | convolution fusion | flops 2954887168 | bytes 8519680 | tf_op jit(solution)/shard_map/dot_general | solution.py:21
  261.4 7.5 %convolution_convert_fusion.5 = bf16[704,2048]{1,0:T(8,128)(2,1)} fusion(bf16[1024,704]{0,1:T(8,128)(2,1)} %copy-done.66, bf16[1024,2048]{1,0:T(8,128)(2,1)} %all-gather.5.cloned.1.call-done), kind=kOutput, calls=%fused_computation.11 | convolution fusion | flops 2954231808 | bytes 8519680 | tf_op jit(solution)/shard_map/dot_general | solution.py:21
  272.7 4.5 convolution_convert_fusion.4
  277.3 10.9 %collective-permute-done.29 = bf16[176,2048]{1,0:T(8,128)(2,1)} collective-permute-done((bf16[176,2048]{1,0:T(8,128)(2,1)S(1)}, bf16[176,2048]{1,0:T(8,128)(2,1)}, u32[]{:S(2)}, u32[]{:S(2)}) %collective-permute-start.29) | collective-permute-done | bytes 720928 | tf_op jit(solution)/shard_map/ppermute | solution.py:400
  288.7 5.0 %reduce-scatter.7.cloned.1.call-done.terms_ref = bf16[128,2048]{1,0:T(8,128)(2,1)} async-done(((bf16[1024,2048]{1,0:T(8,128)(2,1)}), bf16[128,2048]{1,0:T(8,128)(2,1)}) %reduce-scatter.7.cloned.1.call-update) | async-done | bytes 524304 | tf_op jit(solution)/shard_map/reduce_scatter | solution.py:454
  314.5 6.6 %collective-permute-done.35 = bf16[88,2048]{1,0:T(8,128)(2,1)S(1)} collective-permute-done((bf16[88,2048]{1,0:T(8,128)(2,1)S(1)}, bf16[88,2048]{1,0:T(8,128)(2,1)S(1)}, u32[]{:S(2)}, u32[]{:S(2)}) %collective-permute-start.35) | collective-permute-done | bytes 360480 | tf_op jit(solution)/shard_map/ppermute | solution.py:400
  323.7 9.0 %collective-permute-done.33 = bf16[176,2048]{1,0:T(8,128)(2,1)} collective-permute-done((bf16[176,2048]{1,0:T(8,128)(2,1)S(1)}, bf16[176,2048]{1,0:T(8,128)(2,1)}, u32[]{:S(2)}, u32[]{:S(2)}) %collective-permute-start.33) | collective-permute-done | bytes 720928 | tf_op jit(solution)/shard_map/ppermute | solution.py:400
  332.7 11.2 %all-gather.7.cloned.1.call-done = bf16[1024,2048]{1,0:T(8,128)(2,1)} async-done(((bf16[128,2048]{1,0:T(8,128)(2,1)}), bf16[1024,2048]{1,0:T(8,128)(2,1)}) %all-gather.7.cloned.1.call-update) | async-done | bytes 4194320 | tf_op jit(solution)/shard_map/all_gather | solution.py:450
  350.8 13.7 %attention_backward.1 = bf16[1024,768]{1,0:T(8,128)(2,1)S(1)} custom-call(bf16[1024,256]{1,0:T(8,128)(2,1)S(1)} %copy-done.18, bf16[1024,256]{1,0:T(8,128)(2,1)S(1)} %copy-done.20, bf16[1024,768]{1,0:T(8,128)(2,1)} %copy-done.2, bf16[1024,256]{1,0:T(8,128)(2,1)S(1)} %convolution_convert_fusion.8.context_grad_ref, ...), custom_call_target="tpu_custom_call" | custom-call | flops 1 | bytes 1 | tf_op jit(solution)/shard_map/attention_backward/pallas_call | solution.py:373
  365.3 4.1 convolution_convert_fusion.3
  372.5 7.1 %convolution_convert_fusion.2.terms_ref = bf16[1024,2048]{1,0:T(8,128)(2,1)} fusion(bf16[1024,768]{1,0:T(8,128)(2,1)S(1)} %attention_backward.1, bf16[2048,768]{1,0:T(8,128)(2,1)} %copy-done.29), kind=kOutput, calls=%fused_computation.8 | convolution fusion | flops 3223322624 | bytes 8912896 | tf_op jit(solution)/shard_map/dot_general | solution.py:21
  381.9 8.3 %norm_sums.1 = f32[8,2048]{1,0:T(8,128)S(1)} custom-call(bf16[1024,2048]{1,0:T(8,128)(2,1)S(1)} %bitcast.119, bf16[1024,2048]{1,0:T(8,128)(2,1)} %convolution_convert_fusion.2.terms_ref, f32[1,2048]{1,0:T(1,128)S(1)} %bitcast.120, f32[1,2048]{1,0:T(1,128)S(1)} %slice.185.gain_ref), custom_call_target="tpu_custom_call" | custom-call | flops 1 | bytes 1 | tf_op jit(solution)/shard_map/norm_sums/pallas_call | solution.py:324
  402.8 11.2 %collective-permute-done.40 = f32[8,14,64]{2,1,0:T(8,128)S(1)} collective-permute-done((f32[8,14,64]{2,1,0:T(8,128)S(1)}, f32[8,14,64]{2,1,0:T(8,128)S(1)}, u32[]{:S(2)}, u32[]{:S(2)}) %collective-permute-start.40) | collective-permute-done | bytes 28704 | tf_op jit(solution)/shard_map/ppermute | solution.py:400
  435.0 3.7 collective-permute-start.52
  443.2 13.8 %collective-permute-done.52 = f32[14,64]{1,0:T(8,128)S(1)} collective-permute-done((f32[14,64]{1,0:T(8,128)S(1)}, f32[14,64]{1,0:T(8,128)S(1)}, u32[]{:S(2)}, u32[]{:S(2)}) %collective-permute-start.52) | collective-permute-done | bytes 3616 | tf_op jit(solution)/shard_map/ppermute | solution.py:400
  (410 shorter events, 206.8 us)
Async XLA Ops:
  11.2 46.2 %all-to-all-start = ((bf16[8,80,768]{2,1,0:T(8,128)(2,1)}), bf16[8,80,768]{2,1,0:T(8,128)(2,1)S(1)}, u32[]{:S(2)}, u32[]{:S(2)}) async-start(bf16[8,80,768]{2,1,0:T(8,128)(2,1)} %deal_columns.1), calls=%async_computation | async-start | bytes 1966080 | tf_op jit(solution)/shard_map/all_to_all | solution.py:554
  17.5 60.8 %all-gather.9.cloned.1.call-start = ((), (), s32[]{:S(2)}) async-start(), calls=%async_computation.12 | async-start | bytes 4718592 | tf_op jit(solution)/shard_map/all_gather | solution.py:450
  17.6 31.3 %collective-permute-start.3 = (bf16[176,2048]{1,0:T(8,128)(2,1)}, bf16[176,2048]{1,0:T(8,128)(2,1)S(1)}, u32[]{:S(2)}, u32[]{:S(2)}) collective-permute-start(bf16[176,2048]{1,0:T(8,128)(2,1)} %bitcast.4), channel_id=1, source_target_pairs={{0,8},{8,0},{16,24},{24,16},{1,9},{9,1},{17,25},{25,17},{2,10},{10... | collective-permute-start | bytes 2162696 | tf_op jit(solution)/shard_map/ppermute | solution.py:400
  19.1 29.8 %collective-permute-start.4 = (bf16[176,2048]{1,0:T(8,128)(2,1)}, bf16[176,2048]{1,0:T(8,128)(2,1)S(1)}, u32[]{:S(2)}, u32[]{:S(2)}) collective-permute-start(bf16[176,2048]{1,0:T(8,128)(2,1)} %bitcast.4), channel_id=1, source_target_pairs={{0,16},{8,24},{16,0},{24,8},{1,17},{9,25},{17,1},{25,9},{2,18},{10... | collective-permute-start | bytes 2162696 | tf_op jit(solution)/shard_map/ppermute | solution.py:400
  20.7 21.9 %collective-permute-start = (bf16[64,2048]{1,0:T(8,128)(2,1)S(1)}, bf16[64,2048]{1,0:T(8,128)(2,1)}, u32[]{:S(2)}, u32[]{:S(2)}) collective-permute-start(bf16[64,2048]{1,0:T(8,128)(2,1)S(1)} %copy-done.55), channel_id=1, source_target_pairs={{0,8},{8,0},{16,24},{24,16},{1,9},{9,1},{17,25},{25,17},{2,10},{10... | collective-permute-start | bytes 786440 | tf_op jit(solution)/shard_map/ppermute | solution.py:400
  21.2 27.7 %collective-permute-start.1 = (bf16[64,2048]{1,0:T(8,128)(2,1)S(1)}, bf16[64,2048]{1,0:T(8,128)(2,1)}, u32[]{:S(2)}, u32[]{:S(2)}) collective-permute-start(bf16[64,2048]{1,0:T(8,128)(2,1)S(1)} %copy-done.55), channel_id=1, source_target_pairs={{0,16},{8,24},{16,0},{24,8},{1,17},{9,25},{17,1},{25,9},{2,18},{10... | collective-permute-start | bytes 786440 | tf_op jit(solution)/shard_map/ppermute | solution.py:400
  21.7 27.2 %collective-permute-start.2 = (bf16[64,2048]{1,0:T(8,128)(2,1)S(1)}, bf16[64,2048]{1,0:T(8,128)(2,1)S(1)}, u32[]{:S(2)}, u32[]{:S(2)}) collective-permute-start(bf16[64,2048]{1,0:T(8,128)(2,1)S(1)} %copy-done.55), channel_id=1, source_target_pairs={{0,24},{8,16},{16,8},{24,0},{1,25},{9,17},{17,9},{25,1},{2,26},{10... | collective-permute-start | bytes 786440 | tf_op jit(solution)/shard_map/ppermute | solution.py:400
  24.2 152.1 %reduce-scatter.5.cloned.1.call-start = ((), (), s32[]{:S(2)}) async-start(), calls=%async_computation.6 | async-start | bytes 4718592 | tf_op jit(solution)/shard_map/reduce_scatter | solution.py:454
  61.2 26.1 %collective-permute-start.5 = (bf16[512,768]{1,0:T(8,128)(2,1)S(1)}, bf16[512,768]{1,0:T(8,128)(2,1)S(1)}, u32[]{:S(2)}, u32[]{:S(2)}) collective-permute-start(bf16[512,768]{1,0:T(8,128)(2,1)S(1)} %bitcast.123), channel_id=1, source_target_pairs={{0,8},{8,0},{16,24},{24,16},{1,9},{9,1},{17,25},{25,17},{2,10},{10... | collective-permute-start | bytes 2359304 | tf_op jit(solution)/shard_map/ppermute | solution.py:400
  62.7 24.5 %collective-permute-start.6 = (bf16[512,768]{1,0:T(8,128)(2,1)S(1)}, bf16[512,768]{1,0:T(8,128)(2,1)}, u32[]{:S(2)}, u32[]{:S(2)}) collective-permute-start(bf16[512,768]{1,0:T(8,128)(2,1)S(1)} %bitcast.124), channel_id=1, source_target_pairs={{0,16},{8,24},{16,0},{24,8},{1,17},{9,25},{17,1},{25,9},{2,18},{10... | collective-permute-start | bytes 2359304 | tf_op jit(solution)/shard_map/ppermute | solution.py:400
  78.3 48.2 %collective-permute-start.12 = (bf16[128,2048]{1,0:T(8,128)(2,1)}, bf16[128,2048]{1,0:T(8,128)(2,1)}, u32[]{:S(2)}, u32[]{:S(2)}) collective-permute-start(bf16[128,2048]{1,0:T(8,128)(2,1)} %bitcast.17.base_ref), channel_id=1, source_target_pairs={{0,4},{1,5},{2,6},{3,7},{4,0},{5,1},{6,2},{7,3},{8,12},{9,13},{10,... | collective-permute-start | bytes 1572872 | tf_op jit(solution)/shard_map/ppermute | solution.py:400
  78.3 48.2 %collective-permute-start.13 = (bf16[128,2048]{1,0:T(8,128)(2,1)}, bf16[128,2048]{1,0:T(8,128)(2,1)}, u32[]{:S(2)}, u32[]{:S(2)}) collective-permute-start(bf16[128,2048]{1,0:T(8,128)(2,1)} %bitcast.17.base_ref), channel_id=1, source_target_pairs={{0,6},{1,7},{2,4},{3,5},{4,2},{5,3},{6,0},{7,1},{8,14},{9,15},{10,... | collective-permute-start | bytes 1572872 | tf_op jit(solution)/shard_map/ppermute | solution.py:400
  126.5 97.5 %all-gather.5.cloned.1.call-start = ((), (), s32[]{:S(2)}) async-start(), calls=%async_computation.7 | async-start | bytes 4718592 | tf_op jit(solution)/shard_map/all_gather | solution.py:450
  178.5 115.1 %reduce-scatter.7.cloned.1.call-start = ((), (), s32[]{:S(2)}) async-start(), calls=%async_computation.8 | async-start | bytes 4718592 | tf_op jit(solution)/shard_map/reduce_scatter | solution.py:454
  178.6 25.2 %collective-permute-start.20 = (bf16[176,2048]{1,0:T(8,128)(2,1)}, bf16[176,2048]{1,0:T(8,128)(2,1)S(1)}, u32[]{:S(2)}, u32[]{:S(2)}) collective-permute-start(bf16[176,2048]{1,0:T(8,128)(2,1)} %param.28), channel_id=1, source_target_pairs={{0,8},{8,0},{16,24},{24,16},{1,9},{9,1},{17,25},{25,17},{2,10},{10... | collective-permute-start | bytes 2162696 | tf_op jit(solution)/shard_map/ppermute | solution.py:400
  180.1 23.6 %collective-permute-start.21 = (bf16[176,2048]{1,0:T(8,128)(2,1)}, bf16[176,2048]{1,0:T(8,128)(2,1)S(1)}, u32[]{:S(2)}, u32[]{:S(2)}) collective-permute-start(bf16[176,2048]{1,0:T(8,128)(2,1)} %param.28), channel_id=1, source_target_pairs={{0,16},{8,24},{16,0},{24,8},{1,17},{9,25},{17,1},{25,9},{2,18},{10... | collective-permute-start | bytes 2162696 | tf_op jit(solution)/shard_map/ppermute | solution.py:400
  182.6 19.7 %collective-permute-start.22 = (bf16[88,2048]{1,0:T(8,128)(2,1)S(1)}, bf16[88,2048]{1,0:T(8,128)(2,1)S(1)}, u32[]{:S(2)}, u32[]{:S(2)}) collective-permute-start(bf16[88,2048]{1,0:T(8,128)(2,1)S(1)} %slice.163), channel_id=1, source_target_pairs={{0,8},{8,0},{16,24},{24,16},{1,9},{9,1},{17,25},{25,17},{2,10},{10... | collective-permute-start | bytes 1081352 | tf_op jit(solution)/shard_map/ppermute | solution.py:400
  184.3 19.4 %collective-permute-start.23 = (bf16[88,2048]{1,0:T(8,128)(2,1)S(1)}, bf16[88,2048]{1,0:T(8,128)(2,1)S(1)}, u32[]{:S(2)}, u32[]{:S(2)}) collective-permute-start(bf16[88,2048]{1,0:T(8,128)(2,1)S(1)} %slice.164), channel_id=1, source_target_pairs={{0,16},{8,24},{16,0},{24,8},{1,17},{9,25},{17,1},{25,9},{2,18},{10... | collective-permute-start | bytes 1081352 | tf_op jit(solution)/shard_map/ppermute | solution.py:400
  244.7 99.2 %all-gather.7.cloned.1.call-start = ((), (), s32[]{:S(2)}) async-start(), calls=%async_computation.9 | async-start | bytes 4718592 | tf_op jit(solution)/shard_map/all_gather | solution.py:450
  298.5 116.8 %reduce-scatter.11.cloned.1.call-start = ((), (), s32[]{:S(2)}) async-start(), calls=%async_computation.11 | async-start | bytes 4718592 | tf_op jit(solution)/shard_map/reduce_scatter | solution.py:454
  312.1 20.6 %collective-permute-start.33 = (bf16[176,2048]{1,0:T(8,128)(2,1)S(1)}, bf16[176,2048]{1,0:T(8,128)(2,1)}, u32[]{:S(2)}, u32[]{:S(2)}) collective-permute-start(bf16[176,2048]{1,0:T(8,128)(2,1)S(1)} %pad_maximum_fusion.8), channel_id=1, source_target_pairs={{0,16},{8,24},{16,0},{24,8},{1,17},{9,25},{17,1},{25,9},{2,18},{10... | collective-permute-start | bytes 2162696 | tf_op jit(solution)/shard_map/ppermute | solution.py:400
  343.9 120.4 %reduce-scatter.9.cloned.1.call-start = ((), (), s32[]{:S(2)}) async-start(), calls=%async_computation.10 | async-start | bytes 4718592 | tf_op jit(solution)/shard_map/reduce_scatter | solution.py:454
  344.2 20.2 %collective-permute-start.36 = (bf16[176,2048]{1,0:T(8,128)(2,1)}, bf16[176,2048]{1,0:T(8,128)(2,1)S(1)}, u32[]{:S(2)}, u32[]{:S(2)}) collective-permute-start(bf16[176,2048]{1,0:T(8,128)(2,1)} %pad_maximum_fusion.9), channel_id=1, source_target_pairs={{0,8},{8,0},{16,24},{24,16},{1,9},{9,1},{17,25},{25,17},{2,10},{10... | collective-permute-start | bytes 2162696 | tf_op jit(solution)/shard_map/ppermute | solution.py:400
  345.8 19.6 %collective-permute-start.37 = (bf16[176,2048]{1,0:T(8,128)(2,1)}, bf16[176,2048]{1,0:T(8,128)(2,1)}, u32[]{:S(2)}, u32[]{:S(2)}) collective-permute-start(bf16[176,2048]{1,0:T(8,128)(2,1)} %pad_maximum_fusion.10), channel_id=1, source_target_pairs={{0,16},{8,24},{16,0},{24,8},{1,17},{9,25},{17,1},{25,9},{2,18},{10... | collective-permute-start | bytes 2162696 | tf_op jit(solution)/shard_map/ppermute | solution.py:400
  371.2 19.5 %collective-permute-start.38 = (bf16[512,768]{1,0:T(8,128)(2,1)}, bf16[512,768]{1,0:T(8,128)(2,1)}, u32[]{:S(2)}, u32[]{:S(2)}) collective-permute-start(bf16[512,768]{1,0:T(8,128)(2,1)} %get-tuple-element.259), channel_id=1, source_target_pairs={{0,8},{8,0},{16,24},{24,16},{1,9},{9,1},{17,25},{25,17},{2,10},{10... | collective-permute-start | bytes 2359304 | tf_op jit(solution)/shard_map/ppermute | solution.py:400
  393.0 22.3 %collective-permute-start.43 = (bf16[512,768]{1,0:T(8,128)(2,1)}, bf16[512,768]{1,0:T(8,128)(2,1)S(1)}, u32[]{:S(2)}, u32[]{:S(2)}) collective-permute-start(bf16[512,768]{1,0:T(8,128)(2,1)} %get-tuple-element.275), channel_id=1, source_target_pairs={{0,24},{8,16},{16,8},{24,0},{1,25},{9,17},{17,9},{25,1},{2,26},{10... | collective-permute-start | bytes 2359304 | tf_op jit(solution)/shard_map/ppermute | solution.py:400
  418.0 20.8 %collective-permute-start.48 = (f32[14,64]{1,0:T(8,128)S(1)}, f32[14,64]{1,0:T(8,128)S(1)}, u32[]{:S(2)}, u32[]{:S(2)}) collective-permute-start(f32[14,64]{1,0:T(8,128)S(1)} %get-tuple-element.309), channel_id=1, source_target_pairs={{0,2},{1,3},{2,0},{3,1},{4,6},{5,7},{6,4},{7,5},{8,10},{9,11},{10,... | collective-permute-start | bytes 10760 | tf_op jit(solution)/shard_map/ppermute | solution.py:400
  418.0 20.8 %collective-permute-start.49 = (f32[14,64]{1,0:T(8,128)S(1)}, f32[14,64]{1,0:T(8,128)S(1)}, u32[]{:S(2)}, u32[]{:S(2)}) collective-permute-start(f32[14,64]{1,0:T(8,128)S(1)} %get-tuple-element.310), channel_id=1, source_target_pairs={{0,3},{1,2},{2,1},{3,0},{4,7},{5,6},{6,5},{7,4},{8,11},{9,10},{10,... | collective-permute-start | bytes 10760 | tf_op jit(solution)/shard_map/ppermute | solution.py:400
  419.8 20.4 %collective-permute-start.50 = (f32[14,64]{1,0:T(8,128)S(1)}, f32[14,64]{1,0:T(8,128)S(1)}, u32[]{:S(2)}, u32[]{:S(2)}) collective-permute-start(f32[14,64]{1,0:T(8,128)S(1)} %get-tuple-element.311), channel_id=1, source_target_pairs={{0,4},{1,5},{2,6},{3,7},{4,0},{5,1},{6,2},{7,3},{8,12},{9,13},{10,... | collective-permute-start | bytes 10760 | tf_op jit(solution)/shard_map/ppermute | solution.py:400
  420.7 20.8 %collective-permute-start.51 = (f32[14,64]{1,0:T(8,128)S(1)}, f32[14,64]{1,0:T(8,128)S(1)}, u32[]{:S(2)}, u32[]{:S(2)}) collective-permute-start(f32[14,64]{1,0:T(8,128)S(1)} %get-tuple-element.312), channel_id=1, source_target_pairs={{0,5},{1,4},{2,7},{3,6},{4,1},{5,0},{6,3},{7,2},{8,13},{9,12},{10,... | collective-permute-start | bytes 10760 | tf_op jit(solution)/shard_map/ppermute | solution.py:400
  422.4 36.8 %all-to-all-start.1 = ((bf16[8,64,768]{2,1,0:T(8,128)(2,1)}), bf16[8,64,768]{2,1,0:T(8,128)(2,1)S(1)}, u32[]{:S(2)}, u32[]{:S(2)}) async-start(bf16[8,64,768]{2,1,0:T(8,128)(2,1)} %bitcast.39), calls=%async_computation.5 | async-start | bytes 1572864 | tf_op jit(solution)/shard_map/all_to_all | solution.py:706
  435.0 22.0 %collective-permute-start.52 = (f32[14,64]{1,0:T(8,128)S(1)}, f32[14,64]{1,0:T(8,128)S(1)}, u32[]{:S(2)}, u32[]{:S(2)}) collective-permute-start(f32[14,64]{1,0:T(8,128)S(1)} %get-tuple-element.313), channel_id=1, source_target_pairs={{0,6},{1,7},{2,4},{3,5},{4,2},{5,3},{6,0},{7,1},{8,14},{9,15},{10,... | collective-permute-start | bytes 10760 | tf_op jit(solution)/shard_map/ppermute | solution.py:400
  (102 other events, 1088.7 us)
Sparse Core Ops, SparseCore 0:
  24.3 53.9 all-gather.8
  126.6 49.6 reduce-scatter.4
  178.7 45.3 all-gather.4
  244.8 48.7 reduce-scatter.6
  298.6 45.2 all-gather.6
  346.1 48.7 reduce-scatter.10
  397.1 61.8 reduce-scatter.8
